TPU v7x, 256 devices: a whole 4x4x8 slice. The times are simulated.
256 devices in a mesh: cnec: 8 (over y_lo, x), bus: 16 (over z, y_hi), act: 2 (over core).
Axes of the slice: x: 4, y: 4 (y_hi: 2, y_lo: 2; y = y_hi * 2 + y_lo), z: 8, core: 2. Of those that a mesh axis runs over, the one named last changes fastest.
Arguments:
- nodal_sensitivity: bfloat16 [4096, 131072], P('cnec', 'bus'), may hold values from -1 to 1, as said below
- shift_weight: float32 [131072], P('bus'), may hold values from 0 to 48, as said below
- bus_zone: int32 [131072], P('bus'), may hold values from 0 to 63, as said below
- branch_buses: int32 [2, 4096], replicated, may hold values from 0 to 131071, as said below
- switched_rows: int32 [64, 8], P('act'), may hold values from 0 to 4095, as said below
- net_position: float32 [64], replicated, may hold values from -4 to 4
- flow_limit: float32 [4096], P(('cnec', 'bus')), may hold values from 1 to 4
Outputs:
- zonal_after: float32 [64, 4096, 64], P('act', ('cnec', 'bus'))
- loading: float32 [64, 4096], P('act', ('cnec', 'bus'))
- remaining_margin: float32 [64, 4096], P('act', ('cnec', 'bus'))
Inputs may be any that keep to these rules, and one draw needn't show every extreme that they name: For each CNEC c with branch ends f and t, nodal_sensitivity[c, f] - nodal_sensitivity[c, t] lies between 0.2 and 0.45; every action's coupling has a dominant diagonal. `bus_zone`: every zone holds at least one bus. `branch_buses`: the two buses of a branch differ and lie in one zone; no bus ends two CNEC branches. `switched_rows`: the 8 branches of one action differ. `shift_weight`: every zone holds a bus of positive weight; each weight is 0 or at least 0.5.
All inputs are finite; a program needn't handle non-finite values.
Results may differ from a plain program's by a relative error of at most 0.0016.
Values sent between devices are 32-bit elements; how exact they have to be, the bound alone decides.
No kernel may reach another device: no remote copies, remote signals or barrier semaphores. Data moves between devices by JAX's collectives and lax.ppermute only.
A program may use at most 64 MiB of HBM per device.

v0:
```python
import jax
import jax.numpy as jnp
from jax import lax
from jax.sharding import PartitionSpec as P


def eliminate(coupling, right):
    size = coupling.shape[1]
    positions = jnp.arange(size)
    for pivot in range(size):
        diagonal = coupling[:, pivot, pivot]
        row_now = coupling[:, pivot, :] / diagonal[:, None]
        right_now = right[:, pivot, :] / diagonal[:, None]
        factor = jnp.where(positions[None, :] == pivot, 0.0, coupling[:, :, pivot])
        coupling = coupling - factor[:, :, None] * row_now[:, None, :]
        right = right - factor[:, :, None] * right_now[:, None, :]
        is_pivot = (positions == pivot)[None, :, None]
        coupling = jnp.where(is_pivot, row_now[:, None, :], coupling)
        right = jnp.where(is_pivot, right_now[:, None, :], right)
    return right


def body(
    nodal_sensitivity, shift_weight, bus_zone, branch_buses, switched_rows, net_position, flow_limit
):
    rows_dev, cols_dev = nodal_sensitivity.shape
    zone_count = net_position.shape[0]
    action_count, rank_size = switched_rows.shape
    bus_count = lax.axis_size("bus")
    onehot = (bus_zone[:, None] == jnp.arange(zone_count)[None, :]).astype(jnp.float32)
    zone_total = lax.psum(jnp.sum(onehot * shift_weight[:, None], axis=0), "bus")
    shift_key = (onehot * shift_weight[:, None] / zone_total[None, :]).astype(jnp.bfloat16)
    bus_start = lax.axis_index("bus") * cols_dev
    row_start = lax.axis_index("cnec") * rows_dev
    share_rows = rows_dev // bus_count
    from_local = (branch_buses[0][switched_rows] - bus_start).reshape(-1)
    to_local = (branch_buses[1][switched_rows] - bus_start).reshape(-1)
    from_owned = (from_local >= 0) & (from_local < cols_dev)
    to_owned = (to_local >= 0) & (to_local < cols_dev)
    from_index = jnp.clip(from_local, 0, cols_dev - 1)
    to_index = jnp.clip(to_local, 0, cols_dev - 1)

    def columns(index, owned):
        picked = jnp.take(nodal_sensitivity, index, axis=1).astype(jnp.float32)
        return jnp.where(owned[None, :], picked, 0.0)

    column_diff = columns(from_index, from_owned) - columns(to_index, to_owned)
    zonal_part = jnp.dot(nodal_sensitivity, shift_key, preferred_element_type=jnp.float32)
    zonal_local, diff_local = (
        lax.psum_scatter(zonal_part, "bus", scatter_dimension=0, tiled=True),
        lax.psum_scatter(column_diff, "bus", scatter_dimension=0, tiled=True),
    )
    switched_flat = switched_rows.reshape(-1)
    local_start = row_start + lax.axis_index("bus") * share_rows
    row_local = switched_flat - local_start
    row_owned = (row_local >= 0) & (row_local < share_rows)
    clipped = jnp.clip(row_local, 0, share_rows - 1)
    switched_zonal = jnp.where(
        row_owned[:, None], jnp.take(zonal_local, clipped, axis=0), 0.0
    ).reshape(action_count, rank_size, zone_count)
    diff_rows = jnp.where(row_owned[:, None], jnp.take(diff_local, clipped, axis=0), 0.0)
    diff_rows = diff_rows.reshape(action_count, rank_size, action_count, rank_size)
    coupled_part = jnp.einsum("aiaj->aij", diff_rows)
    coupled, switched_zonal = lax.psum((coupled_part, switched_zonal), ("cnec", "bus"))
    coupling = jnp.eye(rank_size, dtype=jnp.float32)[None, :, :] - coupled
    solved = eliminate(coupling, switched_zonal)
    diff_three = diff_local.reshape(share_rows, action_count, rank_size)
    zonal_after = zonal_local[None, :, :] + jnp.einsum(
        "caj,ajz->acz", diff_three, solved, precision=lax.Precision.HIGHEST
    )
    flow = jnp.einsum("acz,z->ac", zonal_after, net_position, precision=lax.Precision.HIGHEST)
    loading = flow / flow_limit[None, :]
    remaining_margin = flow_limit[None, :] - jnp.abs(flow)
    return (zonal_after, loading, remaining_margin)


def solution(mesh):
    return jax.shard_map(
        body,
        mesh=mesh,
        in_specs=(
            P("cnec", "bus"),
            P("bus"),
            P("bus"),
            P(),
            P("act", None),
            P(),
            P(("cnec", "bus")),
        ),
        out_specs=(
            P("act", ("cnec", "bus"), None),
            P("act", ("cnec", "bus")),
            P("act", ("cnec", "bus")),
        ),
        check_vma=False,
    )
```

profile of v0, /device:TPU:0, one launch (start us, length us, event | category | flops | bytes accessed | tf_op | source)
XLA Modules:
  0.0 1180.1 jit_solution(11334280973626996361)
XLA Ops:
  7.2 1.1 select_reduce_fusion.1
  8.3 43.4 %psum.21 = f32[64]{0:T(128)S(1)} all-reduce(f32[64]{0:T(128)S(1)} %select_reduce_fusion.1), channel_id=1, replica_groups=mesh['cnec'=8,'bus'=16,'act'=2] {'bus'}, use_global_device_ids=true, to_apply=%region_1.0 | all-reduce | flops 64 | bytes 512 | tf_op jit(solution)/shard_map/psum | solution.py:31
  51.7 6.1 convolution_bitcast_fusion
  57.8 0.9 copy.105
  59.0 1.7 gather_fusion
  60.7 1.7 gather_fusion.1
  62.5 12.0 %copy.86 = bf16[512,8192]{0,1:T(8,128)(2,1)} copy(bf16[512,8192]{1,0:T(8,128)(2,1)} %param.9) | data formatting | bytes 16777216 | tf_op args[0]
  74.5 5.7 gather_fusion.4
  80.2 5.7 gather_fusion.5
  85.9 0.2 select_subtract_fusion
  86.1 1.0 copy.107
  87.7 166.7 %reduce-scatter.7.cloned.1.call-done = f32[32,64]{1,0:T(8,128)} async-done(((f32[512,64]{1,0:T(8,128)}), f32[32,64]{1,0:T(8,128)}) %reduce-scatter.7.cloned.1.call-update) | async-done | bytes 8208 | tf_op jit(solution)/shard_map/reduce_scatter | solution.py:50
  254.4 1.4 gather_fusion.2
  255.8 0.8 fusion.13
  256.6 201.9 %reduce-scatter.9.cloned.1.call-done = f32[32,256]{1,0:T(8,128)} async-done(((f32[512,256]{1,0:T(8,128)}), f32[32,256]{1,0:T(8,128)}) %reduce-scatter.9.cloned.1.call-update) | async-done | bytes 32784 | tf_op jit(solution)/shard_map/reduce_scatter | solution.py:51
  458.5 1.7 gather_fusion.3
  460.2 3.6 gather.26
  463.8 3.5 select_reduce_fusion
  467.4 686.4 %psum.23 = f32[32,8,8]{2,0,1:T(8,128)S(1)} all-reduce(f32[32,8,8]{2,0,1:T(8,128)S(1)} %bitcast.69), channel_id=1, replica_groups=mesh['cnec'=8,'bus'=16,'act'=2] {'cnec','bus'}, use_global_device_ids=true, to_apply=%region_6.8 | all-reduce | flops 2048 | bytes 16384 | tf_op jit(solution)/shard_map/psum | solution.py:64
  1154.0 0.2 fusion.12
  1154.4 0.2 slice_reduce_fusion.6
  1154.7 0.2 fusion.11
  1155.1 0.2 slice_reduce_fusion.5
  1155.4 0.2 fusion.10
  1155.6 0.2 subtract_select_fusion.8
  1156.1 0.2 fusion.9
  1156.4 0.2 subtract_select_fusion.6
  1156.9 0.2 fusion.8
  1157.2 0.3 subtract_select_fusion.4
  1157.5 0.2 slice_reduce_fusion.2
  1157.7 0.2 fusion.7
  1158.0 0.3 subtract_select_fusion.2
  1158.3 0.2 slice_reduce_fusion.1
  1158.6 0.2 fusion.6
  1158.9 0.4 subtract_select_fusion
  1159.3 0.2 slice_reduce_fusion
  1159.5 1.0 slice_divide_fusion.14
  1160.5 1.0 subtract_select_fusion.13
  1161.6 1.0 subtract_select_fusion.11
  1162.8 1.1 subtract_select_fusion.9
  1164.0 1.1 subtract_select_fusion.7
  1165.2 1.2 subtract_select_fusion.5
  1166.5 1.2 subtract_select_fusion.3
  1167.9 0.3 copy.104
  1168.2 1.2 subtract_select_fusion.1
  1169.6 1.1 convolution_add_fusion
  1170.8 2.1 fusion.29
  1172.9 0.6 abs_subtract_fusion
  (75 shorter events, 3.7 us)
Async XLA Ops:
  7.2 1163.6 %copy-start = (f32[64]{0:T(128)S(1)}, f32[64]{0:T(128)}, u32[]{:S(2)}) copy-start(f32[64]{0:T(128)} %param.14) | copy-start | bytes 772
  7.2 247.2 %reduce-scatter.7.cloned.1.call-start = ((), (), s32[]{:S(2)}) async-start(), calls=%async_computation.3 | async-start | bytes 278528 | tf_op jit(solution)/shard_map/reduce_scatter | solution.py:50
  51.7 7.1 copy-start.4
  51.7 7.1 copy-start.5
  58.7 399.8 %reduce-scatter.9.cloned.1.call-start = ((), (), s32[]{:S(2)}) async-start(), calls=%async_computation.4 | async-start | bytes 557056 | tf_op jit(solution)/shard_map/reduce_scatter | solution.py:51
  87.1 1072.3 %all-reduce.2.cloned.1.call-start = ((), (), s32[]{:S(2)}) async-start(), calls=%async_computation.2 | async-start | bytes 262144 | tf_op jit(solution)/shard_map/psum | solution.py:64
  467.4 702.1 %copy-start.1 = (f32[32,256]{1,0:T(8,128)S(1)}, f32[32,256]{1,0:T(8,128)}, u32[]{:S(2)}) copy-start(f32[32,256]{1,0:T(8,128)} %reduce-scatter.9.cloned.1.call-done) | copy-start | bytes 98308
  467.4 702.2 %copy-start.2 = (f32[32,64]{1,0:T(8,128)S(1)}, f32[32,64]{1,0:T(8,128)}, u32[]{:S(2)}) copy-start(f32[32,64]{1,0:T(8,128)} %reduce-scatter.7.cloned.1.call-done) | copy-start | bytes 24580
  1154.7 18.2 %copy-start.6 = (f32[32]{0:T(128)S(1)}, f32[32]{0:T(128)}, u32[]{:S(2)}) copy-start(f32[32]{0:T(128)} %param.15) | copy-start | bytes 388
  1170.7 2.8 copy-start.3
Sparse Core Ops, SparseCore 0:
  58.8 195.5 reduce-scatter.6
  259.3 199.2 reduce-scatter.8
  463.9 209.5 all-reduce.1
where the time goes:
time: 1180 us
  blocking collectives  730 us (62%)
  waiting for transfers between devices  369 us (31%)
  local copies, waits for them, and re-layouts  38.3 us (3%)
  other arithmetic  19.6 us (2%)
  between operations  14.3 us (1%)
    psum x1, blocking collectives, body(): lax.psum((coupled_part, switched_zonal), ('cnec', 'bus'))  686 us
    reduce_scatter x1, waiting for transfers between devices, body(): lax.psum_scatter(column_diff, 'bus', scatter_dimension=0, tiled=True)  202 us
    reduce_scatter x1, waiting for transfers between devices, body(): lax.psum_scatter(zonal_part, 'bus', scatter_dimension=0, tiled=True)  167 us
    psum x1, blocking collectives, body(): lax.psum(jnp.sum(onehot * shift_weight[:, None], axis=0), 'bus')  43.4 us
  transfers between devices with their start and end apart: 3, of which 2 were waited for; matrix products, arithmetic and copies ran while one was open for 4% of the time, Pallas kernels for 0%

commit v1 on v0

v1 whole, which is shorter than its diff:
```python
import functools

import jax
import jax.numpy as jnp
from jax import lax
from jax.experimental import pallas as pl
from jax.experimental.pallas import tpu as pltpu
from jax.sharding import PartitionSpec as P

HIGHEST = lax.Precision.HIGHEST
LANES = 128
HALF = 64
SUB = 8
BLOCK = 1024


def iota(shape, dim):
    return lax.broadcasted_iota(jnp.int32, shape, dim)


def dot_nt(x, y, precision=None):
    return lax.dot_general(
        x, y, (((1,), (1,)), ((), ())), precision=precision, preferred_element_type=jnp.float32
    )


def dot(x, y):
    return jnp.dot(x, y, preferred_element_type=jnp.float32)


def pick_rows(local, values):
    pick = jnp.where(iota((local.shape[0], values.shape[0]), 1) == local, 1.0, 0.0)
    pick = pick.astype(jnp.bfloat16)
    high = values.astype(jnp.bfloat16)
    rest = values - high.astype(jnp.float32)
    middle = rest.astype(jnp.bfloat16)
    low = (rest - middle.astype(jnp.float32)).astype(jnp.bfloat16)
    return dot(pick, high) + dot(pick, middle) + dot(pick, low)


def pack_actions(rows):
    return rows.reshape(rows.shape[0] // (2 * SUB), 2, SUB, rows.shape[1])


def total_kernel(zones, weight_ref, zone_ref, out_ref):
    cols = weight_ref.shape[1]
    acc = jnp.zeros((zones, LANES), jnp.float32)
    ids = iota((zones, LANES), 0)
    for start in range(0, cols, LANES):
        weight = weight_ref[:, pl.ds(start, LANES)]
        zone = zone_ref[:, pl.ds(start, LANES)]
        acc += jnp.where(zone == ids, weight, 0.0)
    column = jnp.sum(acc, axis=1, keepdims=True)
    row = jnp.sum(jnp.where(ids == iota((zones, LANES), 1), column, 0.0), axis=0, keepdims=True)
    out_ref[...] = jnp.broadcast_to(row, out_ref.shape)


def column_kernel(
    starts_ref, s_row_ref, s_col_ref, branch_ref, sens_hbm, diff_ref, coup_ref, sens_ref, sems
):
    rows, cols = sens_ref.shape
    picks = s_row_ref.shape[1]
    rank = SUB
    copies = []
    for step in range(cols // BLOCK):
        at = pl.ds(step * BLOCK, BLOCK)
        copies.append(
            pltpu.make_async_copy(sens_hbm.at[:, at], sens_ref.at[:, at], sems.at[step])
        )
        copies[-1].start()

    branches = branch_ref.shape[1]
    s_row = s_row_ref[...]
    found = jnp.zeros((SUB, picks), jnp.float32)
    for start in range(0, branches, BLOCK):
        ends = branch_ref[:, pl.ds(start, BLOCK)]
        pieces = jnp.concatenate(
            [ends >> 12, (ends >> 6) & 63, ends & 63, jnp.zeros_like(ends)], axis=0
        ).astype(jnp.bfloat16)
        onehot = jnp.where(iota((BLOCK, picks), 0) + start == s_row, 1.0, 0.0)
        found += dot(pieces, onehot.astype(jnp.bfloat16))
    ends = found[0:2] * 4096.0 + found[2:4] * 64.0 + found[4:6]
    ends = ends.astype(jnp.int32) - starts_ref[0]

    for step in range(cols // BLOCK):
        at = iota((BLOCK, picks), 0) + step * BLOCK
        select = jnp.where(at == ends[0:1], 1.0, jnp.where(at == ends[1:2], -1.0, 0.0))
        select = select.astype(jnp.bfloat16)
        copies[step].wait()
        part = dot(sens_ref[:, pl.ds(step * BLOCK, BLOCK)], select)
        if step:
            diff_ref[...] += part
        else:
            diff_ref[...] = part

    found = pick_rows(s_col_ref[...] - starts_ref[1], diff_ref[...])
    same = iota((picks, picks), 0) // rank == iota((picks, picks), 1) // rank
    found = jnp.where(same, found, 0.0)
    folded = found[:, 0:LANES]
    for start in range(LANES, picks, LANES):
        folded = folded + found[:, start:start + LANES]
    shift = HALF
    while shift >= rank:
        folded = folded + pltpu.roll(folded, shift, 1)
        shift //= 2
    folded = pack_actions(folded)
    first = iota((1, SUB, LANES), 2) < HALF
    coup_ref[...] = jnp.where(first, folded[:, 0], folded[:, 1])


def zonal_kernel(
    zones, starts_ref, total_ref, weight_ref, zone_ref, s_col_ref, coup_ref, sens_ref, out_ref
):
    rows, cols = sens_ref.shape
    parts = out_ref.shape[0]
    total = total_ref[0:1, :]
    eye = iota((zones, LANES), 0) == iota((zones, LANES), 1)
    column = jnp.sum(jnp.where(eye, total, 0.0), axis=1, keepdims=True)
    zonal = jnp.zeros((rows, zones), jnp.float32)
    for start in range(0, cols, BLOCK):
        at = pl.ds(start, BLOCK)
        key = jnp.where(zone_ref[:, at] == iota((zones, BLOCK), 0), weight_ref[:, at] / column, 0.0)
        zonal += dot_nt(sens_ref[:, at], key.astype(jnp.bfloat16))
    switched = pack_actions(pick_rows(s_col_ref[...] - starts_ref[1], zonal))
    share = zonal.reshape(parts, rows // parts // SUB, SUB, zones)
    lower = starts_ref[2] == 0
    share = [jnp.where(lower, share[:, at], share[:, at + 2]) for at in (0, 1)]
    out_ref[:, 0:SUB, :] = jnp.concatenate(share, axis=2)
    out_ref[:, SUB:2 * SUB, :] = jnp.concatenate([switched[:, 0], switched[:, 1]], axis=2)
    out_ref[:, 2 * SUB:, :] = coup_ref[...]


def solve_kernel(rank, parts_ref, diff_ref, out_ref, sum_ref):
    sum_ref[...] = jnp.sum(diff_ref[...], axis=0)
    right = parts_ref[0:SUB]
    row_id = iota((SUB, LANES), 0)
    lane = iota((SUB, LANES), 1)
    first = lane < HALF
    left = jnp.where(lane % rank == row_id, 1.0, 0.0) - parts_ref[SUB:]
    for pivot in range(rank):
        factor = jnp.where(first, left[:, pivot:pivot + 1], left[:, HALF + pivot:HALF + pivot + 1])
        diagonal = factor[pivot:pivot + 1]
        left_now = left[pivot:pivot + 1] / diagonal
        right_now = right[pivot:pivot + 1] / diagonal
        left = jnp.where(row_id == pivot, left_now, left - factor * left_now)
        right = jnp.where(row_id == pivot, right_now, right - factor * right_now)
    out_ref[...] = jnp.broadcast_to(right[None], out_ref.shape)


def final_kernel(
    rank, starts_ref, mine_ref, other_ref, diff_ref, solved_ref, position_ref, limit_ref,
    after_ref, loading_ref, margin_ref
):
    actions, share, zones = after_ref.shape
    picks = actions * rank
    lower = starts_ref[2] == 0
    mine, other = mine_ref[...], other_ref[...]
    low, high = jnp.where(lower, mine, other), jnp.where(lower, other, mine)
    zonal = jnp.concatenate(
        [low[:, :HALF], low[:, HALF:], high[:, :HALF], high[:, HALF:]], axis=0
    )
    zonal_twice = jnp.concatenate([zonal, zonal], axis=1)
    diff = diff_ref[...]
    first = iota((share, LANES), 1) < HALF
    for pair in range(actions // 2):
        total = zonal_twice
        for j in range(rank):
            at = pair * 2 * rank + j
            factor = jnp.where(first, diff[:, at:at + 1], diff[:, at + rank:at + rank + 1])
            total = total + factor * solved_ref[pair, j:j + 1, :]
        after_ref[2 * pair] = total[:, :HALF]
        after_ref[2 * pair + 1] = total[:, HALF:]
    position = position_ref[...]
    solved = solved_ref[...].reshape(actions // 2 * rank, LANES)
    moved = [
        dot_nt(position, solved[:, at:at + HALF], HIGHEST) for at in (0, HALF)
    ]
    flow = dot_nt(position, zonal, HIGHEST)
    half = picks // 2
    mask = iota((actions, half), 1) // rank == iota((actions, half), 0) // 2
    side = iota((actions, half), 0) % 2 == 0
    diff_pairs = diff.reshape(share, picks)
    spread = [
        jnp.concatenate(
            [diff_pairs[:, (2 * pair + at) * rank:(2 * pair + at + 1) * rank] for pair in range(actions // 2)],
            axis=1,
        )
        for at in (0, 1)
    ]
    flow = (
        flow
        + dot_nt(jnp.where(mask & side, moved[0], 0.0), spread[0], HIGHEST)
        + dot_nt(jnp.where(mask & ~side, moved[1], 0.0), spread[1], HIGHEST)
    )
    limit = limit_ref[...]
    loading_ref[...] = flow / limit
    margin_ref[...] = limit - jnp.abs(flow)


def params():
    return pltpu.CompilerParams(vmem_limit_bytes=48 * 1024 * 1024)


def sum_over(x, axis, size, group, stride):
    total = x
    for offset in range(1, group):
        pairs = []
        for source in range(size):
            place = source // stride % group
            target = source + ((place + offset) % group - place) * stride
            pairs.append((source, target))
        total = total + lax.ppermute(x, axis, pairs)
    return total


def body(
    nodal_sensitivity, shift_weight, bus_zone, branch_buses, switched_rows, net_position, flow_limit
):
    rows, cols = nodal_sensitivity.shape
    zones = net_position.shape[0]
    actions, rank = switched_rows.shape
    picks = actions * rank
    n_bus, n_cnec = lax.axis_size("bus"), lax.axis_size("cnec")
    share = rows // n_bus
    f32 = jnp.float32

    starts = jnp.stack(
        [lax.axis_index("bus") * cols, lax.axis_index("cnec") * rows, lax.axis_index("act")]
    ).astype(jnp.int32)
    weight = shift_weight.reshape(1, cols)
    zone = bus_zone.reshape(1, cols)
    s_row = switched_rows.reshape(1, picks)
    s_col = switched_rows.reshape(picks, 1)
    smem = pl.BlockSpec(memory_space=pltpu.SMEM)
    vmem = pl.BlockSpec(memory_space=pltpu.VMEM)
    hbm = pl.BlockSpec(memory_space=pltpu.HBM)

    total = pl.pallas_call(
        functools.partial(total_kernel, zones),
        out_shape=jax.ShapeDtypeStruct((SUB, LANES), f32),
        in_specs=[vmem, vmem],
        out_specs=vmem,
        compiler_params=params(),
        name="zone_totals",
    )(weight, zone)
    total = sum_over(total, "bus", n_bus, 4, 1)
    total = sum_over(total, "bus", n_bus, n_bus // 4, 4)

    diff, coupled, sens = pl.pallas_call(
        column_kernel,
        out_shape=(
            jax.ShapeDtypeStruct((rows, picks), f32),
            jax.ShapeDtypeStruct((n_bus, SUB, LANES), f32),
            pltpu.VMEM((rows, cols), jnp.bfloat16),
        ),
        in_specs=[smem, vmem, vmem, vmem, hbm],
        out_specs=(vmem, vmem, vmem),
        scratch_shapes=[pltpu.SemaphoreType.DMA((cols // BLOCK,))],
        compiler_params=params(),
        name="columns",
    )(starts, s_row, s_col, branch_buses, nodal_sensitivity)
    sens = pltpu.with_memory_space_constraint(sens, pltpu.VMEM)
    diff = lax.all_to_all(diff.reshape(n_bus, share, picks), "bus", 0, 0, tiled=True)

    partial = pl.pallas_call(
        functools.partial(zonal_kernel, zones),
        out_shape=jax.ShapeDtypeStruct((n_bus, 3 * SUB, LANES), f32),
        in_specs=[smem] + [vmem] * 6,
        out_specs=vmem,
        compiler_params=params(),
        name="zonal",
    )(starts, total, weight, zone, s_col, coupled, sens)
    local = jnp.sum(lax.all_to_all(partial, "bus", 0, 0, tiled=True), axis=0)

    mine = local[0:SUB]
    other = lax.ppermute(mine, "act", [(0, 1), (1, 0)])
    joined = sum_over(local[SUB:], "cnec", n_cnec, n_cnec, 1)
    solved, diff = pl.pallas_call(
        functools.partial(solve_kernel, rank),
        out_shape=(
            jax.ShapeDtypeStruct((n_bus, SUB, LANES), f32),
            jax.ShapeDtypeStruct((share, picks), f32),
        ),
        in_specs=[vmem, vmem],
        out_specs=(vmem, vmem),
        compiler_params=params(),
        name="solve",
    )(joined, diff)
    solved = lax.all_to_all(solved, "bus", 0, 0, tiled=True)

    return pl.pallas_call(
        functools.partial(final_kernel, rank),
        out_shape=(
            jax.ShapeDtypeStruct((actions, share, zones), f32),
            jax.ShapeDtypeStruct((actions, share), f32),
            jax.ShapeDtypeStruct((actions, share), f32),
        ),
        in_specs=[smem] + [vmem] * 6,
        out_specs=(vmem, vmem, vmem),
        compiler_params=params(),
        name="update",
    )(starts, mine, other, diff, solved, net_position.reshape(1, zones), flow_limit.reshape(1, share))


def solution(mesh):
    return jax.shard_map(
        body,
        mesh=mesh,
        in_specs=(
            P("cnec", "bus"),
            P("bus"),
            P("bus"),
            P(),
            P("act", None),
            P(),
            P(("cnec", "bus")),
        ),
        out_specs=(
            P("act", ("cnec", "bus"), None),
            P("act", ("cnec", "bus")),
            P("act", ("cnec", "bus")),
        ),
        check_vma=False,
    )
```

time: 1180 us -> 104 us (0.09)
  the two profiles are of different devices: /device:TPU:0 before, /device:TPU:8 now
where the time goes in v1:
time: 104 us; the launch traced here: 103 us
  starting transfers between devices  40.6 us (39%)
  waiting for transfers between devices  20.5 us (20%)
  Pallas kernels  20 us (19%)
  blocking collectives  16.2 us (16%)
  local copies, waits for them, and re-layouts  3.68 us (4%)
  other arithmetic  1.19 us (1%)
    ppermute x13, starting transfers between devices, sum_over(): total = total + lax.ppermute(x, axis, pairs)  27.2 us
    all_to_all x1, blocking collectives, body(): local = jnp.sum(lax.all_to_all(partial, 'bus', 0, 0, tiled=True), axis=0)  16.2 us
    ppermute x13, waiting for transfers between devices, sum_over(): total = total + lax.ppermute(x, axis, pairs)  10.1 us
    all_to_all x1, starting transfers between devices, body(): solved = lax.all_to_all(solved, 'bus', 0, 0, tiled=True)  9.55 us
    pallas_call x1, Pallas kernels, body(): pl.pallas_call(column_kernel, out_shape=(jax.ShapeDtypeStruct((rows, pick...  9.49 us
    all_to_all x1, waiting for transfers between devices, body(): solved = lax.all_to_all(solved, 'bus', 0, 0, tiled=True)  9.29 us
    pallas_call x1, Pallas kernels, body(): pl.pallas_call(functools.partial(zonal_kernel, zones), out_shape=jax.Shap...  4.77 us
    pallas_call x1, Pallas kernels, body(): pl.pallas_call(functools.partial(final_kernel, rank), out_shape=(jax.Shap...  4.07 us
  transfers between devices with their start and end apart: 16, of which 6 were waited for; matrix products, arithmetic and copies ran while one was open for 3% of the time, Pallas kernels for 9%

profile of v1, /device:TPU:8, one launch (start us, length us, event | category | flops | bytes accessed | tf_op | source)
XLA Modules:
  0.0 103.0 jit_solution(17220217349077958057)
XLA Ops:
  0.6 0.0 copy-start
  0.6 0.7 copy-done
  1.4 0.8 copy-done.1
  2.1 0.4 zone_totals.1
  2.5 3.7 %collective-permute-start.2 = (f32[8,128]{1,0:T(8,128)S(1)}, f32[8,128]{1,0:T(8,128)S(1)}, u32[]{:S(2)}, u32[]{:S(2)}) collective-permute-start(f32[8,128]{1,0:T(8,128)S(1)} %zone_totals.1), channel_id=1, source_target_pairs={{0,6},{2,0},{4,2},{6,4},{8,14},{10,8},{12,10},{14,12},{16,22},{18,... | collective-permute-start | bytes 12296 | tf_op jit(solution)/shard_map/ppermute | solution.py:212
  6.2 0.1 collective-permute-start.1
  6.3 1.7 %collective-permute-start = (f32[8,128]{1,0:T(8,128)S(1)}, f32[8,128]{1,0:T(8,128)S(1)}, u32[]{:S(2)}, u32[]{:S(2)}) collective-permute-start(f32[8,128]{1,0:T(8,128)S(1)} %zone_totals.1), channel_id=1, source_target_pairs={{0,2},{2,4},{4,6},{6,0},{8,10},{10,12},{12,14},{14,8},{16,18},{18,... | collective-permute-start | bytes 12296 | tf_op jit(solution)/shard_map/ppermute | solution.py:212
  8.0 0.0 collective-permute-done.2
  8.0 1.8 %collective-permute-done.1 = f32[8,128]{1,0:T(8,128)S(1)} collective-permute-done((f32[8,128]{1,0:T(8,128)S(1)}, f32[8,128]{1,0:T(8,128)S(1)}, u32[]{:S(2)}, u32[]{:S(2)}) %collective-permute-start.1) | collective-permute-done | bytes 4128 | tf_op jit(solution)/shard_map/ppermute | solution.py:212
  9.8 2.5 %collective-permute-done = f32[8,128]{1,0:T(8,128)S(1)} collective-permute-done((f32[8,128]{1,0:T(8,128)S(1)}, f32[8,128]{1,0:T(8,128)S(1)}, u32[]{:S(2)}, u32[]{:S(2)}) %collective-permute-start) | collective-permute-done | bytes 4128 | tf_op jit(solution)/shard_map/ppermute | solution.py:212
  12.3 6.3 %collective-permute-start.5 = (f32[8,128]{1,0:T(8,128)S(1)}, f32[8,128]{1,0:T(8,128)S(1)}, u32[]{:S(2)}, u32[]{:S(2)}) collective-permute-start(f32[8,128]{1,0:T(8,128)S(1)} %add_add_fusion.2), channel_id=1, source_target_pairs={{0,24},{2,26},{4,28},{6,30},{8,0},{10,2},{12,4},{14,6},{16,8},{18,... | collective-permute-start | bytes 12296 | tf_op jit(solution)/shard_map/ppermute | solution.py:212
  18.6 1.0 collective-permute-start.4
  19.6 2.8 %collective-permute-start.3 = (f32[8,128]{1,0:T(8,128)S(1)}, f32[8,128]{1,0:T(8,128)S(1)}, u32[]{:S(2)}, u32[]{:S(2)}) collective-permute-start(f32[8,128]{1,0:T(8,128)S(1)} %add_add_fusion.2), channel_id=1, source_target_pairs={{0,8},{2,10},{4,12},{6,14},{8,16},{10,18},{12,20},{14,22},{16,24},... | collective-permute-start | bytes 12296 | tf_op jit(solution)/shard_map/ppermute | solution.py:212
  22.4 0.6 pad_add_fusion.starts_ref
  23.0 0.8 copy.12
  23.7 0.7 reshape.30.s_row_ref
  24.4 0.7 reshape.34.s_col_ref
  25.1 9.5 %columns.1 = (f32[512,256]{1,0:T(8,128)}, f32[16,8,128]{2,1,0:T(8,128)}, bf16[512,8192]{1,0:T(8,128)(2,1)S(1)}) custom-call(s32[3]{0:T(128)} %pad_add_fusion.starts_ref, s32[1,256]{1,0:T(1,128)} %reshape.30.s_row_ref, s32[256,1]{1,0:T(8,128)} %reshape.34.s_col_ref, s32[2,4096]{1,0:T(2,128)} %branch_ref.1, bf16[512,8192]{1,0:T(8,128)(2,1)} %sens_hbm.1), custom_call_target="tpu_custom_call" | custom-call | tf_op jit(solution)/shard_map/columns/pallas_call | solution.py:249
  34.6 0.0 collective-permute-done.5
  34.7 0.0 collective-permute-done.4
  34.7 0.0 collective-permute-done.3
  34.7 0.6 add_add_fusion.1.total_ref
  35.3 4.8 %zonal.1 = f32[16,24,128]{2,1,0:T(8,128)} custom-call(s32[3]{0:T(128)} %pad_add_fusion.starts_ref, f32[8,128]{1,0:T(8,128)} %add_add_fusion.1.total_ref, f32[1,8192]{1,0:T(1,128)} %bitcast.8, s32[1,8192]{1,0:T(1,128)} %bitcast.10, s32[256,1]{1,0:T(8,128)} %reshape.34.s_col_ref, f32[16,8,128]{2,1,0:T(8,128)} %get-tuple-element.8.coup_ref, ...), custom_call_target="tpu_custom_call" | custom-call | tf_op jit(solution)/shard_map/zonal/pallas_call | solution.py:265
  40.0 16.2 %all_to_all.15 = f32[16,24,128]{2,1,0:T(8,128)S(1)} all-to-all(f32[16,24,128]{2,1,0:T(8,128)} %zonal.1), channel_id=1, replica_groups=mesh['cnec'=8,'bus'=16,'act'=2] {'bus'}, dimensions={0} | all-to-all | bytes 393216 | tf_op jit(solution)/shard_map/all_to_all | solution.py:273
  56.2 3.8 %all-to-all-start.1 = ((f32[16,32,256]{2,1,0:T(8,128)}), f32[16,32,256]{2,1,0:T(8,128)S(1)}, u32[]{:S(2)}, u32[]{:S(2)}) async-start(f32[16,32,256]{2,1,0:T(8,128)} %bitcast.5), calls=%async_computation.1 | async-start | bytes 1048576 | tf_op jit(solution)/shard_map/all_to_all | solution.py:263
  60.1 3.9 %collective-permute-start.12 = (f32[16,128]{1,0:T(8,128)S(1)}, f32[16,128]{1,0:T(8,128)S(1)}, u32[]{:S(2)}, u32[]{:S(2)}) collective-permute-start(f32[16,128]{1,0:T(8,128)S(1)} %slice.9), channel_id=1, source_target_pairs={{0,192},{32,224},{64,0},{96,32},{128,64},{160,96},{192,128},{224,1... | collective-permute-start | bytes 24584 | tf_op jit(solution)/shard_map/ppermute | solution.py:212
  63.9 0.7 collective-permute-start.11
  64.6 1.4 %collective-permute-start.10 = (f32[16,128]{1,0:T(8,128)S(1)}, f32[16,128]{1,0:T(8,128)S(1)}, u32[]{:S(2)}, u32[]{:S(2)}) collective-permute-start(f32[16,128]{1,0:T(8,128)S(1)} %slice.9), channel_id=1, source_target_pairs={{0,128},{32,160},{64,192},{96,224},{128,0},{160,32},{192,64},{224,... | collective-permute-start | bytes 24584 | tf_op jit(solution)/shard_map/ppermute | solution.py:212
  66.0 1.9 %collective-permute-start.9 = (f32[16,128]{1,0:T(8,128)S(1)}, f32[16,128]{1,0:T(8,128)S(1)}, u32[]{:S(2)}, u32[]{:S(2)}) collective-permute-start(f32[16,128]{1,0:T(8,128)S(1)} %slice.9), channel_id=1, source_target_pairs={{0,96},{32,128},{64,160},{96,192},{128,224},{160,0},{192,32},{224,... | collective-permute-start | bytes 24584 | tf_op jit(solution)/shard_map/ppermute | solution.py:212
  67.9 0.2 collective-permute-start.8
  68.1 0.0 collective-permute-done.12
  68.1 3.6 %collective-permute-start.13 = (f32[16,128]{1,0:T(8,128)S(1)}, f32[16,128]{1,0:T(8,128)S(1)}, u32[]{:S(2)}, u32[]{:S(2)}) collective-permute-start(f32[16,128]{1,0:T(8,128)S(1)} %slice.9), channel_id=1, source_target_pairs={{0,224},{32,0},{64,32},{96,64},{128,96},{160,128},{192,160},{224,1... | collective-permute-start | bytes 24584 | tf_op jit(solution)/shard_map/ppermute | solution.py:212
  71.7 0.0 collective-permute-done.11
  71.7 0.0 collective-permute-start.7
  71.7 0.0 collective-permute-done.10
  71.7 0.0 collective-permute-done.9
  71.7 2.2 %collective-permute-done.8 = f32[16,128]{1,0:T(8,128)S(1)} collective-permute-done((f32[16,128]{1,0:T(8,128)S(1)}, f32[16,128]{1,0:T(8,128)S(1)}, u32[]{:S(2)}, u32[]{:S(2)}) %collective-permute-start.8) | collective-permute-done | bytes 8224 | tf_op jit(solution)/shard_map/ppermute | solution.py:212
  73.9 0.0 collective-permute-done.13
  73.9 3.6 %collective-permute-done.7 = f32[16,128]{1,0:T(8,128)S(1)} collective-permute-done((f32[16,128]{1,0:T(8,128)S(1)}, f32[16,128]{1,0:T(8,128)S(1)}, u32[]{:S(2)}, u32[]{:S(2)}) %collective-permute-start.7) | collective-permute-done | bytes 8224 | tf_op jit(solution)/shard_map/ppermute | solution.py:212
  77.5 0.0 all-to-all-done.1.diff_ref
  77.5 1.3 %solve.1 = (f32[16,8,128]{2,1,0:T(8,128)}, f32[32,256]{1,0:T(8,128)S(1)}) custom-call(f32[16,128]{1,0:T(8,128)S(1)} %add_add_fusion.parts_ref, f32[16,32,256]{2,1,0:T(8,128)S(1)} %all-to-all-done.1.diff_ref), custom_call_target="tpu_custom_call" | custom-call | tf_op jit(solution)/shard_map/solve/pallas_call | solution.py:278
  78.8 9.5 %all-to-all-start.2 = ((f32[16,8,128]{2,1,0:T(8,128)}), f32[16,8,128]{2,1,0:T(8,128)S(1)}, u32[]{:S(2)}, u32[]{:S(2)}) async-start(f32[16,8,128]{2,1,0:T(8,128)} %get-tuple-element.12), calls=%async_computation.2 | async-start | bytes 131072 | tf_op jit(solution)/shard_map/all_to_all | solution.py:289
  88.3 0.1 collective-permute-start.6
  88.4 1.2 %collective-permute-done.6.other_ref = f32[8,128]{1,0:T(8,128)S(1)} collective-permute-done((f32[8,128]{1,0:T(8,128)S(1)}, f32[8,128]{1,0:T(8,128)S(1)}, u32[]{:S(2)}, u32[]{:S(2)}) %collective-permute-start.6) | collective-permute-done | bytes 4128 | tf_op jit(solution)/shard_map/ppermute | solution.py:276
  89.6 9.3 %all-to-all-done.2.solved_ref = f32[16,8,128]{2,1,0:T(8,128)S(1)} async-done(((f32[16,8,128]{2,1,0:T(8,128)}), f32[16,8,128]{2,1,0:T(8,128)S(1)}, u32[]{:S(2)}, u32[]{:S(2)}) %all-to-all-start.2) | async-done | bytes 65568 | tf_op jit(solution)/shard_map/all_to_all | solution.py:289
  98.9 0.0 copy-done.2
  98.9 0.0 copy-done.3
  98.9 4.1 %update.1 = (f32[32,32,64]{2,1,0:T(8,128)}, f32[32,32]{1,0:T(8,128)}, f32[32,32]{1,0:T(8,128)}) custom-call(s32[3]{0:T(128)S(1)} %copy-done.2, f32[8,128]{1,0:T(8,128)S(1)} %slice.8.mine_ref, f32[8,128]{1,0:T(8,128)S(1)} %collective-permute-done.6.other_ref, f32[32,256]{1,0:T(8,128)S(1)} %get-tuple-element.11.diff_ref, ...), custom_call_target="tpu_custom_call" | custom-call | tf_op jit(solution)/shard_map/update/pallas_call | solution.py:291
  (10 shorter events, 0.1 us)
Async XLA Ops:
  0.6 0.8 copy-start
  1.4 0.8 copy-start.1
  2.5 5.5 %collective-permute-start.2 = (f32[8,128]{1,0:T(8,128)S(1)}, f32[8,128]{1,0:T(8,128)S(1)}, u32[]{:S(2)}, u32[]{:S(2)}) collective-permute-start(f32[8,128]{1,0:T(8,128)S(1)} %zone_totals.1), channel_id=1, source_target_pairs={{0,6},{2,0},{4,2},{6,4},{8,14},{10,8},{12,10},{14,12},{16,22},{18,... | collective-permute-start | bytes 12296 | tf_op jit(solution)/shard_map/ppermute | solution.py:212
  6.2 3.6 %collective-permute-start.1 = (f32[8,128]{1,0:T(8,128)S(1)}, f32[8,128]{1,0:T(8,128)S(1)}, u32[]{:S(2)}, u32[]{:S(2)}) collective-permute-start(f32[8,128]{1,0:T(8,128)S(1)} %zone_totals.1), channel_id=1, source_target_pairs={{0,4},{2,6},{4,0},{6,2},{8,12},{10,14},{12,8},{14,10},{16,20},{18,... | collective-permute-start | bytes 12296 | tf_op jit(solution)/shard_map/ppermute | solution.py:212
  6.3 6.0 %collective-permute-start = (f32[8,128]{1,0:T(8,128)S(1)}, f32[8,128]{1,0:T(8,128)S(1)}, u32[]{:S(2)}, u32[]{:S(2)}) collective-permute-start(f32[8,128]{1,0:T(8,128)S(1)} %zone_totals.1), channel_id=1, source_target_pairs={{0,2},{2,4},{4,6},{6,0},{8,10},{10,12},{12,14},{14,8},{16,18},{18,... | collective-permute-start | bytes 12296 | tf_op jit(solution)/shard_map/ppermute | solution.py:212
  12.3 22.3 %collective-permute-start.5 = (f32[8,128]{1,0:T(8,128)S(1)}, f32[8,128]{1,0:T(8,128)S(1)}, u32[]{:S(2)}, u32[]{:S(2)}) collective-permute-start(f32[8,128]{1,0:T(8,128)S(1)} %add_add_fusion.2), channel_id=1, source_target_pairs={{0,24},{2,26},{4,28},{6,30},{8,0},{10,2},{12,4},{14,6},{16,8},{18,... | collective-permute-start | bytes 12296 | tf_op jit(solution)/shard_map/ppermute | solution.py:212
  18.6 16.1 %collective-permute-start.4 = (f32[8,128]{1,0:T(8,128)S(1)}, f32[8,128]{1,0:T(8,128)S(1)}, u32[]{:S(2)}, u32[]{:S(2)}) collective-permute-start(f32[8,128]{1,0:T(8,128)S(1)} %add_add_fusion.2), channel_id=1, source_target_pairs={{0,16},{2,18},{4,20},{6,22},{8,24},{10,26},{12,28},{14,30},{16,0},... | collective-permute-start | bytes 12296 | tf_op jit(solution)/shard_map/ppermute | solution.py:212
  19.6 15.1 %collective-permute-start.3 = (f32[8,128]{1,0:T(8,128)S(1)}, f32[8,128]{1,0:T(8,128)S(1)}, u32[]{:S(2)}, u32[]{:S(2)}) collective-permute-start(f32[8,128]{1,0:T(8,128)S(1)} %add_add_fusion.2), channel_id=1, source_target_pairs={{0,8},{2,10},{4,12},{6,14},{8,16},{10,18},{12,20},{14,22},{16,24},... | collective-permute-start | bytes 12296 | tf_op jit(solution)/shard_map/ppermute | solution.py:212
  25.1 73.7 %copy-start.2 = (s32[3]{0:T(128)S(1)}, s32[3]{0:T(128)}, u32[]{:S(2)}) copy-start(s32[3]{0:T(128)} %pad_add_fusion.starts_ref) | copy-start | bytes 40
  25.1 73.7 %copy-start.3 = (f32[64]{0:T(128)S(1)}, f32[64]{0:T(128)}, u32[]{:S(2)}) copy-start(f32[64]{0:T(128)} %param.12) | copy-start | bytes 772
  25.1 73.7 %copy-start.4 = (f32[32]{0:T(128)S(1)}, f32[32]{0:T(128)}, u32[]{:S(2)}) copy-start(f32[32]{0:T(128)} %param.13) | copy-start | bytes 388
  56.2 21.2 %all-to-all-start.1 = ((f32[16,32,256]{2,1,0:T(8,128)}), f32[16,32,256]{2,1,0:T(8,128)S(1)}, u32[]{:S(2)}, u32[]{:S(2)}) async-start(f32[16,32,256]{2,1,0:T(8,128)} %bitcast.5), calls=%async_computation.1 | async-start | bytes 1048576 | tf_op jit(solution)/shard_map/all_to_all | solution.py:263
  60.1 8.0 %collective-permute-start.12 = (f32[16,128]{1,0:T(8,128)S(1)}, f32[16,128]{1,0:T(8,128)S(1)}, u32[]{:S(2)}, u32[]{:S(2)}) collective-permute-start(f32[16,128]{1,0:T(8,128)S(1)} %slice.9), channel_id=1, source_target_pairs={{0,192},{32,224},{64,0},{96,32},{128,64},{160,96},{192,128},{224,1... | collective-permute-start | bytes 24584 | tf_op jit(solution)/shard_map/ppermute | solution.py:212
  63.9 7.8 %collective-permute-start.11 = (f32[16,128]{1,0:T(8,128)S(1)}, f32[16,128]{1,0:T(8,128)S(1)}, u32[]{:S(2)}, u32[]{:S(2)}) collective-permute-start(f32[16,128]{1,0:T(8,128)S(1)} %slice.9), channel_id=1, source_target_pairs={{0,160},{32,192},{64,224},{96,0},{128,32},{160,64},{192,96},{224,1... | collective-permute-start | bytes 24584 | tf_op jit(solution)/shard_map/ppermute | solution.py:212
  64.6 7.1 %collective-permute-start.10 = (f32[16,128]{1,0:T(8,128)S(1)}, f32[16,128]{1,0:T(8,128)S(1)}, u32[]{:S(2)}, u32[]{:S(2)}) collective-permute-start(f32[16,128]{1,0:T(8,128)S(1)} %slice.9), channel_id=1, source_target_pairs={{0,128},{32,160},{64,192},{96,224},{128,0},{160,32},{192,64},{224,... | collective-permute-start | bytes 24584 | tf_op jit(solution)/shard_map/ppermute | solution.py:212
  66.0 5.7 %collective-permute-start.9 = (f32[16,128]{1,0:T(8,128)S(1)}, f32[16,128]{1,0:T(8,128)S(1)}, u32[]{:S(2)}, u32[]{:S(2)}) collective-permute-start(f32[16,128]{1,0:T(8,128)S(1)} %slice.9), channel_id=1, source_target_pairs={{0,96},{32,128},{64,160},{96,192},{128,224},{160,0},{192,32},{224,... | collective-permute-start | bytes 24584 | tf_op jit(solution)/shard_map/ppermute | solution.py:212
  67.9 6.1 %collective-permute-start.8 = (f32[16,128]{1,0:T(8,128)S(1)}, f32[16,128]{1,0:T(8,128)S(1)}, u32[]{:S(2)}, u32[]{:S(2)}) collective-permute-start(f32[16,128]{1,0:T(8,128)S(1)} %slice.9), channel_id=1, source_target_pairs={{0,64},{32,96},{64,128},{96,160},{128,192},{160,224},{192,0},{224,... | collective-permute-start | bytes 24584 | tf_op jit(solution)/shard_map/ppermute | solution.py:212
  68.1 5.8 %collective-permute-start.13 = (f32[16,128]{1,0:T(8,128)S(1)}, f32[16,128]{1,0:T(8,128)S(1)}, u32[]{:S(2)}, u32[]{:S(2)}) collective-permute-start(f32[16,128]{1,0:T(8,128)S(1)} %slice.9), channel_id=1, source_target_pairs={{0,224},{32,0},{64,32},{96,64},{128,96},{160,128},{192,160},{224,1... | collective-permute-start | bytes 24584 | tf_op jit(solution)/shard_map/ppermute | solution.py:212
  71.7 5.8 %collective-permute-start.7 = (f32[16,128]{1,0:T(8,128)S(1)}, f32[16,128]{1,0:T(8,128)S(1)}, u32[]{:S(2)}, u32[]{:S(2)}) collective-permute-start(f32[16,128]{1,0:T(8,128)S(1)} %slice.9), channel_id=1, source_target_pairs={{0,32},{32,64},{64,96},{96,128},{128,160},{160,192},{192,224},{224... | collective-permute-start | bytes 24584 | tf_op jit(solution)/shard_map/ppermute | solution.py:212
  78.8 20.1 %all-to-all-start.2 = ((f32[16,8,128]{2,1,0:T(8,128)}), f32[16,8,128]{2,1,0:T(8,128)S(1)}, u32[]{:S(2)}, u32[]{:S(2)}) async-start(f32[16,8,128]{2,1,0:T(8,128)} %get-tuple-element.12), calls=%async_computation.2 | async-start | bytes 131072 | tf_op jit(solution)/shard_map/all_to_all | solution.py:289
  88.3 1.3 %collective-permute-start.6 = (f32[8,128]{1,0:T(8,128)S(1)}, f32[8,128]{1,0:T(8,128)S(1)}, u32[]{:S(2)}, u32[]{:S(2)}) collective-permute-start(f32[8,128]{1,0:T(8,128)S(1)} %slice.8.mine_ref), channel_id=1, source_target_pairs={{0,1},{1,0},{2,3},{3,2},{4,5},{5,4},{6,7},{7,6},{8,9},{9,8},{10,11... | collective-permute-start | bytes 12296 | tf_op jit(solution)/shard_map/ppermute | solution.py:276

commit v2 on v0

v2 whole, which is shorter than its diff:
```python
import jax
import jax.numpy as jnp
from jax import lax
from jax.experimental import pallas as pl
from jax.experimental.pallas import tpu as pltpu
from jax.sharding import Mesh
from jax.sharding import PartitionSpec as P

HIGHEST = lax.Precision.HIGHEST
LANES = 128
HALF = 64
SUB = 8
BLOCK = 1024
CNEC, BUS = ("yl", "x"), ("z", "yh")
PLANE = ("yl", "x", "yh")


def iota(shape, dim):
    return lax.broadcasted_iota(jnp.int32, shape, dim)


def dot_nt(x, y, precision=None):
    return lax.dot_general(
        x, y, (((1,), (1,)), ((), ())), precision=precision, preferred_element_type=jnp.float32
    )


def dot(x, y, precision=None):
    return jnp.dot(x, y, precision=precision, preferred_element_type=jnp.float32)


def three_parts(values):
    high = values.astype(jnp.bfloat16)
    rest = values - high.astype(jnp.float32)
    middle = rest.astype(jnp.bfloat16)
    return high, middle, (rest - middle.astype(jnp.float32)).astype(jnp.bfloat16)


def digits(values, base, count):
    return [((values >> (base * at)) & ((1 << base) - 1)).astype(jnp.float32).astype(jnp.bfloat16)
            for at in reversed(range(count))]


def partial_kernel(
    swt_hbm, branch_hbm, weight_hbm, zone_hbm, sens_hbm, pay_ref,
    swt_ref, branch_ref, weight_ref, zone_ref, sens_ref, acc_ref, zonal_ref, total_ref, sems
):
    rows, cols = sens_ref.shape
    rank, actions = swt_ref.shape
    picks = rank * actions
    zones = HALF
    steps = cols // BLOCK
    small = [
        pltpu.make_async_copy(source, target, sems.at[steps + at])
        for at, (source, target) in enumerate(
            [(swt_hbm, swt_ref), (branch_hbm, branch_ref), (weight_hbm, weight_ref), (zone_hbm, zone_ref)]
        )
    ]
    for copy in small:
        copy.start()

    def block_copy(step):
        at = pl.ds(pl.multiple_of(step * BLOCK, BLOCK), BLOCK)
        return pltpu.make_async_copy(sens_hbm.at[:, at], sens_ref.at[:, at], sems.at[step])

    for step in range(steps):
        block_copy(step).start()

    bus_start = lax.axis_index(BUS) * cols
    row_start = lax.axis_index(CNEC) * rows
    acc_ref[...] = jnp.zeros_like(acc_ref)
    zonal_ref[...] = jnp.zeros_like(zonal_ref)
    total_ref[...] = jnp.zeros_like(total_ref)

    for copy in small[:2]:
        copy.wait()
    swt = swt_ref[...]
    pick_id = iota((picks, actions), 0)
    of_action = pick_id % LANES // rank * 2 + pick_id // LANES == iota((picks, actions), 1)
    of_action = jnp.where(of_action, 1.0, 0.0).astype(jnp.bfloat16)
    high, low = digits(swt, 6, 2)
    column = dot_nt(of_action, high) * 64.0 + dot_nt(of_action, low)
    column = jnp.where(iota((picks, rank), 0) % rank == iota((picks, rank), 1), column, 0.0)
    column = jnp.sum(column, axis=1, keepdims=True).astype(jnp.int32)
    row = dot_nt(high, of_action) * 64.0 + dot_nt(low, of_action)
    row = jnp.where(iota((rank, picks), 1) % rank == iota((rank, picks), 0), row, 0.0)
    row = jnp.sum(row, axis=0, keepdims=True).astype(jnp.int32)

    tiles = branch_ref.shape[1] // LANES
    table = jnp.concatenate(
        [branch_ref[:, at * LANES:(at + 1) * LANES] for at in range(tiles)], axis=0
    )
    onehot = jnp.where(iota((LANES, picks), 0) == row % LANES, 1.0, 0.0).astype(jnp.bfloat16)
    high, middle, low = [dot(part, onehot) for part in digits(table, 6, 3)]
    found = high * 4096.0 + middle * 64.0 + low
    line = iota((2 * tiles, picks), 0) - row // LANES * 2
    ends = [
        jnp.sum(jnp.where(line == end, found, 0.0), axis=0, keepdims=True).astype(jnp.int32)
        - bus_start
        for end in (0, 1)
    ]
    for copy in small[2:]:
        copy.wait()

    def step_body(step, carry):
        at = pl.ds(pl.multiple_of(step * BLOCK, BLOCK), BLOCK)
        bus = iota((BLOCK, picks), 0)
        first, second = [end - step * BLOCK for end in ends]
        select = jnp.where(bus == first, 1.0, jnp.where(bus == second, -1.0, 0.0))
        select = select.astype(jnp.bfloat16)
        inside = zone_ref[:, at] == iota((zones, BLOCK), 0)
        weight = weight_ref[:, at]
        part = jnp.where(inside, weight, 0.0)
        total = part[:, 0:LANES]
        for start in range(LANES, BLOCK, LANES):
            total = total + part[:, start:start + LANES]
        total_ref[...] += total
        high = weight.astype(jnp.bfloat16).astype(jnp.float32)
        key = jnp.concatenate(
            [jnp.where(inside, high, 0.0), jnp.where(inside, weight - high, 0.0)], axis=0
        ).astype(jnp.bfloat16)
        block_copy(step).wait()
        sens = sens_ref[:, at]
        acc_ref[...] += dot(sens, select)
        zonal_ref[...] += dot_nt(sens, key)
        return carry

    lax.fori_loop(0, steps, step_body, 0)

    chunks = pay_ref.shape[0]
    diff = acc_ref[...]
    zonal = zonal_ref[:, 0:zones] + zonal_ref[:, zones:2 * zones]
    choose = jnp.where(iota((picks, rows), 1) == column - row_start, 1.0, 0.0).astype(jnp.bfloat16)
    switched = dot(choose, jnp.concatenate(three_parts(zonal), axis=1))
    switched = switched[:, 0:zones] + switched[:, zones:2 * zones] + switched[:, 2 * zones:]
    high, middle, low = [dot(choose, part) for part in three_parts(diff)]
    coupled = high + middle + low
    same = iota((picks, picks), 0) // rank == iota((picks, picks), 1) // rank
    coupled = jnp.where(same, coupled, 0.0)
    pick_id = iota((picks, LANES), 0)
    lane = (pick_id // rank % 2 * 2 + pick_id // LANES) * rank + pick_id % rank
    fold = jnp.where(lane == iota((picks, LANES), 1), 1.0, 0.0).astype(jnp.bfloat16)
    high, middle, low = [dot(part, fold) for part in three_parts(coupled)]
    coupled = jnp.sum((high + middle + low).reshape(2, chunks, 2, SUB, LANES), axis=(0, 2))
    total = jnp.sum(total_ref[...], axis=1, keepdims=True)
    eye = iota((zones, LANES), 0) == iota((zones, LANES), 1) - HALF
    total = jnp.sum(jnp.where(eye, total, 0.0), axis=0, keepdims=True)

    share = zonal.reshape(chunks, 2, 2, 2, SUB, zones)
    share = jnp.where(lax.axis_index("act") == 0, share[:, :, 0], share[:, :, 1])
    share = jnp.concatenate([share[:, :, 0], share[:, :, 1]], axis=-1)
    switched = switched.reshape(2, actions // 2, rank, zones)
    switched = jnp.concatenate([switched[0], switched[1]], axis=-1)
    half = rows // chunks // 2
    diff = diff.reshape(chunks, 2, half, picks)
    part = SUB + 2 * half
    for at in range(2):
        start = at * part
        pay_ref[:, start:start + SUB, :] = share[:, at]
        pay_ref[:, start + SUB:start + SUB + half, :] = diff[:, at, :, 0:LANES]
        pay_ref[:, start + SUB + half:start + part, :] = diff[:, at, :, LANES:]
    start = 2 * part
    pay_ref[:, start:start + 2 * SUB, :] = switched.reshape(chunks, 2 * SUB, LANES)
    pay_ref[:, start + 2 * SUB:, :] = coupled + total


def solve_kernel(parts_ref, out_ref, total_ref):
    full = jnp.sum(parts_ref[...], axis=0)
    extra = full[2 * SUB:]
    total = extra[0:1, HALF:] / lax.axis_size(CNEC)
    total = jnp.concatenate([total, total], axis=1)
    total_ref[...] = jnp.broadcast_to(total, total_ref.shape)
    row_id = iota((SUB, LANES), 0)
    lane = iota((SUB, LANES), 1)
    eye = jnp.where(lane % SUB == row_id, 1.0, 0.0)
    source = iota((LANES, LANES), 0)
    target = iota((LANES, LANES), 1)
    for tile in range(2):
        spread = (source // SUB == tile * 2 + target // HALF) & (source % SUB == target % SUB)
        left = eye - dot(extra, jnp.where(spread, 1.0, 0.0), HIGHEST)
        right = full[tile * SUB:(tile + 1) * SUB] / total
        for pivot in range(SUB):
            factor = jnp.where(
                lane < HALF, left[:, pivot:pivot + 1], left[:, HALF + pivot:HALF + pivot + 1]
            )
            diagonal = factor[pivot:pivot + 1]
            left_now = left[pivot:pivot + 1] / diagonal
            right_now = right[pivot:pivot + 1] / diagonal
            left = jnp.where(row_id == pivot, left_now, left - factor * left_now)
            right = jnp.where(row_id == pivot, right_now, right - factor * right_now)
        out_ref[:, tile * SUB:(tile + 1) * SUB, :] = jnp.broadcast_to(
            right[None], (out_ref.shape[0], SUB, LANES)
        )


def final_kernel(
    mine_ref, theirs_ref, other_ref, total_ref, solved_ref, position_ref, limit_ref,
    after_ref, loading_ref, margin_ref
):
    actions, share, zones = after_ref.shape
    pairs = actions // 2
    lower = lax.axis_index("act") == 0
    whole = mine_ref[...] + theirs_ref[...]
    mine, other = whole[0:SUB], other_ref[...]
    low, high = jnp.where(lower, mine, other), jnp.where(lower, other, mine)
    zonal = jnp.concatenate(
        [low[:, :HALF], low[:, HALF:], high[:, :HALF], high[:, HALF:]], axis=0
    ) / total_ref[0:1, :HALF]
    zonal_twice = jnp.concatenate([zonal, zonal], axis=1)
    even, odd = whole[SUB:SUB + share], whole[SUB + share:]
    first = iota((share, LANES), 1) < HALF
    for pair in range(pairs):
        total = zonal_twice
        for j in range(SUB):
            at = pair * SUB + j
            factor = jnp.where(first, even[:, at:at + 1], odd[:, at:at + 1])
            total = total + factor * solved_ref[pair, j:j + 1, :]
        after_ref[2 * pair] = total[:, :HALF]
        after_ref[2 * pair + 1] = total[:, HALF:]
    position = position_ref[...]
    solved = solved_ref[...].reshape(pairs * SUB, LANES)
    flow = dot_nt(position, zonal, HIGHEST)
    shape = (actions, pairs * SUB)
    same = iota(shape, 1) // SUB == iota(shape, 0) // 2
    for side, part in enumerate((even, odd)):
        moved = dot_nt(position, solved[:, side * HALF:(side + 1) * HALF], HIGHEST)
        mask = same & (iota(shape, 0) % 2 == side)
        flow = flow + dot_nt(jnp.where(mask, moved, 0.0), part, HIGHEST)
    limit = limit_ref[...]
    loading_ref[...] = flow / limit
    margin_ref[...] = limit - jnp.abs(flow)


def params():
    return pltpu.CompilerParams(vmem_limit_bytes=48 * 1024 * 1024)


def body(
    nodal_sensitivity, shift_weight, bus_zone, branch_buses, switched_rows, net_position, flow_limit
):
    rows, cols = nodal_sensitivity.shape
    zones = net_position.shape[0]
    actions, rank = switched_rows.shape
    picks = actions * rank
    n_z, n_yh, n_plane = lax.axis_size("z"), lax.axis_size("yh"), lax.axis_size(PLANE)
    share = rows // n_z // n_yh
    f32, i32 = jnp.float32, jnp.int32
    vmem = pl.BlockSpec(memory_space=pltpu.VMEM)
    hbm = pl.BlockSpec(memory_space=pltpu.HBM)

    part = SUB + 2 * share
    pay = pl.pallas_call(
        partial_kernel,
        out_shape=jax.ShapeDtypeStruct((n_z, n_yh * part + 3 * SUB, LANES), f32),
        in_specs=[hbm] * 5,
        out_specs=vmem,
        scratch_shapes=[
            pltpu.VMEM((rank, actions), i32),
            pltpu.VMEM(branch_buses.shape, i32),
            pltpu.VMEM((1, cols), f32),
            pltpu.VMEM((1, cols), i32),
            pltpu.VMEM((rows, cols), jnp.bfloat16),
            pltpu.VMEM((rows, picks), f32),
            pltpu.VMEM((rows, 2 * zones), f32),
            pltpu.VMEM((zones, LANES), f32),
            pltpu.SemaphoreType.DMA((cols // BLOCK + 4,)),
        ],
        compiler_params=params(),
        name="partials",
    )(
        *[
            pltpu.with_memory_space_constraint(x, pltpu.HBM)
            for x in (
                switched_rows.T, branch_buses, shift_weight.reshape(1, cols),
                bus_zone.reshape(1, cols), nodal_sensitivity,
            )
        ]
    )

    local = jnp.sum(lax.all_to_all(pay, "z", 0, 0, tiled=True), axis=0)
    spread = jnp.broadcast_to(local[n_yh * part:][None], (n_plane, 3 * SUB, LANES))
    spread = lax.all_to_all(spread, PLANE, 0, 0, tiled=True)

    swap = [(0, 1), (1, 0)]
    here = lax.axis_index("yh")
    mine = lax.dynamic_slice_in_dim(local, here * part, part)
    theirs = lax.ppermute(lax.dynamic_slice_in_dim(local, (1 - here) * part, part), "yh", swap)
    other = lax.ppermute(mine[:SUB] + theirs[:SUB], "act", swap)

    solved, total = pl.pallas_call(
        solve_kernel,
        out_shape=(
            jax.ShapeDtypeStruct((n_z, 2 * SUB, LANES), f32),
            jax.ShapeDtypeStruct((SUB, LANES), f32),
        ),
        in_specs=[vmem],
        out_specs=(vmem, vmem),
        compiler_params=params(),
        name="solve",
    )(spread)
    solved = lax.all_to_all(solved, "z", 0, 0, tiled=True).reshape(actions // 2, SUB, LANES)

    return pl.pallas_call(
        final_kernel,
        out_shape=(
            jax.ShapeDtypeStruct((actions, share, zones), f32),
            jax.ShapeDtypeStruct((actions, share), f32),
            jax.ShapeDtypeStruct((actions, share), f32),
        ),
        in_specs=[vmem] * 7,
        out_specs=(vmem, vmem, vmem),
        compiler_params=params(),
        name="update",
    )(
        mine, theirs, other, total, solved,
        net_position.reshape(1, zones), flow_limit.reshape(1, share),
    )


def solution(mesh):
    n_cnec, n_bus, n_act = mesh.devices.shape
    split = Mesh(
        mesh.devices.reshape(2, n_cnec // 2, n_bus // 2, 2, n_act), ("yl", "x", "z", "yh", "act")
    )
    return jax.shard_map(
        body,
        mesh=split,
        in_specs=(
            P(CNEC, BUS),
            P(BUS),
            P(BUS),
            P(),
            P("act", None),
            P(),
            P(CNEC + BUS),
        ),
        out_specs=(
            P("act", CNEC + BUS, None),
            P("act", CNEC + BUS),
            P("act", CNEC + BUS),
        ),
        check_vma=False,
    )
```

time: 1180 us -> 73.7 us (0.06)
  the two profiles are of different devices: /device:TPU:0 before, /device:TPU:6 now
where the time goes in v2:
time: 73.7 us; the launch traced here: 72.6 us
  blocking collectives  29.3 us (40%)
  Pallas kernels  16.5 us (22%)
  starting transfers between devices  13.9 us (19%)
  waiting for transfers between devices  11.5 us (16%)
    all_to_all x1, blocking collectives, body(): local = jnp.sum(lax.all_to_all(pay, 'z', 0, 0, tiled=True), axis=0)  29.3 us
    pallas_call x1, Pallas kernels, body(): pl.pallas_call(partial_kernel, out_shape=jax.ShapeDtypeStruct((n_z, n_yh...  11.7 us
    all_to_all x1, starting transfers between devices, body(): spread = lax.all_to_all(spread, PLANE, 0, 0, tiled=True)  7.42 us
    all_to_all x1, waiting for transfers between devices, body(): lax.all_to_all(solved, 'z', 0, 0, tiled=True)  7.01 us
    all_to_all x1, starting transfers between devices, body(): lax.all_to_all(solved, 'z', 0, 0, tiled=True)  3.35 us
    all_to_all x1, waiting for transfers between devices, body(): spread = lax.all_to_all(spread, PLANE, 0, 0, tiled=True)  3.3 us
    pallas_call x1, Pallas kernels, body(): pl.pallas_call(final_kernel, out_shape=(jax.ShapeDtypeStruct((actions, sh...  3.26 us
    ppermute x1, starting transfers between devices, body(): lax.ppermute(lax.dynamic_slice_in_dim(local, (1 - here) * part, part), 'y...  3.05 us
  transfers between devices with their start and end apart: 4, of which 3 were waited for; matrix products, arithmetic and copies ran while one was open for 0% of the time, Pallas kernels for 2%

profile of v2, /device:TPU:6, one launch (start us, length us, event | category | flops | bytes accessed | tf_op | source)
XLA Modules:
  0.0 72.6 jit_solution(7999296179563235644)
XLA Ops:
  0.6 0.0 copy-start
  0.6 0.0 copy-start.1
  0.7 11.7 %partials.1 = f32[8,168,128]{2,1,0:T(8,128)S(1)} custom-call(s32[8,32]{1,0:T(8,128)} %bitcast.11, s32[2,4096]{1,0:T(2,128)} %branch_hbm.1, f32[1,8192]{1,0:T(1,128)} %bitcast.9, s32[1,8192]{1,0:T(1,128)} %bitcast.10, bf16[512,8192]{1,0:T(8,128)(2,1)} %sens_hbm.1), custom_call_target="tpu_custom_call" | custom-call | tf_op jit(solution)/shard_map/partials/pallas_call | solution.py:252
  12.3 29.3 %all_to_all.15 = f32[8,168,128]{2,1,0:T(8,128)S(1)} all-to-all(f32[8,168,128]{2,1,0:T(8,128)S(1)} %partials.1), channel_id=1, replica_groups=mesh['yl'=2,'x'=4,'z'=8,'yh'=2,'act'=2] {'z'}, dimensions={0} | all-to-all | bytes 1376256 | tf_op jit(solution)/shard_map/all_to_all | solution.py:280
  41.7 0.7 broadcast_in_dim.2
  42.4 7.4 %all-to-all-start.1 = ((f32[16,24,128]{2,1,0:T(8,128)}), f32[16,24,128]{2,1,0:T(8,128)S(1)}, u32[]{:S(2)}, u32[]{:S(2)}) async-start(f32[16,24,128]{2,1,0:T(8,128)} %broadcast_in_dim.2), calls=%async_computation.1 | async-start | bytes 393216 | tf_op jit(solution)/shard_map/all_to_all | solution.py:282
  49.8 3.1 %collective-permute-start = (f32[72,128]{1,0:T(8,128)S(1)}, f32[72,128]{1,0:T(8,128)S(1)}, u32[]{:S(2)}, u32[]{:S(2)}) collective-permute-start(f32[72,128]{1,0:T(8,128)S(1)} %get-tuple-element.7), channel_id=1, source_target_pairs={{0,2},{2,0},{1,3},{3,1},{4,6},{6,4},{5,7},{7,5},{8,10},{10,8},{9,1... | collective-permute-start | bytes 110600 | tf_op jit(solution)/shard_map/ppermute | solution.py:287
  52.8 3.3 %all-to-all-done.1.parts_ref = f32[16,24,128]{2,1,0:T(8,128)S(1)} async-done(((f32[16,24,128]{2,1,0:T(8,128)}), f32[16,24,128]{2,1,0:T(8,128)S(1)}, u32[]{:S(2)}, u32[]{:S(2)}) %all-to-all-start.1) | async-done | bytes 196640 | tf_op jit(solution)/shard_map/all_to_all | solution.py:282
  56.1 1.5 %solve.1 = (f32[8,16,128]{2,1,0:T(8,128)}, f32[8,128]{1,0:T(8,128)S(1)}) custom-call(f32[16,24,128]{2,1,0:T(8,128)S(1)} %all-to-all-done.1.parts_ref), custom_call_target="tpu_custom_call" | custom-call | tf_op jit(solution)/shard_map/solve/pallas_call | solution.py:290
  57.7 3.4 %all-to-all-start.2 = ((f32[8,16,128]{2,1,0:T(8,128)}), f32[8,16,128]{2,1,0:T(8,128)S(1)}, u32[]{:S(2)}, u32[]{:S(2)}) async-start(f32[8,16,128]{2,1,0:T(8,128)} %get-tuple-element.6), calls=%async_computation.2 | async-start | bytes 131072 | tf_op jit(solution)/shard_map/all_to_all | solution.py:301
  61.0 0.0 collective-permute-done.theirs_ref
  61.1 0.1 collective-permute-start.1
  61.2 1.2 %collective-permute-done.1.other_ref = f32[8,128]{1,0:T(8,128)S(1)} collective-permute-done((f32[8,128]{1,0:T(8,128)S(1)}, f32[8,128]{1,0:T(8,128)S(1)}, u32[]{:S(2)}, u32[]{:S(2)}) %collective-permute-start.1) | collective-permute-done | bytes 4128 | tf_op jit(solution)/shard_map/ppermute | solution.py:288
  62.3 7.0 %all-to-all-done.2 = f32[8,16,128]{2,1,0:T(8,128)S(1)} async-done(((f32[8,16,128]{2,1,0:T(8,128)}), f32[8,16,128]{2,1,0:T(8,128)S(1)}, u32[]{:S(2)}, u32[]{:S(2)}) %all-to-all-start.2) | async-done | bytes 65568 | tf_op jit(solution)/shard_map/all_to_all | solution.py:301
  69.3 0.0 copy-done
  69.3 0.0 copy-done.1
  69.3 3.3 %update.1 = (f32[32,32,64]{2,1,0:T(8,128)}, f32[32,32]{1,0:T(8,128)}, f32[32,32]{1,0:T(8,128)}) custom-call(f32[72,128]{1,0:T(8,128)S(1)} %get-tuple-element.8.mine_ref, f32[72,128]{1,0:T(8,128)S(1)} %collective-permute-done.theirs_ref, f32[8,128]{1,0:T(8,128)S(1)} %collective-permute-done.1.other_ref, f32[8,128]{1,0:T(8,128)S(1)} %get-tuple-element.5.total_ref, ...), custom_call_target="tpu_custom_call" | custom-call | tf_op jit(solution)/shard_map/update/pallas_call | solution.py:303
  (4 shorter events, 0.1 us)
Async XLA Ops:
  0.6 68.7 %copy-start = (f32[64]{0:T(128)S(1)}, f32[64]{0:T(128)}, u32[]{:S(2)}) copy-start(f32[64]{0:T(128)} %param.12) | copy-start | bytes 772
  0.6 68.7 %copy-start.1 = (f32[32]{0:T(128)S(1)}, f32[32]{0:T(128)}, u32[]{:S(2)}) copy-start(f32[32]{0:T(128)} %param.13) | copy-start | bytes 388
  42.4 13.8 %all-to-all-start.1 = ((f32[16,24,128]{2,1,0:T(8,128)}), f32[16,24,128]{2,1,0:T(8,128)S(1)}, u32[]{:S(2)}, u32[]{:S(2)}) async-start(f32[16,24,128]{2,1,0:T(8,128)} %broadcast_in_dim.2), calls=%async_computation.1 | async-start | bytes 393216 | tf_op jit(solution)/shard_map/all_to_all | solution.py:282
  49.8 11.2 %collective-permute-start = (f32[72,128]{1,0:T(8,128)S(1)}, f32[72,128]{1,0:T(8,128)S(1)}, u32[]{:S(2)}, u32[]{:S(2)}) collective-permute-start(f32[72,128]{1,0:T(8,128)S(1)} %get-tuple-element.7), channel_id=1, source_target_pairs={{0,2},{2,0},{1,3},{3,1},{4,6},{6,4},{5,7},{7,5},{8,10},{10,8},{9,1... | collective-permute-start | bytes 110600 | tf_op jit(solution)/shard_map/ppermute | solution.py:287
  57.7 11.7 %all-to-all-start.2 = ((f32[8,16,128]{2,1,0:T(8,128)}), f32[8,16,128]{2,1,0:T(8,128)S(1)}, u32[]{:S(2)}, u32[]{:S(2)}) async-start(f32[8,16,128]{2,1,0:T(8,128)} %get-tuple-element.6), calls=%async_computation.2 | async-start | bytes 131072 | tf_op jit(solution)/shard_map/all_to_all | solution.py:301
  61.1 1.3 %collective-permute-start.1 = (f32[8,128]{1,0:T(8,128)S(1)}, f32[8,128]{1,0:T(8,128)S(1)}, u32[]{:S(2)}, u32[]{:S(2)}) collective-permute-start(f32[8,128]{1,0:T(8,128)S(1)} %slice_add_fusion), channel_id=1, source_target_pairs={{0,1},{1,0},{2,3},{3,2},{4,5},{5,4},{6,7},{7,6},{8,9},{9,8},{10,11... | collective-permute-start | bytes 12296 | tf_op jit(solution)/shard_map/ppermute | solution.py:288

commit v3 on v2

v3 whole, which is shorter than its diff:
```python
import jax
import jax.numpy as jnp
from jax import lax
from jax.experimental import pallas as pl
from jax.experimental.pallas import tpu as pltpu
from jax.sharding import Mesh
from jax.sharding import PartitionSpec as P

HIGHEST = lax.Precision.HIGHEST
LANES = 128
HALF = 64
SUB = 8
BLOCK = 2048
CNEC, BUS = ("yl", "x"), ("z", "yh")


def iota(shape, dim):
    return lax.broadcasted_iota(jnp.int32, shape, dim)


def dot_nt(x, y, precision=None):
    return lax.dot_general(
        x, y, (((1,), (1,)), ((), ())), precision=precision, preferred_element_type=jnp.float32
    )


def dot(x, y, precision=None):
    return jnp.dot(x, y, precision=precision, preferred_element_type=jnp.float32)


def two_parts(values):
    high = values.astype(jnp.bfloat16)
    return high, (values - high.astype(jnp.float32)).astype(jnp.bfloat16)


def digits(values, base, count):
    return [((values >> (base * at)) & ((1 << base) - 1)).astype(jnp.float32).astype(jnp.bfloat16)
            for at in reversed(range(count))]


def partial_kernel(
    swt_hbm, branch_hbm, weight_hbm, zone_hbm, sens_hbm, pay_ref, diff_ref,
    swt_ref, branch_ref, weight_ref, zone_ref, sens_ref, select_ref, acc_ref, zonal_ref, sems
):
    cols = sens_ref.shape[1]
    rows = acc_ref.shape[0]
    rank, actions = swt_ref.shape
    picks = rank * actions
    zones = HALF
    steps = cols // BLOCK
    bf16 = jnp.bfloat16
    small = [
        pltpu.make_async_copy(source, target, sems.at[steps + at])
        for at, (source, target) in enumerate(
            [(swt_hbm, swt_ref), (branch_hbm, branch_ref), (weight_hbm, weight_ref), (zone_hbm, zone_ref)]
        )
    ]
    for copy in small:
        copy.start()

    def block_copy(step):
        at = pl.ds(pl.multiple_of(step * BLOCK, BLOCK), BLOCK)
        return pltpu.make_async_copy(sens_hbm.at[:, at], sens_ref.at[0:rows, at], sems.at[step])

    for step in range(steps):
        block_copy(step).start()

    bus_start = lax.axis_index(BUS) * cols
    row_start = lax.axis_index(CNEC) * rows
    acc_ref[...] = jnp.zeros_like(acc_ref)
    zonal_ref[...] = jnp.zeros_like(zonal_ref)
    sens_ref[rows:, :] = jnp.ones((sens_ref.shape[0] - rows, cols), bf16)

    for copy in small[:2]:
        copy.wait()
    swt = swt_ref[...]
    pick_id = iota((picks, actions), 0)
    of_action = pick_id % LANES // rank * 2 + pick_id // LANES == iota((picks, actions), 1)
    of_action = jnp.where(of_action, 1.0, 0.0).astype(bf16)
    high, low = digits(swt, 6, 2)
    column = dot_nt(of_action, high) * 64.0 + dot_nt(of_action, low)
    column = jnp.where(iota((picks, rank), 0) % rank == iota((picks, rank), 1), column, 0.0)
    column = jnp.sum(column, axis=1, keepdims=True).astype(jnp.int32)
    row = dot_nt(high, of_action) * 64.0 + dot_nt(low, of_action)
    row = jnp.where(iota((rank, picks), 1) % rank == iota((rank, picks), 0), row, 0.0)
    row = jnp.sum(row, axis=0, keepdims=True).astype(jnp.int32)

    tiles = branch_ref.shape[1] // LANES
    table = jnp.concatenate(
        [branch_ref[:, at * LANES:(at + 1) * LANES] for at in range(tiles)], axis=0
    )
    onehot = jnp.where(iota((LANES, picks), 0) == row % LANES, 1.0, 0.0).astype(bf16)
    high, middle, low = [dot(part, onehot) for part in digits(table, 6, 3)]
    found = high * 4096.0 + middle * 64.0 + low
    line = iota((2 * tiles, picks), 0) - row // LANES * 2
    ends = [
        jnp.sum(jnp.where(line == end, found, 0.0), axis=0, keepdims=True).astype(jnp.int32)
        - bus_start
        for end in (0, 1)
    ]
    group = [end >> 7 for end in ends]
    within = [(end & (LANES - 1)).astype(jnp.float32) for end in ends]
    bus = iota((LANES, picks), 0).astype(jnp.float32).astype(bf16)
    zone_id = iota((zones, BLOCK), 0).astype(jnp.float32).astype(bf16)
    for copy in small[2:]:
        copy.wait()

    def step_body(step, carry):
        at = pl.ds(pl.multiple_of(step * BLOCK, BLOCK), BLOCK)
        for part in range(BLOCK // LANES):
            here = step * (BLOCK // LANES) + part
            first, second = [
                jnp.where(g == here, w, -1.0).astype(bf16) for g, w in zip(group, within)
            ]
            select_ref[part * LANES:(part + 1) * LANES, :] = jnp.where(
                bus == first, bf16(1.0), jnp.where(bus == second, bf16(-1.0), bf16(0.0))
            )
        inside = zone_ref[:, at].astype(jnp.float32).astype(bf16) == zone_id
        high, low = two_parts(weight_ref[:, at])
        key = jnp.concatenate(
            [jnp.where(inside, high, bf16(0.0)), jnp.where(inside, low, bf16(0.0))], axis=0
        )
        block_copy(step).wait()
        acc_ref[...] += dot(sens_ref[0:rows, at], select_ref[...])
        zonal_ref[...] += dot_nt(sens_ref[:, at], key)
        return carry

    lax.fori_loop(0, steps, step_body, 0)

    chunks = pay_ref.shape[0]
    diff = acc_ref[...]
    zonal = zonal_ref[:, 0:zones] + zonal_ref[:, zones:2 * zones]
    total = zonal_ref[rows:rows + 1, :]
    total = total + pltpu.roll(total, HALF, 1)
    total = jnp.where(iota((1, LANES), 1) < HALF, 0.0, total)
    zonal = zonal[0:rows]
    choose = jnp.where(iota((picks, rows), 1) == column - row_start, 1.0, 0.0).astype(bf16)
    switched = dot(choose, jnp.concatenate(two_parts(zonal), axis=1))
    switched = switched[:, 0:zones] + switched[:, zones:]
    high, low = [dot(choose, part) for part in two_parts(diff)]
    coupled = high + low
    same = iota((picks, picks), 0) // rank == iota((picks, picks), 1) // rank
    coupled = jnp.where(same, coupled, 0.0)
    pick_id = iota((picks, LANES), 0)
    lane = (pick_id // rank % 2 * 2 + pick_id // LANES) * rank + pick_id % rank
    fold = jnp.where(lane == iota((picks, LANES), 1), 1.0, 0.0).astype(bf16)
    high, low = [dot(part, fold) for part in two_parts(coupled)]
    coupled = jnp.sum((high + low).reshape(2, chunks, 2, SUB, LANES), axis=(0, 2))

    share = zonal.reshape(chunks, 2, 2, 2, SUB, zones)
    share = jnp.where(lax.axis_index("act") == 0, share[:, :, 0], share[:, :, 1])
    share = jnp.concatenate([share[:, :, 0], share[:, :, 1]], axis=-1)
    switched = switched.reshape(2, actions // 2, rank, zones)
    switched = jnp.concatenate([switched[0], switched[1]], axis=-1)
    half = rows // chunks // 2
    diff = diff.reshape(chunks, 2, half, picks)
    for at in range(2):
        start = at * 2 * half
        pay_ref[:, at * SUB:(at + 1) * SUB, :] = share[:, at]
        diff_ref[:, start:start + half, :] = diff[:, at, :, 0:LANES]
        diff_ref[:, start + half:start + 2 * half, :] = diff[:, at, :, LANES:]
    pay_ref[:, 2 * SUB:4 * SUB, :] = switched.reshape(chunks, 2 * SUB, LANES)
    pay_ref[:, 4 * SUB:, :] = coupled + total


def solve_kernel(parts_ref, diff_ref, out_ref, total_ref, mine_ref, theirs_ref):
    half = mine_ref.shape[0]
    first, second = [
        jnp.sum(diff_ref[:, at * half:(at + 1) * half, :], axis=0) for at in (0, 1)
    ]
    lower = lax.axis_index("yh") == 0
    mine_ref[...] = jnp.where(lower, first, second)
    theirs_ref[...] = jnp.where(lower, second, first)
    full = parts_ref[...]
    extra = full[2 * SUB:]
    total = extra[0:1, HALF:] / lax.axis_size(CNEC)
    total = jnp.concatenate([total, total], axis=1)
    total_ref[...] = jnp.broadcast_to(total, total_ref.shape)
    row_id = iota((SUB, LANES), 0)
    lane = iota((SUB, LANES), 1)
    eye = jnp.where(lane % SUB == row_id, 1.0, 0.0)
    source = iota((LANES, LANES), 0)
    target = iota((LANES, LANES), 1)
    for tile in range(2):
        spread = (source // SUB == tile * 2 + target // HALF) & (source % SUB == target % SUB)
        left = eye - dot(extra, jnp.where(spread, 1.0, 0.0), HIGHEST)
        right = full[tile * SUB:(tile + 1) * SUB] / total
        for pivot in range(SUB):
            factor = jnp.where(
                lane < HALF, left[:, pivot:pivot + 1], left[:, HALF + pivot:HALF + pivot + 1]
            )
            diagonal = factor[pivot:pivot + 1]
            left_now = left[pivot:pivot + 1] / diagonal
            right_now = right[pivot:pivot + 1] / diagonal
            left = jnp.where(row_id == pivot, left_now, left - factor * left_now)
            right = jnp.where(row_id == pivot, right_now, right - factor * right_now)
        out_ref[:, tile * SUB:(tile + 1) * SUB, :] = jnp.broadcast_to(
            right[None], (out_ref.shape[0], SUB, LANES)
        )


def final_kernel(
    mine_ref, other_ref, diff_ref, diff_theirs_ref, total_ref, solved_ref, position_ref, limit_ref,
    after_ref, loading_ref, margin_ref
):
    actions, share, zones = after_ref.shape
    pairs = actions // 2
    lower = lax.axis_index("act") == 0
    diff = diff_ref[...] + diff_theirs_ref[...]
    mine, other = mine_ref[...], other_ref[...]
    low, high = jnp.where(lower, mine, other), jnp.where(lower, other, mine)
    zonal = jnp.concatenate(
        [low[:, :HALF], low[:, HALF:], high[:, :HALF], high[:, HALF:]], axis=0
    ) / total_ref[0:1, :HALF]
    zonal_twice = jnp.concatenate([zonal, zonal], axis=1)
    even, odd = diff[0:share], diff[share:]
    first = iota((share, LANES), 1) < HALF
    for pair in range(pairs):
        total = zonal_twice
        for j in range(SUB):
            at = pair * SUB + j
            factor = jnp.where(first, even[:, at:at + 1], odd[:, at:at + 1])
            total = total + factor * solved_ref[pair, j:j + 1, :]
        after_ref[2 * pair] = total[:, :HALF]
        after_ref[2 * pair + 1] = total[:, HALF:]
    position = position_ref[...]
    solved = solved_ref[...].reshape(pairs * SUB, LANES)
    flow = dot_nt(position, zonal, HIGHEST)
    shape = (actions, pairs * SUB)
    same = iota(shape, 1) // SUB == iota(shape, 0) // 2
    for side, part in enumerate((even, odd)):
        moved = dot_nt(position, solved[:, side * HALF:(side + 1) * HALF], HIGHEST)
        mask = same & (iota(shape, 0) % 2 == side)
        flow = flow + dot_nt(jnp.where(mask, moved, 0.0), part, HIGHEST)
    limit = limit_ref[...]
    loading_ref[...] = flow / limit
    margin_ref[...] = limit - jnp.abs(flow)


def params():
    return pltpu.CompilerParams(vmem_limit_bytes=48 * 1024 * 1024)


def body(
    nodal_sensitivity, shift_weight, bus_zone, branch_buses, switched_rows, net_position, flow_limit
):
    rows, cols = nodal_sensitivity.shape
    zones = net_position.shape[0]
    actions, rank = switched_rows.shape
    picks = actions * rank
    n_z, n_yh = lax.axis_size("z"), lax.axis_size("yh")
    share = rows // n_z // n_yh
    f32, i32 = jnp.float32, jnp.int32
    vmem = pl.BlockSpec(memory_space=pltpu.VMEM)
    hbm = pl.BlockSpec(memory_space=pltpu.HBM)

    pay, diff = pl.pallas_call(
        partial_kernel,
        out_shape=(
            jax.ShapeDtypeStruct((n_z, 5 * SUB, LANES), f32),
            jax.ShapeDtypeStruct((n_z, n_yh * 2 * share, LANES), f32),
        ),
        in_specs=[hbm] * 5,
        out_specs=(vmem, vmem),
        scratch_shapes=[
            pltpu.VMEM((rank, actions), i32),
            pltpu.VMEM(branch_buses.shape, i32),
            pltpu.VMEM((1, cols), f32),
            pltpu.VMEM((1, cols), i32),
            pltpu.VMEM((rows + 2 * SUB, cols), jnp.bfloat16),
            pltpu.VMEM((BLOCK, picks), jnp.bfloat16),
            pltpu.VMEM((rows, picks), f32),
            pltpu.VMEM((rows + 2 * SUB, 2 * zones), f32),
            pltpu.SemaphoreType.DMA((cols // BLOCK + 4,)),
        ],
        compiler_params=params(),
        name="partials",
    )(
        *[
            pltpu.with_memory_space_constraint(x, pltpu.HBM)
            for x in (
                switched_rows.T, branch_buses, shift_weight.reshape(1, cols),
                bus_zone.reshape(1, cols), nodal_sensitivity,
            )
        ]
    )

    swap = [(0, 1), (1, 0)]
    here = lax.axis_index("yh")

    local = jnp.sum(lax.all_to_all(pay, "z", 0, 0, tiled=True), axis=0)
    diff = lax.all_to_all(diff, "z", 0, 0, tiled=True)

    full = local[2 * SUB:]
    for axis, pairs in (
        ("x", [(0, 1), (1, 0), (2, 3), (3, 2)]),
        ("x", [(0, 3), (3, 0), (1, 2), (2, 1)]),
        ("yl", swap),
        (("yl", "yh"), [(0, 3), (3, 0), (1, 2), (2, 1)]),
    ):
        full = full + lax.ppermute(full, axis, pairs)

    theirs = lax.dynamic_slice_in_dim(local, (1 - here) * SUB, SUB)
    mine = lax.dynamic_slice_in_dim(local, here * SUB, SUB) + lax.ppermute(theirs, "yh", swap)
    other = lax.ppermute(mine, "act", swap)

    solved, total, diff, theirs = pl.pallas_call(
        solve_kernel,
        out_shape=(
            jax.ShapeDtypeStruct((n_z, 2 * SUB, LANES), f32),
            jax.ShapeDtypeStruct((SUB, LANES), f32),
            jax.ShapeDtypeStruct((2 * share, LANES), f32),
            jax.ShapeDtypeStruct((2 * share, LANES), f32),
        ),
        in_specs=[vmem, vmem],
        out_specs=(vmem,) * 4,
        compiler_params=params(),
        name="solve",
    )(full, diff)
    diff_theirs = lax.ppermute(theirs, "yh", swap)
    solved = lax.all_to_all(solved, "z", 0, 0, tiled=True).reshape(actions // 2, SUB, LANES)

    return pl.pallas_call(
        final_kernel,
        out_shape=(
            jax.ShapeDtypeStruct((actions, share, zones), f32),
            jax.ShapeDtypeStruct((actions, share), f32),
            jax.ShapeDtypeStruct((actions, share), f32),
        ),
        in_specs=[vmem] * 8,
        out_specs=(vmem, vmem, vmem),
        compiler_params=params(),
        name="update",
    )(
        mine, other, diff, diff_theirs, total, solved,
        net_position.reshape(1, zones), flow_limit.reshape(1, share),
    )


def solution(mesh):
    n_cnec, n_bus, n_act = mesh.devices.shape
    split = Mesh(
        mesh.devices.reshape(2, n_cnec // 2, n_bus // 2, 2, n_act), ("yl", "x", "z", "yh", "act")
    )
    return jax.shard_map(
        body,
        mesh=split,
        in_specs=(
            P(CNEC, BUS),
            P(BUS),
            P(BUS),
            P(),
            P("act", None),
            P(),
            P(CNEC + BUS),
        ),
        out_specs=(
            P("act", CNEC + BUS, None),
            P("act", CNEC + BUS),
            P("act", CNEC + BUS),
        ),
        check_vma=False,
    )
```

time: 73.7 us -> 71.1 us (0.965)
  blocking collectives: 29.3 us -> 18 us
  waiting for transfers between devices: 11.5 us -> 18.9 us
  starting transfers between devices: 13.9 us -> 19.4 us
  Pallas kernels: 16.5 us -> 13.5 us
    all_to_all x1, blocking collectives: 29.3 us -> 18 us  [body(): local = jnp.sum(lax.all_to_all(pay, 'z', 0, 0, tiled=True), axis=0)]
    ppermute x2 -> x7, waiting for transfers between devices: 1.16 us -> 11.8 us  [the longest x4 10.7 us: body(): full = full + lax.ppermute(full, axis, pairs)]
    ppermute x2 -> x7, starting transfers between devices: 3.15 us -> 8.69 us  [the longest x4 5.99 us: body(): full = full + lax.ppermute(full, axis, pairs)]
    all_to_all x1, starting transfers between devices: 7.42 us -> 3.49 us  [body(): diff = lax.all_to_all(diff, 'z', 0, 0, tiled=True)]
    all_to_all x1, starting transfers between devices: 3.35 us -> 7.18 us  [body(): lax.all_to_all(solved, 'z', 0, 0, tiled=True)]
    all_to_all x1, waiting for transfers between devices: 3.3 us -> 0.01 us  [body(): diff = lax.all_to_all(diff, 'z', 0, 0, tiled=True)]
    pallas_call x1, Pallas kernels: 11.7 us -> 8.67 us  [body(): pl.pallas_call(partial_kernel, out_shape=(jax.ShapeDtypeStruct((n_z, 5 *...]
  transfers between devices with their start and end apart: 4 -> 9, of which waited for: 3 -> 6; matrix products, arithmetic and copies ran while one was open for 0% -> 0% of each run, Pallas kernels for 2% -> 2%
where the time goes in v3:
time: 71.1 us; the launch traced here: 70.5 us
  starting transfers between devices  19.4 us (27%)
  waiting for transfers between devices  18.9 us (27%)
  blocking collectives  18 us (25%)
  Pallas kernels  13.5 us (19%)
    all_to_all x1, blocking collectives, body(): local = jnp.sum(lax.all_to_all(pay, 'z', 0, 0, tiled=True), axis=0)  18 us
    ppermute x4, waiting for transfers between devices, body(): full = full + lax.ppermute(full, axis, pairs)  10.7 us
    pallas_call x1, Pallas kernels, body(): pl.pallas_call(partial_kernel, out_shape=(jax.ShapeDtypeStruct((n_z, 5 *...  8.67 us
    all_to_all x1, starting transfers between devices, body(): lax.all_to_all(solved, 'z', 0, 0, tiled=True)  7.18 us
    all_to_all x1, waiting for transfers between devices, body(): lax.all_to_all(solved, 'z', 0, 0, tiled=True)  7.1 us
    ppermute x4, starting transfers between devices, body(): full = full + lax.ppermute(full, axis, pairs)  5.99 us
    all_to_all x1, starting transfers between devices, body(): diff = lax.all_to_all(diff, 'z', 0, 0, tiled=True)  3.49 us
    pallas_call x1, Pallas kernels, body(): pl.pallas_call(final_kernel, out_shape=(jax.ShapeDtypeStruct((actions, sh...  3.26 us
  transfers between devices with their start and end apart: 9, of which 6 were waited for; matrix products, arithmetic and copies ran while one was open for 0% of the time, Pallas kernels for 2%

profile of v3, /device:TPU:6, one launch (start us, length us, event | category | flops | bytes accessed | tf_op | source)
XLA Modules:
  0.0 70.5 jit_solution(2816183616183072425)
XLA Ops:
  0.6 0.0 copy-start
  0.6 0.0 copy-start.1
  0.7 8.7 %partials.1 = (f32[8,40,128]{2,1,0:T(8,128)S(1)}, f32[8,128,128]{2,1,0:T(8,128)}) custom-call(s32[8,32]{1,0:T(8,128)} %bitcast.11, s32[2,4096]{1,0:T(2,128)} %branch_hbm.1, f32[1,8192]{1,0:T(1,128)} %bitcast.9, s32[1,8192]{1,0:T(1,128)} %bitcast.10, bf16[512,8192]{1,0:T(8,128)(2,1)} %sens_hbm.1), custom_call_target="tpu_custom_call" | custom-call | tf_op jit(solution)/shard_map/partials/pallas_call | solution.py:257
  9.3 18.0 %all_to_all.15 = f32[8,40,128]{2,1,0:T(8,128)S(1)} all-to-all(f32[8,40,128]{2,1,0:T(8,128)S(1)} %get-tuple-element.9), channel_id=1, replica_groups=mesh['yl'=2,'x'=4,'z'=8,'yh'=2,'act'=2] {'z'}, dimensions={0} | all-to-all | bytes 327680 | tf_op jit(solution)/shard_map/all_to_all | solution.py:291
  27.4 3.5 %all-to-all-start.1 = ((f32[8,128,128]{2,1,0:T(8,128)}), f32[8,128,128]{2,1,0:T(8,128)S(1)}, u32[]{:S(2)}, u32[]{:S(2)}) async-start(f32[8,128,128]{2,1,0:T(8,128)} %get-tuple-element.10), calls=%async_computation.1 | async-start | bytes 1048576 | tf_op jit(solution)/shard_map/all_to_all | solution.py:292
  30.9 0.9 %collective-permute-start.2 = (f32[24,128]{1,0:T(8,128)S(1)}, f32[24,128]{1,0:T(8,128)S(1)}, u32[]{:S(2)}, u32[]{:S(2)}) collective-permute-start(f32[24,128]{1,0:T(8,128)S(1)} %slice.4), channel_id=1, source_target_pairs={{0,32},{32,0},{64,96},{96,64},{1,33},{33,1},{65,97},{97,65},{2,34}... | collective-permute-start | bytes 36872 | tf_op jit(solution)/shard_map/ppermute | solution.py:301
  31.8 2.9 %collective-permute-done.2 = f32[24,128]{1,0:T(8,128)S(1)} collective-permute-done((f32[24,128]{1,0:T(8,128)S(1)}, f32[24,128]{1,0:T(8,128)S(1)}, u32[]{:S(2)}, u32[]{:S(2)}) %collective-permute-start.2) | collective-permute-done | bytes 12320 | tf_op jit(solution)/shard_map/ppermute | solution.py:301
  34.7 0.5 collective-permute-start.3
  35.2 4.4 %collective-permute-done.3 = f32[24,128]{1,0:T(8,128)S(1)} collective-permute-done((f32[24,128]{1,0:T(8,128)S(1)}, f32[24,128]{1,0:T(8,128)S(1)}, u32[]{:S(2)}, u32[]{:S(2)}) %collective-permute-start.3) | collective-permute-done | bytes 12320 | tf_op jit(solution)/shard_map/ppermute | solution.py:301
  39.6 1.6 %collective-permute-start.4 = (f32[24,128]{1,0:T(8,128)S(1)}, f32[24,128]{1,0:T(8,128)S(1)}, u32[]{:S(2)}, u32[]{:S(2)}) collective-permute-start(f32[24,128]{1,0:T(8,128)S(1)} %add.25), channel_id=1, source_target_pairs={{0,128},{128,0},{1,129},{129,1},{2,130},{130,2},{3,131},{131,3},{4... | collective-permute-start | bytes 36872 | tf_op jit(solution)/shard_map/ppermute | solution.py:301
  41.2 2.1 %collective-permute-done.4 = f32[24,128]{1,0:T(8,128)S(1)} collective-permute-done((f32[24,128]{1,0:T(8,128)S(1)}, f32[24,128]{1,0:T(8,128)S(1)}, u32[]{:S(2)}, u32[]{:S(2)}) %collective-permute-start.4) | collective-permute-done | bytes 12320 | tf_op jit(solution)/shard_map/ppermute | solution.py:301
  43.3 3.0 %collective-permute-start.5 = (f32[24,128]{1,0:T(8,128)S(1)}, f32[24,128]{1,0:T(8,128)S(1)}, u32[]{:S(2)}, u32[]{:S(2)}) collective-permute-start(f32[24,128]{1,0:T(8,128)S(1)} %add.26), channel_id=1, source_target_pairs={{0,130},{130,0},{2,128},{128,2},{1,131},{131,1},{3,129},{129,3},{4... | collective-permute-start | bytes 36872 | tf_op jit(solution)/shard_map/ppermute | solution.py:301
  46.3 0.6 collective-permute-start
  46.9 1.3 %collective-permute-done.5 = f32[24,128]{1,0:T(8,128)S(1)} collective-permute-done((f32[24,128]{1,0:T(8,128)S(1)}, f32[24,128]{1,0:T(8,128)S(1)}, u32[]{:S(2)}, u32[]{:S(2)}) %collective-permute-start.5) | collective-permute-done | bytes 12320 | tf_op jit(solution)/shard_map/ppermute | solution.py:301
  48.2 0.0 all-to-all-done.1.diff_ref
  48.2 1.5 %solve.1 = (f32[8,16,128]{2,1,0:T(8,128)}, f32[8,128]{1,0:T(8,128)S(1)}, f32[64,128]{1,0:T(8,128)S(1)}, f32[64,128]{1,0:T(8,128)S(1)}) custom-call(f32[24,128]{1,0:T(8,128)S(1)} %add.27.parts_ref, f32[8,128,128]{2,1,0:T(8,128)S(1)} %all-to-all-done.1.diff_ref), custom_call_target="tpu_custom_call" | custom-call | tf_op jit(solution)/shard_map/solve/pallas_call | solution.py:307
  49.7 2.0 %collective-permute-start.6 = (f32[64,128]{1,0:T(8,128)S(1)}, f32[64,128]{1,0:T(8,128)S(1)}, u32[]{:S(2)}, u32[]{:S(2)}) collective-permute-start(f32[64,128]{1,0:T(8,128)S(1)} %get-tuple-element.12), channel_id=1, source_target_pairs={{0,2},{2,0},{1,3},{3,1},{4,6},{6,4},{5,7},{7,5},{8,10},{10,8},{9,1... | collective-permute-start | bytes 98312 | tf_op jit(solution)/shard_map/ppermute | solution.py:320
  51.7 7.2 %all-to-all-start.2 = ((f32[8,16,128]{2,1,0:T(8,128)}), f32[8,16,128]{2,1,0:T(8,128)S(1)}, u32[]{:S(2)}, u32[]{:S(2)}) async-start(f32[8,16,128]{2,1,0:T(8,128)} %get-tuple-element.14), calls=%async_computation.2 | async-start | bytes 131072 | tf_op jit(solution)/shard_map/all_to_all | solution.py:321
  58.9 0.0 collective-permute-done
  58.9 0.1 collective-permute-start.1
  59.0 1.2 %collective-permute-done.1.other_ref = f32[8,128]{1,0:T(8,128)S(1)} collective-permute-done((f32[8,128]{1,0:T(8,128)S(1)}, f32[8,128]{1,0:T(8,128)S(1)}, u32[]{:S(2)}, u32[]{:S(2)}) %collective-permute-start.1) | collective-permute-done | bytes 4128 | tf_op jit(solution)/shard_map/ppermute | solution.py:305
  60.2 0.0 collective-permute-done.6.diff_theirs_ref
  60.2 7.1 %all-to-all-done.2 = f32[8,16,128]{2,1,0:T(8,128)S(1)} async-done(((f32[8,16,128]{2,1,0:T(8,128)}), f32[8,16,128]{2,1,0:T(8,128)S(1)}, u32[]{:S(2)}, u32[]{:S(2)}) %all-to-all-start.2) | async-done | bytes 65568 | tf_op jit(solution)/shard_map/all_to_all | solution.py:321
  67.3 0.0 copy-done
  67.3 0.0 copy-done.1
  67.3 3.3 %update.1 = (f32[32,32,64]{2,1,0:T(8,128)}, f32[32,32]{1,0:T(8,128)}, f32[32,32]{1,0:T(8,128)}) custom-call(f32[8,128]{1,0:T(8,128)S(1)} %dynamic-slice_add_fusion.mine_ref, f32[8,128]{1,0:T(8,128)S(1)} %collective-permute-done.1.other_ref, f32[64,128]{1,0:T(8,128)S(1)} %get-tuple-element.11.diff_ref, f32[64,128]{1,0:T(8,128)S(1)} %collective-permute-done.6.diff_theirs_ref, ...), custom_call_target="tpu_custom_call" | custom-call | tf_op jit(solution)/shard_map/update/pallas_call | solution.py:323
  (8 shorter events, 0.0 us)
Async XLA Ops:
  0.6 66.6 %copy-start = (f32[64]{0:T(128)S(1)}, f32[64]{0:T(128)}, u32[]{:S(2)}) copy-start(f32[64]{0:T(128)} %param.12) | copy-start | bytes 772
  0.6 66.6 %copy-start.1 = (f32[32]{0:T(128)S(1)}, f32[32]{0:T(128)}, u32[]{:S(2)}) copy-start(f32[32]{0:T(128)} %param.13) | copy-start | bytes 388
  27.4 20.8 %all-to-all-start.1 = ((f32[8,128,128]{2,1,0:T(8,128)}), f32[8,128,128]{2,1,0:T(8,128)S(1)}, u32[]{:S(2)}, u32[]{:S(2)}) async-start(f32[8,128,128]{2,1,0:T(8,128)} %get-tuple-element.10), calls=%async_computation.1 | async-start | bytes 1048576 | tf_op jit(solution)/shard_map/all_to_all | solution.py:292
  30.9 3.8 %collective-permute-start.2 = (f32[24,128]{1,0:T(8,128)S(1)}, f32[24,128]{1,0:T(8,128)S(1)}, u32[]{:S(2)}, u32[]{:S(2)}) collective-permute-start(f32[24,128]{1,0:T(8,128)S(1)} %slice.4), channel_id=1, source_target_pairs={{0,32},{32,0},{64,96},{96,64},{1,33},{33,1},{65,97},{97,65},{2,34}... | collective-permute-start | bytes 36872 | tf_op jit(solution)/shard_map/ppermute | solution.py:301
  34.7 4.9 %collective-permute-start.3 = (f32[24,128]{1,0:T(8,128)S(1)}, f32[24,128]{1,0:T(8,128)S(1)}, u32[]{:S(2)}, u32[]{:S(2)}) collective-permute-start(f32[24,128]{1,0:T(8,128)S(1)} %slice_add_fusion), channel_id=1, source_target_pairs={{0,96},{96,0},{32,64},{64,32},{1,97},{97,1},{33,65},{65,33},{2,98}... | collective-permute-start | bytes 36872 | tf_op jit(solution)/shard_map/ppermute | solution.py:301
  39.6 3.7 %collective-permute-start.4 = (f32[24,128]{1,0:T(8,128)S(1)}, f32[24,128]{1,0:T(8,128)S(1)}, u32[]{:S(2)}, u32[]{:S(2)}) collective-permute-start(f32[24,128]{1,0:T(8,128)S(1)} %add.25), channel_id=1, source_target_pairs={{0,128},{128,0},{1,129},{129,1},{2,130},{130,2},{3,131},{131,3},{4... | collective-permute-start | bytes 36872 | tf_op jit(solution)/shard_map/ppermute | solution.py:301
  43.3 4.9 %collective-permute-start.5 = (f32[24,128]{1,0:T(8,128)S(1)}, f32[24,128]{1,0:T(8,128)S(1)}, u32[]{:S(2)}, u32[]{:S(2)}) collective-permute-start(f32[24,128]{1,0:T(8,128)S(1)} %add.26), channel_id=1, source_target_pairs={{0,130},{130,0},{2,128},{128,2},{1,131},{131,1},{3,129},{129,3},{4... | collective-permute-start | bytes 36872 | tf_op jit(solution)/shard_map/ppermute | solution.py:301
  46.3 12.6 %collective-permute-start = (f32[8,128]{1,0:T(8,128)S(1)}, f32[8,128]{1,0:T(8,128)S(1)}, u32[]{:S(2)}, u32[]{:S(2)}) collective-permute-start(f32[8,128]{1,0:T(8,128)S(1)} %constant_dynamic-slice_fusion), channel_id=1, source_target_pairs={{0,2},{2,0},{1,3},{3,1},{4,6},{6,4},{5,7},{7,5},{8,10},{10,8},{9,1... | collective-permute-start | bytes 12296 | tf_op jit(solution)/shard_map/ppermute | solution.py:304
  49.7 10.4 %collective-permute-start.6 = (f32[64,128]{1,0:T(8,128)S(1)}, f32[64,128]{1,0:T(8,128)S(1)}, u32[]{:S(2)}, u32[]{:S(2)}) collective-permute-start(f32[64,128]{1,0:T(8,128)S(1)} %get-tuple-element.12), channel_id=1, source_target_pairs={{0,2},{2,0},{1,3},{3,1},{4,6},{6,4},{5,7},{7,5},{8,10},{10,8},{9,1... | collective-permute-start | bytes 98312 | tf_op jit(solution)/shard_map/ppermute | solution.py:320
  51.7 15.6 %all-to-all-start.2 = ((f32[8,16,128]{2,1,0:T(8,128)}), f32[8,16,128]{2,1,0:T(8,128)S(1)}, u32[]{:S(2)}, u32[]{:S(2)}) async-start(f32[8,16,128]{2,1,0:T(8,128)} %get-tuple-element.14), calls=%async_computation.2 | async-start | bytes 131072 | tf_op jit(solution)/shard_map/all_to_all | solution.py:321
  58.9 1.3 %collective-permute-start.1 = (f32[8,128]{1,0:T(8,128)S(1)}, f32[8,128]{1,0:T(8,128)S(1)}, u32[]{:S(2)}, u32[]{:S(2)}) collective-permute-start(f32[8,128]{1,0:T(8,128)S(1)} %dynamic-slice_add_fusion.mine_ref), channel_id=1, source_target_pairs={{0,1},{1,0},{2,3},{3,2},{4,5},{5,4},{6,7},{7,6},{8,9},{9,8},{10,11... | collective-permute-start | bytes 12296 | tf_op jit(solution)/shard_map/ppermute | solution.py:305

commit v4 on v3

v4 whole, which is shorter than its diff:
```python
import jax
import jax.numpy as jnp
from jax import lax
from jax.experimental import pallas as pl
from jax.experimental.pallas import tpu as pltpu
from jax.sharding import Mesh
from jax.sharding import PartitionSpec as P

HIGHEST = lax.Precision.HIGHEST
LANES = 128
HALF = 64
SUB = 8
BLOCK = 2048
SLOTS = 64
CNEC, BUS = ("yl", "x"), ("z", "yh")


def iota(shape, dim):
    return lax.broadcasted_iota(jnp.int32, shape, dim)


def dot_nt(x, y, precision=None):
    return lax.dot_general(
        x, y, (((1,), (1,)), ((), ())), precision=precision, preferred_element_type=jnp.float32
    )


def dot(x, y, precision=None):
    return jnp.dot(x, y, precision=precision, preferred_element_type=jnp.float32)


def two_parts(values):
    high = values.astype(jnp.bfloat16)
    return high, (values - high.astype(jnp.float32)).astype(jnp.bfloat16)


def digits(values, base, count):
    return [((values >> (base * at)) & ((1 << base) - 1)).astype(jnp.float32).astype(jnp.bfloat16)
            for at in reversed(range(count))]


def find_picks(swt, branch_ref):
    rank, actions = swt.shape
    picks = rank * actions
    pick_id = iota((picks, actions), 0)
    of_action = pick_id % LANES // rank * 2 + pick_id // LANES == iota((picks, actions), 1)
    of_action = jnp.where(of_action, 1.0, 0.0).astype(jnp.bfloat16)
    high, low = digits(swt, 6, 2)
    column = dot_nt(of_action, high) * 64.0 + dot_nt(of_action, low)
    column = jnp.where(iota((picks, rank), 0) % rank == iota((picks, rank), 1), column, 0.0)
    column = jnp.sum(column, axis=1, keepdims=True).astype(jnp.int32)
    row = dot_nt(high, of_action) * 64.0 + dot_nt(low, of_action)
    row = jnp.where(iota((rank, picks), 1) % rank == iota((rank, picks), 0), row, 0.0)
    row = jnp.sum(row, axis=0, keepdims=True).astype(jnp.int32)
    tiles = branch_ref.shape[1] // LANES
    table = jnp.concatenate(
        [branch_ref[:, at * LANES:(at + 1) * LANES] for at in range(tiles)], axis=0
    )
    onehot = jnp.where(iota((LANES, picks), 0) == row % LANES, 1.0, 0.0).astype(jnp.bfloat16)
    high, middle, low = [dot(part, onehot) for part in digits(table, 6, 3)]
    found = high * 4096.0 + middle * 64.0 + low
    line = iota((2 * tiles, picks), 0) - row // LANES * 2
    ends = [
        jnp.sum(jnp.where(line == end, found, 0.0), axis=0, keepdims=True).astype(jnp.int32)
        for end in (0, 1)
    ]
    return column, ends


def slot_matrix(slots, count):
    shape = (count, slots[0].shape[1])
    first, second = [jnp.where(iota(shape, 0) == slot, 1.0, 0.0) for slot in slots]
    return (first - second).astype(jnp.bfloat16)


def partial_kernel(
    swt_hbm, branch_hbm, weight_hbm, zone_hbm, sens_hbm, pay_ref, meta_ref,
    swt_ref, branch_ref, weight_ref, zone_ref, sens_ref, acc_ref, coupled_ref, sems
):
    cols = sens_ref.shape[1]
    rows = sens_ref.shape[0] - 2 * SUB
    rank, actions = swt_ref.shape
    picks = rank * actions
    zones = HALF
    steps = cols // BLOCK
    bf16 = jnp.bfloat16
    small = [
        pltpu.make_async_copy(source, target, sems.at[steps + at])
        for at, (source, target) in enumerate(
            [(swt_hbm, swt_ref), (branch_hbm, branch_ref), (weight_hbm, weight_ref), (zone_hbm, zone_ref)]
        )
    ]
    for copy in small:
        copy.start()

    def block_copy(step):
        at = pl.ds(pl.multiple_of(step * BLOCK, BLOCK), BLOCK)
        return pltpu.make_async_copy(sens_hbm.at[:, at], sens_ref.at[0:rows, at], sems.at[step])

    for step in range(steps):
        block_copy(step).start()

    shard = lax.axis_index(BUS)
    row_start = lax.axis_index(CNEC) * rows
    acc_ref[...] = jnp.zeros_like(acc_ref)
    sens_ref[rows:, :] = jnp.ones((sens_ref.shape[0] - rows, cols), bf16)

    for copy in small[:2]:
        copy.wait()
    column, ends = find_picks(swt_ref[...], branch_ref)

    bus = jnp.concatenate(ends, axis=1)
    held = bus // cols
    count = 2 * picks
    shards = lax.axis_size(BUS)
    inside = iota((shards, count), 0) == held
    before = jnp.where(iota((count, count), 0) < iota((count, count), 1), 1.0, 0.0).astype(bf16)
    place = dot(jnp.where(inside, 1.0, 0.0).astype(bf16), before)
    place = jnp.sum(jnp.where(inside, place, 0.0), axis=0, keepdims=True)
    over = jnp.where(jnp.max(place, axis=1, keepdims=True) >= SLOTS, 1.0, 0.0)
    meta = jnp.concatenate([held.astype(jnp.float32), place, jnp.broadcast_to(over, (1, count))], axis=0)
    meta_ref[...] = jnp.concatenate([meta, jnp.zeros((SUB - 3, count), jnp.float32)], axis=0)
    place = place.astype(jnp.int32)
    mine = held == shard
    slot = jnp.where(mine, place, -1)
    local = bus - shard * cols

    def buses_of(group):
        match = iota((SLOTS, count), 0) + group * SLOTS == slot
        return jnp.sum(jnp.where(match, (local + 1).astype(jnp.float32), 0.0), axis=1, keepdims=True).astype(jnp.int32) - 1

    first_buses = buses_of(0)
    zone_id = iota((zones, BLOCK), 0).astype(jnp.float32).astype(bf16)
    lane = iota((SLOTS, BLOCK), 1)
    for copy in small[2:]:
        copy.wait()

    def select(buses, step):
        return jnp.where(lane == buses - step * BLOCK, 1.0, 0.0).astype(bf16)

    def step_body(step, carry):
        at = pl.ds(pl.multiple_of(step * BLOCK, BLOCK), BLOCK)
        inside = zone_ref[:, at].astype(jnp.float32).astype(bf16) == zone_id
        high, low = two_parts(weight_ref[:, at])
        key = jnp.concatenate(
            [
                jnp.where(inside, high, bf16(0.0)),
                jnp.where(inside, low, bf16(0.0)),
                select(first_buses, step),
            ],
            axis=0,
        )
        block_copy(step).wait()
        acc_ref[...] += dot_nt(sens_ref[:, at], key)
        return carry

    lax.fori_loop(0, steps, step_body, 0)

    chunks = pay_ref.shape[0]
    zonal = acc_ref[0:rows, 0:zones] + acc_ref[0:rows, zones:2 * zones]
    total = acc_ref[rows:rows + 1, 0:2 * zones]
    total = total + pltpu.roll(total, HALF, 1)
    total = jnp.where(iota((1, LANES), 1) < HALF, 0.0, total)
    held_columns = acc_ref[0:rows, 2 * zones:]
    choose = jnp.where(iota((picks, rows), 1) == column - row_start, 1.0, 0.0).astype(bf16)
    chosen = dot(
        choose, jnp.concatenate([*two_parts(zonal), held_columns.astype(bf16)], axis=1)
    )
    switched = chosen[:, 0:zones] + chosen[:, zones:2 * zones]

    def coupled_of(chosen_columns, group):
        slots = [slot[:, at * picks:(at + 1) * picks] - group * SLOTS for at in (0, 1)]
        return dot(chosen_columns.astype(bf16), slot_matrix(slots, SLOTS))

    coupled_ref[...] = coupled_of(chosen[:, 2 * zones:], 0)

    def group_body(group, carry):
        buses = buses_of(group)
        columns = jnp.zeros((rows, SLOTS), jnp.float32)
        for step in range(steps):
            at = pl.ds(step * BLOCK, BLOCK)
            columns += dot_nt(sens_ref[0:rows, at], select(buses, step))
        coupled_ref[...] += coupled_of(dot(choose, columns.astype(bf16)), group)
        return carry

    groups = (jnp.sum(jnp.where(mine, 1.0, 0.0)).astype(jnp.int32) + SLOTS - 1) // SLOTS
    lax.fori_loop(1, groups, group_body, 0)

    same = iota((picks, picks), 0) // rank == iota((picks, picks), 1) // rank
    coupled = jnp.where(same, coupled_ref[...], 0.0)
    pick_id = iota((picks, LANES), 0)
    lane_of = (pick_id // rank % 2 * 2 + pick_id // LANES) * rank + pick_id % rank
    fold = jnp.where(lane_of == iota((picks, LANES), 1), 1.0, 0.0).astype(bf16)
    high, low = [dot(part, fold) for part in two_parts(coupled)]
    coupled = jnp.sum((high + low).reshape(2, chunks, 2, SUB, LANES), axis=(0, 2))

    share = zonal.reshape(chunks, 2, 2, 2, SUB, zones)
    share = jnp.where(lax.axis_index("act") == 0, share[:, :, 0], share[:, :, 1])
    share = jnp.concatenate([share[:, :, 0], share[:, :, 1]], axis=-1)
    switched = switched.reshape(2, actions // 2, rank, zones)
    switched = jnp.concatenate([switched[0], switched[1]], axis=-1)
    held_columns = held_columns.reshape(chunks, 2, rows // chunks // 2, SLOTS)
    pay_ref[:, 0:2 * SUB, :] = share.reshape(chunks, 2 * SUB, LANES)
    pay_ref[:, 2 * SUB:4 * SUB, :] = switched.reshape(chunks, 2 * SUB, LANES)
    pay_ref[:, 4 * SUB:5 * SUB, :] = coupled + total
    pay_ref[:, 5 * SUB:, :] = jnp.concatenate([held_columns[:, 0], held_columns[:, 1]], axis=-1)


def place_kernel(parts_ref, local_ref, meta_ref, mine_ref, theirs_ref):
    chunks = parts_ref.shape[0]
    picks = meta_ref.shape[1] // 2
    half = parts_ref.shape[1] - 5 * SUB
    y_here, y_size = lax.axis_index("yh"), lax.axis_size("yh")
    held = meta_ref[0:1, :].astype(jnp.int32)
    place = meta_ref[1:2, :].astype(jnp.int32)
    known = (held % y_size == y_here) & (place < SLOTS)
    slot = jnp.where(known, held // y_size * SLOTS + place, -1)
    spread = slot_matrix([slot[:, at * picks:(at + 1) * picks] for at in (0, 1)], chunks * SLOTS)
    columns = [
        jnp.concatenate(
            [parts_ref[z, 5 * SUB:, at * SLOTS:(at + 1) * SLOTS] for z in range(chunks)], axis=1
        )
        for at in (0, 1)
    ]
    diff = dot(jnp.concatenate(columns, axis=0).astype(jnp.bfloat16), spread)
    lower = y_here == 0
    for ref, first in ((mine_ref, lower), (theirs_ref, ~lower)):
        ref[0:SUB, :] = jnp.where(first, local_ref[0:SUB, :], local_ref[SUB:2 * SUB, :])
        part = jnp.where(first, diff[0:half], diff[half:])
        ref[SUB:SUB + half, :] = part[:, 0:LANES]
        ref[SUB + half:, :] = part[:, LANES:]


def dense_kernel(swt_ref, branch_ref, sens_ref, diff_ref):
    step = pl.program_id(0)
    rows, block = sens_ref.shape
    picks = swt_ref.shape[0] * swt_ref.shape[1]
    chunks = diff_ref.shape[0]
    half = rows // chunks // 2
    first, second = [
        end - lax.axis_index(BUS) * (block * pl.num_programs(0)) - step * block
        for end in find_picks(swt_ref[...], branch_ref)[1]
    ]

    @pl.when(step == 0)
    def _():
        diff_ref[...] = jnp.zeros_like(diff_ref)

    bus = iota((block, picks), 0)
    select = jnp.where(bus == first, 1.0, jnp.where(bus == second, -1.0, 0.0))
    diff = dot(sens_ref[...], select.astype(jnp.bfloat16)).reshape(chunks, 2, half, picks)
    for at in range(2):
        start = at * 2 * half
        diff_ref[:, start:start + half, :] += diff[:, at, :, 0:LANES]
        diff_ref[:, start + half:start + 2 * half, :] += diff[:, at, :, LANES:]


def solve_kernel(parts_ref, out_ref, total_ref):
    full = parts_ref[...]
    extra = full[2 * SUB:]
    total = extra[0:1, HALF:] / lax.axis_size(CNEC)
    total = jnp.concatenate([total, total], axis=1)
    total_ref[...] = jnp.broadcast_to(total, total_ref.shape)
    row_id = iota((SUB, LANES), 0)
    lane = iota((SUB, LANES), 1)
    eye = jnp.where(lane % SUB == row_id, 1.0, 0.0)
    source = iota((LANES, LANES), 0)
    target = iota((LANES, LANES), 1)
    for tile in range(2):
        spread = (source // SUB == tile * 2 + target // HALF) & (source % SUB == target % SUB)
        left = eye - dot(extra, jnp.where(spread, 1.0, 0.0), HIGHEST)
        right = full[tile * SUB:(tile + 1) * SUB] / total
        for pivot in range(SUB):
            factor = jnp.where(
                lane < HALF, left[:, pivot:pivot + 1], left[:, HALF + pivot:HALF + pivot + 1]
            )
            diagonal = factor[pivot:pivot + 1]
            left_now = left[pivot:pivot + 1] / diagonal
            right_now = right[pivot:pivot + 1] / diagonal
            left = jnp.where(row_id == pivot, left_now, left - factor * left_now)
            right = jnp.where(row_id == pivot, right_now, right - factor * right_now)
        out_ref[:, tile * SUB:(tile + 1) * SUB, :] = jnp.broadcast_to(
            right[None], (out_ref.shape[0], SUB, LANES)
        )


def final_kernel(
    mine_ref, theirs_ref, other_ref, total_ref, solved_ref, position_ref, limit_ref,
    after_ref, loading_ref, margin_ref
):
    actions, share, zones = after_ref.shape
    pairs = actions // 2
    lower = lax.axis_index("act") == 0
    whole = mine_ref[...] + theirs_ref[...]
    mine, other = whole[0:SUB], other_ref[0:SUB]
    low, high = jnp.where(lower, mine, other), jnp.where(lower, other, mine)
    zonal = jnp.concatenate(
        [low[:, :HALF], low[:, HALF:], high[:, :HALF], high[:, HALF:]], axis=0
    ) / total_ref[0:1, :HALF]
    zonal_twice = jnp.concatenate([zonal, zonal], axis=1)
    even, odd = whole[SUB:SUB + share], whole[SUB + share:]
    first = iota((share, LANES), 1) < HALF
    for pair in range(pairs):
        total = zonal_twice
        for j in range(SUB):
            at = pair * SUB + j
            factor = jnp.where(first, even[:, at:at + 1], odd[:, at:at + 1])
            total = total + factor * solved_ref[pair, j:j + 1, :]
        after_ref[2 * pair] = total[:, :HALF]
        after_ref[2 * pair + 1] = total[:, HALF:]
    position = position_ref[...]
    solved = solved_ref[...].reshape(pairs * SUB, LANES)
    flow = dot_nt(position, zonal, HIGHEST)
    shape = (actions, pairs * SUB)
    same = iota(shape, 1) // SUB == iota(shape, 0) // 2
    for side, part in enumerate((even, odd)):
        moved = dot_nt(position, solved[:, side * HALF:(side + 1) * HALF], HIGHEST)
        mask = same & (iota(shape, 0) % 2 == side)
        flow = flow + dot_nt(jnp.where(mask, moved, 0.0), part, HIGHEST)
    limit = limit_ref[...]
    loading_ref[...] = flow / limit
    margin_ref[...] = limit - jnp.abs(flow)


def in_hbm(x):
    return pltpu.with_memory_space_constraint(x, pltpu.HBM)


def params():
    return pltpu.CompilerParams(vmem_limit_bytes=48 * 1024 * 1024)


def body(
    nodal_sensitivity, shift_weight, bus_zone, branch_buses, switched_rows, net_position, flow_limit
):
    rows, cols = nodal_sensitivity.shape
    zones = net_position.shape[0]
    actions, rank = switched_rows.shape
    picks = actions * rank
    n_z, n_yh = lax.axis_size("z"), lax.axis_size("yh")
    share = rows // n_z // n_yh
    f32, i32 = jnp.float32, jnp.int32
    vmem = pl.BlockSpec(memory_space=pltpu.VMEM)
    hbm = pl.BlockSpec(memory_space=pltpu.HBM)

    weight, zone = shift_weight.reshape(1, cols), bus_zone.reshape(1, cols)
    pay, meta = pl.pallas_call(
        partial_kernel,
        out_shape=(
            jax.ShapeDtypeStruct((n_z, 5 * SUB + share, LANES), f32),
            jax.ShapeDtypeStruct((SUB, 2 * picks), f32),
        ),
        in_specs=[hbm] * 5,
        out_specs=(vmem, vmem),
        scratch_shapes=[
            pltpu.VMEM((rank, actions), i32),
            pltpu.VMEM(branch_buses.shape, i32),
            pltpu.VMEM((1, cols), f32),
            pltpu.VMEM((1, cols), i32),
            pltpu.VMEM((rows + 2 * SUB, cols), jnp.bfloat16),
            pltpu.VMEM((rows + 2 * SUB, 2 * zones + SLOTS), f32),
            pltpu.VMEM((picks, picks), f32),
            pltpu.SemaphoreType.DMA((cols // BLOCK + 4,)),
        ],
        compiler_params=params(),
        name="partials",
    )(
        *[in_hbm(x) for x in (switched_rows.T, branch_buses, weight, zone, nodal_sensitivity)]
    )

    swap = [(0, 1), (1, 0)]
    parts = lax.all_to_all(pay, "z", 0, 0, tiled=True)
    local = jnp.sum(parts[:, :5 * SUB], axis=0)

    full = local[2 * SUB:]
    for axis, pairs in (
        ("x", [(0, 1), (1, 0), (2, 3), (3, 2)]),
        ("x", [(0, 3), (3, 0), (1, 2), (2, 1)]),
        ("yl", swap),
        (("yl", "yh"), [(0, 3), (3, 0), (1, 2), (2, 1)]),
    ):
        full = full + lax.ppermute(full, axis, pairs)

    part = jax.ShapeDtypeStruct((SUB + 2 * share, LANES), f32)
    mine, theirs = pl.pallas_call(
        place_kernel,
        out_shape=(part, part),
        in_specs=[vmem] * 3,
        out_specs=(vmem, vmem),
        compiler_params=params(),
        name="place",
    )(parts, local, meta)
    theirs = lax.ppermute(theirs, "yh", swap)
    other = lax.ppermute(
        jnp.concatenate([mine[:SUB] + theirs[:SUB], meta[:, :LANES]], axis=0), "act", swap
    )

    solved, total = pl.pallas_call(
        solve_kernel,
        out_shape=(
            jax.ShapeDtypeStruct((n_z, 2 * SUB, LANES), f32),
            jax.ShapeDtypeStruct((SUB, LANES), f32),
        ),
        in_specs=[vmem],
        out_specs=(vmem, vmem),
        compiler_params=params(),
        name="solve",
    )(full)
    solved = lax.all_to_all(solved, "z", 0, 0, tiled=True).reshape(actions // 2, SUB, LANES)

    def finish(mine, theirs):
        return pl.pallas_call(
            final_kernel,
            out_shape=(
                jax.ShapeDtypeStruct((actions, share, zones), f32),
                jax.ShapeDtypeStruct((actions, share), f32),
                jax.ShapeDtypeStruct((actions, share), f32),
            ),
            in_specs=[vmem] * 7,
            out_specs=(vmem, vmem, vmem),
            compiler_params=params(),
            name="update",
        )(
            mine, theirs, other, total, solved,
            net_position.reshape(1, zones), flow_limit.reshape(1, share),
        )

    def dense():
        diff = pl.pallas_call(
            dense_kernel,
            grid=(cols // BLOCK,),
            out_shape=jax.ShapeDtypeStruct((n_z, n_yh * 2 * share, LANES), f32),
            in_specs=[
                pl.BlockSpec((rank, actions), lambda i: (0, 0)),
                pl.BlockSpec(branch_buses.shape, lambda i: (0, 0)),
                pl.BlockSpec((rows, BLOCK), lambda i: (0, i)),
            ],
            out_specs=pl.BlockSpec((n_z, n_yh * 2 * share, LANES), lambda i: (0, 0, 0)),
            compiler_params=params(),
            name="dense",
        )(*[in_hbm(x) for x in (switched_rows.T, branch_buses, nodal_sensitivity)])
        diff = jnp.sum(lax.all_to_all(diff, "z", 0, 0, tiled=True), axis=0)
        here, size = lax.axis_index("yh"), 2 * share
        own = lax.dynamic_slice_in_dim(diff, here * size, size)
        sent = lax.dynamic_slice_in_dim(diff, (1 - here) * size, size)
        sent = lax.ppermute(sent, "yh", swap)
        return finish(
            jnp.concatenate([mine[:SUB], own], axis=0),
            jnp.concatenate([theirs[:SUB], sent], axis=0),
        )

    over = jnp.maximum(meta[2, 0], other[SUB + 2, 0]) > 0.5
    return lax.cond(over, dense, lambda: finish(mine, theirs))


def solution(mesh):
    n_cnec, n_bus, n_act = mesh.devices.shape
    split = Mesh(
        mesh.devices.reshape(2, n_cnec // 2, n_bus // 2, 2, n_act), ("yl", "x", "z", "yh", "act")
    )
    return jax.shard_map(
        body,
        mesh=split,
        in_specs=(
            P(CNEC, BUS),
            P(BUS),
            P(BUS),
            P(),
            P("act", None),
            P(),
            P(CNEC + BUS),
        ),
        out_specs=(
            P("act", CNEC + BUS, None),
            P("act", CNEC + BUS),
            P("act", CNEC + BUS),
        ),
        check_vma=False,
    )
```

time: 71.1 us -> 62.1 us (0.87)
  starting transfers between devices: 19.4 us -> 12 us
  waiting for transfers between devices: 18.9 us -> 15 us
  blocking collectives: 18 us -> 20.8 us
  Pallas kernels: 13.5 us -> 10.9 us
  between operations: 0.71 us -> 2.01 us
  local copies, waits for them, and re-layouts: 0.01 us -> 1.04 us
    all_to_all x1, starting transfers between devices: 7.18 us -> 3.35 us  [body(): lax.all_to_all(solved, 'z', 0, 0, tiled=True)]
    all_to_all x1 -> x0, starting transfers between devices: 3.49 us -> none  [body(): diff = lax.all_to_all(diff, 'z', 0, 0, tiled=True)]
    all_to_all x1, blocking collectives: 18 us -> 20.8 us  [body(): parts = lax.all_to_all(pay, 'z', 0, 0, tiled=True)]
    pallas_call x1, Pallas kernels: 8.67 us -> 5.88 us  [body(): pl.pallas_call(partial_kernel, out_shape=(jax.ShapeDtypeStruct((n_z, 5 *...]
    all_to_all x1, waiting for transfers between devices: 7.1 us -> 5.21 us  [body(): lax.all_to_all(solved, 'z', 0, 0, tiled=True)]
    ppermute x4, waiting for transfers between devices: 10.7 us -> 9.13 us  [body(): full = full + lax.ppermute(full, axis, pairs)]
    slice x0 -> x3, local copies, waits for them, and re-layouts: none -> 1.03 us  [the longest x2 1.03 us: body(): over = jnp.maximum(meta[2, 0], other[SUB + 2, 0]) > 0.5]
    ppermute x3 -> x2, starting transfers between devices: 2.71 us -> 3.38 us  [the longest x1 3.28 us: body(): theirs = lax.ppermute(theirs, 'yh', swap)]
  transfers between devices with their start and end apart: 9 -> 7, of which waited for: 6 -> 5; matrix products, arithmetic and copies ran while one was open for 0% -> 2% of each run, Pallas kernels for 2% -> 0%
where the time goes in v4:
time: 62.1 us; the launch traced here: 61.8 us
  blocking collectives  20.8 us (33%)
  waiting for transfers between devices  15 us (24%)
  starting transfers between devices  12 us (19%)
  Pallas kernels  10.9 us (18%)
  between operations  2.01 us (3%)
  local copies, waits for them, and re-layouts  1.04 us (2%)
    all_to_all x1, blocking collectives, body(): parts = lax.all_to_all(pay, 'z', 0, 0, tiled=True)  20.8 us
    ppermute x4, waiting for transfers between devices, body(): full = full + lax.ppermute(full, axis, pairs)  9.13 us
    pallas_call x1, Pallas kernels, body(): pl.pallas_call(partial_kernel, out_shape=(jax.ShapeDtypeStruct((n_z, 5 *...  5.88 us
    ppermute x4, starting transfers between devices, body(): full = full + lax.ppermute(full, axis, pairs)  5.28 us
    all_to_all x1, waiting for transfers between devices, body(): lax.all_to_all(solved, 'z', 0, 0, tiled=True)  5.21 us
    all_to_all x1, starting transfers between devices, body(): lax.all_to_all(solved, 'z', 0, 0, tiled=True)  3.35 us
    ppermute x1, starting transfers between devices, body(): theirs = lax.ppermute(theirs, 'yh', swap)  3.28 us
    pallas_call x1, Pallas kernels, finish(): pl.pallas_call(final_kernel, out_shape=(jax.ShapeDtypeStruct((actions, sh...  3.26 us
  transfers between devices with their start and end apart: 7, of which 5 were waited for; matrix products, arithmetic and copies ran while one was open for 2% of the time, Pallas kernels for 0%

profile of v4, /device:TPU:6, one launch (start us, length us, event | category | flops | bytes accessed | tf_op | source)
XLA Modules:
  0.0 61.8 jit_solution(7806291996068253647)
XLA Ops:
  0.6 0.0 copy-start.1
  0.6 0.0 copy-start
  0.7 5.9 %partials.1 = (f32[8,72,128]{2,1,0:T(8,128)S(1)}, f32[8,512]{1,0:T(8,128)S(1)}) custom-call(s32[8,32]{1,0:T(8,128)} %bitcast.14, s32[2,4096]{1,0:T(2,128)} %branch_hbm.1, f32[1,8192]{1,0:T(1,128)} %bitcast.12, s32[1,8192]{1,0:T(1,128)} %bitcast.13, bf16[512,8192]{1,0:T(8,128)(2,1)} %sens_hbm.1), custom_call_target="tpu_custom_call" | custom-call | tf_op jit(solution)/shard_map/partials/pallas_call | solution.py:347
  6.5 20.8 %all_to_all.14.parts_ref = f32[8,72,128]{2,1,0:T(8,128)S(1)} all-to-all(f32[8,72,128]{2,1,0:T(8,128)S(1)} %get-tuple-element.61), channel_id=1, replica_groups=mesh['yl'=2,'x'=4,'z'=8,'yh'=2,'act'=2] {'z'}, dimensions={0} | all-to-all | bytes 589824 | tf_op jit(solution)/shard_map/all_to_all | solution.py:372
  27.4 0.9 %collective-permute-start.3 = (f32[24,128]{1,0:T(8,128)S(1)}, f32[24,128]{1,0:T(8,128)S(1)}, u32[]{:S(2)}, u32[]{:S(2)}) collective-permute-start(f32[24,128]{1,0:T(8,128)S(1)} %slice.37), channel_id=1, source_target_pairs={{0,32},{32,0},{64,96},{96,64},{1,33},{33,1},{65,97},{97,65},{2,34}... | collective-permute-start | bytes 36872 | tf_op jit(solution)/shard_map/ppermute | solution.py:382
  28.3 0.2 place.1
  28.6 3.3 %collective-permute-start.1 = (f32[72,128]{1,0:T(8,128)S(1)}, f32[72,128]{1,0:T(8,128)S(1)}, u32[]{:S(2)}, u32[]{:S(2)}) collective-permute-start(f32[72,128]{1,0:T(8,128)S(1)} %get-tuple-element.63), channel_id=1, source_target_pairs={{0,2},{2,0},{1,3},{3,1},{4,6},{6,4},{5,7},{7,5},{8,10},{10,8},{9,1... | collective-permute-start | bytes 110600 | tf_op jit(solution)/shard_map/ppermute | solution.py:393
  31.9 0.0 collective-permute-done.3
  31.9 1.1 %collective-permute-start.4 = (f32[24,128]{1,0:T(8,128)S(1)}, f32[24,128]{1,0:T(8,128)S(1)}, u32[]{:S(2)}, u32[]{:S(2)}) collective-permute-start(f32[24,128]{1,0:T(8,128)S(1)} %slice_add_fusion.1), channel_id=1, source_target_pairs={{0,96},{96,0},{32,64},{64,32},{1,97},{97,1},{33,65},{65,33},{2,98}... | collective-permute-start | bytes 36872 | tf_op jit(solution)/shard_map/ppermute | solution.py:382
  33.0 3.8 %collective-permute-done.4 = f32[24,128]{1,0:T(8,128)S(1)} collective-permute-done((f32[24,128]{1,0:T(8,128)S(1)}, f32[24,128]{1,0:T(8,128)S(1)}, u32[]{:S(2)}, u32[]{:S(2)}) %collective-permute-start.4) | collective-permute-done | bytes 12320 | tf_op jit(solution)/shard_map/ppermute | solution.py:382
  36.8 0.9 %collective-permute-start.5 = (f32[24,128]{1,0:T(8,128)S(1)}, f32[24,128]{1,0:T(8,128)S(1)}, u32[]{:S(2)}, u32[]{:S(2)}) collective-permute-start(f32[24,128]{1,0:T(8,128)S(1)} %add.23), channel_id=1, source_target_pairs={{0,128},{128,0},{1,129},{129,1},{2,130},{130,2},{3,131},{131,3},{4... | collective-permute-start | bytes 36872 | tf_op jit(solution)/shard_map/ppermute | solution.py:382
  37.7 2.8 %collective-permute-done.5 = f32[24,128]{1,0:T(8,128)S(1)} collective-permute-done((f32[24,128]{1,0:T(8,128)S(1)}, f32[24,128]{1,0:T(8,128)S(1)}, u32[]{:S(2)}, u32[]{:S(2)}) %collective-permute-start.5) | collective-permute-done | bytes 12320 | tf_op jit(solution)/shard_map/ppermute | solution.py:382
  40.5 2.3 %collective-permute-start.6 = (f32[24,128]{1,0:T(8,128)S(1)}, f32[24,128]{1,0:T(8,128)S(1)}, u32[]{:S(2)}, u32[]{:S(2)}) collective-permute-start(f32[24,128]{1,0:T(8,128)S(1)} %add.24), channel_id=1, source_target_pairs={{0,130},{130,0},{2,128},{128,2},{1,131},{131,1},{3,129},{129,3},{4... | collective-permute-start | bytes 36872 | tf_op jit(solution)/shard_map/ppermute | solution.py:382
  42.8 0.0 collective-permute-done.1
  42.8 2.6 %collective-permute-done.6 = f32[24,128]{1,0:T(8,128)S(1)} collective-permute-done((f32[24,128]{1,0:T(8,128)S(1)}, f32[24,128]{1,0:T(8,128)S(1)}, u32[]{:S(2)}, u32[]{:S(2)}) %collective-permute-start.6) | collective-permute-done | bytes 12320 | tf_op jit(solution)/shard_map/ppermute | solution.py:382
  45.4 1.5 %solve.1 = (f32[8,16,128]{2,1,0:T(8,128)}, f32[8,128]{1,0:T(8,128)S(1)}) custom-call(f32[24,128]{1,0:T(8,128)S(1)} %add.25.parts_ref), custom_call_target="tpu_custom_call" | custom-call | tf_op jit(solution)/shard_map/solve/pallas_call | solution.py:398
  46.9 3.4 %all-to-all-start.2 = ((f32[8,16,128]{2,1,0:T(8,128)}), f32[8,16,128]{2,1,0:T(8,128)S(1)}, u32[]{:S(2)}, u32[]{:S(2)}) async-start(f32[8,16,128]{2,1,0:T(8,128)} %get-tuple-element.65), calls=%async_computation.2 | async-start | bytes 131072 | tf_op jit(solution)/shard_map/all_to_all | solution.py:409
  50.3 0.1 collective-permute-start.2
  50.4 0.5 slice.27
  50.9 0.6 %collective-permute-done.2 = f32[16,128]{1,0:T(8,128)S(1)} collective-permute-done((f32[16,128]{1,0:T(8,128)S(1)}, f32[16,128]{1,0:T(8,128)S(1)}, u32[]{:S(2)}, u32[]{:S(2)}) %collective-permute-start.2) | collective-permute-done | bytes 8224 | tf_op jit(solution)/shard_map/ppermute | solution.py:394
  51.5 0.5 slice.36
  53.3 5.2 %all-to-all-done.2 = f32[8,16,128]{2,1,0:T(8,128)S(1)} async-done(((f32[8,16,128]{2,1,0:T(8,128)}), f32[8,16,128]{2,1,0:T(8,128)S(1)}, u32[]{:S(2)}, u32[]{:S(2)}) %all-to-all-start.2) | async-done | bytes 65568 | tf_op jit(solution)/shard_map/all_to_all | solution.py:409
  58.6 0.0 copy-done.1
  58.6 0.0 copy-done
  58.6 3.3 %conditional.1 = ((f32[32,32,64]{2,1,0:T(8,128)}, f32[32,32]{1,0:T(8,128)}, f32[32,32]{1,0:T(8,128)})) conditional(s32[]{:T(128)} %bitcast.8, (f32[64]{0:T(128)S(1)}, f32[32]{0:T(128)S(1)}, f32[72,128]{1,0:T(8,128)S(1)}, f32[72,128]{1,0:T(8,128)S(1)}, f32[16,128]{1,0:T(8,128)S(1)}, /*index=5*/f32[8,128]{1,0:T(8,128)S(1)}, ...), branch_computations={%region_1.0_spmd, %region_2.0_spmd} | conditional | flops 133132 | bytes 2588900 | solution.py:453
  58.6 3.3 %update.2 = (f32[32,32,64]{2,1,0:T(8,128)}, f32[32,32]{1,0:T(8,128)}, f32[32,32]{1,0:T(8,128)}) custom-call(f32[72,128]{1,0:T(8,128)S(1)} %get-tuple-element.34.mine_ref, f32[72,128]{1,0:T(8,128)S(1)} %get-tuple-element.35.theirs_ref, f32[16,128]{1,0:T(8,128)S(1)} %get-tuple-element.36.other_ref, f32[8,128]{1,0:T(8,128)S(1)} %get-tuple-element.37.total_ref, ...), custom_call_target="tpu_custom_call" | custom-call | tf_op jit(solution)/shard_map/cond/branch_0_fun/update/pallas_call | solution.py:412
  (9 shorter events, 0.0 us)
Async XLA Ops:
  0.6 57.9 %copy-start.1 = (f32[32]{0:T(128)S(1)}, f32[32]{0:T(128)}, u32[]{:S(2)}) copy-start(f32[32]{0:T(128)} %param.15) | copy-start | bytes 388
  0.6 57.9 %copy-start = (f32[64]{0:T(128)S(1)}, f32[64]{0:T(128)}, u32[]{:S(2)}) copy-start(f32[64]{0:T(128)} %param.14) | copy-start | bytes 772
  27.4 4.5 %collective-permute-start.3 = (f32[24,128]{1,0:T(8,128)S(1)}, f32[24,128]{1,0:T(8,128)S(1)}, u32[]{:S(2)}, u32[]{:S(2)}) collective-permute-start(f32[24,128]{1,0:T(8,128)S(1)} %slice.37), channel_id=1, source_target_pairs={{0,32},{32,0},{64,96},{96,64},{1,33},{33,1},{65,97},{97,65},{2,34}... | collective-permute-start | bytes 36872 | tf_op jit(solution)/shard_map/ppermute | solution.py:382
  28.6 14.2 %collective-permute-start.1 = (f32[72,128]{1,0:T(8,128)S(1)}, f32[72,128]{1,0:T(8,128)S(1)}, u32[]{:S(2)}, u32[]{:S(2)}) collective-permute-start(f32[72,128]{1,0:T(8,128)S(1)} %get-tuple-element.63), channel_id=1, source_target_pairs={{0,2},{2,0},{1,3},{3,1},{4,6},{6,4},{5,7},{7,5},{8,10},{10,8},{9,1... | collective-permute-start | bytes 110600 | tf_op jit(solution)/shard_map/ppermute | solution.py:393
  31.9 4.9 %collective-permute-start.4 = (f32[24,128]{1,0:T(8,128)S(1)}, f32[24,128]{1,0:T(8,128)S(1)}, u32[]{:S(2)}, u32[]{:S(2)}) collective-permute-start(f32[24,128]{1,0:T(8,128)S(1)} %slice_add_fusion.1), channel_id=1, source_target_pairs={{0,96},{96,0},{32,64},{64,32},{1,97},{97,1},{33,65},{65,33},{2,98}... | collective-permute-start | bytes 36872 | tf_op jit(solution)/shard_map/ppermute | solution.py:382
  36.8 3.7 %collective-permute-start.5 = (f32[24,128]{1,0:T(8,128)S(1)}, f32[24,128]{1,0:T(8,128)S(1)}, u32[]{:S(2)}, u32[]{:S(2)}) collective-permute-start(f32[24,128]{1,0:T(8,128)S(1)} %add.23), channel_id=1, source_target_pairs={{0,128},{128,0},{1,129},{129,1},{2,130},{130,2},{3,131},{131,3},{4... | collective-permute-start | bytes 36872 | tf_op jit(solution)/shard_map/ppermute | solution.py:382
  40.5 4.9 %collective-permute-start.6 = (f32[24,128]{1,0:T(8,128)S(1)}, f32[24,128]{1,0:T(8,128)S(1)}, u32[]{:S(2)}, u32[]{:S(2)}) collective-permute-start(f32[24,128]{1,0:T(8,128)S(1)} %add.24), channel_id=1, source_target_pairs={{0,130},{130,0},{2,128},{128,2},{1,131},{131,1},{3,129},{129,3},{4... | collective-permute-start | bytes 36872 | tf_op jit(solution)/shard_map/ppermute | solution.py:382
  46.9 11.7 %all-to-all-start.2 = ((f32[8,16,128]{2,1,0:T(8,128)}), f32[8,16,128]{2,1,0:T(8,128)S(1)}, u32[]{:S(2)}, u32[]{:S(2)}) async-start(f32[8,16,128]{2,1,0:T(8,128)} %get-tuple-element.65), calls=%async_computation.2 | async-start | bytes 131072 | tf_op jit(solution)/shard_map/all_to_all | solution.py:409
  50.3 1.3 %collective-permute-start.2 = (f32[16,128]{1,0:T(8,128)S(1)}, f32[16,128]{1,0:T(8,128)S(1)}, u32[]{:S(2)}, u32[]{:S(2)}) collective-permute-start(f32[16,128]{1,0:T(8,128)S(1)} %pad_maximum_fusion.2), channel_id=1, source_target_pairs={{0,1},{1,0},{2,3},{3,2},{4,5},{5,4},{6,7},{7,6},{8,9},{9,8},{10,11... | collective-permute-start | bytes 24584 | tf_op jit(solution)/shard_map/ppermute | solution.py:394

commit v5 on v4

--- a/solution.py
+++ b/solution.py
@@ -32,6 +32,12 @@
 def two_parts(values):
     high = values.astype(jnp.bfloat16)
     return high, (values - high.astype(jnp.float32)).astype(jnp.bfloat16)
+
+
+def by_parts(product, x, y):
+    x_high, x_low = two_parts(x)
+    y_high, y_low = two_parts(y)
+    return product(x_high, y_high) + product(x_high, y_low) + product(x_low, y_high)
 
 
 def digits(values, base, count):
@@ -154,7 +160,8 @@
         acc_ref[...] += dot_nt(sens_ref[:, at], key)
         return carry
 
-    lax.fori_loop(0, steps, step_body, 0)
+    for step in range(steps):
+        step_body(step, 0)
 
     chunks = pay_ref.shape[0]
     zonal = acc_ref[0:rows, 0:zones] + acc_ref[0:rows, zones:2 * zones]
@@ -222,13 +229,20 @@
         )
         for at in (0, 1)
     ]
-    diff = dot(jnp.concatenate(columns, axis=0).astype(jnp.bfloat16), spread)
+    columns = jnp.concatenate(columns, axis=0).astype(jnp.bfloat16)
+    diff = lax.dot_general(
+        spread, columns, (((0,), (1,)), ((), ())), preferred_element_type=jnp.float32
+    )
+    diff = diff.reshape(2, picks // (2 * SUB), SUB, 2 * half)
+    diff = jnp.concatenate([diff[0], diff[1]], axis=1).reshape(4, picks // 4, 2 * half)
     lower = y_here == 0
+    packed = [
+        jnp.concatenate([diff[g, :, at * half:(at + 1) * half] for g in range(4)], axis=1)
+        for at in (0, 1)
+    ]
     for ref, first in ((mine_ref, lower), (theirs_ref, ~lower)):
         ref[0:SUB, :] = jnp.where(first, local_ref[0:SUB, :], local_ref[SUB:2 * SUB, :])
-        part = jnp.where(first, diff[0:half], diff[half:])
-        ref[SUB:SUB + half, :] = part[:, 0:LANES]
-        ref[SUB + half:, :] = part[:, LANES:]
+        ref[SUB:, :] = jnp.where(first, packed[0], packed[1])
 
 
 def dense_kernel(swt_ref, branch_ref, sens_ref, diff_ref):
@@ -266,21 +280,25 @@
     eye = jnp.where(lane % SUB == row_id, 1.0, 0.0)
     source = iota((LANES, LANES), 0)
     target = iota((LANES, LANES), 1)
+    lefts, rights = [], []
     for tile in range(2):
         spread = (source // SUB == tile * 2 + target // HALF) & (source % SUB == target % SUB)
-        left = eye - dot(extra, jnp.where(spread, 1.0, 0.0), HIGHEST)
-        right = full[tile * SUB:(tile + 1) * SUB] / total
-        for pivot in range(SUB):
+        lefts.append(eye - dot(extra, jnp.where(spread, 1.0, 0.0), HIGHEST))
+        rights.append(full[tile * SUB:(tile + 1) * SUB] / total)
+    for pivot in range(SUB):
+        for tile in range(2):
+            left, right = lefts[tile], rights[tile]
             factor = jnp.where(
                 lane < HALF, left[:, pivot:pivot + 1], left[:, HALF + pivot:HALF + pivot + 1]
             )
             diagonal = factor[pivot:pivot + 1]
             left_now = left[pivot:pivot + 1] / diagonal
             right_now = right[pivot:pivot + 1] / diagonal
-            left = jnp.where(row_id == pivot, left_now, left - factor * left_now)
-            right = jnp.where(row_id == pivot, right_now, right - factor * right_now)
+            lefts[tile] = jnp.where(row_id == pivot, left_now, left - factor * left_now)
+            rights[tile] = jnp.where(row_id == pivot, right_now, right - factor * right_now)
+    for tile in range(2):
         out_ref[:, tile * SUB:(tile + 1) * SUB, :] = jnp.broadcast_to(
-            right[None], (out_ref.shape[0], SUB, LANES)
+            rights[tile][None], (out_ref.shape[0], SUB, LANES)
         )
 
 
@@ -292,31 +310,43 @@
     pairs = actions // 2
     lower = lax.axis_index("act") == 0
     whole = mine_ref[...] + theirs_ref[...]
-    mine, other = whole[0:SUB], other_ref[0:SUB]
+    mine, other = whole[0:SUB], other_ref[...]
     low, high = jnp.where(lower, mine, other), jnp.where(lower, other, mine)
     zonal = jnp.concatenate(
         [low[:, :HALF], low[:, HALF:], high[:, :HALF], high[:, HALF:]], axis=0
     ) / total_ref[0:1, :HALF]
     zonal_twice = jnp.concatenate([zonal, zonal], axis=1)
-    even, odd = whole[SUB:SUB + share], whole[SUB + share:]
-    first = iota((share, LANES), 1) < HALF
+    groups = [whole[SUB:, g * share:(g + 1) * share] for g in range(LANES // share)]
+    diff = jnp.concatenate(groups, axis=0)
+    solved = solved_ref[...]
+    first = iota(solved.shape, 2) < HALF
+    solved = jnp.concatenate(
+        [jnp.where(first, solved, 0.0), jnp.where(first, 0.0, solved)], axis=1
+    )
+    diff_high, diff_low = two_parts(diff)
+    solved_high, solved_low = two_parts(solved)
+
+    def product(x, y):
+        return lax.dot_general(
+            x, y, (((0,), (0,)), ((), ())), preferred_element_type=jnp.float32
+        )
+
+    size = 2 * SUB
     for pair in range(pairs):
-        total = zonal_twice
-        for j in range(SUB):
-            at = pair * SUB + j
-            factor = jnp.where(first, even[:, at:at + 1], odd[:, at:at + 1])
-            total = total + factor * solved_ref[pair, j:j + 1, :]
+        at = slice(pair * size, (pair + 1) * size)
+        left = jnp.concatenate([diff_high[at], diff_high[at], diff_low[at]], axis=0)
+        right = jnp.concatenate(
+            [solved_high[pair], solved_low[pair], solved_high[pair]], axis=0
+        )
+        total = zonal_twice + product(left, right)
         after_ref[2 * pair] = total[:, :HALF]
         after_ref[2 * pair + 1] = total[:, HALF:]
     position = position_ref[...]
-    solved = solved_ref[...].reshape(pairs * SUB, LANES)
-    flow = dot_nt(position, zonal, HIGHEST)
-    shape = (actions, pairs * SUB)
-    same = iota(shape, 1) // SUB == iota(shape, 0) // 2
-    for side, part in enumerate((even, odd)):
-        moved = dot_nt(position, solved[:, side * HALF:(side + 1) * HALF], HIGHEST)
-        mask = same & (iota(shape, 0) % 2 == side)
-        flow = flow + dot_nt(jnp.where(mask, moved, 0.0), part, HIGHEST)
+    twice = jnp.concatenate([position, position], axis=1)
+    moved = by_parts(dot_nt, twice, solved.reshape(pairs * size, LANES))
+    shape = (actions, pairs * size)
+    same = iota(shape, 1) // SUB == iota(shape, 0)
+    flow = by_parts(dot_nt, position, zonal) + by_parts(dot, jnp.where(same, moved, 0.0), diff)
     limit = limit_ref[...]
     loading_ref[...] = flow / limit
     margin_ref[...] = limit - jnp.abs(flow)
@@ -373,13 +403,13 @@
     local = jnp.sum(parts[:, :5 * SUB], axis=0)
 
     full = local[2 * SUB:]
-    for axis, pairs in (
-        ("x", [(0, 1), (1, 0), (2, 3), (3, 2)]),
-        ("x", [(0, 3), (3, 0), (1, 2), (2, 1)]),
-        ("yl", swap),
-        (("yl", "yh"), [(0, 3), (3, 0), (1, 2), (2, 1)]),
-    ):
-        full = full + lax.ppermute(full, axis, pairs)
+    for axis in ("x", ("yl", "yh")):
+        size = lax.axis_size(axis)
+        others = [
+            lax.ppermute(full, axis, [(at, (at + by) % size) for at in range(size)])
+            for by in range(1, size)
+        ]
+        full = sum(others, full)
 
     part = jax.ShapeDtypeStruct((SUB + 2 * share, LANES), f32)
     mine, theirs = pl.pallas_call(
@@ -391,9 +421,7 @@
         name="place",
     )(parts, local, meta)
     theirs = lax.ppermute(theirs, "yh", swap)
-    other = lax.ppermute(
-        jnp.concatenate([mine[:SUB] + theirs[:SUB], meta[:, :LANES]], axis=0), "act", swap
-    )
+    other = lax.ppermute(mine[:SUB] + theirs[:SUB], "act", swap)
 
     solved, total = pl.pallas_call(
         solve_kernel,
@@ -444,13 +472,17 @@
         own = lax.dynamic_slice_in_dim(diff, here * size, size)
         sent = lax.dynamic_slice_in_dim(diff, (1 - here) * size, size)
         sent = lax.ppermute(sent, "yh", swap)
+
+        def packed(x):
+            x = x.reshape(2, share, 4, actions // 8, rank)
+            return x.transpose(3, 0, 4, 2, 1).reshape(picks // 4, 4 * share)
+
         return finish(
-            jnp.concatenate([mine[:SUB], own], axis=0),
-            jnp.concatenate([theirs[:SUB], sent], axis=0),
-        )
-
-    over = jnp.maximum(meta[2, 0], other[SUB + 2, 0]) > 0.5
-    return lax.cond(over, dense, lambda: finish(mine, theirs))
+            jnp.concatenate([mine[:SUB], packed(own)], axis=0),
+            jnp.concatenate([theirs[:SUB], packed(sent)], axis=0),
+        )
+
+    return lax.cond(meta[2, 0] > 0.5, dense, lambda: finish(mine, theirs))
 
 
 def solution(mesh):

time: 62.1 us -> 60.8 us (0.979)
  the two profiles are of different devices: /device:TPU:6 before, /device:TPU:16 now
where the time goes in v5:
time: 60.8 us; the launch traced here: 60.5 us
  blocking collectives  20.8 us (34%)
  starting transfers between devices  14.9 us (25%)
  waiting for transfers between devices  12 us (20%)
  Pallas kernels  10.9 us (18%)
  between operations  1.38 us (2%)
    all_to_all x1, blocking collectives, body(): parts = lax.all_to_all(pay, 'z', 0, 0, tiled=True)  20.8 us
    ppermute x6, starting transfers between devices, body(): lax.ppermute(full, axis, [(at, (at + by) % size) for at in range(size)])  9.05 us
    pallas_call x1, Pallas kernels, body(): pl.pallas_call(partial_kernel, out_shape=(jax.ShapeDtypeStruct((n_z, 5 *...  7.68 us
    all_to_all x1, waiting for transfers between devices, body(): lax.all_to_all(solved, 'z', 0, 0, tiled=True)  6.81 us
    ppermute x6, waiting for transfers between devices, body(): lax.ppermute(full, axis, [(at, (at + by) % size) for at in range(size)])  5.17 us
    all_to_all x1, starting transfers between devices, body(): lax.all_to_all(solved, 'z', 0, 0, tiled=True)  3.35 us
    ppermute x1, starting transfers between devices, body(): theirs = lax.ppermute(theirs, 'yh', swap)  2.21 us
    pallas_call x1, Pallas kernels, body(): pl.pallas_call(solve_kernel, out_shape=(jax.ShapeDtypeStruct((n_z, 2 * SU...  1.51 us
  transfers between devices with their start and end apart: 9, of which 5 were waited for; matrix products, arithmetic and copies ran while one was open for 1% of the time, Pallas kernels for 3%

profile of v5, /device:TPU:16, one launch (start us, length us, event | category | flops | bytes accessed | tf_op | source)
XLA Modules:
  0.0 60.5 jit_solution(9159244634486792245)
XLA Ops:
  0.6 0.0 copy-start.1
  0.6 0.0 copy-start
  0.7 7.7 %partials.1 = (f32[8,72,128]{2,1,0:T(8,128)S(1)}, f32[8,512]{1,0:T(8,128)S(1)}) custom-call(s32[8,32]{1,0:T(8,128)} %bitcast.22, s32[2,4096]{1,0:T(2,128)} %branch_hbm.1, f32[1,8192]{1,0:T(1,128)} %bitcast.20, s32[1,8192]{1,0:T(1,128)} %bitcast.21, bf16[512,8192]{1,0:T(8,128)(2,1)} %sens_hbm.1), custom_call_target="tpu_custom_call" | custom-call | tf_op jit(solution)/shard_map/partials/pallas_call | solution.py:377
  8.3 20.8 %all_to_all.14.parts_ref = f32[8,72,128]{2,1,0:T(8,128)S(1)} all-to-all(f32[8,72,128]{2,1,0:T(8,128)S(1)} %get-tuple-element.61), channel_id=1, replica_groups=mesh['yl'=2,'x'=4,'z'=8,'yh'=2,'act'=2] {'z'}, dimensions={0} | all-to-all | bytes 589824 | tf_op jit(solution)/shard_map/all_to_all | solution.py:402
  29.2 3.1 %collective-permute-start.4 = (f32[24,128]{1,0:T(8,128)S(1)}, f32[24,128]{1,0:T(8,128)S(1)}, u32[]{:S(2)}, u32[]{:S(2)}) collective-permute-start(f32[24,128]{1,0:T(8,128)S(1)} %slice.28), channel_id=1, source_target_pairs={{0,64},{32,96},{64,0},{96,32},{1,65},{33,97},{65,1},{97,33},{2,66}... | collective-permute-start | bytes 36872 | tf_op jit(solution)/shard_map/ppermute | solution.py:409
  32.3 1.1 %collective-permute-start.5 = (f32[24,128]{1,0:T(8,128)S(1)}, f32[24,128]{1,0:T(8,128)S(1)}, u32[]{:S(2)}, u32[]{:S(2)}) collective-permute-start(f32[24,128]{1,0:T(8,128)S(1)} %slice.28), channel_id=1, source_target_pairs={{0,96},{32,0},{64,32},{96,64},{1,97},{33,1},{65,33},{97,65},{2,98}... | collective-permute-start | bytes 36872 | tf_op jit(solution)/shard_map/ppermute | solution.py:409
  33.5 0.9 %collective-permute-start.3 = (f32[24,128]{1,0:T(8,128)S(1)}, f32[24,128]{1,0:T(8,128)S(1)}, u32[]{:S(2)}, u32[]{:S(2)}) collective-permute-start(f32[24,128]{1,0:T(8,128)S(1)} %slice.28), channel_id=1, source_target_pairs={{0,32},{32,64},{64,96},{96,0},{1,33},{33,65},{65,97},{97,1},{2,34}... | collective-permute-start | bytes 36872 | tf_op jit(solution)/shard_map/ppermute | solution.py:409
  34.3 0.1 collective-permute-done.4
  34.5 1.5 %collective-permute-done.5 = f32[24,128]{1,0:T(8,128)S(1)} collective-permute-done((f32[24,128]{1,0:T(8,128)S(1)}, f32[24,128]{1,0:T(8,128)S(1)}, u32[]{:S(2)}, u32[]{:S(2)}) %collective-permute-start.5) | collective-permute-done | bytes 12320 | tf_op jit(solution)/shard_map/ppermute | solution.py:409
  36.0 2.4 %collective-permute-done.3 = f32[24,128]{1,0:T(8,128)S(1)} collective-permute-done((f32[24,128]{1,0:T(8,128)S(1)}, f32[24,128]{1,0:T(8,128)S(1)}, u32[]{:S(2)}, u32[]{:S(2)}) %collective-permute-start.3) | collective-permute-done | bytes 12320 | tf_op jit(solution)/shard_map/ppermute | solution.py:409
  38.4 0.3 collective-permute-start.8
  38.7 2.2 %collective-permute-start.7 = (f32[24,128]{1,0:T(8,128)S(1)}, f32[24,128]{1,0:T(8,128)S(1)}, u32[]{:S(2)}, u32[]{:S(2)}) collective-permute-start(f32[24,128]{1,0:T(8,128)S(1)} %add_add_fusion.1), channel_id=1, source_target_pairs={{0,128},{2,130},{128,0},{130,2},{1,129},{3,131},{129,1},{131,3},{4... | collective-permute-start | bytes 36872 | tf_op jit(solution)/shard_map/ppermute | solution.py:409
  40.9 1.4 %collective-permute-start.6 = (f32[24,128]{1,0:T(8,128)S(1)}, f32[24,128]{1,0:T(8,128)S(1)}, u32[]{:S(2)}, u32[]{:S(2)}) collective-permute-start(f32[24,128]{1,0:T(8,128)S(1)} %add_add_fusion.1), channel_id=1, source_target_pairs={{0,2},{2,128},{128,130},{130,0},{1,3},{3,129},{129,131},{131,1},{4... | collective-permute-start | bytes 36872 | tf_op jit(solution)/shard_map/ppermute | solution.py:409
  42.3 0.4 place.1
  42.7 2.2 %collective-permute-start.1 = (f32[72,128]{1,0:T(8,128)S(1)}, f32[72,128]{1,0:T(8,128)S(1)}, u32[]{:S(2)}, u32[]{:S(2)}) collective-permute-start(f32[72,128]{1,0:T(8,128)S(1)} %get-tuple-element.63), channel_id=1, source_target_pairs={{0,2},{2,0},{1,3},{3,1},{4,6},{6,4},{5,7},{7,5},{8,10},{10,8},{9,1... | collective-permute-start | bytes 110600 | tf_op jit(solution)/shard_map/ppermute | solution.py:423
  44.9 0.0 collective-permute-done.8
  44.9 0.0 collective-permute-done.7
  44.9 1.1 %collective-permute-done.6 = f32[24,128]{1,0:T(8,128)S(1)} collective-permute-done((f32[24,128]{1,0:T(8,128)S(1)}, f32[24,128]{1,0:T(8,128)S(1)}, u32[]{:S(2)}, u32[]{:S(2)}) %collective-permute-start.6) | collective-permute-done | bytes 12320 | tf_op jit(solution)/shard_map/ppermute | solution.py:409
  46.1 1.5 %solve.1 = (f32[8,16,128]{2,1,0:T(8,128)}, f32[8,128]{1,0:T(8,128)S(1)}) custom-call(f32[24,128]{1,0:T(8,128)S(1)} %add_add_fusion.parts_ref), custom_call_target="tpu_custom_call" | custom-call | tf_op jit(solution)/shard_map/solve/pallas_call | solution.py:426
  47.6 3.4 %all-to-all-start.2 = ((f32[8,16,128]{2,1,0:T(8,128)}), f32[8,16,128]{2,1,0:T(8,128)S(1)}, u32[]{:S(2)}, u32[]{:S(2)}) async-start(f32[8,16,128]{2,1,0:T(8,128)} %get-tuple-element.65), calls=%async_computation.2 | async-start | bytes 131072 | tf_op jit(solution)/shard_map/all_to_all | solution.py:437
  51.0 0.0 collective-permute-done.1
  51.0 0.3 collective-permute-start.2
  51.3 0.5 slice.21
  52.4 0.0 collective-permute-done.2
  52.4 6.8 %all-to-all-done.2 = f32[8,16,128]{2,1,0:T(8,128)S(1)} async-done(((f32[8,16,128]{2,1,0:T(8,128)}), f32[8,16,128]{2,1,0:T(8,128)S(1)}, u32[]{:S(2)}, u32[]{:S(2)}) %all-to-all-start.2) | async-done | bytes 65568 | tf_op jit(solution)/shard_map/all_to_all | solution.py:437
  59.3 0.0 copy-done.1
  59.3 0.0 copy-done
  59.3 1.3 %conditional.1 = ((f32[32,32,64]{2,1,0:T(8,128)}, f32[32,32]{1,0:T(8,128)}, f32[32,32]{1,0:T(8,128)})) conditional(s32[]{:T(128)} %bitcast.10, (f32[64]{0:T(128)S(1)}, f32[32]{0:T(128)S(1)}, f32[72,128]{1,0:T(8,128)S(1)}, f32[72,128]{1,0:T(8,128)S(1)}, f32[8,128]{1,0:T(8,128)S(1)}, /*index=5*/f32[8,128]{1,0:T(8,128)S(1)}, ...), branch_computations={%region_1.0_spmd, %region_2.0_spmd} | conditional | flops 133132 | bytes 3113188 | solution.py:485
  59.3 1.3 %update.2 = (f32[32,32,64]{2,1,0:T(8,128)}, f32[32,32]{1,0:T(8,128)}, f32[32,32]{1,0:T(8,128)}) custom-call(f32[72,128]{1,0:T(8,128)S(1)} %get-tuple-element.34.mine_ref, f32[72,128]{1,0:T(8,128)S(1)} %get-tuple-element.35.theirs_ref, f32[8,128]{1,0:T(8,128)S(1)} %get-tuple-element.36.other_ref, f32[8,128]{1,0:T(8,128)S(1)} %get-tuple-element.37.total_ref, ...), custom_call_target="tpu_custom_call" | custom-call | tf_op jit(solution)/shard_map/cond/branch_0_fun/update/pallas_call | solution.py:440
  (5 shorter events, 0.0 us)
Async XLA Ops:
  0.6 58.6 %copy-start.1 = (f32[32]{0:T(128)S(1)}, f32[32]{0:T(128)}, u32[]{:S(2)}) copy-start(f32[32]{0:T(128)} %param.15) | copy-start | bytes 388
  0.6 58.6 %copy-start = (f32[64]{0:T(128)S(1)}, f32[64]{0:T(128)}, u32[]{:S(2)}) copy-start(f32[64]{0:T(128)} %param.14) | copy-start | bytes 772
  29.2 5.3 %collective-permute-start.4 = (f32[24,128]{1,0:T(8,128)S(1)}, f32[24,128]{1,0:T(8,128)S(1)}, u32[]{:S(2)}, u32[]{:S(2)}) collective-permute-start(f32[24,128]{1,0:T(8,128)S(1)} %slice.28), channel_id=1, source_target_pairs={{0,64},{32,96},{64,0},{96,32},{1,65},{33,97},{65,1},{97,33},{2,66}... | collective-permute-start | bytes 36872 | tf_op jit(solution)/shard_map/ppermute | solution.py:409
  32.3 3.7 %collective-permute-start.5 = (f32[24,128]{1,0:T(8,128)S(1)}, f32[24,128]{1,0:T(8,128)S(1)}, u32[]{:S(2)}, u32[]{:S(2)}) collective-permute-start(f32[24,128]{1,0:T(8,128)S(1)} %slice.28), channel_id=1, source_target_pairs={{0,96},{32,0},{64,32},{96,64},{1,97},{33,1},{65,33},{97,65},{2,98}... | collective-permute-start | bytes 36872 | tf_op jit(solution)/shard_map/ppermute | solution.py:409
  33.5 4.9 %collective-permute-start.3 = (f32[24,128]{1,0:T(8,128)S(1)}, f32[24,128]{1,0:T(8,128)S(1)}, u32[]{:S(2)}, u32[]{:S(2)}) collective-permute-start(f32[24,128]{1,0:T(8,128)S(1)} %slice.28), channel_id=1, source_target_pairs={{0,32},{32,64},{64,96},{96,0},{1,33},{33,65},{65,97},{97,1},{2,34}... | collective-permute-start | bytes 36872 | tf_op jit(solution)/shard_map/ppermute | solution.py:409
  38.4 6.6 %collective-permute-start.8 = (f32[24,128]{1,0:T(8,128)S(1)}, f32[24,128]{1,0:T(8,128)S(1)}, u32[]{:S(2)}, u32[]{:S(2)}) collective-permute-start(f32[24,128]{1,0:T(8,128)S(1)} %add_add_fusion.1), channel_id=1, source_target_pairs={{0,130},{2,0},{128,2},{130,128},{1,131},{3,1},{129,3},{131,129},{4... | collective-permute-start | bytes 36872 | tf_op jit(solution)/shard_map/ppermute | solution.py:409
  38.7 6.2 %collective-permute-start.7 = (f32[24,128]{1,0:T(8,128)S(1)}, f32[24,128]{1,0:T(8,128)S(1)}, u32[]{:S(2)}, u32[]{:S(2)}) collective-permute-start(f32[24,128]{1,0:T(8,128)S(1)} %add_add_fusion.1), channel_id=1, source_target_pairs={{0,128},{2,130},{128,0},{130,2},{1,129},{3,131},{129,1},{131,3},{4... | collective-permute-start | bytes 36872 | tf_op jit(solution)/shard_map/ppermute | solution.py:409
  40.9 5.2 %collective-permute-start.6 = (f32[24,128]{1,0:T(8,128)S(1)}, f32[24,128]{1,0:T(8,128)S(1)}, u32[]{:S(2)}, u32[]{:S(2)}) collective-permute-start(f32[24,128]{1,0:T(8,128)S(1)} %add_add_fusion.1), channel_id=1, source_target_pairs={{0,2},{2,128},{128,130},{130,0},{1,3},{3,129},{129,131},{131,1},{4... | collective-permute-start | bytes 36872 | tf_op jit(solution)/shard_map/ppermute | solution.py:409
  42.7 8.2 %collective-permute-start.1 = (f32[72,128]{1,0:T(8,128)S(1)}, f32[72,128]{1,0:T(8,128)S(1)}, u32[]{:S(2)}, u32[]{:S(2)}) collective-permute-start(f32[72,128]{1,0:T(8,128)S(1)} %get-tuple-element.63), channel_id=1, source_target_pairs={{0,2},{2,0},{1,3},{3,1},{4,6},{6,4},{5,7},{7,5},{8,10},{10,8},{9,1... | collective-permute-start | bytes 110600 | tf_op jit(solution)/shard_map/ppermute | solution.py:423
  47.6 11.7 %all-to-all-start.2 = ((f32[8,16,128]{2,1,0:T(8,128)}), f32[8,16,128]{2,1,0:T(8,128)S(1)}, u32[]{:S(2)}, u32[]{:S(2)}) async-start(f32[8,16,128]{2,1,0:T(8,128)} %get-tuple-element.65), calls=%async_computation.2 | async-start | bytes 131072 | tf_op jit(solution)/shard_map/all_to_all | solution.py:437
  51.0 1.5 %collective-permute-start.2 = (f32[8,128]{1,0:T(8,128)S(1)}, f32[8,128]{1,0:T(8,128)S(1)}, u32[]{:S(2)}, u32[]{:S(2)}) collective-permute-start(f32[8,128]{1,0:T(8,128)S(1)} %slice_add_fusion), channel_id=1, source_target_pairs={{0,1},{1,0},{2,3},{3,2},{4,5},{5,4},{6,7},{7,6},{8,9},{9,8},{10,11... | collective-permute-start | bytes 12296 | tf_op jit(solution)/shard_map/ppermute | solution.py:424

commit v6 on v5

v6 whole, which is shorter than its diff:
```python
import jax
import jax.numpy as jnp
from jax import lax
from jax.experimental import pallas as pl
from jax.experimental.pallas import tpu as pltpu
from jax.sharding import Mesh
from jax.sharding import PartitionSpec as P

HIGHEST = lax.Precision.HIGHEST
LANES = 128
HALF = 64
SUB = 8
BLOCK = 2048
SLOTS = 64
BLOCK_ROWS = SLOTS // 2 + SUB
SUMMED = 2 * SUB + BLOCK_ROWS
CNEC, BUS = ("yl", "x"), ("z", "yh")


def iota(shape, dim):
    return lax.broadcasted_iota(jnp.int32, shape, dim)


def dot_nt(x, y, precision=None):
    return lax.dot_general(
        x, y, (((1,), (1,)), ((), ())), precision=precision, preferred_element_type=jnp.float32
    )


def dot(x, y, precision=None):
    return jnp.dot(x, y, precision=precision, preferred_element_type=jnp.float32)


def two_parts(values):
    high = values.astype(jnp.bfloat16)
    return high, (values - high.astype(jnp.float32)).astype(jnp.bfloat16)


def by_parts(product, x, y):
    x_high, x_low = two_parts(x)
    y_high, y_low = two_parts(y)
    return product(x_high, y_high) + product(x_high, y_low) + product(x_low, y_high)


def digits(values, base, count):
    return [((values >> (base * at)) & ((1 << base) - 1)).astype(jnp.float32).astype(jnp.bfloat16)
            for at in reversed(range(count))]


def find_picks(swt, branch_ref):
    rank, actions = swt.shape
    picks = rank * actions
    pick_id = iota((picks, actions), 0)
    of_action = pick_id % LANES // rank * 2 + pick_id // LANES == iota((picks, actions), 1)
    of_action = jnp.where(of_action, 1.0, 0.0).astype(jnp.bfloat16)
    high, low = digits(swt, 6, 2)
    row = dot_nt(high, of_action) * 64.0 + dot_nt(low, of_action)
    row = jnp.where(iota((rank, picks), 1) % rank == iota((rank, picks), 0), row, 0.0)
    row = jnp.sum(row, axis=0, keepdims=True).astype(jnp.int32)
    tiles = branch_ref.shape[1] // LANES
    table = jnp.concatenate(
        [branch_ref[:, at * LANES:(at + 1) * LANES] for at in range(tiles)], axis=0
    )
    onehot = jnp.where(iota((LANES, picks), 0) == row % LANES, 1.0, 0.0).astype(jnp.bfloat16)
    high, middle, low = [dot(part, onehot) for part in digits(table, 6, 3)]
    found = high * 4096.0 + middle * 64.0 + low
    line = iota((2 * tiles, picks), 0) - row // LANES * 2
    ends = [
        jnp.sum(jnp.where(line == end, found, 0.0), axis=0, keepdims=True).astype(jnp.int32)
        for end in (0, 1)
    ]
    return row, ends


def slot_matrix(slots, count):
    shape = (count, slots[0].shape[1])
    first, second = [jnp.where(iota(shape, 0) == slot, 1.0, 0.0) for slot in slots]
    return (first - second).astype(jnp.bfloat16)


def partial_kernel(
    swt_hbm, branch_hbm, weight_hbm, zone_hbm, sens_hbm, pay_ref, meta_ref,
    swt_ref, branch_ref, weight_ref, zone_ref, sens_ref, acc_ref, coupled_ref, sems
):
    cols = sens_ref.shape[1]
    rows = sens_ref.shape[0] - 2 * SUB
    rank, actions = swt_ref.shape
    picks = rank * actions
    zones = HALF
    steps = cols // BLOCK
    bf16 = jnp.bfloat16
    small = [
        pltpu.make_async_copy(source, target, sems.at[steps + at])
        for at, (source, target) in enumerate(
            [(swt_hbm, swt_ref), (branch_hbm, branch_ref), (weight_hbm, weight_ref), (zone_hbm, zone_ref)]
        )
    ]
    for copy in small:
        copy.start()

    def block_copy(step):
        at = pl.ds(pl.multiple_of(step * BLOCK, BLOCK), BLOCK)
        return pltpu.make_async_copy(sens_hbm.at[:, at], sens_ref.at[0:rows, at], sems.at[step])

    for step in range(steps):
        block_copy(step).start()

    shard = lax.axis_index(BUS)
    row_start = lax.axis_index(CNEC) * rows
    acc_ref[...] = jnp.zeros_like(acc_ref)
    sens_ref[rows:, :] = jnp.ones((sens_ref.shape[0] - rows, cols), bf16)

    for copy in small[:2]:
        copy.wait()
    row, ends = find_picks(swt_ref[...], branch_ref)

    def ranks(owner, owners):
        count = owner.shape[1]
        inside = iota((owners, count), 0) == owner
        before = jnp.where(iota((count, count), 0) < iota((count, count), 1), 1.0, 0.0)
        place = dot(jnp.where(inside, 1.0, 0.0).astype(bf16), before.astype(bf16))
        return jnp.sum(jnp.where(inside, place, 0.0), axis=0, keepdims=True)

    bus = jnp.concatenate(ends, axis=1)
    count = 2 * picks
    held, place = bus // cols, ranks(bus // cols, lax.axis_size(BUS))
    owner, row_place = row // rows, ranks(row // rows, lax.axis_size(CNEC))
    most = jnp.maximum(
        jnp.max(place, axis=1, keepdims=True), jnp.max(row_place, axis=1, keepdims=True)
    )
    over = jnp.where(most >= SLOTS, 1.0, 0.0)
    meta_ref[0:1, :] = held.astype(jnp.float32)
    meta_ref[1:2, :] = place
    meta_ref[2:3, :] = jnp.broadcast_to(over, (1, count))
    meta_ref[3:4, :] = jnp.concatenate([owner.astype(jnp.float32), row_place], axis=1)
    meta_ref[4:, :] = jnp.zeros((SUB - 4, count), jnp.float32)
    place = place.astype(jnp.int32)
    mine = held == shard
    slot = jnp.where(mine, place, -1)
    local = bus - shard * cols

    def buses_of(group):
        match = iota((SLOTS, count), 0) + group * SLOTS == slot
        return jnp.sum(jnp.where(match, (local + 1).astype(jnp.float32), 0.0), axis=1, keepdims=True).astype(jnp.int32) - 1

    first_buses = buses_of(0)
    row_slot = jnp.where(owner == lax.axis_index(CNEC), row_place.astype(jnp.int32), -1)
    match = iota((SLOTS, picks), 0) == row_slot
    slot_row = jnp.where(match, (row - row_start + 1).astype(jnp.float32), 0.0)
    slot_row = jnp.sum(slot_row, axis=1, keepdims=True).astype(jnp.int32) - 1
    action_of = iota((SLOTS, picks), 1) // rank
    slot_action = jnp.where(match, action_of.astype(jnp.float32), 0.0)
    slot_action = jnp.sum(slot_action, axis=1, keepdims=True).astype(jnp.int32)
    zone_id = iota((zones, BLOCK), 0).astype(jnp.float32).astype(bf16)
    lane = iota((SLOTS, BLOCK), 1)
    for copy in small[2:]:
        copy.wait()

    def select(buses, step):
        return jnp.where(lane == buses - step * BLOCK, 1.0, 0.0).astype(bf16)

    def step_body(step, carry):
        at = pl.ds(pl.multiple_of(step * BLOCK, BLOCK), BLOCK)
        inside = zone_ref[:, at].astype(jnp.float32).astype(bf16) == zone_id
        high, low = two_parts(weight_ref[:, at])
        key = jnp.concatenate(
            [
                jnp.where(inside, high, bf16(0.0)),
                jnp.where(inside, low, bf16(0.0)),
                select(first_buses, step),
            ],
            axis=0,
        )
        block_copy(step).wait()
        acc_ref[...] += dot_nt(sens_ref[:, at], key)
        return carry

    lax.fori_loop(0, steps, step_body, 0)

    chunks = pay_ref.shape[0]
    zonal = acc_ref[0:rows, 0:zones] + acc_ref[0:rows, zones:2 * zones]
    total = acc_ref[rows:rows + 1, 0:2 * zones]
    total = total + pltpu.roll(total, HALF, 1)
    total = jnp.where(iota((1, LANES), 1) < HALF, 0.0, total)
    held_columns = acc_ref[0:rows, 2 * zones:]
    choose = jnp.where(iota((SLOTS, rows), 1) == slot_row, 1.0, 0.0).astype(bf16)
    chosen = dot(
        choose, jnp.concatenate([*two_parts(zonal), held_columns.astype(bf16)], axis=1)
    )
    switched = chosen[:, 0:zones] + chosen[:, zones:2 * zones]

    def coupled_of(chosen_columns, group):
        slots = [slot[:, at * picks:(at + 1) * picks] - group * SLOTS for at in (0, 1)]
        return dot(chosen_columns.astype(bf16), slot_matrix(slots, SLOTS))

    coupled_ref[...] = coupled_of(chosen[:, 2 * zones:], 0)

    def group_body(group, carry):
        buses = buses_of(group)
        columns = jnp.zeros((rows, SLOTS), jnp.float32)
        for step in range(steps):
            at = pl.ds(step * BLOCK, BLOCK)
            columns += dot_nt(sens_ref[0:rows, at], select(buses, step))
        coupled_ref[...] += coupled_of(dot(choose, columns.astype(bf16)), group)
        return carry

    groups = (jnp.sum(jnp.where(mine, 1.0, 0.0)).astype(jnp.int32) + SLOTS - 1) // SLOTS
    lax.fori_loop(1, groups, group_body, 0)

    coupled = jnp.where(action_of == slot_action, coupled_ref[...], 0.0)
    fold = jnp.where(iota((picks, LANES), 0) % rank == iota((picks, LANES), 1) % rank, 1.0, 0.0)
    high, low = [dot(part, fold.astype(bf16)) for part in two_parts(coupled)]
    shape = (SLOTS, LANES)
    coupled = jnp.where(iota(shape, 1) // rank == iota(shape, 0) // SUB, high + low, 0.0)
    coupled = jnp.sum(coupled.reshape(SLOTS // SUB, SUB, LANES), axis=0)

    share = zonal.reshape(chunks, 2, 2, 2, SUB, zones)
    share = jnp.where(lax.axis_index("act") == 0, share[:, :, 0], share[:, :, 1])
    share = jnp.concatenate([share[:, :, 0], share[:, :, 1]], axis=-1)
    half = SLOTS // 2
    switched = jnp.concatenate([switched[:half], switched[half:]], axis=1)
    block = jnp.concatenate([switched, coupled + total], axis=0)
    held_columns = held_columns.reshape(chunks, 2, rows // chunks // 2, SLOTS)
    pay_ref[:, 0:2 * SUB, :] = share.reshape(chunks, 2 * SUB, LANES)
    pay_ref[:, 2 * SUB:SUMMED, :] = jnp.broadcast_to(block[None], (chunks, *block.shape))
    pay_ref[:, SUMMED:, :] = jnp.concatenate([held_columns[:, 0], held_columns[:, 1]], axis=-1)


def place_kernel(parts_ref, local_ref, meta_ref, mine_ref, theirs_ref):
    chunks = parts_ref.shape[0]
    picks = meta_ref.shape[1] // 2
    half = parts_ref.shape[1] - SUMMED
    y_here, y_size = lax.axis_index("yh"), lax.axis_size("yh")
    held = meta_ref[0:1, :].astype(jnp.int32)
    place = meta_ref[1:2, :].astype(jnp.int32)
    known = (held % y_size == y_here) & (place < SLOTS)
    slot = jnp.where(known, held // y_size * SLOTS + place, -1)
    spread = slot_matrix([slot[:, at * picks:(at + 1) * picks] for at in (0, 1)], chunks * SLOTS)
    columns = [
        jnp.concatenate(
            [parts_ref[z, SUMMED:, at * SLOTS:(at + 1) * SLOTS] for z in range(chunks)], axis=1
        )
        for at in (0, 1)
    ]
    columns = jnp.concatenate(columns, axis=0).astype(jnp.bfloat16)
    diff = lax.dot_general(
        spread, columns, (((0,), (1,)), ((), ())), preferred_element_type=jnp.float32
    )
    diff = diff.reshape(2, picks // (2 * SUB), SUB, 2 * half)
    diff = jnp.concatenate([diff[0], diff[1]], axis=1).reshape(4, picks // 4, 2 * half)
    lower = y_here == 0
    packed = [
        jnp.concatenate([diff[g, :, at * half:(at + 1) * half] for g in range(4)], axis=1)
        for at in (0, 1)
    ]
    for ref, first in ((mine_ref, lower), (theirs_ref, ~lower)):
        ref[0:SUB, :] = jnp.where(first, local_ref[0:SUB, :], local_ref[SUB:2 * SUB, :])
        ref[SUB:, :] = jnp.where(first, packed[0], packed[1])


def copy_kernel(*refs):
    count = len(refs) // 2
    copies = [
        pltpu.make_async_copy(refs[at], refs[count + at], refs[-1].at[at]) for at in range(count)
    ]
    for copy in copies:
        copy.start()
    for copy in copies:
        copy.wait()


def final_kernel(
    meta_ref, mine_ref, theirs_ref, other_ref, here_ref, x1_ref, x2_ref, x3_ref, position_ref,
    limit_ref, after_ref, loading_ref, margin_ref
):
    actions, share, zones = after_ref.shape
    pairs = actions // 2
    picks = actions * SUB
    bf16 = jnp.bfloat16

    size_x = lax.axis_size("x")
    owner = meta_ref[3:4, :picks].astype(jnp.int32)
    slot = meta_ref[3:4, picks:].astype(jnp.int32)
    back = (lax.axis_index("x") - owner % size_x + size_x) % size_x
    flip = jnp.where(owner // size_x == lax.axis_index("yl"), 0, 1)
    blocks = [
        ref[at * BLOCK_ROWS:(at + 1) * BLOCK_ROWS, :]
        for ref in (here_ref, x1_ref, x2_ref, x3_ref)
        for at in (0, 1)
    ]
    count = len(blocks) * SLOTS
    spread = iota((count, picks), 0) == (back * 2 + flip) * SLOTS + slot
    spread = jnp.where(spread, 1.0, 0.0).astype(bf16)
    half = SLOTS // 2
    switched, coupled = [], []
    lane = iota((half, LANES), 1)
    for block in blocks:
        rows = block[0:half]
        turned = pltpu.roll(rows, HALF, 1)
        switched += [jnp.where(lane < HALF, rows, turned), jnp.where(lane < HALF, turned, rows)]
        extra = block[half:]
        for g in range(SLOTS // SUB):
            coupled.append(jnp.where(iota(extra.shape, 1) // SUB == g, extra, 0.0))
    parts = two_parts(jnp.concatenate(switched, axis=0)) + two_parts(jnp.concatenate(coupled, axis=0))
    found = lax.dot_general(
        spread, jnp.concatenate(parts, axis=1), (((0,), (0,)), ((), ())),
        preferred_element_type=jnp.float32,
    )
    switched = found[:, 0:LANES] + found[:, LANES:2 * LANES]
    coupled = found[:, 2 * LANES:3 * LANES] + found[:, 3 * LANES:]
    shape = (LANES, LANES)
    repeat = (iota(shape, 0) < SLOTS) & (iota(shape, 0) % SUB == iota(shape, 1) % SUB)
    repeat = jnp.where(repeat, 1.0, 0.0).astype(bf16)
    high, low = [dot(part, repeat) for part in two_parts(coupled)]
    coupled = high + low

    total = here_ref[half:half + 1, HALF:]
    total = jnp.concatenate([total, total], axis=1)
    shape = (pairs, SUB, LANES)
    row_id, lane = iota(shape, 1), iota(shape, 2)

    def side_by_side(x):
        return jnp.where(
            lane < HALF, x[:picks // 2].reshape(shape), x[picks // 2:].reshape(shape)
        )

    left = jnp.where(lane % SUB == row_id, 1.0, 0.0) - side_by_side(coupled)
    right = side_by_side(switched) / total[None]
    for pivot in range(SUB):
        factor = jnp.where(
            lane < HALF, left[:, :, pivot:pivot + 1], left[:, :, HALF + pivot:HALF + pivot + 1]
        )
        diagonal = factor[:, pivot:pivot + 1]
        left_now = left[:, pivot:pivot + 1] / diagonal
        right_now = right[:, pivot:pivot + 1] / diagonal
        left = jnp.where(row_id == pivot, left_now, left - factor * left_now)
        right = jnp.where(row_id == pivot, right_now, right - factor * right_now)

    lower = lax.axis_index("act") == 0
    whole = mine_ref[...] + theirs_ref[BLOCK_ROWS:]
    mine, other = whole[0:SUB], other_ref[...]
    low, high = jnp.where(lower, mine, other), jnp.where(lower, other, mine)
    zonal = jnp.concatenate(
        [low[:, :HALF], low[:, HALF:], high[:, :HALF], high[:, HALF:]], axis=0
    ) / total[:, :HALF]
    zonal_twice = jnp.concatenate([zonal, zonal], axis=1)
    groups = [whole[SUB:, g * share:(g + 1) * share] for g in range(LANES // share)]
    diff = jnp.concatenate(groups, axis=0)
    solved = jnp.concatenate(
        [jnp.where(lane < HALF, right, 0.0), jnp.where(lane < HALF, 0.0, right)], axis=1
    )
    diff_high, diff_low = two_parts(diff)
    solved_high, solved_low = two_parts(solved)

    def product(x, y):
        return lax.dot_general(
            x, y, (((0,), (0,)), ((), ())), preferred_element_type=jnp.float32
        )

    size = 2 * SUB
    for pair in range(pairs):
        at = slice(pair * size, (pair + 1) * size)
        left = jnp.concatenate([diff_high[at], diff_high[at], diff_low[at]], axis=0)
        right = jnp.concatenate(
            [solved_high[pair], solved_low[pair], solved_high[pair]], axis=0
        )
        total = zonal_twice + product(left, right)
        after_ref[2 * pair] = total[:, :HALF]
        after_ref[2 * pair + 1] = total[:, HALF:]
    position = position_ref[...]
    twice = jnp.concatenate([position, position], axis=1)
    moved = by_parts(dot_nt, twice, solved.reshape(pairs * size, LANES))
    shape = (actions, pairs * size)
    same = iota(shape, 1) // SUB == iota(shape, 0)
    flow = by_parts(dot_nt, position, zonal) + by_parts(dot, jnp.where(same, moved, 0.0), diff)
    limit = limit_ref[...]
    loading_ref[...] = flow / limit
    margin_ref[...] = limit - jnp.abs(flow)


def in_hbm(x):
    return pltpu.with_memory_space_constraint(x, pltpu.HBM)


def copied(arrays):
    hbm = pl.BlockSpec(memory_space=pltpu.HBM)
    return pl.pallas_call(
        copy_kernel,
        out_shape=[jax.ShapeDtypeStruct(x.shape, x.dtype) for x in arrays],
        in_specs=[hbm] * len(arrays),
        out_specs=[hbm] * len(arrays),
        scratch_shapes=[pltpu.SemaphoreType.DMA((len(arrays),))],
        name="copies",
    )(*[in_hbm(x) for x in arrays])


def params():
    return pltpu.CompilerParams(vmem_limit_bytes=48 * 1024 * 1024)


def body(
    nodal_sensitivity, shift_weight, bus_zone, branch_buses, switched_rows, net_position, flow_limit
):
    rows, cols = nodal_sensitivity.shape
    zones = net_position.shape[0]
    actions, rank = switched_rows.shape
    picks = actions * rank
    n_z, n_yh = lax.axis_size("z"), lax.axis_size("yh")
    share = rows // n_z // n_yh
    f32, i32 = jnp.float32, jnp.int32
    vmem = pl.BlockSpec(memory_space=pltpu.VMEM)
    hbm = pl.BlockSpec(memory_space=pltpu.HBM)

    weight, zone = shift_weight.reshape(1, cols), bus_zone.reshape(1, cols)
    pay, meta = pl.pallas_call(
        partial_kernel,
        out_shape=(
            jax.ShapeDtypeStruct((n_z, SUMMED + share, LANES), f32),
            jax.ShapeDtypeStruct((SUB, 2 * picks), f32),
        ),
        in_specs=[hbm] * 5,
        out_specs=(vmem, vmem),
        scratch_shapes=[
            pltpu.VMEM((rank, actions), i32),
            pltpu.VMEM(branch_buses.shape, i32),
            pltpu.VMEM((1, cols), f32),
            pltpu.VMEM((1, cols), i32),
            pltpu.VMEM((rows + 2 * SUB, cols), jnp.bfloat16),
            pltpu.VMEM((rows + 2 * SUB, 2 * zones + SLOTS), f32),
            pltpu.VMEM((SLOTS, picks), f32),
            pltpu.SemaphoreType.DMA((cols // BLOCK + 4,)),
        ],
        compiler_params=params(),
        name="partials",
    )(
        *[in_hbm(x) for x in (switched_rows.T, branch_buses, weight, zone, nodal_sensitivity)]
    )

    swap = [(0, 1), (1, 0)]
    parts = lax.all_to_all(pay, "z", 0, 0, tiled=True)
    local = jnp.sum(parts[:, :SUMMED], axis=0)
    part = jax.ShapeDtypeStruct((SUB + 2 * share, LANES), f32)
    mine, theirs = pl.pallas_call(
        place_kernel,
        out_shape=(part, part),
        in_specs=[vmem] * 3,
        out_specs=(vmem, vmem),
        compiler_params=params(),
        name="place",
    )(parts, local, meta)

    block = local[2 * SUB:]
    theirs = lax.ppermute(jnp.concatenate([block, theirs], axis=0), "yh", swap)
    beside = lax.ppermute(block, "yl", swap)
    across = lax.ppermute(block, ("yl", "yh"), [(0, 3), (3, 0), (1, 2), (2, 1)])
    here = jnp.concatenate([block + theirs[:BLOCK_ROWS], beside + across], axis=0)
    n_x = lax.axis_size("x")
    others = [
        lax.ppermute(here, "x", [(at, (at + by) % n_x) for at in range(n_x)])
        for by in range(1, n_x)
    ]
    other = lax.ppermute(
        mine[:SUB] + theirs[BLOCK_ROWS:BLOCK_ROWS + SUB], "act", swap
    )

    def compact():
        outputs = pl.pallas_call(
            final_kernel,
            out_shape=(
                jax.ShapeDtypeStruct((actions, share, zones), f32),
                jax.ShapeDtypeStruct((actions, share), f32),
                jax.ShapeDtypeStruct((actions, share), f32),
            ),
            in_specs=[vmem] * 10,
            out_specs=(vmem, vmem, vmem),
            compiler_params=params(),
            name="update",
        )(
            meta, mine, theirs, other, here, *others,
            net_position.reshape(1, zones), flow_limit.reshape(1, share),
        )
        return tuple(outputs)

    def general():
        inputs = nodal_sensitivity, shift_weight, bus_zone, branch_buses, switched_rows
        return tuple(copied(plain(*copied(inputs), net_position, flow_limit)))

    return lax.cond(meta[2, 0] > 0.5, general, compact)


def sum_over(x, axes):
    spread = jnp.broadcast_to(x[None], (lax.axis_size(axes), *x.shape))
    return jnp.sum(lax.all_to_all(spread, axes, 0, 0, tiled=True), axis=0)


def scattered_sum(x):
    shares = lax.axis_size(BUS)
    x = x.reshape(shares, x.shape[0] // shares, x.shape[1])
    return jnp.sum(lax.all_to_all(x, BUS, 0, 0, tiled=True), axis=0)


def plain(
    nodal_sensitivity, shift_weight, bus_zone, branch_buses, switched_rows, net_position, flow_limit
):
    rows, cols = nodal_sensitivity.shape
    zones = net_position.shape[0]
    actions, rank = switched_rows.shape
    onehot = (bus_zone[:, None] == jnp.arange(zones)[None, :]).astype(jnp.float32)
    total = sum_over(jnp.sum(onehot * shift_weight[:, None], axis=0), BUS)
    key = (onehot * shift_weight[:, None] / total[None, :]).astype(jnp.bfloat16)
    zonal = jnp.dot(nodal_sensitivity, key, preferred_element_type=jnp.float32)
    picks = switched_rows.reshape(-1)

    def columns(buses):
        local = buses - lax.axis_index(BUS) * cols
        owned = (local >= 0) & (local < cols)
        picked = jnp.take(nodal_sensitivity, jnp.clip(local, 0, cols - 1), axis=1)
        return jnp.where(owned[None, :], picked.astype(jnp.float32), 0.0)

    diff = columns(branch_buses[0][picks]) - columns(branch_buses[1][picks])
    zonal, diff = scattered_sum(zonal), scattered_sum(diff)
    share = rows // lax.axis_size(BUS)
    local = picks - lax.axis_index(CNEC) * rows - lax.axis_index(BUS) * share
    owned = ((local >= 0) & (local < share))[:, None]
    local = jnp.clip(local, 0, share - 1)
    switched = jnp.where(owned, jnp.take(zonal, local, axis=0), 0.0)
    coupled = jnp.where(owned, jnp.take(diff, local, axis=0), 0.0)
    coupled = jnp.einsum("aiaj->aij", coupled.reshape(actions, rank, actions, rank))
    both = jnp.concatenate([switched, coupled.reshape(actions * rank, rank)], axis=1)
    both = sum_over(sum_over(both, BUS), CNEC).reshape(actions, rank, zones + rank)
    left, right = jnp.eye(rank, dtype=jnp.float32)[None] - both[:, :, zones:], both[:, :, :zones]
    for pivot in range(rank):
        is_pivot = (jnp.arange(rank) == pivot)[None, :, None]
        factor = left[:, :, pivot:pivot + 1]
        diagonal = factor[:, pivot:pivot + 1]
        left_now, right_now = left[:, pivot:pivot + 1] / diagonal, right[:, pivot:pivot + 1] / diagonal
        left = jnp.where(is_pivot, left_now, left - factor * left_now)
        right = jnp.where(is_pivot, right_now, right - factor * right_now)
    after = zonal[None] + jnp.einsum(
        "caj,ajz->acz", diff.reshape(share, actions, rank), right, precision=HIGHEST
    )
    flow = jnp.einsum("acz,z->ac", after, net_position, precision=HIGHEST)
    return after, flow / flow_limit[None, :], flow_limit[None, :] - jnp.abs(flow)


def solution(mesh):
    n_cnec, n_bus, n_act = mesh.devices.shape
    split = Mesh(
        mesh.devices.reshape(2, n_cnec // 2, n_bus // 2, 2, n_act), ("yl", "x", "z", "yh", "act")
    )
    return jax.shard_map(
        body,
        mesh=split,
        in_specs=(
            P(CNEC, BUS),
            P(BUS),
            P(BUS),
            P(),
            P("act", None),
            P(),
            P(CNEC + BUS),
        ),
        out_specs=(
            P("act", CNEC + BUS, None),
            P("act", CNEC + BUS),
            P("act", CNEC + BUS),
        ),
        check_vma=False,
    )
```

time: 60.8 us -> 49.4 us (0.81)
  the two profiles are of different devices: /device:TPU:16 before, /device:TPU:6 now
where the time goes in v6:
time: 49.4 us; the launch traced here: 49 us
  blocking collectives  22.3 us (45%)
  Pallas kernels  8.86 us (18%)
  waiting for transfers between devices  8.63 us (17%)
  starting transfers between devices  7.31 us (15%)
  between operations  1.39 us (3%)
  local copies, waits for them, and re-layouts  0.53 us (1%)
    all_to_all x1, blocking collectives, body(): parts = lax.all_to_all(pay, 'z', 0, 0, tiled=True)  22.3 us
    pallas_call x1, Pallas kernels, body(): pl.pallas_call(partial_kernel, out_shape=(jax.ShapeDtypeStruct((n_z, SUMM...  5.73 us
    ppermute x3, waiting for transfers between devices, body(): lax.ppermute(here, 'x', [(at, (at + by) % n_x) for at in range(n_x)])  4.01 us
    ppermute x1, starting transfers between devices, body(): theirs = lax.ppermute(jnp.concatenate([block, theirs], axis=0), 'yh', swap)  3.28 us
    ppermute x3, starting transfers between devices, body(): lax.ppermute(here, 'x', [(at, (at + by) % n_x) for at in range(n_x)])  2.97 us
    ppermute x1, waiting for transfers between devices, body(): beside = lax.ppermute(block, 'yl', swap)  2.73 us
    pallas_call x1, Pallas kernels, compact(): pl.pallas_call(final_kernel, out_shape=(jax.ShapeDtypeStruct((actions, sh...  2.71 us
    ppermute x1, waiting for transfers between devices, body(): across = lax.ppermute(block, ('yl', 'yh'), [(0, 3), (3, 0), (1, 2), (2, 1)])  1.89 us
  transfers between devices with their start and end apart: 7, of which 4 were waited for; matrix products, arithmetic and copies ran while one was open for 1% of the time, Pallas kernels for 0%

profile of v6, /device:TPU:6, one launch (start us, length us, event | category | flops | bytes accessed | tf_op | source)
XLA Modules:
  0.0 49.0 jit_solution(15411277241032333650)
XLA Ops:
  0.6 0.0 copy-start.4
  0.6 0.0 copy-start.5
  0.7 0.0 copy-start.6
  0.7 5.7 %partials.1 = (f32[8,88,128]{2,1,0:T(8,128)S(1)}, f32[8,512]{1,0:T(8,128)S(1)}) custom-call(s32[8,32]{1,0:T(8,128)} %bitcast.211, s32[2,4096]{1,0:T(2,128)} %branch_hbm.1, f32[1,8192]{1,0:T(1,128)} %bitcast.203, s32[1,8192]{1,0:T(1,128)} %bitcast.204, bf16[512,8192]{1,0:T(8,128)(2,1)} %sens_hbm.1), custom_call_target="tpu_custom_call" | custom-call | tf_op jit(solution)/shard_map/partials/pallas_call | solution.py:415
  6.4 22.3 %all_to_all.26.parts_ref = f32[8,88,128]{2,1,0:T(8,128)S(1)} all-to-all(f32[8,88,128]{2,1,0:T(8,128)S(1)} %get-tuple-element.65), channel_id=1, replica_groups=mesh['yl'=2,'x'=4,'z'=8,'yh'=2,'act'=2] {'z'}, dimensions={0} | all-to-all | bytes 720896 | tf_op jit(solution)/shard_map/all_to_all | solution.py:440
  28.7 0.4 place.1
  29.1 3.3 %collective-permute-start = (f32[112,128]{1,0:T(8,128)S(1)}, f32[112,128]{1,0:T(8,128)S(1)}, u32[]{:S(2)}, u32[]{:S(2)}) collective-permute-start(f32[112,128]{1,0:T(8,128)S(1)} %pad_maximum_fusion.1), channel_id=1, source_target_pairs={{0,2},{2,0},{1,3},{3,1},{4,6},{6,4},{5,7},{7,5},{8,10},{10,8},{9,1... | collective-permute-start | bytes 172040 | tf_op jit(solution)/shard_map/ppermute | solution.py:453
  32.4 0.7 %collective-permute-start.2 = (f32[40,128]{1,0:T(8,128)S(1)}, f32[40,128]{1,0:T(8,128)S(1)}, u32[]{:S(2)}, u32[]{:S(2)}) collective-permute-start(f32[40,128]{1,0:T(8,128)S(1)} %slice.184), channel_id=1, source_target_pairs={{0,128},{128,0},{1,129},{129,1},{2,130},{130,2},{3,131},{131,3},{4... | collective-permute-start | bytes 61448 | tf_op jit(solution)/shard_map/ppermute | solution.py:454
  33.1 0.4 collective-permute-start.3
  33.5 2.7 %collective-permute-done.2 = f32[40,128]{1,0:T(8,128)S(1)} collective-permute-done((f32[40,128]{1,0:T(8,128)S(1)}, f32[40,128]{1,0:T(8,128)S(1)}, u32[]{:S(2)}, u32[]{:S(2)}) %collective-permute-start.2) | collective-permute-done | bytes 20512 | tf_op jit(solution)/shard_map/ppermute | solution.py:454
  36.2 1.9 %collective-permute-done.3 = f32[40,128]{1,0:T(8,128)S(1)} collective-permute-done((f32[40,128]{1,0:T(8,128)S(1)}, f32[40,128]{1,0:T(8,128)S(1)}, u32[]{:S(2)}, u32[]{:S(2)}) %collective-permute-start.3) | collective-permute-done | bytes 20512 | tf_op jit(solution)/shard_map/ppermute | solution.py:455
  38.1 0.0 collective-permute-done
  38.1 0.6 %collective-permute-start.4 = (f32[80,128]{1,0:T(8,128)S(1)}, f32[80,128]{1,0:T(8,128)S(1)}, u32[]{:S(2)}, u32[]{:S(2)}) collective-permute-start(f32[80,128]{1,0:T(8,128)S(1)} %pad_maximum_fusion.2), channel_id=1, source_target_pairs={{0,32},{32,64},{64,96},{96,0},{1,33},{33,65},{65,97},{97,1},{2,34}... | collective-permute-start | bytes 122888 | tf_op jit(solution)/shard_map/ppermute | solution.py:459
  38.7 2.4 %collective-permute-start.5 = (f32[80,128]{1,0:T(8,128)S(1)}, f32[80,128]{1,0:T(8,128)S(1)}, u32[]{:S(2)}, u32[]{:S(2)}) collective-permute-start(f32[80,128]{1,0:T(8,128)S(1)} %pad_maximum_fusion.2), channel_id=1, source_target_pairs={{0,64},{32,96},{64,0},{96,32},{1,65},{33,97},{65,1},{97,33},{2,66}... | collective-permute-start | bytes 122888 | tf_op jit(solution)/shard_map/ppermute | solution.py:459
  41.1 0.0 collective-permute-start.6
  41.1 0.0 collective-permute-start.1
  41.1 0.5 %slice.132 = f32[1,1]{1,0:T(1,128)} slice(f32[8,512]{1,0:T(8,128)S(1)} %get-tuple-element.64.meta_ref), slice={[2:3], [0:1]} | slice | bytes 8 | tf_op jit(solution)/shard_map/slice | solution.py:488
  42.3 0.0 collective-permute-done.1
  42.3 0.0 collective-permute-done.4
  42.3 1.9 %collective-permute-done.5 = f32[80,128]{1,0:T(8,128)S(1)} collective-permute-done((f32[80,128]{1,0:T(8,128)S(1)}, f32[80,128]{1,0:T(8,128)S(1)}, u32[]{:S(2)}, u32[]{:S(2)}) %collective-permute-start.5) | collective-permute-done | bytes 40992 | tf_op jit(solution)/shard_map/ppermute | solution.py:459
  44.2 2.1 %collective-permute-done.6 = f32[80,128]{1,0:T(8,128)S(1)} collective-permute-done((f32[80,128]{1,0:T(8,128)S(1)}, f32[80,128]{1,0:T(8,128)S(1)}, u32[]{:S(2)}, u32[]{:S(2)}) %collective-permute-start.6) | collective-permute-done | bytes 40992 | tf_op jit(solution)/shard_map/ppermute | solution.py:459
  46.3 0.0 copy-done.4
  46.3 0.0 copy-done.5
  46.3 0.0 copy-done.6
  46.3 2.7 %conditional.1 = ((f32[32,32,64]{2,1,0:T(8,128)}, f32[32,32]{1,0:T(8,128)}, f32[32,32]{1,0:T(8,128)})) conditional(s32[]{:T(128)} %bitcast.59, (f32[64]{0:T(128)S(1)}, f32[32]{0:T(128)S(1)}, f32[8,512]{1,0:T(8,128)S(1)}, f32[72,128]{1,0:T(8,128)S(1)}, f32[112,128]{1,0:T(8,128)S(1)}, /*index=5*/f32[8,128]{1,0:T(8,128)S(1)}, f32[80,128]{1,0:T(8,128)S(1)}, ...), branch_computations={%region_1.0_spmd, %region_2.11_spmd} | conditional | flops 551126016 | bytes 46937896 | solution.py:488
  46.3 2.7 %update.1 = (f32[32,32,64]{2,1,0:T(8,128)}, f32[32,32]{1,0:T(8,128)}, f32[32,32]{1,0:T(8,128)}) custom-call(f32[8,512]{1,0:T(8,128)S(1)} %get-tuple-element.26.meta_ref, f32[72,128]{1,0:T(8,128)S(1)} %get-tuple-element.36.mine_ref, f32[112,128]{1,0:T(8,128)S(1)} %get-tuple-element.37.theirs_ref, f32[8,128]{1,0:T(8,128)S(1)} %get-tuple-element.38.other_ref, ...), custom_call_target="tpu_custom_call" | custom-call | tf_op jit(solution)/shard_map/cond/branch_0_fun/update/pallas_call | solution.py:467
  (7 shorter events, 0.0 us)
Async XLA Ops:
  0.6 45.7 %copy-start.4 = (s32[32,8]{0,1:T(8,128)S(1)}, s32[32,8]{0,1:T(8,128)}, u32[]{:S(2)}) copy-start(s32[32,8]{0,1:T(8,128)} %param.15) | copy-start | bytes 3076
  0.6 45.7 %copy-start.5 = (f32[64]{0:T(128)S(1)}, f32[64]{0:T(128)}, u32[]{:S(2)}) copy-start(f32[64]{0:T(128)} %param.16) | copy-start | bytes 772
  0.7 45.7 %copy-start.6 = (f32[32]{0:T(128)S(1)}, f32[32]{0:T(128)}, u32[]{:S(2)}) copy-start(f32[32]{0:T(128)} %param.17) | copy-start | bytes 388
  29.1 9.0 %collective-permute-start = (f32[112,128]{1,0:T(8,128)S(1)}, f32[112,128]{1,0:T(8,128)S(1)}, u32[]{:S(2)}, u32[]{:S(2)}) collective-permute-start(f32[112,128]{1,0:T(8,128)S(1)} %pad_maximum_fusion.1), channel_id=1, source_target_pairs={{0,2},{2,0},{1,3},{3,1},{4,6},{6,4},{5,7},{7,5},{8,10},{10,8},{9,1... | collective-permute-start | bytes 172040 | tf_op jit(solution)/shard_map/ppermute | solution.py:453
  32.4 3.8 %collective-permute-start.2 = (f32[40,128]{1,0:T(8,128)S(1)}, f32[40,128]{1,0:T(8,128)S(1)}, u32[]{:S(2)}, u32[]{:S(2)}) collective-permute-start(f32[40,128]{1,0:T(8,128)S(1)} %slice.184), channel_id=1, source_target_pairs={{0,128},{128,0},{1,129},{129,1},{2,130},{130,2},{3,131},{131,3},{4... | collective-permute-start | bytes 61448 | tf_op jit(solution)/shard_map/ppermute | solution.py:454
  33.1 5.0 %collective-permute-start.3 = (f32[40,128]{1,0:T(8,128)S(1)}, f32[40,128]{1,0:T(8,128)S(1)}, u32[]{:S(2)}, u32[]{:S(2)}) collective-permute-start(f32[40,128]{1,0:T(8,128)S(1)} %slice.184), channel_id=1, source_target_pairs={{0,130},{130,0},{2,128},{128,2},{1,131},{131,1},{3,129},{129,3},{4... | collective-permute-start | bytes 61448 | tf_op jit(solution)/shard_map/ppermute | solution.py:455
  38.1 4.2 %collective-permute-start.4 = (f32[80,128]{1,0:T(8,128)S(1)}, f32[80,128]{1,0:T(8,128)S(1)}, u32[]{:S(2)}, u32[]{:S(2)}) collective-permute-start(f32[80,128]{1,0:T(8,128)S(1)} %pad_maximum_fusion.2), channel_id=1, source_target_pairs={{0,32},{32,64},{64,96},{96,0},{1,33},{33,65},{65,97},{97,1},{2,34}... | collective-permute-start | bytes 122888 | tf_op jit(solution)/shard_map/ppermute | solution.py:459
  38.7 5.5 %collective-permute-start.5 = (f32[80,128]{1,0:T(8,128)S(1)}, f32[80,128]{1,0:T(8,128)S(1)}, u32[]{:S(2)}, u32[]{:S(2)}) collective-permute-start(f32[80,128]{1,0:T(8,128)S(1)} %pad_maximum_fusion.2), channel_id=1, source_target_pairs={{0,64},{32,96},{64,0},{96,32},{1,65},{33,97},{65,1},{97,33},{2,66}... | collective-permute-start | bytes 122888 | tf_op jit(solution)/shard_map/ppermute | solution.py:459
  41.1 5.2 %collective-permute-start.6 = (f32[80,128]{1,0:T(8,128)S(1)}, f32[80,128]{1,0:T(8,128)S(1)}, u32[]{:S(2)}, u32[]{:S(2)}) collective-permute-start(f32[80,128]{1,0:T(8,128)S(1)} %pad_maximum_fusion.2), channel_id=1, source_target_pairs={{0,96},{32,0},{64,32},{96,64},{1,97},{33,1},{65,33},{97,65},{2,98}... | collective-permute-start | bytes 122888 | tf_op jit(solution)/shard_map/ppermute | solution.py:459
  41.1 1.2 %collective-permute-start.1 = (f32[8,128]{1,0:T(8,128)S(1)}, f32[8,128]{1,0:T(8,128)S(1)}, u32[]{:S(2)}, u32[]{:S(2)}) collective-permute-start(f32[8,128]{1,0:T(8,128)S(1)} %slice_add_fusion.1), channel_id=1, source_target_pairs={{0,1},{1,0},{2,3},{3,2},{4,5},{5,4},{6,7},{7,6},{8,9},{9,8},{10,11... | collective-permute-start | bytes 12296 | tf_op jit(solution)/shard_map/ppermute | solution.py:462

commit v7 on v6

--- a/solution.py
+++ b/solution.py
@@ -34,6 +34,13 @@
 def two_parts(values):
     high = values.astype(jnp.bfloat16)
     return high, (values - high.astype(jnp.float32)).astype(jnp.bfloat16)
+
+
+def three_parts(values):
+    high = values.astype(jnp.bfloat16)
+    rest = values - high.astype(jnp.float32)
+    middle = rest.astype(jnp.bfloat16)
+    return high, middle, (rest - middle.astype(jnp.float32)).astype(jnp.bfloat16)
 
 
 def by_parts(product, x, y):
@@ -78,29 +85,44 @@
     return (first - second).astype(jnp.bfloat16)
 
 
-def partial_kernel(
-    swt_hbm, branch_hbm, weight_hbm, zone_hbm, sens_hbm, pay_ref, meta_ref,
-    swt_ref, branch_ref, weight_ref, zone_ref, sens_ref, acc_ref, coupled_ref, sems
+def total_kernel(weight_hbm, zone_hbm, out_ref, weight_ref, zone_ref, sems):
+    copies = [
+        pltpu.make_async_copy(weight_hbm, weight_ref, sems.at[0]),
+        pltpu.make_async_copy(zone_hbm, zone_ref, sems.at[1]),
+    ]
+    for copy in copies:
+        copy.start()
+    for copy in copies:
+        copy.wait()
+    ids = iota((HALF, LANES), 0)
+    total = jnp.zeros((HALF, LANES), jnp.float32)
+    for start in range(0, weight_ref.shape[1], LANES):
+        at = pl.ds(start, LANES)
+        total += jnp.where(zone_ref[:, at] == ids, weight_ref[:, at], 0.0)
+    total = jnp.sum(total, axis=1, keepdims=True)
+    total = jnp.sum(jnp.where(ids == iota((HALF, LANES), 1), total, 0.0), axis=0, keepdims=True)
+    out_ref[...] = jnp.broadcast_to(total[None], out_ref.shape)
+
+
+def column_kernel(
+    swt_hbm, branch_hbm, sens_hbm, held_ref, meta_ref, extra_ref, sens_ref,
+    swt_ref, branch_ref, acc_ref, coupled_ref, sems
 ):
-    cols = sens_ref.shape[1]
-    rows = sens_ref.shape[0] - 2 * SUB
+    rows, cols = sens_ref.shape
     rank, actions = swt_ref.shape
     picks = rank * actions
-    zones = HALF
     steps = cols // BLOCK
     bf16 = jnp.bfloat16
     small = [
-        pltpu.make_async_copy(source, target, sems.at[steps + at])
-        for at, (source, target) in enumerate(
-            [(swt_hbm, swt_ref), (branch_hbm, branch_ref), (weight_hbm, weight_ref), (zone_hbm, zone_ref)]
-        )
+        pltpu.make_async_copy(swt_hbm, swt_ref, sems.at[steps]),
+        pltpu.make_async_copy(branch_hbm, branch_ref, sems.at[steps + 1]),
     ]
     for copy in small:
         copy.start()
 
     def block_copy(step):
         at = pl.ds(pl.multiple_of(step * BLOCK, BLOCK), BLOCK)
-        return pltpu.make_async_copy(sens_hbm.at[:, at], sens_ref.at[0:rows, at], sems.at[step])
+        return pltpu.make_async_copy(sens_hbm.at[:, at], sens_ref.at[:, at], sems.at[step])
 
     for step in range(steps):
         block_copy(step).start()
@@ -108,9 +130,7 @@
     shard = lax.axis_index(BUS)
     row_start = lax.axis_index(CNEC) * rows
     acc_ref[...] = jnp.zeros_like(acc_ref)
-    sens_ref[rows:, :] = jnp.ones((sens_ref.shape[0] - rows, cols), bf16)
-
-    for copy in small[:2]:
+    for copy in small:
         copy.wait()
     row, ends = find_picks(swt_ref[...], branch_ref)
 
@@ -141,67 +161,49 @@
 
     def buses_of(group):
         match = iota((SLOTS, count), 0) + group * SLOTS == slot
-        return jnp.sum(jnp.where(match, (local + 1).astype(jnp.float32), 0.0), axis=1, keepdims=True).astype(jnp.int32) - 1
+        match = jnp.where(match, (local + 1).astype(jnp.float32), 0.0)
+        return jnp.sum(match, axis=1, keepdims=True).astype(jnp.int32) - 1
 
     first_buses = buses_of(0)
     row_slot = jnp.where(owner == lax.axis_index(CNEC), row_place.astype(jnp.int32), -1)
     match = iota((SLOTS, picks), 0) == row_slot
     slot_row = jnp.where(match, (row - row_start + 1).astype(jnp.float32), 0.0)
-    slot_row = jnp.sum(slot_row, axis=1, keepdims=True).astype(jnp.int32) - 1
+    slot_row = jnp.sum(slot_row, axis=1, keepdims=True) - 1.0
     action_of = iota((SLOTS, picks), 1) // rank
     slot_action = jnp.where(match, action_of.astype(jnp.float32), 0.0)
     slot_action = jnp.sum(slot_action, axis=1, keepdims=True).astype(jnp.int32)
-    zone_id = iota((zones, BLOCK), 0).astype(jnp.float32).astype(bf16)
+    extra_ref[0:SLOTS, :] = jnp.broadcast_to(slot_row, (SLOTS, LANES))
+    choose = iota((SLOTS, rows), 1) == slot_row.astype(jnp.int32)
+    choose = jnp.where(choose, 1.0, 0.0).astype(bf16)
     lane = iota((SLOTS, BLOCK), 1)
-    for copy in small[2:]:
-        copy.wait()
 
     def select(buses, step):
         return jnp.where(lane == buses - step * BLOCK, 1.0, 0.0).astype(bf16)
 
     def step_body(step, carry):
         at = pl.ds(pl.multiple_of(step * BLOCK, BLOCK), BLOCK)
-        inside = zone_ref[:, at].astype(jnp.float32).astype(bf16) == zone_id
-        high, low = two_parts(weight_ref[:, at])
-        key = jnp.concatenate(
-            [
-                jnp.where(inside, high, bf16(0.0)),
-                jnp.where(inside, low, bf16(0.0)),
-                select(first_buses, step),
-            ],
-            axis=0,
-        )
+        chosen = select(first_buses, step)
         block_copy(step).wait()
-        acc_ref[...] += dot_nt(sens_ref[:, at], key)
+        acc_ref[...] += dot_nt(sens_ref[:, at], chosen)
         return carry
 
     lax.fori_loop(0, steps, step_body, 0)
 
-    chunks = pay_ref.shape[0]
-    zonal = acc_ref[0:rows, 0:zones] + acc_ref[0:rows, zones:2 * zones]
-    total = acc_ref[rows:rows + 1, 0:2 * zones]
-    total = total + pltpu.roll(total, HALF, 1)
-    total = jnp.where(iota((1, LANES), 1) < HALF, 0.0, total)
-    held_columns = acc_ref[0:rows, 2 * zones:]
-    choose = jnp.where(iota((SLOTS, rows), 1) == slot_row, 1.0, 0.0).astype(bf16)
-    chosen = dot(
-        choose, jnp.concatenate([*two_parts(zonal), held_columns.astype(bf16)], axis=1)
-    )
-    switched = chosen[:, 0:zones] + chosen[:, zones:2 * zones]
-
-    def coupled_of(chosen_columns, group):
+    def coupled_of(columns, group):
         slots = [slot[:, at * picks:(at + 1) * picks] - group * SLOTS for at in (0, 1)]
-        return dot(chosen_columns.astype(bf16), slot_matrix(slots, SLOTS))
-
-    coupled_ref[...] = coupled_of(chosen[:, 2 * zones:], 0)
+        chosen = dot(choose, columns.astype(bf16))
+        return dot(chosen.astype(bf16), slot_matrix(slots, SLOTS))
+
+    columns = acc_ref[...]
+    coupled_ref[...] = coupled_of(columns, 0)
 
     def group_body(group, carry):
         buses = buses_of(group)
         columns = jnp.zeros((rows, SLOTS), jnp.float32)
         for step in range(steps):
             at = pl.ds(step * BLOCK, BLOCK)
-            columns += dot_nt(sens_ref[0:rows, at], select(buses, step))
-        coupled_ref[...] += coupled_of(dot(choose, columns.astype(bf16)), group)
+            columns += dot_nt(sens_ref[:, at], select(buses, step))
+        coupled_ref[...] += coupled_of(columns, group)
         return carry
 
     groups = (jnp.sum(jnp.where(mine, 1.0, 0.0)).astype(jnp.int32) + SLOTS - 1) // SLOTS
@@ -212,18 +214,58 @@
     high, low = [dot(part, fold.astype(bf16)) for part in two_parts(coupled)]
     shape = (SLOTS, LANES)
     coupled = jnp.where(iota(shape, 1) // rank == iota(shape, 0) // SUB, high + low, 0.0)
-    coupled = jnp.sum(coupled.reshape(SLOTS // SUB, SUB, LANES), axis=0)
-
+    extra_ref[SLOTS:, :] = jnp.sum(coupled.reshape(SLOTS // SUB, SUB, LANES), axis=0)
+    chunks = held_ref.shape[0]
+    columns = columns.reshape(chunks, 2, rows // chunks // 2, SLOTS)
+    held_ref[...] = jnp.concatenate([columns[:, 0], columns[:, 1]], axis=-1)
+
+
+def zonal_kernel(totals_ref, weight_hbm, zone_hbm, sens_ref, held_ref, extra_ref, pay_ref,
+                 weight_ref, zone_ref, acc_ref, sems):
+    copies = [
+        pltpu.make_async_copy(weight_hbm, weight_ref, sems.at[0]),
+        pltpu.make_async_copy(zone_hbm, zone_ref, sems.at[1]),
+    ]
+    for copy in copies:
+        copy.start()
+    rows, cols = sens_ref.shape
+    zones = HALF
+    bf16 = jnp.bfloat16
+    acc_ref[...] = jnp.zeros_like(acc_ref)
+    pay_ref[:, SUMMED:, :] = held_ref[...]
+    total = jnp.sum(totals_ref[...], axis=0)[:, :zones]
+    part = iota(total.shape, 0)
+    high, middle, low = [x.astype(jnp.float32) for x in three_parts(total)]
+    total = jnp.where(part == 0, high, jnp.where(part == 1, middle, low)).astype(bf16)
+    zone_id = iota((zones, BLOCK), 0).astype(jnp.float32).astype(bf16)
+    for copy in copies:
+        copy.wait()
+
+    def step_body(step, carry):
+        at = pl.ds(pl.multiple_of(step * BLOCK, BLOCK), BLOCK)
+        inside = zone_ref[:, at].astype(jnp.float32).astype(bf16) == zone_id
+        of_bus = dot(total, jnp.where(inside, bf16(1.0), bf16(0.0)))
+        of_bus = (of_bus[0:1] + of_bus[1:2]) + of_bus[2:3]
+        key = (weight_ref[:, at] / of_bus).astype(bf16)
+        acc_ref[...] += dot_nt(sens_ref[:, at], jnp.where(inside, key, bf16(0.0)))
+        return carry
+
+    lax.fori_loop(0, cols // BLOCK, step_body, 0)
+
+    chunks = pay_ref.shape[0]
+    zonal = acc_ref[...]
+    choose = iota((SLOTS, rows), 1) == extra_ref[0:SLOTS, 0:1].astype(jnp.int32)
+    choose = jnp.where(choose, 1.0, 0.0).astype(bf16)
+    switched = dot(choose, jnp.concatenate(two_parts(zonal), axis=1))
+    switched = switched[:, 0:zones] + switched[:, zones:]
     share = zonal.reshape(chunks, 2, 2, 2, SUB, zones)
     share = jnp.where(lax.axis_index("act") == 0, share[:, :, 0], share[:, :, 1])
     share = jnp.concatenate([share[:, :, 0], share[:, :, 1]], axis=-1)
     half = SLOTS // 2
     switched = jnp.concatenate([switched[:half], switched[half:]], axis=1)
-    block = jnp.concatenate([switched, coupled + total], axis=0)
-    held_columns = held_columns.reshape(chunks, 2, rows // chunks // 2, SLOTS)
+    block = jnp.concatenate([switched, extra_ref[SLOTS:, :]], axis=0)
     pay_ref[:, 0:2 * SUB, :] = share.reshape(chunks, 2 * SUB, LANES)
     pay_ref[:, 2 * SUB:SUMMED, :] = jnp.broadcast_to(block[None], (chunks, *block.shape))
-    pay_ref[:, SUMMED:, :] = jnp.concatenate([held_columns[:, 0], held_columns[:, 1]], axis=-1)
 
 
 def place_kernel(parts_ref, local_ref, meta_ref, mine_ref, theirs_ref):
@@ -314,8 +356,6 @@
     high, low = [dot(part, repeat) for part in two_parts(coupled)]
     coupled = high + low
 
-    total = here_ref[half:half + 1, HALF:]
-    total = jnp.concatenate([total, total], axis=1)
     shape = (pairs, SUB, LANES)
     row_id, lane = iota(shape, 1), iota(shape, 2)
 
@@ -325,7 +365,7 @@
         )
 
     left = jnp.where(lane % SUB == row_id, 1.0, 0.0) - side_by_side(coupled)
-    right = side_by_side(switched) / total[None]
+    right = side_by_side(switched)
     for pivot in range(SUB):
         factor = jnp.where(
             lane < HALF, left[:, :, pivot:pivot + 1], left[:, :, HALF + pivot:HALF + pivot + 1]
@@ -342,7 +382,7 @@
     low, high = jnp.where(lower, mine, other), jnp.where(lower, other, mine)
     zonal = jnp.concatenate(
         [low[:, :HALF], low[:, HALF:], high[:, :HALF], high[:, HALF:]], axis=0
-    ) / total[:, :HALF]
+    )
     zonal_twice = jnp.concatenate([zonal, zonal], axis=1)
     groups = [whole[SUB:, g * share:(g + 1) * share] for g in range(LANES // share)]
     diff = jnp.concatenate(groups, axis=0)
@@ -382,6 +422,10 @@
     return pltpu.with_memory_space_constraint(x, pltpu.HBM)
 
 
+def in_vmem(x):
+    return pltpu.with_memory_space_constraint(x, pltpu.VMEM)
+
+
 def copied(arrays):
     hbm = pl.BlockSpec(memory_space=pltpu.HBM)
     return pl.pallas_call(
@@ -412,29 +456,49 @@
     hbm = pl.BlockSpec(memory_space=pltpu.HBM)
 
     weight, zone = shift_weight.reshape(1, cols), bus_zone.reshape(1, cols)
-    pay, meta = pl.pallas_call(
-        partial_kernel,
+    weight, zone = in_hbm(weight), in_hbm(zone)
+    bus_scratch = [pltpu.VMEM((1, cols), f32), pltpu.VMEM((1, cols), i32)]
+    totals = pl.pallas_call(
+        total_kernel,
+        out_shape=jax.ShapeDtypeStruct((lax.axis_size(BUS), SUB, LANES), f32),
+        in_specs=[hbm] * 2,
+        out_specs=vmem,
+        scratch_shapes=[*bus_scratch, pltpu.SemaphoreType.DMA((2,))],
+        compiler_params=params(),
+        name="totals",
+    )(weight, zone)
+    totals = lax.all_to_all(totals, BUS, 0, 0, tiled=True)
+    held, meta, extra, sens = pl.pallas_call(
+        column_kernel,
         out_shape=(
-            jax.ShapeDtypeStruct((n_z, SUMMED + share, LANES), f32),
+            pltpu.VMEM((n_z, share, LANES), f32),
             jax.ShapeDtypeStruct((SUB, 2 * picks), f32),
+            pltpu.VMEM((SLOTS + SUB, LANES), f32),
+            pltpu.VMEM((rows, cols), jnp.bfloat16),
         ),
-        in_specs=[hbm] * 5,
-        out_specs=(vmem, vmem),
+        in_specs=[hbm] * 3,
+        out_specs=(vmem,) * 4,
         scratch_shapes=[
             pltpu.VMEM((rank, actions), i32),
             pltpu.VMEM(branch_buses.shape, i32),
-            pltpu.VMEM((1, cols), f32),
-            pltpu.VMEM((1, cols), i32),
-            pltpu.VMEM((rows + 2 * SUB, cols), jnp.bfloat16),
-            pltpu.VMEM((rows + 2 * SUB, 2 * zones + SLOTS), f32),
+            pltpu.VMEM((rows, SLOTS), f32),
             pltpu.VMEM((SLOTS, picks), f32),
-            pltpu.SemaphoreType.DMA((cols // BLOCK + 4,)),
+            pltpu.SemaphoreType.DMA((cols // BLOCK + 2,)),
         ],
         compiler_params=params(),
-        name="partials",
-    )(
-        *[in_hbm(x) for x in (switched_rows.T, branch_buses, weight, zone, nodal_sensitivity)]
-    )
+        name="columns",
+    )(*[in_hbm(x) for x in (switched_rows.T, branch_buses, nodal_sensitivity)])
+    pay = pl.pallas_call(
+        zonal_kernel,
+        out_shape=jax.ShapeDtypeStruct((n_z, SUMMED + share, LANES), f32),
+        in_specs=[vmem, hbm, hbm, vmem, vmem, vmem],
+        out_specs=vmem,
+        scratch_shapes=[
+            *bus_scratch, pltpu.VMEM((rows, zones), f32), pltpu.SemaphoreType.DMA((2,))
+        ],
+        compiler_params=params(),
+        name="zonal",
+    )(totals, weight, zone, *[in_vmem(x) for x in (sens, held, extra)])
 
     swap = [(0, 1), (1, 0)]
     parts = lax.all_to_all(pay, "z", 0, 0, tiled=True)

time: 49.4 us -> 73.6 us (1.49)
  starting transfers between devices: 7.31 us -> 18.4 us
  Pallas kernels: 8.86 us -> 16.2 us
  local copies, waits for them, and re-layouts: 0.53 us -> 7.76 us
  blocking collectives: 22.3 us -> 18.3 us
  waiting for transfers between devices: 8.63 us -> 10.8 us
    all_to_all x0 -> x1, starting transfers between devices: none -> 11.2 us  [body(): totals = lax.all_to_all(totals, BUS, 0, 0, tiled=True)]
    pallas_call x1 -> x3, Pallas kernels: 5.73 us -> 13.1 us  [the longest x1 6.22 us: body(): pl.pallas_call(zonal_kernel, out_shape=jax.ShapeDtypeStruct((n_z, SUMMED...]
    unnamed x6 -> x12, local copies, waits for them, and re-layouts: 0.01 us -> 7.24 us
    all_to_all x1, blocking collectives: 22.3 us -> 18.3 us  [body(): parts = lax.all_to_all(pay, 'z', 0, 0, tiled=True)]
    all_to_all x0 -> x1, waiting for transfers between devices: none -> 2.24 us  [body(): totals = lax.all_to_all(totals, BUS, 0, 0, tiled=True)]
  transfers between devices with their start and end apart: 7 -> 8, of which waited for: 4 -> 5; matrix products, arithmetic and copies ran while one was open for 1% -> 1% of each run, Pallas kernels for 0% -> 7%
where the time goes in v7:
time: 73.6 us; the launch traced here: 72.9 us
  starting transfers between devices  18.4 us (25%)
  blocking collectives  18.3 us (25%)
  Pallas kernels  16.2 us (22%)
  waiting for transfers between devices  10.8 us (15%)
  local copies, waits for them, and re-layouts  7.76 us (11%)
  between operations  1.4 us (2%)
    all_to_all x1, blocking collectives, body(): parts = lax.all_to_all(pay, 'z', 0, 0, tiled=True)  18.3 us
    all_to_all x1, starting transfers between devices, body(): totals = lax.all_to_all(totals, BUS, 0, 0, tiled=True)  11.2 us
    unnamed x12, local copies, waits for them, and re-layouts  7.24 us
    pallas_call x1, Pallas kernels, body(): pl.pallas_call(zonal_kernel, out_shape=jax.ShapeDtypeStruct((n_z, SUMMED...  6.22 us
    pallas_call x1, Pallas kernels, body(): pl.pallas_call(column_kernel, out_shape=(pltpu.VMEM((n_z, share, LANES),...  5.08 us
    ppermute x3, waiting for transfers between devices, body(): lax.ppermute(here, 'x', [(at, (at + by) % n_x) for at in range(n_x)])  4.01 us
    ppermute x1, starting transfers between devices, body(): theirs = lax.ppermute(jnp.concatenate([block, theirs], axis=0), 'yh', swap)  3.06 us
    ppermute x3, starting transfers between devices, body(): lax.ppermute(here, 'x', [(at, (at + by) % n_x) for at in range(n_x)])  2.97 us
  transfers between devices with their start and end apart: 8, of which 5 were waited for; matrix products, arithmetic and copies ran while one was open for 1% of the time, Pallas kernels for 7%

profile of v7, /device:TPU:6, one launch (start us, length us, event | category | flops | bytes accessed | tf_op | source)
XLA Modules:
  0.0 72.9 jit_solution(8865912598029553853)
XLA Ops:
  0.6 1.8 %totals.1 = f32[16,8,128]{2,1,0:T(8,128)} custom-call(f32[1,8192]{1,0:T(1,128)} %bitcast.190, s32[1,8192]{1,0:T(1,128)} %bitcast.192), custom_call_target="tpu_custom_call" | custom-call | tf_op jit(solution)/shard_map/totals/pallas_call | solution.py:461
  2.4 11.2 %all-to-all-start.5 = ((f32[16,8,128]{2,1,0:T(8,128)}), f32[16,8,128]{2,1,0:T(8,128)S(1)}, u32[]{:S(2)}, u32[]{:S(2)}) async-start(f32[16,8,128]{2,1,0:T(8,128)} %totals.1), calls=%async_computation.5 | async-start | bytes 131072 | tf_op jit(solution)/shard_map/all_to_all | solution.py:470
  13.6 5.1 %columns.1 = (f32[8,32,128]{2,1,0:T(8,128)S(1)}, f32[8,512]{1,0:T(8,128)S(1)}, f32[72,128]{1,0:T(8,128)S(1)}, bf16[512,8192]{1,0:T(8,128)(2,1)S(1)}) custom-call(s32[8,32]{1,0:T(8,128)} %bitcast.213, s32[2,4096]{1,0:T(2,128)} %branch_hbm.1, bf16[512,8192]{1,0:T(8,128)(2,1)} %sens_hbm.1), custom_call_target="tpu_custom_call" | custom-call | tf_op jit(solution)/shard_map/columns/pallas_call | solution.py:471
  18.7 0.0 copy-start
  18.7 3.2 %copy-done = bf16[512,8192]{1,0:T(8,128)(2,1)} copy-done((bf16[512,8192]{1,0:T(8,128)(2,1)}, bf16[512,8192]{1,0:T(8,128)(2,1)S(1)}, u32[]{:S(2)}) %copy-start) | copy-done | bytes 8388632
  21.9 2.2 %all-to-all-done.5.totals_ref = f32[16,8,128]{2,1,0:T(8,128)S(1)} async-done(((f32[16,8,128]{2,1,0:T(8,128)}), f32[16,8,128]{2,1,0:T(8,128)S(1)}, u32[]{:S(2)}, u32[]{:S(2)}) %all-to-all-start.5) | async-done | bytes 65568 | tf_op jit(solution)/shard_map/all_to_all | solution.py:470
  24.2 0.0 copy-start.3
  24.2 0.6 copy-done.3
  24.8 0.0 copy-start.1
  24.8 3.4 %copy-done.1 = bf16[512,8192]{1,0:T(8,128)(2,1)S(1)} copy-done((bf16[512,8192]{1,0:T(8,128)(2,1)S(1)}, bf16[512,8192]{1,0:T(8,128)(2,1)}, u32[]{:S(2)}) %copy-start.1) | copy-done | bytes 8388632
  28.2 0.0 copy-start.7
  28.2 0.0 copy-start.8
  28.2 0.0 copy-start.9
  28.2 6.2 %zonal.1 = f32[8,88,128]{2,1,0:T(8,128)} custom-call(f32[16,8,128]{2,1,0:T(8,128)} %copy-done.3, f32[1,8192]{1,0:T(1,128)} %bitcast.191, s32[1,8192]{1,0:T(1,128)} %bitcast.193, bf16[512,8192]{1,0:T(8,128)(2,1)S(1)} %copy-done.1, f32[8,32,128]{2,1,0:T(8,128)S(1)} %get-tuple-element.68.held_ref, f32[72,128]{1,0:T(8,128)S(1)} %get-tuple-element.69.extra_ref), custom_call_target="tpu_custom_call" | custom-call | tf_op jit(solution)/shard_map/zonal/pallas_call | solution.py:491
  34.4 18.3 %all_to_all.31.parts_ref = f32[8,88,128]{2,1,0:T(8,128)S(1)} all-to-all(f32[8,88,128]{2,1,0:T(8,128)} %zonal.1), channel_id=1, replica_groups=mesh['yl'=2,'x'=4,'z'=8,'yh'=2,'act'=2] {'z'}, dimensions={0} | all-to-all | bytes 720896 | tf_op jit(solution)/shard_map/all_to_all | solution.py:504
  52.8 0.4 place.1
  53.2 3.1 %collective-permute-start = (f32[112,128]{1,0:T(8,128)S(1)}, f32[112,128]{1,0:T(8,128)S(1)}, u32[]{:S(2)}, u32[]{:S(2)}) collective-permute-start(f32[112,128]{1,0:T(8,128)S(1)} %pad_maximum_fusion.1), channel_id=1, source_target_pairs={{0,2},{2,0},{1,3},{3,1},{4,6},{6,4},{5,7},{7,5},{8,10},{10,8},{9,1... | collective-permute-start | bytes 172040 | tf_op jit(solution)/shard_map/ppermute | solution.py:517
  56.3 0.7 collective-permute-start.2
  56.9 0.4 collective-permute-start.3
  57.4 2.7 %collective-permute-done.2 = f32[40,128]{1,0:T(8,128)S(1)} collective-permute-done((f32[40,128]{1,0:T(8,128)S(1)}, f32[40,128]{1,0:T(8,128)S(1)}, u32[]{:S(2)}, u32[]{:S(2)}) %collective-permute-start.2) | collective-permute-done | bytes 20512 | tf_op jit(solution)/shard_map/ppermute | solution.py:518
  60.0 1.9 %collective-permute-done.3 = f32[40,128]{1,0:T(8,128)S(1)} collective-permute-done((f32[40,128]{1,0:T(8,128)S(1)}, f32[40,128]{1,0:T(8,128)S(1)}, u32[]{:S(2)}, u32[]{:S(2)}) %collective-permute-start.3) | collective-permute-done | bytes 20512 | tf_op jit(solution)/shard_map/ppermute | solution.py:519
  61.9 0.0 collective-permute-done
  62.0 0.6 collective-permute-start.4
  62.5 2.4 %collective-permute-start.5 = (f32[80,128]{1,0:T(8,128)S(1)}, f32[80,128]{1,0:T(8,128)S(1)}, u32[]{:S(2)}, u32[]{:S(2)}) collective-permute-start(f32[80,128]{1,0:T(8,128)S(1)} %pad_maximum_fusion.2), channel_id=1, source_target_pairs={{0,64},{32,96},{64,0},{96,32},{1,65},{33,97},{65,1},{97,33},{2,66}... | collective-permute-start | bytes 122888 | tf_op jit(solution)/shard_map/ppermute | solution.py:523
  64.9 0.0 collective-permute-start.6
  64.9 0.0 collective-permute-start.1
  64.9 0.5 slice.132
  66.1 0.0 collective-permute-done.1
  66.1 0.0 collective-permute-done.4
  66.1 1.9 %collective-permute-done.5 = f32[80,128]{1,0:T(8,128)S(1)} collective-permute-done((f32[80,128]{1,0:T(8,128)S(1)}, f32[80,128]{1,0:T(8,128)S(1)}, u32[]{:S(2)}, u32[]{:S(2)}) %collective-permute-start.5) | collective-permute-done | bytes 40992 | tf_op jit(solution)/shard_map/ppermute | solution.py:523
  68.0 2.1 %collective-permute-done.6 = f32[80,128]{1,0:T(8,128)S(1)} collective-permute-done((f32[80,128]{1,0:T(8,128)S(1)}, f32[80,128]{1,0:T(8,128)S(1)}, u32[]{:S(2)}, u32[]{:S(2)}) %collective-permute-start.6) | collective-permute-done | bytes 40992 | tf_op jit(solution)/shard_map/ppermute | solution.py:523
  70.1 0.0 copy-done.7
  70.1 0.0 copy-done.8
  70.2 0.0 copy-done.9
  70.2 2.7 %conditional.1 = ((f32[32,32,64]{2,1,0:T(8,128)}, f32[32,32]{1,0:T(8,128)}, f32[32,32]{1,0:T(8,128)})) conditional(s32[]{:T(128)} %bitcast.57, (f32[64]{0:T(128)S(1)}, f32[32]{0:T(128)S(1)}, f32[8,512]{1,0:T(8,128)S(1)}, f32[72,128]{1,0:T(8,128)S(1)}, f32[112,128]{1,0:T(8,128)S(1)}, /*index=5*/f32[8,128]{1,0:T(8,128)S(1)}, f32[80,128]{1,0:T(8,128)S(1)}, ...), branch_computations={%region_1.0_spmd, %region_2.11_spmd} | conditional | flops 551126016 | bytes 46937896 | solution.py:552
  70.2 2.7 %update.1 = (f32[32,32,64]{2,1,0:T(8,128)}, f32[32,32]{1,0:T(8,128)}, f32[32,32]{1,0:T(8,128)}) custom-call(f32[8,512]{1,0:T(8,128)S(1)} %get-tuple-element.26.meta_ref, f32[72,128]{1,0:T(8,128)S(1)} %get-tuple-element.36.mine_ref, f32[112,128]{1,0:T(8,128)S(1)} %get-tuple-element.37.theirs_ref, f32[8,128]{1,0:T(8,128)S(1)} %get-tuple-element.38.other_ref, ...), custom_call_target="tpu_custom_call" | custom-call | tf_op jit(solution)/shard_map/cond/branch_0_fun/update/pallas_call | solution.py:531
  (7 shorter events, 0.0 us)
Async XLA Ops:
  2.4 21.8 %all-to-all-start.5 = ((f32[16,8,128]{2,1,0:T(8,128)}), f32[16,8,128]{2,1,0:T(8,128)S(1)}, u32[]{:S(2)}, u32[]{:S(2)}) async-start(f32[16,8,128]{2,1,0:T(8,128)} %totals.1), calls=%async_computation.5 | async-start | bytes 131072 | tf_op jit(solution)/shard_map/all_to_all | solution.py:470
  18.7 3.2 %copy-start = (bf16[512,8192]{1,0:T(8,128)(2,1)}, bf16[512,8192]{1,0:T(8,128)(2,1)S(1)}, u32[]{:S(2)}) copy-start(bf16[512,8192]{1,0:T(8,128)(2,1)S(1)} %get-tuple-element.67.sens_ref) | copy-start | bytes 25165828
  24.2 0.6 copy-start.3
  24.8 3.4 %copy-start.1 = (bf16[512,8192]{1,0:T(8,128)(2,1)S(1)}, bf16[512,8192]{1,0:T(8,128)(2,1)}, u32[]{:S(2)}) copy-start(bf16[512,8192]{1,0:T(8,128)(2,1)} %copy-done) | copy-start | bytes 25165828
  28.2 42.0 %copy-start.7 = (s32[32,8]{0,1:T(8,128)S(1)}, s32[32,8]{0,1:T(8,128)}, u32[]{:S(2)}) copy-start(s32[32,8]{0,1:T(8,128)} %param.15) | copy-start | bytes 3076
  28.2 42.0 %copy-start.8 = (f32[64]{0:T(128)S(1)}, f32[64]{0:T(128)}, u32[]{:S(2)}) copy-start(f32[64]{0:T(128)} %param.16) | copy-start | bytes 772
  28.2 42.0 %copy-start.9 = (f32[32]{0:T(128)S(1)}, f32[32]{0:T(128)}, u32[]{:S(2)}) copy-start(f32[32]{0:T(128)} %param.17) | copy-start | bytes 388
  53.2 8.7 %collective-permute-start = (f32[112,128]{1,0:T(8,128)S(1)}, f32[112,128]{1,0:T(8,128)S(1)}, u32[]{:S(2)}, u32[]{:S(2)}) collective-permute-start(f32[112,128]{1,0:T(8,128)S(1)} %pad_maximum_fusion.1), channel_id=1, source_target_pairs={{0,2},{2,0},{1,3},{3,1},{4,6},{6,4},{5,7},{7,5},{8,10},{10,8},{9,1... | collective-permute-start | bytes 172040 | tf_op jit(solution)/shard_map/ppermute | solution.py:517
  56.3 3.8 %collective-permute-start.2 = (f32[40,128]{1,0:T(8,128)S(1)}, f32[40,128]{1,0:T(8,128)S(1)}, u32[]{:S(2)}, u32[]{:S(2)}) collective-permute-start(f32[40,128]{1,0:T(8,128)S(1)} %slice.184), channel_id=1, source_target_pairs={{0,128},{128,0},{1,129},{129,1},{2,130},{130,2},{3,131},{131,3},{4... | collective-permute-start | bytes 61448 | tf_op jit(solution)/shard_map/ppermute | solution.py:518
  56.9 5.0 %collective-permute-start.3 = (f32[40,128]{1,0:T(8,128)S(1)}, f32[40,128]{1,0:T(8,128)S(1)}, u32[]{:S(2)}, u32[]{:S(2)}) collective-permute-start(f32[40,128]{1,0:T(8,128)S(1)} %slice.184), channel_id=1, source_target_pairs={{0,130},{130,0},{2,128},{128,2},{1,131},{131,1},{3,129},{129,3},{4... | collective-permute-start | bytes 61448 | tf_op jit(solution)/shard_map/ppermute | solution.py:519
  62.0 4.2 %collective-permute-start.4 = (f32[80,128]{1,0:T(8,128)S(1)}, f32[80,128]{1,0:T(8,128)S(1)}, u32[]{:S(2)}, u32[]{:S(2)}) collective-permute-start(f32[80,128]{1,0:T(8,128)S(1)} %pad_maximum_fusion.2), channel_id=1, source_target_pairs={{0,32},{32,64},{64,96},{96,0},{1,33},{33,65},{65,97},{97,1},{2,34}... | collective-permute-start | bytes 122888 | tf_op jit(solution)/shard_map/ppermute | solution.py:523
  62.5 5.5 %collective-permute-start.5 = (f32[80,128]{1,0:T(8,128)S(1)}, f32[80,128]{1,0:T(8,128)S(1)}, u32[]{:S(2)}, u32[]{:S(2)}) collective-permute-start(f32[80,128]{1,0:T(8,128)S(1)} %pad_maximum_fusion.2), channel_id=1, source_target_pairs={{0,64},{32,96},{64,0},{96,32},{1,65},{33,97},{65,1},{97,33},{2,66}... | collective-permute-start | bytes 122888 | tf_op jit(solution)/shard_map/ppermute | solution.py:523
  64.9 5.2 %collective-permute-start.6 = (f32[80,128]{1,0:T(8,128)S(1)}, f32[80,128]{1,0:T(8,128)S(1)}, u32[]{:S(2)}, u32[]{:S(2)}) collective-permute-start(f32[80,128]{1,0:T(8,128)S(1)} %pad_maximum_fusion.2), channel_id=1, source_target_pairs={{0,96},{32,0},{64,32},{96,64},{1,97},{33,1},{65,33},{97,65},{2,98}... | collective-permute-start | bytes 122888 | tf_op jit(solution)/shard_map/ppermute | solution.py:523
  64.9 1.2 %collective-permute-start.1 = (f32[8,128]{1,0:T(8,128)S(1)}, f32[8,128]{1,0:T(8,128)S(1)}, u32[]{:S(2)}, u32[]{:S(2)}) collective-permute-start(f32[8,128]{1,0:T(8,128)S(1)} %slice_add_fusion.1), channel_id=1, source_target_pairs={{0,1},{1,0},{2,3},{3,2},{4,5},{5,4},{6,7},{7,6},{8,9},{9,8},{10,11... | collective-permute-start | bytes 12296 | tf_op jit(solution)/shard_map/ppermute | solution.py:526

commit v8 on v7

--- a/solution.py
+++ b/solution.py
@@ -34,13 +34,6 @@
 def two_parts(values):
     high = values.astype(jnp.bfloat16)
     return high, (values - high.astype(jnp.float32)).astype(jnp.bfloat16)
-
-
-def three_parts(values):
-    high = values.astype(jnp.bfloat16)
-    rest = values - high.astype(jnp.float32)
-    middle = rest.astype(jnp.bfloat16)
-    return high, middle, (rest - middle.astype(jnp.float32)).astype(jnp.bfloat16)
 
 
 def by_parts(product, x, y):
@@ -96,17 +89,16 @@
         copy.wait()
     ids = iota((HALF, LANES), 0)
     total = jnp.zeros((HALF, LANES), jnp.float32)
-    for start in range(0, weight_ref.shape[1], LANES):
-        at = pl.ds(start, LANES)
-        total += jnp.where(zone_ref[:, at] == ids, weight_ref[:, at], 0.0)
+    for at in range(weight_ref.shape[0]):
+        total += jnp.where(zone_ref[at:at + 1, :] == ids, weight_ref[at:at + 1, :], 0.0)
     total = jnp.sum(total, axis=1, keepdims=True)
     total = jnp.sum(jnp.where(ids == iota((HALF, LANES), 1), total, 0.0), axis=0, keepdims=True)
     out_ref[...] = jnp.broadcast_to(total[None], out_ref.shape)
 
 
 def column_kernel(
-    swt_hbm, branch_hbm, sens_hbm, held_ref, meta_ref, extra_ref, sens_ref,
-    swt_ref, branch_ref, acc_ref, coupled_ref, sems
+    swt_hbm, branch_hbm, sens_hbm, held_ref, meta_ref, extra_ref,
+    swt_ref, branch_ref, sens_ref, acc_ref, coupled_ref, sems
 ):
     rows, cols = sens_ref.shape
     rank, actions = swt_ref.shape
@@ -220,37 +212,48 @@
     held_ref[...] = jnp.concatenate([columns[:, 0], columns[:, 1]], axis=-1)
 
 
-def zonal_kernel(totals_ref, weight_hbm, zone_hbm, sens_ref, held_ref, extra_ref, pay_ref,
-                 weight_ref, zone_ref, acc_ref, sems):
+def zonal_kernel(totals_ref, weight_hbm, zone_hbm, sens_hbm, held_ref, extra_ref, pay_ref,
+                 weight_ref, zone_ref, sens_ref, key_ref, sums_ref, acc_ref, sems):
+    rows, cols = sens_ref.shape
+    zones = HALF
+    part = BLOCK // 2
+    steps = cols // part
+    bf16 = jnp.bfloat16
     copies = [
-        pltpu.make_async_copy(weight_hbm, weight_ref, sems.at[0]),
-        pltpu.make_async_copy(zone_hbm, zone_ref, sems.at[1]),
+        pltpu.make_async_copy(weight_hbm, weight_ref, sems.at[steps]),
+        pltpu.make_async_copy(zone_hbm, zone_ref, sems.at[steps + 1]),
     ]
     for copy in copies:
         copy.start()
-    rows, cols = sens_ref.shape
-    zones = HALF
-    bf16 = jnp.bfloat16
+
+    def block_copy(step):
+        at = pl.ds(pl.multiple_of(step * part, part), part)
+        return pltpu.make_async_copy(sens_hbm.at[:, at], sens_ref.at[:, at], sems.at[step])
+
+    for step in range(steps):
+        block_copy(step).start()
+
     acc_ref[...] = jnp.zeros_like(acc_ref)
     pay_ref[:, SUMMED:, :] = held_ref[...]
-    total = jnp.sum(totals_ref[...], axis=0)[:, :zones]
-    part = iota(total.shape, 0)
-    high, middle, low = [x.astype(jnp.float32) for x in three_parts(total)]
-    total = jnp.where(part == 0, high, jnp.where(part == 1, middle, low)).astype(bf16)
-    zone_id = iota((zones, BLOCK), 0).astype(jnp.float32).astype(bf16)
+    total = jnp.sum(totals_ref[...], axis=0)[0:1]
     for copy in copies:
         copy.wait()
+    of_bus = jnp.take_along_axis(
+        jnp.broadcast_to(total, weight_ref.shape), zone_ref[...], axis=1
+    )
+    sums_ref[...] = weight_ref[...] / of_bus
+    ids = iota((zones, LANES), 0)
+    for at in range(cols // LANES):
+        key = jnp.where(zone_ref[at:at + 1, :] == ids, sums_ref[at:at + 1, :], 0.0)
+        key_ref[:, at * LANES:(at + 1) * LANES] = key.astype(bf16)
 
     def step_body(step, carry):
-        at = pl.ds(pl.multiple_of(step * BLOCK, BLOCK), BLOCK)
-        inside = zone_ref[:, at].astype(jnp.float32).astype(bf16) == zone_id
-        of_bus = dot(total, jnp.where(inside, bf16(1.0), bf16(0.0)))
-        of_bus = (of_bus[0:1] + of_bus[1:2]) + of_bus[2:3]
-        key = (weight_ref[:, at] / of_bus).astype(bf16)
-        acc_ref[...] += dot_nt(sens_ref[:, at], jnp.where(inside, key, bf16(0.0)))
+        at = pl.ds(pl.multiple_of(step * part, part), part)
+        block_copy(step).wait()
+        acc_ref[...] += dot_nt(sens_ref[:, at], key_ref[:, at])
         return carry
 
-    lax.fori_loop(0, cols // BLOCK, step_body, 0)
+    lax.fori_loop(0, steps, step_body, 0)
 
     chunks = pay_ref.shape[0]
     zonal = acc_ref[...]
@@ -422,10 +425,6 @@
     return pltpu.with_memory_space_constraint(x, pltpu.HBM)
 
 
-def in_vmem(x):
-    return pltpu.with_memory_space_constraint(x, pltpu.VMEM)
-
-
 def copied(arrays):
     hbm = pl.BlockSpec(memory_space=pltpu.HBM)
     return pl.pallas_call(
@@ -455,9 +454,9 @@
     vmem = pl.BlockSpec(memory_space=pltpu.VMEM)
     hbm = pl.BlockSpec(memory_space=pltpu.HBM)
 
-    weight, zone = shift_weight.reshape(1, cols), bus_zone.reshape(1, cols)
+    weight, zone = [x.reshape(cols // LANES, LANES) for x in (shift_weight, bus_zone)]
     weight, zone = in_hbm(weight), in_hbm(zone)
-    bus_scratch = [pltpu.VMEM((1, cols), f32), pltpu.VMEM((1, cols), i32)]
+    bus_scratch = [pltpu.VMEM((cols // LANES, LANES), kind) for kind in (f32, i32)]
     totals = pl.pallas_call(
         total_kernel,
         out_shape=jax.ShapeDtypeStruct((lax.axis_size(BUS), SUB, LANES), f32),
@@ -468,19 +467,20 @@
         name="totals",
     )(weight, zone)
     totals = lax.all_to_all(totals, BUS, 0, 0, tiled=True)
-    held, meta, extra, sens = pl.pallas_call(
+    sens_scratch = pltpu.VMEM((rows, cols), jnp.bfloat16)
+    held, meta, extra = pl.pallas_call(
         column_kernel,
         out_shape=(
-            pltpu.VMEM((n_z, share, LANES), f32),
+            jax.ShapeDtypeStruct((n_z, share, LANES), f32),
             jax.ShapeDtypeStruct((SUB, 2 * picks), f32),
-            pltpu.VMEM((SLOTS + SUB, LANES), f32),
-            pltpu.VMEM((rows, cols), jnp.bfloat16),
+            jax.ShapeDtypeStruct((SLOTS + SUB, LANES), f32),
         ),
         in_specs=[hbm] * 3,
-        out_specs=(vmem,) * 4,
+        out_specs=(vmem,) * 3,
         scratch_shapes=[
             pltpu.VMEM((rank, actions), i32),
             pltpu.VMEM(branch_buses.shape, i32),
+            sens_scratch,
             pltpu.VMEM((rows, SLOTS), f32),
             pltpu.VMEM((SLOTS, picks), f32),
             pltpu.SemaphoreType.DMA((cols // BLOCK + 2,)),
@@ -491,14 +491,19 @@
     pay = pl.pallas_call(
         zonal_kernel,
         out_shape=jax.ShapeDtypeStruct((n_z, SUMMED + share, LANES), f32),
-        in_specs=[vmem, hbm, hbm, vmem, vmem, vmem],
+        in_specs=[vmem, hbm, hbm, hbm, vmem, vmem],
         out_specs=vmem,
         scratch_shapes=[
-            *bus_scratch, pltpu.VMEM((rows, zones), f32), pltpu.SemaphoreType.DMA((2,))
+            *bus_scratch,
+            sens_scratch,
+            pltpu.VMEM((zones, cols), jnp.bfloat16),
+            pltpu.VMEM((cols // LANES, LANES), f32),
+            pltpu.VMEM((rows, zones), f32),
+            pltpu.SemaphoreType.DMA((2 * cols // BLOCK + 2,)),
         ],
         compiler_params=params(),
         name="zonal",
-    )(totals, weight, zone, *[in_vmem(x) for x in (sens, held, extra)])
+    )(totals, weight, zone, in_hbm(nodal_sensitivity), held, extra)
 
     swap = [(0, 1), (1, 0)]
     parts = lax.all_to_all(pay, "z", 0, 0, tiled=True)

time: 73.6 us -> 64.9 us (0.88)
  local copies, waits for them, and re-layouts: 7.76 us -> 0.53 us
  blocking collectives: 18.3 us -> 15.2 us
  waiting for transfers between devices: 10.8 us -> 13.7 us
  Pallas kernels: 16.2 us -> 15.1 us
    unnamed x12 -> x6, local copies, waits for them, and re-layouts: 7.24 us -> 0.01 us
    all_to_all x1, waiting for transfers between devices: 2.24 us -> 5.45 us  [body(): totals = lax.all_to_all(totals, BUS, 0, 0, tiled=True)]
    all_to_all x1, blocking collectives: 18.3 us -> 15.2 us  [body(): parts = lax.all_to_all(pay, 'z', 0, 0, tiled=True)]
    pallas_call x1, Pallas kernels: 6.22 us -> 5.14 us  [body(): pl.pallas_call(zonal_kernel, out_shape=jax.ShapeDtypeStruct((n_z, SUMMED...]
  transfers between devices with their start and end apart: 8 -> 8, of which waited for: 5 -> 5; matrix products, arithmetic and copies ran while one was open for 1% -> 1% of each run, Pallas kernels for 7% -> 8%
where the time goes in v8:
time: 64.9 us; the launch traced here: 64.4 us
  starting transfers between devices  18.4 us (28%)
  blocking collectives  15.2 us (23%)
  Pallas kernels  15.1 us (23%)
  waiting for transfers between devices  13.7 us (21%)
  between operations  1.39 us (2%)
    all_to_all x1, blocking collectives, body(): parts = lax.all_to_all(pay, 'z', 0, 0, tiled=True)  15.2 us
    all_to_all x1, starting transfers between devices, body(): totals = lax.all_to_all(totals, BUS, 0, 0, tiled=True)  11.2 us
    all_to_all x1, waiting for transfers between devices, body(): totals = lax.all_to_all(totals, BUS, 0, 0, tiled=True)  5.45 us
    pallas_call x1, Pallas kernels, body(): pl.pallas_call(zonal_kernel, out_shape=jax.ShapeDtypeStruct((n_z, SUMMED...  5.14 us
    pallas_call x1, Pallas kernels, body(): pl.pallas_call(column_kernel, out_shape=(jax.ShapeDtypeStruct((n_z, share...  5.09 us
    ppermute x3, waiting for transfers between devices, body(): lax.ppermute(here, 'x', [(at, (at + by) % n_x) for at in range(n_x)])  4.01 us
    ppermute x3, starting transfers between devices, body(): lax.ppermute(here, 'x', [(at, (at + by) % n_x) for at in range(n_x)])  2.98 us
    ppermute x1, starting transfers between devices, body(): theirs = lax.ppermute(jnp.concatenate([block, theirs], axis=0), 'yh', swap)  2.74 us
  transfers between devices with their start and end apart: 8, of which 5 were waited for; matrix products, arithmetic and copies ran while one was open for 1% of the time, Pallas kernels for 8%

profile of v8, /device:TPU:6, one launch (start us, length us, event | category | flops | bytes accessed | tf_op | source)
XLA Modules:
  0.0 64.4 jit_solution(11473535386788680268)
XLA Ops:
  0.6 1.8 %totals.1 = f32[16,8,128]{2,1,0:T(8,128)} custom-call(f32[64,128]{1,0:T(8,128)} %bitcast.190, s32[64,128]{1,0:T(8,128)} %bitcast.192), custom_call_target="tpu_custom_call" | custom-call | tf_op jit(solution)/shard_map/totals/pallas_call | solution.py:460
  2.4 11.2 %all-to-all-start.5 = ((f32[16,8,128]{2,1,0:T(8,128)}), f32[16,8,128]{2,1,0:T(8,128)S(1)}, u32[]{:S(2)}, u32[]{:S(2)}) async-start(f32[16,8,128]{2,1,0:T(8,128)} %totals.1), calls=%async_computation.5 | async-start | bytes 131072 | tf_op jit(solution)/shard_map/all_to_all | solution.py:469
  13.6 5.1 %columns.1 = (f32[8,32,128]{2,1,0:T(8,128)S(1)}, f32[8,512]{1,0:T(8,128)S(1)}, f32[72,128]{1,0:T(8,128)S(1)}) custom-call(s32[8,32]{1,0:T(8,128)} %bitcast.213, s32[2,4096]{1,0:T(2,128)} %branch_hbm.1, bf16[512,8192]{1,0:T(8,128)(2,1)} %sens_hbm.3), custom_call_target="tpu_custom_call" | custom-call | tf_op jit(solution)/shard_map/columns/pallas_call | solution.py:471
  18.7 5.5 %all-to-all-done.5.totals_ref = f32[16,8,128]{2,1,0:T(8,128)S(1)} async-done(((f32[16,8,128]{2,1,0:T(8,128)}), f32[16,8,128]{2,1,0:T(8,128)S(1)}, u32[]{:S(2)}, u32[]{:S(2)}) %all-to-all-start.5) | async-done | bytes 65568 | tf_op jit(solution)/shard_map/all_to_all | solution.py:469
  24.2 0.0 copy-start.4
  24.2 0.0 copy-start.5
  24.2 0.0 copy-start.6
  24.2 5.1 %zonal.1 = f32[8,88,128]{2,1,0:T(8,128)S(1)} custom-call(f32[16,8,128]{2,1,0:T(8,128)S(1)} %all-to-all-done.5.totals_ref, f32[64,128]{1,0:T(8,128)} %bitcast.191, s32[64,128]{1,0:T(8,128)} %bitcast.193, bf16[512,8192]{1,0:T(8,128)(2,1)} %sens_hbm.3, f32[8,32,128]{2,1,0:T(8,128)S(1)} %get-tuple-element.66.held_ref, f32[72,128]{1,0:T(8,128)S(1)} %get-tuple-element.67.extra_ref), custom_call_target="tpu_custom_call" | custom-call | tf_op jit(solution)/shard_map/zonal/pallas_call | solution.py:491
  29.3 15.2 %all_to_all.31.parts_ref = f32[8,88,128]{2,1,0:T(8,128)S(1)} all-to-all(f32[8,88,128]{2,1,0:T(8,128)S(1)} %zonal.1), channel_id=1, replica_groups=mesh['yl'=2,'x'=4,'z'=8,'yh'=2,'act'=2] {'z'}, dimensions={0} | all-to-all | bytes 720896 | tf_op jit(solution)/shard_map/all_to_all | solution.py:509
  44.6 0.4 place.1
  45.0 2.7 %collective-permute-start = (f32[112,128]{1,0:T(8,128)S(1)}, f32[112,128]{1,0:T(8,128)S(1)}, u32[]{:S(2)}, u32[]{:S(2)}) collective-permute-start(f32[112,128]{1,0:T(8,128)S(1)} %pad_maximum_fusion.1), channel_id=1, source_target_pairs={{0,2},{2,0},{1,3},{3,1},{4,6},{6,4},{5,7},{7,5},{8,10},{10,8},{9,1... | collective-permute-start | bytes 172040 | tf_op jit(solution)/shard_map/ppermute | solution.py:522
  47.7 0.7 %collective-permute-start.2 = (f32[40,128]{1,0:T(8,128)S(1)}, f32[40,128]{1,0:T(8,128)S(1)}, u32[]{:S(2)}, u32[]{:S(2)}) collective-permute-start(f32[40,128]{1,0:T(8,128)S(1)} %slice.184), channel_id=1, source_target_pairs={{0,128},{128,0},{1,129},{129,1},{2,130},{130,2},{3,131},{131,3},{4... | collective-permute-start | bytes 61448 | tf_op jit(solution)/shard_map/ppermute | solution.py:523
  48.4 0.8 %collective-permute-start.3 = (f32[40,128]{1,0:T(8,128)S(1)}, f32[40,128]{1,0:T(8,128)S(1)}, u32[]{:S(2)}, u32[]{:S(2)}) collective-permute-start(f32[40,128]{1,0:T(8,128)S(1)} %slice.184), channel_id=1, source_target_pairs={{0,130},{130,0},{2,128},{128,2},{1,131},{131,1},{3,129},{129,3},{4... | collective-permute-start | bytes 61448 | tf_op jit(solution)/shard_map/ppermute | solution.py:524
  49.2 2.3 %collective-permute-done.2 = f32[40,128]{1,0:T(8,128)S(1)} collective-permute-done((f32[40,128]{1,0:T(8,128)S(1)}, f32[40,128]{1,0:T(8,128)S(1)}, u32[]{:S(2)}, u32[]{:S(2)}) %collective-permute-start.2) | collective-permute-done | bytes 20512 | tf_op jit(solution)/shard_map/ppermute | solution.py:523
  51.5 1.9 %collective-permute-done.3 = f32[40,128]{1,0:T(8,128)S(1)} collective-permute-done((f32[40,128]{1,0:T(8,128)S(1)}, f32[40,128]{1,0:T(8,128)S(1)}, u32[]{:S(2)}, u32[]{:S(2)}) %collective-permute-start.3) | collective-permute-done | bytes 20512 | tf_op jit(solution)/shard_map/ppermute | solution.py:524
  53.4 0.0 collective-permute-done
  53.5 0.6 collective-permute-start.4
  54.0 2.4 %collective-permute-start.5 = (f32[80,128]{1,0:T(8,128)S(1)}, f32[80,128]{1,0:T(8,128)S(1)}, u32[]{:S(2)}, u32[]{:S(2)}) collective-permute-start(f32[80,128]{1,0:T(8,128)S(1)} %pad_maximum_fusion.2), channel_id=1, source_target_pairs={{0,64},{32,96},{64,0},{96,32},{1,65},{33,97},{65,1},{97,33},{2,66}... | collective-permute-start | bytes 122888 | tf_op jit(solution)/shard_map/ppermute | solution.py:528
  56.4 0.0 collective-permute-start.6
  56.4 0.0 collective-permute-start.1
  56.4 0.5 slice.132
  57.6 0.0 collective-permute-done.1
  57.6 0.0 collective-permute-done.4
  57.6 1.9 %collective-permute-done.5 = f32[80,128]{1,0:T(8,128)S(1)} collective-permute-done((f32[80,128]{1,0:T(8,128)S(1)}, f32[80,128]{1,0:T(8,128)S(1)}, u32[]{:S(2)}, u32[]{:S(2)}) %collective-permute-start.5) | collective-permute-done | bytes 40992 | tf_op jit(solution)/shard_map/ppermute | solution.py:528
  59.5 2.1 %collective-permute-done.6 = f32[80,128]{1,0:T(8,128)S(1)} collective-permute-done((f32[80,128]{1,0:T(8,128)S(1)}, f32[80,128]{1,0:T(8,128)S(1)}, u32[]{:S(2)}, u32[]{:S(2)}) %collective-permute-start.6) | collective-permute-done | bytes 40992 | tf_op jit(solution)/shard_map/ppermute | solution.py:528
  61.6 0.0 copy-done.4
  61.7 0.0 copy-done.5
  61.7 0.0 copy-done.6
  61.7 2.7 %conditional.1 = ((f32[32,32,64]{2,1,0:T(8,128)}, f32[32,32]{1,0:T(8,128)}, f32[32,32]{1,0:T(8,128)})) conditional(s32[]{:T(128)} %bitcast.57, (f32[64]{0:T(128)S(1)}, f32[32]{0:T(128)S(1)}, f32[8,512]{1,0:T(8,128)S(1)}, f32[72,128]{1,0:T(8,128)S(1)}, f32[112,128]{1,0:T(8,128)S(1)}, /*index=5*/f32[8,128]{1,0:T(8,128)S(1)}, f32[80,128]{1,0:T(8,128)S(1)}, ...), branch_computations={%region_1.0_spmd, %region_2.11_spmd} | conditional | flops 551126016 | bytes 46937896 | solution.py:557
  61.7 2.7 %update.1 = (f32[32,32,64]{2,1,0:T(8,128)}, f32[32,32]{1,0:T(8,128)}, f32[32,32]{1,0:T(8,128)}) custom-call(f32[8,512]{1,0:T(8,128)S(1)} %get-tuple-element.26.meta_ref, f32[72,128]{1,0:T(8,128)S(1)} %get-tuple-element.36.mine_ref, f32[112,128]{1,0:T(8,128)S(1)} %get-tuple-element.37.theirs_ref, f32[8,128]{1,0:T(8,128)S(1)} %get-tuple-element.38.other_ref, ...), custom_call_target="tpu_custom_call" | custom-call | tf_op jit(solution)/shard_map/cond/branch_0_fun/update/pallas_call | solution.py:536
  (7 shorter events, 0.0 us)
Async XLA Ops:
  2.4 21.8 %all-to-all-start.5 = ((f32[16,8,128]{2,1,0:T(8,128)}), f32[16,8,128]{2,1,0:T(8,128)S(1)}, u32[]{:S(2)}, u32[]{:S(2)}) async-start(f32[16,8,128]{2,1,0:T(8,128)} %totals.1), calls=%async_computation.5 | async-start | bytes 131072 | tf_op jit(solution)/shard_map/all_to_all | solution.py:469
  24.2 37.5 %copy-start.4 = (s32[32,8]{0,1:T(8,128)S(1)}, s32[32,8]{0,1:T(8,128)}, u32[]{:S(2)}) copy-start(s32[32,8]{0,1:T(8,128)} %param.15) | copy-start | bytes 3076
  24.2 37.5 %copy-start.5 = (f32[64]{0:T(128)S(1)}, f32[64]{0:T(128)}, u32[]{:S(2)}) copy-start(f32[64]{0:T(128)} %param.16) | copy-start | bytes 772
  24.2 37.5 %copy-start.6 = (f32[32]{0:T(128)S(1)}, f32[32]{0:T(128)}, u32[]{:S(2)}) copy-start(f32[32]{0:T(128)} %param.17) | copy-start | bytes 388
  45.0 8.4 %collective-permute-start = (f32[112,128]{1,0:T(8,128)S(1)}, f32[112,128]{1,0:T(8,128)S(1)}, u32[]{:S(2)}, u32[]{:S(2)}) collective-permute-start(f32[112,128]{1,0:T(8,128)S(1)} %pad_maximum_fusion.1), channel_id=1, source_target_pairs={{0,2},{2,0},{1,3},{3,1},{4,6},{6,4},{5,7},{7,5},{8,10},{10,8},{9,1... | collective-permute-start | bytes 172040 | tf_op jit(solution)/shard_map/ppermute | solution.py:522
  47.7 3.8 %collective-permute-start.2 = (f32[40,128]{1,0:T(8,128)S(1)}, f32[40,128]{1,0:T(8,128)S(1)}, u32[]{:S(2)}, u32[]{:S(2)}) collective-permute-start(f32[40,128]{1,0:T(8,128)S(1)} %slice.184), channel_id=1, source_target_pairs={{0,128},{128,0},{1,129},{129,1},{2,130},{130,2},{3,131},{131,3},{4... | collective-permute-start | bytes 61448 | tf_op jit(solution)/shard_map/ppermute | solution.py:523
  48.4 5.0 %collective-permute-start.3 = (f32[40,128]{1,0:T(8,128)S(1)}, f32[40,128]{1,0:T(8,128)S(1)}, u32[]{:S(2)}, u32[]{:S(2)}) collective-permute-start(f32[40,128]{1,0:T(8,128)S(1)} %slice.184), channel_id=1, source_target_pairs={{0,130},{130,0},{2,128},{128,2},{1,131},{131,1},{3,129},{129,3},{4... | collective-permute-start | bytes 61448 | tf_op jit(solution)/shard_map/ppermute | solution.py:524
  53.5 4.2 %collective-permute-start.4 = (f32[80,128]{1,0:T(8,128)S(1)}, f32[80,128]{1,0:T(8,128)S(1)}, u32[]{:S(2)}, u32[]{:S(2)}) collective-permute-start(f32[80,128]{1,0:T(8,128)S(1)} %pad_maximum_fusion.2), channel_id=1, source_target_pairs={{0,32},{32,64},{64,96},{96,0},{1,33},{33,65},{65,97},{97,1},{2,34}... | collective-permute-start | bytes 122888 | tf_op jit(solution)/shard_map/ppermute | solution.py:528
  54.0 5.5 %collective-permute-start.5 = (f32[80,128]{1,0:T(8,128)S(1)}, f32[80,128]{1,0:T(8,128)S(1)}, u32[]{:S(2)}, u32[]{:S(2)}) collective-permute-start(f32[80,128]{1,0:T(8,128)S(1)} %pad_maximum_fusion.2), channel_id=1, source_target_pairs={{0,64},{32,96},{64,0},{96,32},{1,65},{33,97},{65,1},{97,33},{2,66}... | collective-permute-start | bytes 122888 | tf_op jit(solution)/shard_map/ppermute | solution.py:528
  56.4 5.2 %collective-permute-start.6 = (f32[80,128]{1,0:T(8,128)S(1)}, f32[80,128]{1,0:T(8,128)S(1)}, u32[]{:S(2)}, u32[]{:S(2)}) collective-permute-start(f32[80,128]{1,0:T(8,128)S(1)} %pad_maximum_fusion.2), channel_id=1, source_target_pairs={{0,96},{32,0},{64,32},{96,64},{1,97},{33,1},{65,33},{97,65},{2,98}... | collective-permute-start | bytes 122888 | tf_op jit(solution)/shard_map/ppermute | solution.py:528
  56.4 1.2 %collective-permute-start.1 = (f32[8,128]{1,0:T(8,128)S(1)}, f32[8,128]{1,0:T(8,128)S(1)}, u32[]{:S(2)}, u32[]{:S(2)}) collective-permute-start(f32[8,128]{1,0:T(8,128)S(1)} %slice_add_fusion.1), channel_id=1, source_target_pairs={{0,1},{1,0},{2,3},{3,2},{4,5},{5,4},{6,7},{7,6},{8,9},{9,8},{10,11... | collective-permute-start | bytes 12296 | tf_op jit(solution)/shard_map/ppermute | solution.py:531

commit v9 on v8

--- a/solution.py
+++ b/solution.py
@@ -13,7 +13,6 @@
 BLOCK = 2048
 SLOTS = 64
 BLOCK_ROWS = SLOTS // 2 + SUB
-SUMMED = 2 * SUB + BLOCK_ROWS
 CNEC, BUS = ("yl", "x"), ("z", "yh")
 
 
@@ -92,13 +91,14 @@
     for at in range(weight_ref.shape[0]):
         total += jnp.where(zone_ref[at:at + 1, :] == ids, weight_ref[at:at + 1, :], 0.0)
     total = jnp.sum(total, axis=1, keepdims=True)
-    total = jnp.sum(jnp.where(ids == iota((HALF, LANES), 1), total, 0.0), axis=0, keepdims=True)
-    out_ref[...] = jnp.broadcast_to(total[None], out_ref.shape)
+    eye = ids + HALF == iota((HALF, LANES), 1)
+    total = jnp.sum(jnp.where(eye, total, 0.0), axis=0, keepdims=True)
+    out_ref[...] = jnp.broadcast_to(total, out_ref.shape)
 
 
 def column_kernel(
-    swt_hbm, branch_hbm, sens_hbm, held_ref, meta_ref, extra_ref,
-    swt_ref, branch_ref, sens_ref, acc_ref, coupled_ref, sems
+    swt_hbm, branch_hbm, sens_hbm, held_ref, meta_ref, extra_ref, sens_ref,
+    swt_ref, branch_ref, acc_ref, coupled_ref, sems
 ):
     rows, cols = sens_ref.shape
     rank, actions = swt_ref.shape
@@ -212,34 +212,24 @@
     held_ref[...] = jnp.concatenate([columns[:, 0], columns[:, 1]], axis=-1)
 
 
-def zonal_kernel(totals_ref, weight_hbm, zone_hbm, sens_hbm, held_ref, extra_ref, pay_ref,
-                 weight_ref, zone_ref, sens_ref, key_ref, sums_ref, acc_ref, sems):
+def zonal_kernel(parts_ref, weight_hbm, zone_hbm, sens_ref, extra_ref, pay_ref, coupled_ref,
+                 weight_ref, zone_ref, key_ref, sums_ref, acc_ref, sems):
     rows, cols = sens_ref.shape
     zones = HALF
-    part = BLOCK // 2
-    steps = cols // part
     bf16 = jnp.bfloat16
     copies = [
-        pltpu.make_async_copy(weight_hbm, weight_ref, sems.at[steps]),
-        pltpu.make_async_copy(zone_hbm, zone_ref, sems.at[steps + 1]),
+        pltpu.make_async_copy(weight_hbm, weight_ref, sems.at[0]),
+        pltpu.make_async_copy(zone_hbm, zone_ref, sems.at[1]),
     ]
     for copy in copies:
         copy.start()
-
-    def block_copy(step):
-        at = pl.ds(pl.multiple_of(step * part, part), part)
-        return pltpu.make_async_copy(sens_hbm.at[:, at], sens_ref.at[:, at], sems.at[step])
-
-    for step in range(steps):
-        block_copy(step).start()
-
     acc_ref[...] = jnp.zeros_like(acc_ref)
-    pay_ref[:, SUMMED:, :] = held_ref[...]
-    total = jnp.sum(totals_ref[...], axis=0)[0:1]
+    coupled = jnp.sum(parts_ref[:, SLOTS // 2:, :], axis=0)
+    coupled_ref[...] = coupled
     for copy in copies:
         copy.wait()
     of_bus = jnp.take_along_axis(
-        jnp.broadcast_to(total, weight_ref.shape), zone_ref[...], axis=1
+        jnp.broadcast_to(coupled[0:1], weight_ref.shape), zone_ref[...] + HALF, axis=1
     )
     sums_ref[...] = weight_ref[...] / of_bus
     ids = iota((zones, LANES), 0)
@@ -248,12 +238,11 @@
         key_ref[:, at * LANES:(at + 1) * LANES] = key.astype(bf16)
 
     def step_body(step, carry):
-        at = pl.ds(pl.multiple_of(step * part, part), part)
-        block_copy(step).wait()
+        at = pl.ds(pl.multiple_of(step * BLOCK, BLOCK), BLOCK)
         acc_ref[...] += dot_nt(sens_ref[:, at], key_ref[:, at])
         return carry
 
-    lax.fori_loop(0, steps, step_body, 0)
+    lax.fori_loop(0, cols // BLOCK, step_body, 0)
 
     chunks = pay_ref.shape[0]
     zonal = acc_ref[...]
@@ -266,15 +255,14 @@
     share = jnp.concatenate([share[:, :, 0], share[:, :, 1]], axis=-1)
     half = SLOTS // 2
     switched = jnp.concatenate([switched[:half], switched[half:]], axis=1)
-    block = jnp.concatenate([switched, extra_ref[SLOTS:, :]], axis=0)
     pay_ref[:, 0:2 * SUB, :] = share.reshape(chunks, 2 * SUB, LANES)
-    pay_ref[:, 2 * SUB:SUMMED, :] = jnp.broadcast_to(block[None], (chunks, *block.shape))
+    pay_ref[:, 2 * SUB:, :] = jnp.broadcast_to(switched[None], (chunks, half, LANES))
 
 
 def place_kernel(parts_ref, local_ref, meta_ref, mine_ref, theirs_ref):
     chunks = parts_ref.shape[0]
     picks = meta_ref.shape[1] // 2
-    half = parts_ref.shape[1] - SUMMED
+    half = parts_ref.shape[1] - SUB
     y_here, y_size = lax.axis_index("yh"), lax.axis_size("yh")
     held = meta_ref[0:1, :].astype(jnp.int32)
     place = meta_ref[1:2, :].astype(jnp.int32)
@@ -283,7 +271,7 @@
     spread = slot_matrix([slot[:, at * picks:(at + 1) * picks] for at in (0, 1)], chunks * SLOTS)
     columns = [
         jnp.concatenate(
-            [parts_ref[z, SUMMED:, at * SLOTS:(at + 1) * SLOTS] for z in range(chunks)], axis=1
+            [parts_ref[z, 0:half, at * SLOTS:(at + 1) * SLOTS] for z in range(chunks)], axis=1
         )
         for at in (0, 1)
     ]
@@ -457,30 +445,31 @@
     weight, zone = [x.reshape(cols // LANES, LANES) for x in (shift_weight, bus_zone)]
     weight, zone = in_hbm(weight), in_hbm(zone)
     bus_scratch = [pltpu.VMEM((cols // LANES, LANES), kind) for kind in (f32, i32)]
+    swap = [(0, 1), (1, 0)]
+    turn = [(0, 3), (3, 0), (1, 2), (2, 1)]
     totals = pl.pallas_call(
         total_kernel,
-        out_shape=jax.ShapeDtypeStruct((lax.axis_size(BUS), SUB, LANES), f32),
+        out_shape=jax.ShapeDtypeStruct((SUB, LANES), f32),
         in_specs=[hbm] * 2,
         out_specs=vmem,
         scratch_shapes=[*bus_scratch, pltpu.SemaphoreType.DMA((2,))],
         compiler_params=params(),
         name="totals",
     )(weight, zone)
-    totals = lax.all_to_all(totals, BUS, 0, 0, tiled=True)
-    sens_scratch = pltpu.VMEM((rows, cols), jnp.bfloat16)
-    held, meta, extra = pl.pallas_call(
+    totals = totals + lax.ppermute(totals, ("yl", "yh"), turn)
+    held, meta, extra, sens = pl.pallas_call(
         column_kernel,
         out_shape=(
             jax.ShapeDtypeStruct((n_z, share, LANES), f32),
             jax.ShapeDtypeStruct((SUB, 2 * picks), f32),
             jax.ShapeDtypeStruct((SLOTS + SUB, LANES), f32),
+            pltpu.VMEM((rows, cols), jnp.bfloat16),
         ),
         in_specs=[hbm] * 3,
-        out_specs=(vmem,) * 3,
+        out_specs=(vmem,) * 4,
         scratch_shapes=[
             pltpu.VMEM((rank, actions), i32),
             pltpu.VMEM(branch_buses.shape, i32),
-            sens_scratch,
             pltpu.VMEM((rows, SLOTS), f32),
             pltpu.VMEM((SLOTS, picks), f32),
             pltpu.SemaphoreType.DMA((cols // BLOCK + 2,)),
@@ -488,26 +477,28 @@
         compiler_params=params(),
         name="columns",
     )(*[in_hbm(x) for x in (switched_rows.T, branch_buses, nodal_sensitivity)])
-    pay = pl.pallas_call(
+    coupled = jnp.broadcast_to((extra[SLOTS:] + totals)[None], (n_z, SUB, LANES))
+    parts = jnp.concatenate([held, coupled], axis=1)
+    parts = lax.all_to_all(parts, "z", 0, 0, tiled=True)
+    pay, coupled = pl.pallas_call(
         zonal_kernel,
-        out_shape=jax.ShapeDtypeStruct((n_z, SUMMED + share, LANES), f32),
-        in_specs=[vmem, hbm, hbm, hbm, vmem, vmem],
-        out_specs=vmem,
+        out_shape=(
+            jax.ShapeDtypeStruct((n_z, 2 * SUB + SLOTS // 2, LANES), f32),
+            jax.ShapeDtypeStruct((SUB, LANES), f32),
+        ),
+        in_specs=[vmem, hbm, hbm, vmem, vmem],
+        out_specs=(vmem, vmem),
         scratch_shapes=[
             *bus_scratch,
-            sens_scratch,
             pltpu.VMEM((zones, cols), jnp.bfloat16),
             pltpu.VMEM((cols // LANES, LANES), f32),
             pltpu.VMEM((rows, zones), f32),
-            pltpu.SemaphoreType.DMA((2 * cols // BLOCK + 2,)),
+            pltpu.SemaphoreType.DMA((2,)),
         ],
         compiler_params=params(),
         name="zonal",
-    )(totals, weight, zone, in_hbm(nodal_sensitivity), held, extra)
-
-    swap = [(0, 1), (1, 0)]
-    parts = lax.all_to_all(pay, "z", 0, 0, tiled=True)
-    local = jnp.sum(parts[:, :SUMMED], axis=0)
+    )(parts, weight, zone, pltpu.with_memory_space_constraint(sens, pltpu.VMEM), extra)
+    local = jnp.sum(lax.all_to_all(pay, "z", 0, 0, tiled=True), axis=0)
     part = jax.ShapeDtypeStruct((SUB + 2 * share, LANES), f32)
     mine, theirs = pl.pallas_call(
         place_kernel,
@@ -518,10 +509,10 @@
         name="place",
     )(parts, local, meta)
 
-    block = local[2 * SUB:]
+    block = jnp.concatenate([local[2 * SUB:], coupled], axis=0)
     theirs = lax.ppermute(jnp.concatenate([block, theirs], axis=0), "yh", swap)
     beside = lax.ppermute(block, "yl", swap)
-    across = lax.ppermute(block, ("yl", "yh"), [(0, 3), (3, 0), (1, 2), (2, 1)])
+    across = lax.ppermute(block, ("yl", "yh"), turn)
     here = jnp.concatenate([block + theirs[:BLOCK_ROWS], beside + across], axis=0)
     n_x = lax.axis_size("x")
     others = [

time: 64.9 us -> 73.5 us (1.13)
  blocking collectives: 15.2 us -> 30.9 us
  starting transfers between devices: 18.4 us -> 7.99 us
  other arithmetic: 0.04 us -> 3.01 us
  Pallas kernels: 15.1 us -> 15.9 us
  waiting for transfers between devices: 13.7 us -> 12.9 us
    all_to_all x1 -> x2, blocking collectives: 15.2 us -> 30.9 us  [the longest x1 17.9 us: body(): parts = lax.all_to_all(parts, 'z', 0, 0, tiled=True)]
    all_to_all x1 -> x0, starting transfers between devices: 11.2 us -> none  [body(): totals = lax.all_to_all(totals, BUS, 0, 0, tiled=True)]
    all_to_all x1 -> x0, waiting for transfers between devices: 5.45 us -> none  [body(): totals = lax.all_to_all(totals, BUS, 0, 0, tiled=True)]
    ppermute x1, waiting for transfers between devices: 0.01 us -> 5.05 us  [body(): theirs = lax.ppermute(jnp.concatenate([block, theirs], axis=0), 'yh', swap)]
    ppermute x1 -> x2, starting transfers between devices: 0.76 us -> 4.24 us  [the longest x1 3.1 us: body(): totals = totals + lax.ppermute(totals, ('yl', 'yh'), turn)]
    ppermute x1, starting transfers between devices: 2.74 us -> 0.64 us  [body(): theirs = lax.ppermute(jnp.concatenate([block, theirs], axis=0), 'yh', swap)]
    concatenate x0 -> x1, other arithmetic: none -> 0.92 us  [body(): parts = jnp.concatenate([held, coupled], axis=1)]
    ppermute x1 -> x2, waiting for transfers between devices: 1.89 us -> 1.36 us  [the longest x1 1.36 us: body(): across = lax.ppermute(block, ('yl', 'yh'), turn)]
where the time goes in v9:
time: 73.5 us; the launch traced here: 72.7 us
  blocking collectives  30.9 us (42%)
  Pallas kernels  15.9 us (22%)
  waiting for transfers between devices  12.9 us (18%)
  starting transfers between devices  7.99 us (11%)
  other arithmetic  3.01 us (4%)
  between operations  1.38 us (2%)
    all_to_all x1, blocking collectives, body(): parts = lax.all_to_all(parts, 'z', 0, 0, tiled=True)  17.9 us
    all_to_all x1, blocking collectives, body(): local = jnp.sum(lax.all_to_all(pay, 'z', 0, 0, tiled=True), axis=0)  13.1 us
    pallas_call x1, Pallas kernels, body(): pl.pallas_call(zonal_kernel, out_shape=(jax.ShapeDtypeStruct((n_z, 2 * SU...  5.98 us
    pallas_call x1, Pallas kernels, body(): pl.pallas_call(column_kernel, out_shape=(jax.ShapeDtypeStruct((n_z, share...  5.69 us
    ppermute x1, waiting for transfers between devices, body(): theirs = lax.ppermute(jnp.concatenate([block, theirs], axis=0), 'yh', swap)  5.05 us
    ppermute x3, waiting for transfers between devices, body(): lax.ppermute(here, 'x', [(at, (at + by) % n_x) for at in range(n_x)])  4.01 us
    ppermute x1, starting transfers between devices, body(): totals = totals + lax.ppermute(totals, ('yl', 'yh'), turn)  3.1 us
    ppermute x3, starting transfers between devices, body(): lax.ppermute(here, 'x', [(at, (at + by) % n_x) for at in range(n_x)])  2.97 us
  transfers between devices with their start and end apart: 8, of which 5 were waited for; matrix products, arithmetic and copies ran while one was open for 1% of the time, Pallas kernels for 8%

profile of v9, /device:TPU:6, one launch (start us, length us, event | category | flops | bytes accessed | tf_op | source)
XLA Modules:
  0.0 72.7 jit_solution(2051975609919021514)
XLA Ops:
  0.6 1.1 %totals.1 = f32[8,128]{1,0:T(8,128)S(1)} custom-call(f32[64,128]{1,0:T(8,128)} %bitcast.190, s32[64,128]{1,0:T(8,128)} %bitcast.192), custom_call_target="tpu_custom_call" | custom-call | tf_op jit(solution)/shard_map/totals/pallas_call | solution.py:450
  1.8 3.1 %collective-permute-start = (f32[8,128]{1,0:T(8,128)S(1)}, f32[8,128]{1,0:T(8,128)S(1)}, u32[]{:S(2)}, u32[]{:S(2)}) collective-permute-start(f32[8,128]{1,0:T(8,128)S(1)} %totals.1), channel_id=1, source_target_pairs={{0,130},{130,0},{2,128},{128,2},{1,131},{131,1},{3,129},{129,3},{4... | collective-permute-start | bytes 12296 | tf_op jit(solution)/shard_map/ppermute | solution.py:459
  4.9 5.7 %columns.1 = (f32[8,32,128]{2,1,0:T(8,128)}, f32[8,512]{1,0:T(8,128)S(1)}, f32[72,128]{1,0:T(8,128)}, bf16[512,8192]{1,0:T(8,128)(2,1)S(1)}) custom-call(s32[8,32]{1,0:T(8,128)} %bitcast.213, s32[2,4096]{1,0:T(2,128)} %branch_hbm.1, bf16[512,8192]{1,0:T(8,128)(2,1)} %sens_hbm.1), custom_call_target="tpu_custom_call" | custom-call | tf_op jit(solution)/shard_map/columns/pallas_call | solution.py:460
  10.6 0.0 collective-permute-done
  10.6 0.7 add_add_fusion
  11.3 0.9 %pad_maximum_fusion.1 = f32[8,40,128]{2,1,0:T(8,128)S(1)} fusion(f32[8,8,128]{2,1,0:T(8,128)S(1)} %broadcast_in_dim.312, f32[8,32,128]{2,1,0:T(8,128)} %get-tuple-element.69), kind=kLoop, calls=%fused_computation.102 | loop fusion | flops 40960 | bytes 327680 | tf_op jit(solution)/shard_map/concatenate | solution.py:481
  12.2 17.9 %all_to_all.31.parts_ref = f32[8,40,128]{2,1,0:T(8,128)} all-to-all(f32[8,40,128]{2,1,0:T(8,128)S(1)} %pad_maximum_fusion.1), channel_id=1, replica_groups=mesh['yl'=2,'x'=4,'z'=8,'yh'=2,'act'=2] {'z'}, dimensions={0} | all-to-all | bytes 327680 | tf_op jit(solution)/shard_map/all_to_all | solution.py:482
  30.0 0.0 copy-start
  30.0 0.0 copy-start.5
  30.0 0.0 copy-start.6
  30.0 0.0 copy-start.7
  30.0 6.0 %zonal.1 = (f32[8,48,128]{2,1,0:T(8,128)}, f32[8,128]{1,0:T(8,128)}) custom-call(f32[8,40,128]{2,1,0:T(8,128)} %all_to_all.31.parts_ref, f32[64,128]{1,0:T(8,128)} %bitcast.191, s32[64,128]{1,0:T(8,128)} %bitcast.193, bf16[512,8192]{1,0:T(8,128)(2,1)S(1)} %get-tuple-element.71.sens_ref, f32[72,128]{1,0:T(8,128)} %get-tuple-element.70.extra_ref), custom_call_target="tpu_custom_call" | custom-call | tf_op jit(solution)/shard_map/zonal/pallas_call | solution.py:483
  36.0 13.1 %all_to_all.32 = f32[8,48,128]{2,1,0:T(8,128)S(1)} all-to-all(f32[8,48,128]{2,1,0:T(8,128)} %get-tuple-element.72), channel_id=1, replica_groups=mesh['yl'=2,'x'=4,'z'=8,'yh'=2,'act'=2] {'z'}, dimensions={0} | all-to-all | bytes 393216 | tf_op jit(solution)/shard_map/all_to_all | solution.py:501
  49.1 0.0 copy-done
  49.2 0.4 place.1
  49.6 0.7 pad_maximum_fusion.2
  50.3 0.6 collective-permute-start.1
  50.9 5.0 %collective-permute-done.1 = f32[112,128]{1,0:T(8,128)S(1)} collective-permute-done((f32[112,128]{1,0:T(8,128)S(1)}, f32[112,128]{1,0:T(8,128)S(1)}, u32[]{:S(2)}, u32[]{:S(2)}) %collective-permute-start.1) | collective-permute-done | bytes 57376 | tf_op jit(solution)/shard_map/ppermute | solution.py:513
  56.0 0.7 slice_add_fusion
  56.7 0.1 collective-permute-start.3
  56.8 1.1 %collective-permute-start.4 = (f32[40,128]{1,0:T(8,128)S(1)}, f32[40,128]{1,0:T(8,128)S(1)}, u32[]{:S(2)}, u32[]{:S(2)}) collective-permute-start(f32[40,128]{1,0:T(8,128)S(1)} %get-tuple-element.153), channel_id=1, source_target_pairs={{0,130},{130,0},{2,128},{128,2},{1,131},{131,1},{3,129},{129,3},{4... | collective-permute-start | bytes 61448 | tf_op jit(solution)/shard_map/ppermute | solution.py:515
  57.9 2.5 %collective-permute-done.3 = f32[40,128]{1,0:T(8,128)S(1)} collective-permute-done((f32[40,128]{1,0:T(8,128)S(1)}, f32[40,128]{1,0:T(8,128)S(1)}, u32[]{:S(2)}, u32[]{:S(2)}) %collective-permute-start.3) | collective-permute-done | bytes 20512 | tf_op jit(solution)/shard_map/ppermute | solution.py:514
  60.4 1.4 %collective-permute-done.4 = f32[40,128]{1,0:T(8,128)S(1)} collective-permute-done((f32[40,128]{1,0:T(8,128)S(1)}, f32[40,128]{1,0:T(8,128)S(1)}, u32[]{:S(2)}, u32[]{:S(2)}) %collective-permute-start.4) | collective-permute-done | bytes 20512 | tf_op jit(solution)/shard_map/ppermute | solution.py:515
  61.8 0.6 collective-permute-start.5
  62.4 2.4 %collective-permute-start.6 = (f32[80,128]{1,0:T(8,128)S(1)}, f32[80,128]{1,0:T(8,128)S(1)}, u32[]{:S(2)}, u32[]{:S(2)}) collective-permute-start(f32[80,128]{1,0:T(8,128)S(1)} %pad_maximum_fusion.3), channel_id=1, source_target_pairs={{0,64},{32,96},{64,0},{96,32},{1,65},{33,97},{65,1},{97,33},{2,66}... | collective-permute-start | bytes 122888 | tf_op jit(solution)/shard_map/ppermute | solution.py:519
  64.8 0.0 collective-permute-start.7
  64.8 0.0 collective-permute-start.2
  64.8 0.5 slice.132
  66.0 0.0 collective-permute-done.2
  66.0 0.0 collective-permute-done.5
  66.0 1.9 %collective-permute-done.6 = f32[80,128]{1,0:T(8,128)S(1)} collective-permute-done((f32[80,128]{1,0:T(8,128)S(1)}, f32[80,128]{1,0:T(8,128)S(1)}, u32[]{:S(2)}, u32[]{:S(2)}) %collective-permute-start.6) | collective-permute-done | bytes 40992 | tf_op jit(solution)/shard_map/ppermute | solution.py:519
  67.9 2.1 %collective-permute-done.7 = f32[80,128]{1,0:T(8,128)S(1)} collective-permute-done((f32[80,128]{1,0:T(8,128)S(1)}, f32[80,128]{1,0:T(8,128)S(1)}, u32[]{:S(2)}, u32[]{:S(2)}) %collective-permute-start.7) | collective-permute-done | bytes 40992 | tf_op jit(solution)/shard_map/ppermute | solution.py:519
  70.0 0.0 copy-done.5
  70.0 0.0 copy-done.6
  70.0 0.0 copy-done.7
  70.0 2.7 %conditional.1 = ((f32[32,32,64]{2,1,0:T(8,128)}, f32[32,32]{1,0:T(8,128)}, f32[32,32]{1,0:T(8,128)})) conditional(s32[]{:T(128)} %bitcast.57, (f32[64]{0:T(128)S(1)}, f32[32]{0:T(128)S(1)}, f32[8,512]{1,0:T(8,128)S(1)}, f32[72,128]{1,0:T(8,128)S(1)}, f32[112,128]{1,0:T(8,128)S(1)}, /*index=5*/f32[8,128]{1,0:T(8,128)S(1)}, f32[80,128]{1,0:T(8,128)S(1)}, ...), branch_computations={%region_1.0_spmd, %region_2.11_spmd} | conditional | flops 551126016 | bytes 46937896 | solution.py:548
  70.0 2.7 %update.1 = (f32[32,32,64]{2,1,0:T(8,128)}, f32[32,32]{1,0:T(8,128)}, f32[32,32]{1,0:T(8,128)}) custom-call(f32[8,512]{1,0:T(8,128)S(1)} %get-tuple-element.26.meta_ref, f32[72,128]{1,0:T(8,128)S(1)} %get-tuple-element.36.mine_ref, f32[112,128]{1,0:T(8,128)S(1)} %get-tuple-element.37.theirs_ref, f32[8,128]{1,0:T(8,128)S(1)} %get-tuple-element.38.other_ref, ...), custom_call_target="tpu_custom_call" | custom-call | tf_op jit(solution)/shard_map/cond/branch_0_fun/update/pallas_call | solution.py:527
  (6 shorter events, 0.0 us)
Async XLA Ops:
  1.8 8.8 %collective-permute-start = (f32[8,128]{1,0:T(8,128)S(1)}, f32[8,128]{1,0:T(8,128)S(1)}, u32[]{:S(2)}, u32[]{:S(2)}) collective-permute-start(f32[8,128]{1,0:T(8,128)S(1)} %totals.1), channel_id=1, source_target_pairs={{0,130},{130,0},{2,128},{128,2},{1,131},{131,1},{3,129},{129,3},{4... | collective-permute-start | bytes 12296 | tf_op jit(solution)/shard_map/ppermute | solution.py:459
  30.0 19.1 %copy-start = (f32[8,40,128]{2,1,0:T(8,128)S(1)}, f32[8,40,128]{2,1,0:T(8,128)}, u32[]{:S(2)}) copy-start(f32[8,40,128]{2,1,0:T(8,128)} %all_to_all.31.parts_ref) | copy-start | bytes 491524
  30.0 40.0 %copy-start.5 = (s32[32,8]{0,1:T(8,128)S(1)}, s32[32,8]{0,1:T(8,128)}, u32[]{:S(2)}) copy-start(s32[32,8]{0,1:T(8,128)} %param.15) | copy-start | bytes 3076
  30.0 40.0 %copy-start.6 = (f32[64]{0:T(128)S(1)}, f32[64]{0:T(128)}, u32[]{:S(2)}) copy-start(f32[64]{0:T(128)} %param.16) | copy-start | bytes 772
  30.0 40.0 %copy-start.7 = (f32[32]{0:T(128)S(1)}, f32[32]{0:T(128)}, u32[]{:S(2)}) copy-start(f32[32]{0:T(128)} %param.17) | copy-start | bytes 388
  50.3 5.7 %collective-permute-start.1 = (f32[112,128]{1,0:T(8,128)S(1)}, f32[112,128]{1,0:T(8,128)S(1)}, u32[]{:S(2)}, u32[]{:S(2)}) collective-permute-start(f32[112,128]{1,0:T(8,128)S(1)} %pad_maximum_fusion.2), channel_id=1, source_target_pairs={{0,2},{2,0},{1,3},{3,1},{4,6},{6,4},{5,7},{7,5},{8,10},{10,8},{9,1... | collective-permute-start | bytes 172040 | tf_op jit(solution)/shard_map/ppermute | solution.py:513
  56.7 3.8 %collective-permute-start.3 = (f32[40,128]{1,0:T(8,128)S(1)}, f32[40,128]{1,0:T(8,128)S(1)}, u32[]{:S(2)}, u32[]{:S(2)}) collective-permute-start(f32[40,128]{1,0:T(8,128)S(1)} %get-tuple-element.153), channel_id=1, source_target_pairs={{0,128},{128,0},{1,129},{129,1},{2,130},{130,2},{3,131},{131,3},{4... | collective-permute-start | bytes 61448 | tf_op jit(solution)/shard_map/ppermute | solution.py:514
  56.8 5.0 %collective-permute-start.4 = (f32[40,128]{1,0:T(8,128)S(1)}, f32[40,128]{1,0:T(8,128)S(1)}, u32[]{:S(2)}, u32[]{:S(2)}) collective-permute-start(f32[40,128]{1,0:T(8,128)S(1)} %get-tuple-element.153), channel_id=1, source_target_pairs={{0,130},{130,0},{2,128},{128,2},{1,131},{131,1},{3,129},{129,3},{4... | collective-permute-start | bytes 61448 | tf_op jit(solution)/shard_map/ppermute | solution.py:515
  61.8 4.2 %collective-permute-start.5 = (f32[80,128]{1,0:T(8,128)S(1)}, f32[80,128]{1,0:T(8,128)S(1)}, u32[]{:S(2)}, u32[]{:S(2)}) collective-permute-start(f32[80,128]{1,0:T(8,128)S(1)} %pad_maximum_fusion.3), channel_id=1, source_target_pairs={{0,32},{32,64},{64,96},{96,0},{1,33},{33,65},{65,97},{97,1},{2,34}... | collective-permute-start | bytes 122888 | tf_op jit(solution)/shard_map/ppermute | solution.py:519
  62.4 5.5 %collective-permute-start.6 = (f32[80,128]{1,0:T(8,128)S(1)}, f32[80,128]{1,0:T(8,128)S(1)}, u32[]{:S(2)}, u32[]{:S(2)}) collective-permute-start(f32[80,128]{1,0:T(8,128)S(1)} %pad_maximum_fusion.3), channel_id=1, source_target_pairs={{0,64},{32,96},{64,0},{96,32},{1,65},{33,97},{65,1},{97,33},{2,66}... | collective-permute-start | bytes 122888 | tf_op jit(solution)/shard_map/ppermute | solution.py:519
  64.8 5.2 %collective-permute-start.7 = (f32[80,128]{1,0:T(8,128)S(1)}, f32[80,128]{1,0:T(8,128)S(1)}, u32[]{:S(2)}, u32[]{:S(2)}) collective-permute-start(f32[80,128]{1,0:T(8,128)S(1)} %pad_maximum_fusion.3), channel_id=1, source_target_pairs={{0,96},{32,0},{64,32},{96,64},{1,97},{33,1},{65,33},{97,65},{2,98}... | collective-permute-start | bytes 122888 | tf_op jit(solution)/shard_map/ppermute | solution.py:519
  64.8 1.2 %collective-permute-start.2 = (f32[8,128]{1,0:T(8,128)S(1)}, f32[8,128]{1,0:T(8,128)S(1)}, u32[]{:S(2)}, u32[]{:S(2)}) collective-permute-start(f32[8,128]{1,0:T(8,128)S(1)} %slice_add_fusion.1), channel_id=1, source_target_pairs={{0,1},{1,0},{2,3},{3,2},{4,5},{5,4},{6,7},{7,6},{8,9},{9,8},{10,11... | collective-permute-start | bytes 12296 | tf_op jit(solution)/shard_map/ppermute | solution.py:522

commit v10 on v8

--- a/solution.py
+++ b/solution.py
@@ -1,3 +1,5 @@
+import functools
+
 import jax
 import jax.numpy as jnp
 from jax import lax
@@ -15,6 +17,7 @@
 BLOCK_ROWS = SLOTS // 2 + SUB
 SUMMED = 2 * SUB + BLOCK_ROWS
 CNEC, BUS = ("yl", "x"), ("z", "yh")
+PLANE = ("yl", "x", "yh")
 
 
 def iota(shape, dim):
@@ -93,73 +96,85 @@
         total += jnp.where(zone_ref[at:at + 1, :] == ids, weight_ref[at:at + 1, :], 0.0)
     total = jnp.sum(total, axis=1, keepdims=True)
     total = jnp.sum(jnp.where(ids == iota((HALF, LANES), 1), total, 0.0), axis=0, keepdims=True)
-    out_ref[...] = jnp.broadcast_to(total[None], out_ref.shape)
-
-
-def column_kernel(
-    swt_hbm, branch_hbm, sens_hbm, held_ref, meta_ref, extra_ref,
-    swt_ref, branch_ref, sens_ref, acc_ref, coupled_ref, sems
-):
-    rows, cols = sens_ref.shape
+    out_ref[...] = jnp.broadcast_to(total, out_ref.shape)
+
+
+def slot_kernel(rows, cols, swt_hbm, branch_hbm, meta_ref, swt_ref, branch_ref, sems):
+    copies = [
+        pltpu.make_async_copy(swt_hbm, swt_ref, sems.at[0]),
+        pltpu.make_async_copy(branch_hbm, branch_ref, sems.at[1]),
+    ]
+    for copy in copies:
+        copy.start()
+    for copy in copies:
+        copy.wait()
     rank, actions = swt_ref.shape
     picks = rank * actions
-    steps = cols // BLOCK
-    bf16 = jnp.bfloat16
-    small = [
-        pltpu.make_async_copy(swt_hbm, swt_ref, sems.at[steps]),
-        pltpu.make_async_copy(branch_hbm, branch_ref, sems.at[steps + 1]),
-    ]
-    for copy in small:
-        copy.start()
-
-    def block_copy(step):
-        at = pl.ds(pl.multiple_of(step * BLOCK, BLOCK), BLOCK)
-        return pltpu.make_async_copy(sens_hbm.at[:, at], sens_ref.at[:, at], sems.at[step])
-
-    for step in range(steps):
-        block_copy(step).start()
-
-    shard = lax.axis_index(BUS)
-    row_start = lax.axis_index(CNEC) * rows
-    acc_ref[...] = jnp.zeros_like(acc_ref)
-    for copy in small:
-        copy.wait()
+    shards, groups = lax.axis_size(BUS), lax.axis_size(CNEC)
     row, ends = find_picks(swt_ref[...], branch_ref)
 
     def ranks(owner, owners):
         count = owner.shape[1]
         inside = iota((owners, count), 0) == owner
         before = jnp.where(iota((count, count), 0) < iota((count, count), 1), 1.0, 0.0)
-        place = dot(jnp.where(inside, 1.0, 0.0).astype(bf16), before.astype(bf16))
+        place = dot(jnp.where(inside, 1.0, 0.0).astype(jnp.bfloat16), before.astype(jnp.bfloat16))
         return jnp.sum(jnp.where(inside, place, 0.0), axis=0, keepdims=True)
 
     bus = jnp.concatenate(ends, axis=1)
-    count = 2 * picks
-    held, place = bus // cols, ranks(bus // cols, lax.axis_size(BUS))
-    owner, row_place = row // rows, ranks(row // rows, lax.axis_size(CNEC))
+    held, place = bus // cols, ranks(bus // cols, shards)
+    owner, row_place = row // rows, ranks(row // rows, groups)
     most = jnp.maximum(
         jnp.max(place, axis=1, keepdims=True), jnp.max(row_place, axis=1, keepdims=True)
     )
     over = jnp.where(most >= SLOTS, 1.0, 0.0)
-    meta_ref[0:1, :] = held.astype(jnp.float32)
+    f32 = jnp.float32
+    meta_ref[0:1, :] = held.astype(f32)
     meta_ref[1:2, :] = place
-    meta_ref[2:3, :] = jnp.broadcast_to(over, (1, count))
-    meta_ref[3:4, :] = jnp.concatenate([owner.astype(jnp.float32), row_place], axis=1)
-    meta_ref[4:, :] = jnp.zeros((SUB - 4, count), jnp.float32)
+    meta_ref[2:3, :] = jnp.broadcast_to(over, place.shape)
+    meta_ref[3:4, :] = jnp.concatenate([owner.astype(f32), row_place], axis=1)
+    meta_ref[4:5, :] = (bus - held * cols).astype(f32)
+    row = (row - owner * rows).astype(f32)
+    meta_ref[5:6, :] = jnp.concatenate([row, row], axis=1)
+    meta_ref[6:, :] = jnp.zeros((SUB - 6, place.shape[1]), f32)
+
+
+def column_kernel(
+    meta_ref, after_ref, sens_hbm, held_ref, extra_ref, sens_ref, acc_ref, coupled_ref, sems
+):
+    rows, cols = sens_ref.shape
+    rank = SUB
+    count = meta_ref.shape[1]
+    picks = count // 2
+    steps = cols // BLOCK
+    bf16 = jnp.bfloat16
+
+    def block_copy(step):
+        at = pl.ds(pl.multiple_of(step * BLOCK, BLOCK), BLOCK)
+        return pltpu.make_async_copy(sens_hbm.at[:, at], sens_ref.at[:, at], sems.at[step])
+
+    for step in range(steps):
+        block_copy(step).start()
+
+    acc_ref[...] = jnp.zeros_like(acc_ref)
+    held = meta_ref[0:1, :].astype(jnp.int32)
+    place = meta_ref[1:2, :]
+    owner = meta_ref[3:4, :picks].astype(jnp.int32)
+    row_place = meta_ref[3:4, picks:]
+    local = meta_ref[4:5, :]
+    row = meta_ref[5:6, :picks]
     place = place.astype(jnp.int32)
-    mine = held == shard
+    mine = held == lax.axis_index(BUS)
     slot = jnp.where(mine, place, -1)
-    local = bus - shard * cols
 
     def buses_of(group):
         match = iota((SLOTS, count), 0) + group * SLOTS == slot
-        match = jnp.where(match, (local + 1).astype(jnp.float32), 0.0)
+        match = jnp.where(match, local + 1.0, 0.0)
         return jnp.sum(match, axis=1, keepdims=True).astype(jnp.int32) - 1
 
     first_buses = buses_of(0)
     row_slot = jnp.where(owner == lax.axis_index(CNEC), row_place.astype(jnp.int32), -1)
     match = iota((SLOTS, picks), 0) == row_slot
-    slot_row = jnp.where(match, (row - row_start + 1).astype(jnp.float32), 0.0)
+    slot_row = jnp.where(match, row + 1.0, 0.0)
     slot_row = jnp.sum(slot_row, axis=1, keepdims=True) - 1.0
     action_of = iota((SLOTS, picks), 1) // rank
     slot_action = jnp.where(match, action_of.astype(jnp.float32), 0.0)
@@ -269,6 +284,12 @@
     block = jnp.concatenate([switched, extra_ref[SLOTS:, :]], axis=0)
     pay_ref[:, 0:2 * SUB, :] = share.reshape(chunks, 2 * SUB, LANES)
     pay_ref[:, 2 * SUB:SUMMED, :] = jnp.broadcast_to(block[None], (chunks, *block.shape))
+
+
+def spread_kernel(parts_ref, block_ref, local_ref):
+    local_ref[...] = jnp.sum(parts_ref[:, 0:2 * SUB, :], axis=0)
+    block = jnp.sum(parts_ref[:, 2 * SUB:SUMMED, :], axis=0)
+    block_ref[...] = jnp.broadcast_to(block[None], block_ref.shape)
 
 
 def place_kernel(parts_ref, local_ref, meta_ref, mine_ref, theirs_ref):
@@ -315,26 +336,20 @@
 
 
 def final_kernel(
-    meta_ref, mine_ref, theirs_ref, other_ref, here_ref, x1_ref, x2_ref, x3_ref, position_ref,
-    limit_ref, after_ref, loading_ref, margin_ref
+    meta_ref, mine_ref, theirs_ref, other_ref, blocks_ref, position_ref, limit_ref,
+    after_ref, loading_ref, margin_ref
 ):
     actions, share, zones = after_ref.shape
     pairs = actions // 2
     picks = actions * SUB
     bf16 = jnp.bfloat16
 
-    size_x = lax.axis_size("x")
     owner = meta_ref[3:4, :picks].astype(jnp.int32)
     slot = meta_ref[3:4, picks:].astype(jnp.int32)
-    back = (lax.axis_index("x") - owner % size_x + size_x) % size_x
-    flip = jnp.where(owner // size_x == lax.axis_index("yl"), 0, 1)
-    blocks = [
-        ref[at * BLOCK_ROWS:(at + 1) * BLOCK_ROWS, :]
-        for ref in (here_ref, x1_ref, x2_ref, x3_ref)
-        for at in (0, 1)
-    ]
-    count = len(blocks) * SLOTS
-    spread = iota((count, picks), 0) == (back * 2 + flip) * SLOTS + slot
+    groups = lax.axis_size(CNEC)
+    blocks = [blocks_ref[2 * at] + blocks_ref[2 * at + 1] for at in range(groups)]
+    count = groups * SLOTS
+    spread = iota((count, picks), 0) == owner * SLOTS + slot
     spread = jnp.where(spread, 1.0, 0.0).astype(bf16)
     half = SLOTS // 2
     switched, coupled = [], []
@@ -380,7 +395,7 @@
         right = jnp.where(row_id == pivot, right_now, right - factor * right_now)
 
     lower = lax.axis_index("act") == 0
-    whole = mine_ref[...] + theirs_ref[BLOCK_ROWS:]
+    whole = mine_ref[...] + theirs_ref[...]
     mine, other = whole[0:SUB], other_ref[...]
     low, high = jnp.where(lower, mine, other), jnp.where(lower, other, mine)
     zonal = jnp.concatenate(
@@ -459,35 +474,48 @@
     bus_scratch = [pltpu.VMEM((cols // LANES, LANES), kind) for kind in (f32, i32)]
     totals = pl.pallas_call(
         total_kernel,
-        out_shape=jax.ShapeDtypeStruct((lax.axis_size(BUS), SUB, LANES), f32),
+        out_shape=jax.ShapeDtypeStruct((SUB, LANES), f32),
         in_specs=[hbm] * 2,
         out_specs=vmem,
         scratch_shapes=[*bus_scratch, pltpu.SemaphoreType.DMA((2,))],
         compiler_params=params(),
         name="totals",
     )(weight, zone)
-    totals = lax.all_to_all(totals, BUS, 0, 0, tiled=True)
+    turn = [(0, 3), (3, 0), (1, 2), (2, 1)]
+    totals = totals + lax.ppermute(totals, ("yl", "yh"), turn)
+    meta = pl.pallas_call(
+        functools.partial(slot_kernel, rows, cols),
+        out_shape=jax.ShapeDtypeStruct((SUB, 2 * picks), f32),
+        in_specs=[hbm] * 2,
+        out_specs=vmem,
+        scratch_shapes=[
+            pltpu.VMEM((rank, actions), i32),
+            pltpu.VMEM(branch_buses.shape, i32),
+            pltpu.SemaphoreType.DMA((2,)),
+        ],
+        compiler_params=params(),
+        name="slots",
+    )(in_hbm(switched_rows.T), in_hbm(branch_buses))
     sens_scratch = pltpu.VMEM((rows, cols), jnp.bfloat16)
-    held, meta, extra = pl.pallas_call(
+    held, extra = pl.pallas_call(
         column_kernel,
         out_shape=(
             jax.ShapeDtypeStruct((n_z, share, LANES), f32),
-            jax.ShapeDtypeStruct((SUB, 2 * picks), f32),
             jax.ShapeDtypeStruct((SLOTS + SUB, LANES), f32),
         ),
-        in_specs=[hbm] * 3,
-        out_specs=(vmem,) * 3,
+        in_specs=[vmem, vmem, hbm],
+        out_specs=(vmem,) * 2,
         scratch_shapes=[
-            pltpu.VMEM((rank, actions), i32),
-            pltpu.VMEM(branch_buses.shape, i32),
             sens_scratch,
             pltpu.VMEM((rows, SLOTS), f32),
             pltpu.VMEM((SLOTS, picks), f32),
-            pltpu.SemaphoreType.DMA((cols // BLOCK + 2,)),
+            pltpu.SemaphoreType.DMA((cols // BLOCK,)),
         ],
         compiler_params=params(),
         name="columns",
-    )(*[in_hbm(x) for x in (switched_rows.T, branch_buses, nodal_sensitivity)])
+    )(meta, totals, in_hbm(nodal_sensitivity))
+    totals = jnp.broadcast_to(totals[None], (n_z, SUB, LANES))
+    totals = lax.all_to_all(totals, "z", 0, 0, tiled=True)
     pay = pl.pallas_call(
         zonal_kernel,
         out_shape=jax.ShapeDtypeStruct((n_z, SUMMED + share, LANES), f32),
@@ -507,7 +535,18 @@
 
     swap = [(0, 1), (1, 0)]
     parts = lax.all_to_all(pay, "z", 0, 0, tiled=True)
-    local = jnp.sum(parts[:, :SUMMED], axis=0)
+    block, local = pl.pallas_call(
+        spread_kernel,
+        out_shape=(
+            jax.ShapeDtypeStruct((lax.axis_size(PLANE), BLOCK_ROWS, LANES), f32),
+            jax.ShapeDtypeStruct((2 * SUB, LANES), f32),
+        ),
+        in_specs=[vmem],
+        out_specs=(vmem, vmem),
+        compiler_params=params(),
+        name="spread",
+    )(parts)
+    blocks = lax.all_to_all(block, PLANE, 0, 0, tiled=True)
     part = jax.ShapeDtypeStruct((SUB + 2 * share, LANES), f32)
     mine, theirs = pl.pallas_call(
         place_kernel,
@@ -518,19 +557,8 @@
         name="place",
     )(parts, local, meta)
 
-    block = local[2 * SUB:]
-    theirs = lax.ppermute(jnp.concatenate([block, theirs], axis=0), "yh", swap)
-    beside = lax.ppermute(block, "yl", swap)
-    across = lax.ppermute(block, ("yl", "yh"), [(0, 3), (3, 0), (1, 2), (2, 1)])
-    here = jnp.concatenate([block + theirs[:BLOCK_ROWS], beside + across], axis=0)
-    n_x = lax.axis_size("x")
-    others = [
-        lax.ppermute(here, "x", [(at, (at + by) % n_x) for at in range(n_x)])
-        for by in range(1, n_x)
-    ]
-    other = lax.ppermute(
-        mine[:SUB] + theirs[BLOCK_ROWS:BLOCK_ROWS + SUB], "act", swap
-    )
+    theirs = lax.ppermute(theirs, "yh", swap)
+    other = lax.ppermute(mine[:SUB] + theirs[:SUB], "act", swap)
 
     def compact():
         outputs = pl.pallas_call(
@@ -540,12 +568,12 @@
                 jax.ShapeDtypeStruct((actions, share), f32),
                 jax.ShapeDtypeStruct((actions, share), f32),
             ),
-            in_specs=[vmem] * 10,
+            in_specs=[vmem] * 7,
             out_specs=(vmem, vmem, vmem),
             compiler_params=params(),
             name="update",
         )(
-            meta, mine, theirs, other, here, *others,
+            meta, mine, theirs, other, blocks,
             net_position.reshape(1, zones), flow_limit.reshape(1, share),
         )
         return tuple(outputs)

time: 64.9 us -> 66.8 us (1.029)
  waiting for transfers between devices: 13.7 us -> 6.97 us
  starting transfers between devices: 18.4 us -> 21.8 us
  blocking collectives: 15.2 us -> 17.8 us
  Pallas kernels: 15.1 us -> 16.6 us
    all_to_all x1 -> x2, starting transfers between devices: 11.2 us -> 15.6 us  [the longest x1 8.47 us: body(): totals = lax.all_to_all(totals, 'z', 0, 0, tiled=True)]
    all_to_all x1 -> x2, waiting for transfers between devices: 5.45 us -> 1.56 us  [the longest x1 1.56 us: body(): totals = lax.all_to_all(totals, 'z', 0, 0, tiled=True)]
    ppermute x7 -> x3, waiting for transfers between devices: 8.25 us -> 5.4 us  [the longest x1 3.6 us: body(): theirs = lax.ppermute(theirs, 'yh', swap)]
    all_to_all x1, blocking collectives: 15.2 us -> 17.8 us  [body(): parts = lax.all_to_all(pay, 'z', 0, 0, tiled=True)]
    pallas_call x1 -> x3, Pallas kernels: 1.76 us -> 3.28 us  [the longest x1 1.41 us: body(): pl.pallas_call(functools.partial(slot_kernel, rows, cols), out_shape=jax....]
    ppermute x7 -> x3, starting transfers between devices: 7.16 us -> 6.16 us  [the longest x1 3.1 us: body(): totals = totals + lax.ppermute(totals, ('yl', 'yh'), turn)]
  transfers between devices with their start and end apart: 8 -> 5, of which waited for: 5 -> 3; matrix products, arithmetic and copies ran while one was open for 1% -> 1% of each run, Pallas kernels for 8% -> 10%
where the time goes in v10:
time: 66.8 us; the launch traced here: 65.7 us
  starting transfers between devices  21.8 us (33%)
  blocking collectives  17.8 us (27%)
  Pallas kernels  16.6 us (25%)
  waiting for transfers between devices  6.97 us (10%)
  between operations  1.37 us (2%)
  local copies, waits for them, and re-layouts  1.15 us (2%)
    all_to_all x1, blocking collectives, body(): parts = lax.all_to_all(pay, 'z', 0, 0, tiled=True)  17.8 us
    all_to_all x1, starting transfers between devices, body(): totals = lax.all_to_all(totals, 'z', 0, 0, tiled=True)  8.47 us
    all_to_all x1, starting transfers between devices, body(): blocks = lax.all_to_all(block, PLANE, 0, 0, tiled=True)  7.18 us
    pallas_call x1, Pallas kernels, body(): pl.pallas_call(zonal_kernel, out_shape=jax.ShapeDtypeStruct((n_z, SUMMED...  5.15 us
    pallas_call x1, Pallas kernels, body(): pl.pallas_call(column_kernel, out_shape=(jax.ShapeDtypeStruct((n_z, share...  5.04 us
    ppermute x1, waiting for transfers between devices, body(): theirs = lax.ppermute(theirs, 'yh', swap)  3.6 us
    ppermute x1, starting transfers between devices, body(): totals = totals + lax.ppermute(totals, ('yl', 'yh'), turn)  3.1 us
    ppermute x1, starting transfers between devices, body(): theirs = lax.ppermute(theirs, 'yh', swap)  3.05 us
  transfers between devices with their start and end apart: 5, of which 3 were waited for; matrix products, arithmetic and copies ran while one was open for 1% of the time, Pallas kernels for 10%

profile of v10, /device:TPU:6, one launch (start us, length us, event | category | flops | bytes accessed | tf_op | source)
XLA Modules:
  0.0 65.7 jit_solution(15683470141038028296)
XLA Ops:
  0.6 1.1 %totals.1 = f32[8,128]{1,0:T(8,128)S(1)} custom-call(f32[64,128]{1,0:T(8,128)} %bitcast.190, s32[64,128]{1,0:T(8,128)} %bitcast.192), custom_call_target="tpu_custom_call" | custom-call | tf_op jit(solution)/shard_map/totals/pallas_call | solution.py:475
  1.8 3.1 %collective-permute-start = (f32[8,128]{1,0:T(8,128)S(1)}, f32[8,128]{1,0:T(8,128)S(1)}, u32[]{:S(2)}, u32[]{:S(2)}) collective-permute-start(f32[8,128]{1,0:T(8,128)S(1)} %totals.1), channel_id=1, source_target_pairs={{0,130},{130,0},{2,128},{128,2},{1,131},{131,1},{3,129},{129,3},{4... | collective-permute-start | bytes 12296 | tf_op jit(solution)/shard_map/ppermute | solution.py:485
  4.9 1.8 %collective-permute-done = f32[8,128]{1,0:T(8,128)S(1)} collective-permute-done((f32[8,128]{1,0:T(8,128)S(1)}, f32[8,128]{1,0:T(8,128)S(1)}, u32[]{:S(2)}, u32[]{:S(2)}) %collective-permute-start) | collective-permute-done | bytes 4128 | tf_op jit(solution)/shard_map/ppermute | solution.py:485
  6.7 0.6 broadcast_in_dim.312
  7.3 8.5 %all-to-all-start.5 = ((f32[8,8,128]{2,1,0:T(8,128)}), f32[8,8,128]{2,1,0:T(8,128)S(1)}, u32[]{:S(2)}, u32[]{:S(2)}) async-start(f32[8,8,128]{2,1,0:T(8,128)} %broadcast_in_dim.312), calls=%async_computation.5 | async-start | bytes 65536 | tf_op jit(solution)/shard_map/all_to_all | solution.py:518
  15.8 1.4 %slots.1.meta_ref = f32[8,512]{1,0:T(8,128)S(1)} custom-call(s32[8,32]{1,0:T(8,128)} %bitcast.213, s32[2,4096]{1,0:T(2,128)} %branch_hbm.1), custom_call_target="tpu_custom_call" | custom-call | tf_op jit(solution)/shard_map/slots/pallas_call | solution.py:486
  17.2 5.0 %columns.1 = (f32[8,32,128]{2,1,0:T(8,128)S(1)}, f32[72,128]{1,0:T(8,128)S(1)}) custom-call(f32[8,512]{1,0:T(8,128)S(1)} %slots.1.meta_ref, f32[8,128]{1,0:T(8,128)S(1)} %add.63.after_ref, bf16[512,8192]{1,0:T(8,128)(2,1)} %sens_hbm.3), custom_call_target="tpu_custom_call" | custom-call | tf_op jit(solution)/shard_map/columns/pallas_call | solution.py:500
  22.2 1.6 %all-to-all-done.5.totals_ref = f32[8,8,128]{2,1,0:T(8,128)S(1)} async-done(((f32[8,8,128]{2,1,0:T(8,128)}), f32[8,8,128]{2,1,0:T(8,128)S(1)}, u32[]{:S(2)}, u32[]{:S(2)}) %all-to-all-start.5) | async-done | bytes 32800 | tf_op jit(solution)/shard_map/all_to_all | solution.py:518
  23.8 0.0 copy-start.4
  23.8 0.0 copy-start.5
  23.8 0.0 copy-start.6
  23.8 5.1 %zonal.1 = f32[8,88,128]{2,1,0:T(8,128)S(1)} custom-call(f32[8,8,128]{2,1,0:T(8,128)S(1)} %all-to-all-done.5.totals_ref, f32[64,128]{1,0:T(8,128)} %bitcast.191, s32[64,128]{1,0:T(8,128)} %bitcast.193, bf16[512,8192]{1,0:T(8,128)(2,1)} %sens_hbm.3, f32[8,32,128]{2,1,0:T(8,128)S(1)} %get-tuple-element.57.held_ref, f32[72,128]{1,0:T(8,128)S(1)} %get-tuple-element.58.extra_ref), custom_call_target="tpu_custom_call" | custom-call | tf_op jit(solution)/shard_map/zonal/pallas_call | solution.py:519
  28.9 17.8 %all_to_all.36.parts_ref = f32[8,88,128]{2,1,0:T(8,128)S(1)} all-to-all(f32[8,88,128]{2,1,0:T(8,128)S(1)} %zonal.1), channel_id=1, replica_groups=mesh['yl'=2,'x'=4,'z'=8,'yh'=2,'act'=2] {'z'}, dimensions={0} | all-to-all | bytes 720896 | tf_op jit(solution)/shard_map/all_to_all | solution.py:537
  46.7 0.8 %spread.1 = (f32[16,40,128]{2,1,0:T(8,128)}, f32[16,128]{1,0:T(8,128)S(1)}) custom-call(f32[8,88,128]{2,1,0:T(8,128)S(1)} %all_to_all.36.parts_ref), custom_call_target="tpu_custom_call" | custom-call | tf_op jit(solution)/shard_map/spread/pallas_call | solution.py:538
  47.5 7.2 %all-to-all-start.7 = ((f32[16,40,128]{2,1,0:T(8,128)}), f32[16,40,128]{2,1,0:T(8,128)S(1)}, u32[]{:S(2)}, u32[]{:S(2)}) async-start(f32[16,40,128]{2,1,0:T(8,128)} %get-tuple-element.62), calls=%async_computation.7 | async-start | bytes 655360 | tf_op jit(solution)/shard_map/all_to_all | solution.py:549
  54.7 0.4 place.1
  55.1 3.1 %collective-permute-start.1 = (f32[72,128]{1,0:T(8,128)S(1)}, f32[72,128]{1,0:T(8,128)S(1)}, u32[]{:S(2)}, u32[]{:S(2)}) collective-permute-start(f32[72,128]{1,0:T(8,128)S(1)} %get-tuple-element.61), channel_id=1, source_target_pairs={{0,2},{2,0},{1,3},{3,1},{4,6},{6,4},{5,7},{7,5},{8,10},{10,8},{9,1... | collective-permute-start | bytes 110600 | tf_op jit(solution)/shard_map/ppermute | solution.py:560
  58.2 3.6 %collective-permute-done.1 = f32[72,128]{1,0:T(8,128)S(1)} collective-permute-done((f32[72,128]{1,0:T(8,128)S(1)}, f32[72,128]{1,0:T(8,128)S(1)}, u32[]{:S(2)}, u32[]{:S(2)}) %collective-permute-start.1) | collective-permute-done | bytes 36896 | tf_op jit(solution)/shard_map/ppermute | solution.py:560
  61.8 0.0 collective-permute-start.2
  61.8 0.5 slice.171
  62.9 0.0 collective-permute-done.2
  62.9 0.0 all-to-all-done.7
  62.9 0.0 copy-done.4
  63.0 0.0 copy-done.5
  63.0 0.0 copy-done.6
  63.0 2.7 %conditional.1 = ((f32[32,32,64]{2,1,0:T(8,128)}, f32[32,32]{1,0:T(8,128)}, f32[32,32]{1,0:T(8,128)})) conditional(s32[]{:T(128)} %bitcast.57, (f32[64]{0:T(128)S(1)}, f32[32]{0:T(128)S(1)}, f32[8,512]{1,0:T(8,128)S(1)}, f32[72,128]{1,0:T(8,128)S(1)}, f32[72,128]{1,0:T(8,128)S(1)}, /*index=5*/f32[8,128]{1,0:T(8,128)S(1)}, ...), branch_computations={%region_0.0_spmd, %region_1.10_spmd} | conditional | flops 551126016 | bytes 46937896 | solution.py:585
  63.0 2.7 %update.1 = (f32[32,32,64]{2,1,0:T(8,128)}, f32[32,32]{1,0:T(8,128)}, f32[32,32]{1,0:T(8,128)}) custom-call(f32[8,512]{1,0:T(8,128)S(1)} %get-tuple-element.20.meta_ref, f32[72,128]{1,0:T(8,128)S(1)} %get-tuple-element.30.mine_ref, f32[72,128]{1,0:T(8,128)S(1)} %get-tuple-element.31.theirs_ref, f32[8,128]{1,0:T(8,128)S(1)} %get-tuple-element.32.other_ref, ...), custom_call_target="tpu_custom_call" | custom-call | tf_op jit(solution)/shard_map/cond/branch_0_fun/update/pallas_call | solution.py:564
  (2 shorter events, 0.0 us)
Async XLA Ops:
  1.8 4.9 %collective-permute-start = (f32[8,128]{1,0:T(8,128)S(1)}, f32[8,128]{1,0:T(8,128)S(1)}, u32[]{:S(2)}, u32[]{:S(2)}) collective-permute-start(f32[8,128]{1,0:T(8,128)S(1)} %totals.1), channel_id=1, source_target_pairs={{0,130},{130,0},{2,128},{128,2},{1,131},{131,1},{3,129},{129,3},{4... | collective-permute-start | bytes 12296 | tf_op jit(solution)/shard_map/ppermute | solution.py:485
  7.3 16.5 %all-to-all-start.5 = ((f32[8,8,128]{2,1,0:T(8,128)}), f32[8,8,128]{2,1,0:T(8,128)S(1)}, u32[]{:S(2)}, u32[]{:S(2)}) async-start(f32[8,8,128]{2,1,0:T(8,128)} %broadcast_in_dim.312), calls=%async_computation.5 | async-start | bytes 65536 | tf_op jit(solution)/shard_map/all_to_all | solution.py:518
  23.8 39.2 %copy-start.4 = (s32[32,8]{0,1:T(8,128)S(1)}, s32[32,8]{0,1:T(8,128)}, u32[]{:S(2)}) copy-start(s32[32,8]{0,1:T(8,128)} %param.15) | copy-start | bytes 3076
  23.8 39.2 %copy-start.5 = (f32[64]{0:T(128)S(1)}, f32[64]{0:T(128)}, u32[]{:S(2)}) copy-start(f32[64]{0:T(128)} %param.16) | copy-start | bytes 772
  23.8 39.2 %copy-start.6 = (f32[32]{0:T(128)S(1)}, f32[32]{0:T(128)}, u32[]{:S(2)}) copy-start(f32[32]{0:T(128)} %param.17) | copy-start | bytes 388
  47.5 15.4 %all-to-all-start.7 = ((f32[16,40,128]{2,1,0:T(8,128)}), f32[16,40,128]{2,1,0:T(8,128)S(1)}, u32[]{:S(2)}, u32[]{:S(2)}) async-start(f32[16,40,128]{2,1,0:T(8,128)} %get-tuple-element.62), calls=%async_computation.7 | async-start | bytes 655360 | tf_op jit(solution)/shard_map/all_to_all | solution.py:549
  55.1 6.7 %collective-permute-start.1 = (f32[72,128]{1,0:T(8,128)S(1)}, f32[72,128]{1,0:T(8,128)S(1)}, u32[]{:S(2)}, u32[]{:S(2)}) collective-permute-start(f32[72,128]{1,0:T(8,128)S(1)} %get-tuple-element.61), channel_id=1, source_target_pairs={{0,2},{2,0},{1,3},{3,1},{4,6},{6,4},{5,7},{7,5},{8,10},{10,8},{9,1... | collective-permute-start | bytes 110600 | tf_op jit(solution)/shard_map/ppermute | solution.py:560
  61.8 1.2 %collective-permute-start.2 = (f32[8,128]{1,0:T(8,128)S(1)}, f32[8,128]{1,0:T(8,128)S(1)}, u32[]{:S(2)}, u32[]{:S(2)}) collective-permute-start(f32[8,128]{1,0:T(8,128)S(1)} %slice_add_fusion), channel_id=1, source_target_pairs={{0,1},{1,0},{2,3},{3,2},{4,5},{5,4},{6,7},{7,6},{8,9},{9,8},{10,11... | collective-permute-start | bytes 12296 | tf_op jit(solution)/shard_map/ppermute | solution.py:561

commit v11 on v8

--- a/solution.py
+++ b/solution.py
@@ -235,7 +235,7 @@
 
     acc_ref[...] = jnp.zeros_like(acc_ref)
     pay_ref[:, SUMMED:, :] = held_ref[...]
-    total = jnp.sum(totals_ref[...], axis=0)[0:1]
+    total = jnp.sum(totals_ref[...], axis=0)
     for copy in copies:
         copy.wait()
     of_bus = jnp.take_along_axis(
@@ -373,9 +373,9 @@
         factor = jnp.where(
             lane < HALF, left[:, :, pivot:pivot + 1], left[:, :, HALF + pivot:HALF + pivot + 1]
         )
-        diagonal = factor[:, pivot:pivot + 1]
-        left_now = left[:, pivot:pivot + 1] / diagonal
-        right_now = right[:, pivot:pivot + 1] / diagonal
+        inverse = 1.0 / factor[:, pivot:pivot + 1]
+        left_now = left[:, pivot:pivot + 1] * inverse
+        right_now = right[:, pivot:pivot + 1] * inverse
         left = jnp.where(row_id == pivot, left_now, left - factor * left_now)
         right = jnp.where(row_id == pivot, right_now, right - factor * right_now)
 
@@ -459,7 +459,7 @@
     bus_scratch = [pltpu.VMEM((cols // LANES, LANES), kind) for kind in (f32, i32)]
     totals = pl.pallas_call(
         total_kernel,
-        out_shape=jax.ShapeDtypeStruct((lax.axis_size(BUS), SUB, LANES), f32),
+        out_shape=jax.ShapeDtypeStruct((lax.axis_size(BUS), 1, LANES), f32),
         in_specs=[hbm] * 2,
         out_specs=vmem,
         scratch_shapes=[*bus_scratch, pltpu.SemaphoreType.DMA((2,))],

time: 64.9 us -> 64.9 us (level)
  no operation moved by 1% of the time
where the time goes in v11:
time: 64.9 us; the launch traced here: 64.3 us
  starting transfers between devices  18.4 us (28%)
  blocking collectives  15.5 us (24%)
  Pallas kernels  15.1 us (23%)
  waiting for transfers between devices  13.4 us (21%)
  between operations  1.39 us (2%)
    all_to_all x1, blocking collectives, body(): parts = lax.all_to_all(pay, 'z', 0, 0, tiled=True)  15.5 us
    all_to_all x1, starting transfers between devices, body(): totals = lax.all_to_all(totals, BUS, 0, 0, tiled=True)  11.2 us
    pallas_call x1, Pallas kernels, body(): pl.pallas_call(zonal_kernel, out_shape=jax.ShapeDtypeStruct((n_z, SUMMED...  5.15 us
    pallas_call x1, Pallas kernels, body(): pl.pallas_call(column_kernel, out_shape=(jax.ShapeDtypeStruct((n_z, share...  5.1 us
    all_to_all x1, waiting for transfers between devices, body(): totals = lax.all_to_all(totals, BUS, 0, 0, tiled=True)  4.82 us
    ppermute x3, waiting for transfers between devices, body(): lax.ppermute(here, 'x', [(at, (at + by) % n_x) for at in range(n_x)])  4.01 us
    ppermute x1, starting transfers between devices, body(): theirs = lax.ppermute(jnp.concatenate([block, theirs], axis=0), 'yh', swap)  3.06 us
    ppermute x3, starting transfers between devices, body(): lax.ppermute(here, 'x', [(at, (at + by) % n_x) for at in range(n_x)])  2.99 us
  transfers between devices with their start and end apart: 8, of which 5 were waited for; matrix products, arithmetic and copies ran while one was open for 1% of the time, Pallas kernels for 8%

profile of v11, /device:TPU:6, one launch (start us, length us, event | category | flops | bytes accessed | tf_op | source)
XLA Modules:
  0.0 64.3 jit_solution(15758284648584698973)
XLA Ops:
  0.6 1.7 %totals.1 = f32[16,1,128]{2,1,0:T(1,128)} custom-call(f32[64,128]{1,0:T(8,128)} %bitcast.190, s32[64,128]{1,0:T(8,128)} %bitcast.192), custom_call_target="tpu_custom_call" | custom-call | tf_op jit(solution)/shard_map/totals/pallas_call | solution.py:460
  2.4 11.2 %all-to-all-start.5 = ((f32[16,1,128]{2,1,0:T(1,128)}), f32[16,1,128]{2,1,0:T(1,128)S(1)}, u32[]{:S(2)}, u32[]{:S(2)}) async-start(f32[16,1,128]{2,1,0:T(1,128)} %totals.1), calls=%async_computation.5 | async-start | bytes 16384 | tf_op jit(solution)/shard_map/all_to_all | solution.py:469
  13.6 5.1 %columns.1 = (f32[8,32,128]{2,1,0:T(8,128)S(1)}, f32[8,512]{1,0:T(8,128)S(1)}, f32[72,128]{1,0:T(8,128)S(1)}) custom-call(s32[8,32]{1,0:T(8,128)} %bitcast.213, s32[2,4096]{1,0:T(2,128)} %branch_hbm.1, bf16[512,8192]{1,0:T(8,128)(2,1)} %sens_hbm.3), custom_call_target="tpu_custom_call" | custom-call | tf_op jit(solution)/shard_map/columns/pallas_call | solution.py:471
  18.7 4.8 %all-to-all-done.5.totals_ref = f32[16,1,128]{2,1,0:T(1,128)S(1)} async-done(((f32[16,1,128]{2,1,0:T(1,128)}), f32[16,1,128]{2,1,0:T(1,128)S(1)}, u32[]{:S(2)}, u32[]{:S(2)}) %all-to-all-start.5) | async-done | bytes 8224 | tf_op jit(solution)/shard_map/all_to_all | solution.py:469
  23.5 0.0 copy-start.4
  23.5 0.0 copy-start.5
  23.5 0.0 copy-start.6
  23.5 5.1 %zonal.1 = f32[8,88,128]{2,1,0:T(8,128)S(1)} custom-call(f32[16,1,128]{2,1,0:T(1,128)S(1)} %all-to-all-done.5.totals_ref, f32[64,128]{1,0:T(8,128)} %bitcast.191, s32[64,128]{1,0:T(8,128)} %bitcast.193, bf16[512,8192]{1,0:T(8,128)(2,1)} %sens_hbm.3, f32[8,32,128]{2,1,0:T(8,128)S(1)} %get-tuple-element.66.held_ref, f32[72,128]{1,0:T(8,128)S(1)} %get-tuple-element.67.extra_ref), custom_call_target="tpu_custom_call" | custom-call | tf_op jit(solution)/shard_map/zonal/pallas_call | solution.py:491
  28.7 15.5 %all_to_all.31.parts_ref = f32[8,88,128]{2,1,0:T(8,128)S(1)} all-to-all(f32[8,88,128]{2,1,0:T(8,128)S(1)} %zonal.1), channel_id=1, replica_groups=mesh['yl'=2,'x'=4,'z'=8,'yh'=2,'act'=2] {'z'}, dimensions={0} | all-to-all | bytes 720896 | tf_op jit(solution)/shard_map/all_to_all | solution.py:509
  44.2 0.4 place.1
  44.7 3.1 %collective-permute-start = (f32[112,128]{1,0:T(8,128)S(1)}, f32[112,128]{1,0:T(8,128)S(1)}, u32[]{:S(2)}, u32[]{:S(2)}) collective-permute-start(f32[112,128]{1,0:T(8,128)S(1)} %pad_maximum_fusion.1), channel_id=1, source_target_pairs={{0,2},{2,0},{1,3},{3,1},{4,6},{6,4},{5,7},{7,5},{8,10},{10,8},{9,1... | collective-permute-start | bytes 172040 | tf_op jit(solution)/shard_map/ppermute | solution.py:522
  47.7 0.7 %collective-permute-start.2 = (f32[40,128]{1,0:T(8,128)S(1)}, f32[40,128]{1,0:T(8,128)S(1)}, u32[]{:S(2)}, u32[]{:S(2)}) collective-permute-start(f32[40,128]{1,0:T(8,128)S(1)} %slice.184), channel_id=1, source_target_pairs={{0,128},{128,0},{1,129},{129,1},{2,130},{130,2},{3,131},{131,3},{4... | collective-permute-start | bytes 61448 | tf_op jit(solution)/shard_map/ppermute | solution.py:523
  48.4 0.4 collective-permute-start.3
  48.8 2.7 %collective-permute-done.2 = f32[40,128]{1,0:T(8,128)S(1)} collective-permute-done((f32[40,128]{1,0:T(8,128)S(1)}, f32[40,128]{1,0:T(8,128)S(1)}, u32[]{:S(2)}, u32[]{:S(2)}) %collective-permute-start.2) | collective-permute-done | bytes 20512 | tf_op jit(solution)/shard_map/ppermute | solution.py:523
  51.5 1.9 %collective-permute-done.3 = f32[40,128]{1,0:T(8,128)S(1)} collective-permute-done((f32[40,128]{1,0:T(8,128)S(1)}, f32[40,128]{1,0:T(8,128)S(1)}, u32[]{:S(2)}, u32[]{:S(2)}) %collective-permute-start.3) | collective-permute-done | bytes 20512 | tf_op jit(solution)/shard_map/ppermute | solution.py:524
  53.4 0.0 collective-permute-done
  53.4 0.6 collective-permute-start.4
  54.0 2.4 %collective-permute-start.5 = (f32[80,128]{1,0:T(8,128)S(1)}, f32[80,128]{1,0:T(8,128)S(1)}, u32[]{:S(2)}, u32[]{:S(2)}) collective-permute-start(f32[80,128]{1,0:T(8,128)S(1)} %pad_maximum_fusion.2), channel_id=1, source_target_pairs={{0,64},{32,96},{64,0},{96,32},{1,65},{33,97},{65,1},{97,33},{2,66}... | collective-permute-start | bytes 122888 | tf_op jit(solution)/shard_map/ppermute | solution.py:528
  56.4 0.0 collective-permute-start.6
  56.4 0.0 collective-permute-start.1
  56.4 0.5 slice.132
  57.6 0.0 collective-permute-done.1
  57.6 0.0 collective-permute-done.4
  57.6 1.9 %collective-permute-done.5 = f32[80,128]{1,0:T(8,128)S(1)} collective-permute-done((f32[80,128]{1,0:T(8,128)S(1)}, f32[80,128]{1,0:T(8,128)S(1)}, u32[]{:S(2)}, u32[]{:S(2)}) %collective-permute-start.5) | collective-permute-done | bytes 40992 | tf_op jit(solution)/shard_map/ppermute | solution.py:528
  59.5 2.1 %collective-permute-done.6 = f32[80,128]{1,0:T(8,128)S(1)} collective-permute-done((f32[80,128]{1,0:T(8,128)S(1)}, f32[80,128]{1,0:T(8,128)S(1)}, u32[]{:S(2)}, u32[]{:S(2)}) %collective-permute-start.6) | collective-permute-done | bytes 40992 | tf_op jit(solution)/shard_map/ppermute | solution.py:528
  61.6 0.0 copy-done.4
  61.6 0.0 copy-done.5
  61.6 0.0 copy-done.6
  61.6 2.7 %conditional.1 = ((f32[32,32,64]{2,1,0:T(8,128)}, f32[32,32]{1,0:T(8,128)}, f32[32,32]{1,0:T(8,128)})) conditional(s32[]{:T(128)} %bitcast.57, (f32[64]{0:T(128)S(1)}, f32[32]{0:T(128)S(1)}, f32[8,512]{1,0:T(8,128)S(1)}, f32[72,128]{1,0:T(8,128)S(1)}, f32[112,128]{1,0:T(8,128)S(1)}, /*index=5*/f32[8,128]{1,0:T(8,128)S(1)}, f32[80,128]{1,0:T(8,128)S(1)}, ...), branch_computations={%region_1.0_spmd, %region_2.11_spmd} | conditional | flops 551126016 | bytes 46937896 | solution.py:557
  61.6 2.7 %update.1 = (f32[32,32,64]{2,1,0:T(8,128)}, f32[32,32]{1,0:T(8,128)}, f32[32,32]{1,0:T(8,128)}) custom-call(f32[8,512]{1,0:T(8,128)S(1)} %get-tuple-element.26.meta_ref, f32[72,128]{1,0:T(8,128)S(1)} %get-tuple-element.36.mine_ref, f32[112,128]{1,0:T(8,128)S(1)} %get-tuple-element.37.theirs_ref, f32[8,128]{1,0:T(8,128)S(1)} %get-tuple-element.38.other_ref, ...), custom_call_target="tpu_custom_call" | custom-call | tf_op jit(solution)/shard_map/cond/branch_0_fun/update/pallas_call | solution.py:536
  (7 shorter events, 0.0 us)
Async XLA Ops:
  2.4 21.2 %all-to-all-start.5 = ((f32[16,1,128]{2,1,0:T(1,128)}), f32[16,1,128]{2,1,0:T(1,128)S(1)}, u32[]{:S(2)}, u32[]{:S(2)}) async-start(f32[16,1,128]{2,1,0:T(1,128)} %totals.1), calls=%async_computation.5 | async-start | bytes 16384 | tf_op jit(solution)/shard_map/all_to_all | solution.py:469
  23.5 38.1 %copy-start.4 = (s32[32,8]{0,1:T(8,128)S(1)}, s32[32,8]{0,1:T(8,128)}, u32[]{:S(2)}) copy-start(s32[32,8]{0,1:T(8,128)} %param.15) | copy-start | bytes 3076
  23.5 38.1 %copy-start.5 = (f32[64]{0:T(128)S(1)}, f32[64]{0:T(128)}, u32[]{:S(2)}) copy-start(f32[64]{0:T(128)} %param.16) | copy-start | bytes 772
  23.5 38.1 %copy-start.6 = (f32[32]{0:T(128)S(1)}, f32[32]{0:T(128)}, u32[]{:S(2)}) copy-start(f32[32]{0:T(128)} %param.17) | copy-start | bytes 388
  44.7 8.7 %collective-permute-start = (f32[112,128]{1,0:T(8,128)S(1)}, f32[112,128]{1,0:T(8,128)S(1)}, u32[]{:S(2)}, u32[]{:S(2)}) collective-permute-start(f32[112,128]{1,0:T(8,128)S(1)} %pad_maximum_fusion.1), channel_id=1, source_target_pairs={{0,2},{2,0},{1,3},{3,1},{4,6},{6,4},{5,7},{7,5},{8,10},{10,8},{9,1... | collective-permute-start | bytes 172040 | tf_op jit(solution)/shard_map/ppermute | solution.py:522
  47.7 3.8 %collective-permute-start.2 = (f32[40,128]{1,0:T(8,128)S(1)}, f32[40,128]{1,0:T(8,128)S(1)}, u32[]{:S(2)}, u32[]{:S(2)}) collective-permute-start(f32[40,128]{1,0:T(8,128)S(1)} %slice.184), channel_id=1, source_target_pairs={{0,128},{128,0},{1,129},{129,1},{2,130},{130,2},{3,131},{131,3},{4... | collective-permute-start | bytes 61448 | tf_op jit(solution)/shard_map/ppermute | solution.py:523
  48.4 5.0 %collective-permute-start.3 = (f32[40,128]{1,0:T(8,128)S(1)}, f32[40,128]{1,0:T(8,128)S(1)}, u32[]{:S(2)}, u32[]{:S(2)}) collective-permute-start(f32[40,128]{1,0:T(8,128)S(1)} %slice.184), channel_id=1, source_target_pairs={{0,130},{130,0},{2,128},{128,2},{1,131},{131,1},{3,129},{129,3},{4... | collective-permute-start | bytes 61448 | tf_op jit(solution)/shard_map/ppermute | solution.py:524
  53.4 4.2 %collective-permute-start.4 = (f32[80,128]{1,0:T(8,128)S(1)}, f32[80,128]{1,0:T(8,128)S(1)}, u32[]{:S(2)}, u32[]{:S(2)}) collective-permute-start(f32[80,128]{1,0:T(8,128)S(1)} %pad_maximum_fusion.2), channel_id=1, source_target_pairs={{0,32},{32,64},{64,96},{96,0},{1,33},{33,65},{65,97},{97,1},{2,34}... | collective-permute-start | bytes 122888 | tf_op jit(solution)/shard_map/ppermute | solution.py:528
  54.0 5.5 %collective-permute-start.5 = (f32[80,128]{1,0:T(8,128)S(1)}, f32[80,128]{1,0:T(8,128)S(1)}, u32[]{:S(2)}, u32[]{:S(2)}) collective-permute-start(f32[80,128]{1,0:T(8,128)S(1)} %pad_maximum_fusion.2), channel_id=1, source_target_pairs={{0,64},{32,96},{64,0},{96,32},{1,65},{33,97},{65,1},{97,33},{2,66}... | collective-permute-start | bytes 122888 | tf_op jit(solution)/shard_map/ppermute | solution.py:528
  56.4 5.2 %collective-permute-start.6 = (f32[80,128]{1,0:T(8,128)S(1)}, f32[80,128]{1,0:T(8,128)S(1)}, u32[]{:S(2)}, u32[]{:S(2)}) collective-permute-start(f32[80,128]{1,0:T(8,128)S(1)} %pad_maximum_fusion.2), channel_id=1, source_target_pairs={{0,96},{32,0},{64,32},{96,64},{1,97},{33,1},{65,33},{97,65},{2,98}... | collective-permute-start | bytes 122888 | tf_op jit(solution)/shard_map/ppermute | solution.py:528
  56.4 1.2 %collective-permute-start.1 = (f32[8,128]{1,0:T(8,128)S(1)}, f32[8,128]{1,0:T(8,128)S(1)}, u32[]{:S(2)}, u32[]{:S(2)}) collective-permute-start(f32[8,128]{1,0:T(8,128)S(1)} %slice_add_fusion.1), channel_id=1, source_target_pairs={{0,1},{1,0},{2,3},{3,2},{4,5},{5,4},{6,7},{7,6},{8,9},{9,8},{10,11... | collective-permute-start | bytes 12296 | tf_op jit(solution)/shard_map/ppermute | solution.py:531

commit v12 on v9

--- a/solution.py
+++ b/solution.py
@@ -13,6 +13,7 @@
 BLOCK = 2048
 SLOTS = 64
 BLOCK_ROWS = SLOTS // 2 + SUB
+SUMMED = 2 * SUB + BLOCK_ROWS
 CNEC, BUS = ("yl", "x"), ("z", "yh")
 
 
@@ -93,12 +94,13 @@
     total = jnp.sum(total, axis=1, keepdims=True)
     eye = ids + HALF == iota((HALF, LANES), 1)
     total = jnp.sum(jnp.where(eye, total, 0.0), axis=0, keepdims=True)
-    out_ref[...] = jnp.broadcast_to(total, out_ref.shape)
+    out_ref[...] = jnp.where(iota(out_ref.shape, 0) == 0, total, 0.0)
 
 
 def column_kernel(
-    swt_hbm, branch_hbm, sens_hbm, held_ref, meta_ref, extra_ref, sens_ref,
-    swt_ref, branch_ref, acc_ref, coupled_ref, sems
+    swt_hbm, branch_hbm, weight_hbm, zone_hbm, sens_hbm, pay_ref, meta_ref, extra_ref,
+    swt_ref, branch_ref, weight_ref, zone_ref, sens_ref, rank_ref, chosen_ref, acc_ref,
+    coupled_ref, sems
 ):
     rows, cols = sens_ref.shape
     rank, actions = swt_ref.shape
@@ -106,8 +108,10 @@
     steps = cols // BLOCK
     bf16 = jnp.bfloat16
     small = [
-        pltpu.make_async_copy(swt_hbm, swt_ref, sems.at[steps]),
-        pltpu.make_async_copy(branch_hbm, branch_ref, sems.at[steps + 1]),
+        pltpu.make_async_copy(source, target, sems.at[steps + at])
+        for at, (source, target) in enumerate(
+            [(swt_hbm, swt_ref), (branch_hbm, branch_ref), (weight_hbm, weight_ref), (zone_hbm, zone_ref)]
+        )
     ]
     for copy in small:
         copy.start()
@@ -164,7 +168,33 @@
     action_of = iota((SLOTS, picks), 1) // rank
     slot_action = jnp.where(match, action_of.astype(jnp.float32), 0.0)
     slot_action = jnp.sum(slot_action, axis=1, keepdims=True).astype(jnp.int32)
-    extra_ref[0:SLOTS, :] = jnp.broadcast_to(slot_row, (SLOTS, LANES))
+
+    weight = weight_ref[...]
+    positive = weight > 0.0
+    ones = jnp.where(positive, 1.0, 0.0).astype(bf16)
+    lines = weight.shape[0]
+    before = jnp.where(iota((LANES, LANES), 0) < iota((LANES, LANES), 1), 1.0, 0.0).astype(bf16)
+    above = jnp.where(iota((lines, lines), 1) < iota((lines, lines), 0), 1.0, 0.0).astype(bf16)
+    place = dot(ones, before) + jnp.sum(dot(above, ones), axis=1, keepdims=True)
+    rank_ref[...] = jnp.where(positive, place, -1.0)
+    most = jnp.max(jnp.max(rank_ref[...], axis=0, keepdims=True), axis=1, keepdims=True)
+    over = over + jnp.where(most >= SLOTS, 1.0, 0.0)
+    ids = iota((SLOTS, LANES), 0)
+    slot_id = ids.astype(jnp.float32)
+    slot_weight = jnp.zeros((SLOTS, LANES), jnp.float32)
+    slot_zone = jnp.zeros((SLOTS, LANES), jnp.float32)
+    for at in range(lines):
+        match = rank_ref[at:at + 1, :] == slot_id
+        slot_weight += jnp.where(match, weight_ref[at:at + 1, :], 0.0)
+        slot_zone += jnp.where(match, zone_ref[at:at + 1, :].astype(jnp.float32), 0.0)
+        chosen_ref[:, at * LANES:(at + 1) * LANES] = jnp.where(match, 1.0, 0.0).astype(bf16)
+    eye = ids + HALF == iota((SLOTS, LANES), 1)
+    slot_weight, slot_zone = [
+        jnp.sum(
+            jnp.where(eye, jnp.sum(x, axis=1, keepdims=True), 0.0), axis=0, keepdims=True
+        )
+        for x in (slot_weight, slot_zone)
+    ]
     choose = iota((SLOTS, rows), 1) == slot_row.astype(jnp.int32)
     choose = jnp.where(choose, 1.0, 0.0).astype(bf16)
     lane = iota((SLOTS, BLOCK), 1)
@@ -174,7 +204,7 @@
 
     def step_body(step, carry):
         at = pl.ds(pl.multiple_of(step * BLOCK, BLOCK), BLOCK)
-        chosen = select(first_buses, step)
+        chosen = jnp.concatenate([select(first_buses, step), chosen_ref[:, at]], axis=0)
         block_copy(step).wait()
         acc_ref[...] += dot_nt(sens_ref[:, at], chosen)
         return carry
@@ -186,7 +216,7 @@
         chosen = dot(choose, columns.astype(bf16))
         return dot(chosen.astype(bf16), slot_matrix(slots, SLOTS))
 
-    columns = acc_ref[...]
+    columns = acc_ref[:, 0:SLOTS]
     coupled_ref[...] = coupled_of(columns, 0)
 
     def group_body(group, carry):
@@ -206,63 +236,70 @@
     high, low = [dot(part, fold.astype(bf16)) for part in two_parts(coupled)]
     shape = (SLOTS, LANES)
     coupled = jnp.where(iota(shape, 1) // rank == iota(shape, 0) // SUB, high + low, 0.0)
-    extra_ref[SLOTS:, :] = jnp.sum(coupled.reshape(SLOTS // SUB, SUB, LANES), axis=0)
-    chunks = held_ref.shape[0]
-    columns = columns.reshape(chunks, 2, rows // chunks // 2, SLOTS)
-    held_ref[...] = jnp.concatenate([columns[:, 0], columns[:, 1]], axis=-1)
-
-
-def zonal_kernel(parts_ref, weight_hbm, zone_hbm, sens_ref, extra_ref, pay_ref, coupled_ref,
-                 weight_ref, zone_ref, key_ref, sums_ref, acc_ref, sems):
-    rows, cols = sens_ref.shape
-    zones = HALF
-    bf16 = jnp.bfloat16
-    copies = [
-        pltpu.make_async_copy(weight_hbm, weight_ref, sems.at[0]),
-        pltpu.make_async_copy(zone_hbm, zone_ref, sems.at[1]),
-    ]
-    for copy in copies:
-        copy.start()
-    acc_ref[...] = jnp.zeros_like(acc_ref)
-    coupled = jnp.sum(parts_ref[:, SLOTS // 2:, :], axis=0)
-    coupled_ref[...] = coupled
-    for copy in copies:
-        copy.wait()
-    of_bus = jnp.take_along_axis(
-        jnp.broadcast_to(coupled[0:1], weight_ref.shape), zone_ref[...] + HALF, axis=1
-    )
-    sums_ref[...] = weight_ref[...] / of_bus
-    ids = iota((zones, LANES), 0)
-    for at in range(cols // LANES):
-        key = jnp.where(zone_ref[at:at + 1, :] == ids, sums_ref[at:at + 1, :], 0.0)
-        key_ref[:, at * LANES:(at + 1) * LANES] = key.astype(bf16)
-
-    def step_body(step, carry):
-        at = pl.ds(pl.multiple_of(step * BLOCK, BLOCK), BLOCK)
-        acc_ref[...] += dot_nt(sens_ref[:, at], key_ref[:, at])
-        return carry
-
-    lax.fori_loop(0, cols // BLOCK, step_body, 0)
+    coupled = jnp.sum(coupled.reshape(SLOTS // SUB, SUB, LANES), axis=0)
+    line = iota(coupled.shape, 0)
+    over = jnp.where(iota(coupled.shape, 1) < HALF, 0.0, over)
+    for at, values in ((1, slot_weight), (2, slot_zone), (3, over)):
+        coupled = coupled + jnp.where(line == at, values, 0.0)
+    extra_ref[...] = coupled
 
     chunks = pay_ref.shape[0]
-    zonal = acc_ref[...]
-    choose = iota((SLOTS, rows), 1) == extra_ref[0:SLOTS, 0:1].astype(jnp.int32)
-    choose = jnp.where(choose, 1.0, 0.0).astype(bf16)
-    switched = dot(choose, jnp.concatenate(two_parts(zonal), axis=1))
-    switched = switched[:, 0:zones] + switched[:, zones:]
-    share = zonal.reshape(chunks, 2, 2, 2, SUB, zones)
+    weighted = acc_ref[:, SLOTS:]
+    share = weighted.reshape(chunks, 2, 2, 2, SUB, SLOTS)
     share = jnp.where(lax.axis_index("act") == 0, share[:, :, 0], share[:, :, 1])
     share = jnp.concatenate([share[:, :, 0], share[:, :, 1]], axis=-1)
     half = SLOTS // 2
+    switched = dot(choose, weighted.astype(bf16))
     switched = jnp.concatenate([switched[:half], switched[half:]], axis=1)
     pay_ref[:, 0:2 * SUB, :] = share.reshape(chunks, 2 * SUB, LANES)
-    pay_ref[:, 2 * SUB:, :] = jnp.broadcast_to(switched[None], (chunks, half, LANES))
-
-
-def place_kernel(parts_ref, local_ref, meta_ref, mine_ref, theirs_ref):
+    pay_ref[:, 2 * SUB:2 * SUB + half, :] = jnp.broadcast_to(switched[None], (chunks, half, LANES))
+    pay_ref[:, 2 * SUB + half:SUMMED, :] = jnp.broadcast_to(coupled[None], (chunks, SUB, LANES))
+    columns = columns.reshape(chunks, 2, rows // chunks // 2, SLOTS)
+    pay_ref[:, SUMMED:, :] = jnp.concatenate([columns[:, 0], columns[:, 1]], axis=-1)
+
+
+def place_kernel(parts_ref, meta_ref, mine_ref, send_ref, block_ref):
     chunks = parts_ref.shape[0]
+    start = SUMMED - SUB
+    extra = jnp.sum(parts_ref[:, start:SUMMED, :], axis=0)
+    slot_weight, slot_zone = [
+        jnp.concatenate([parts_ref[z, start + at:start + at + 1, :] for z in range(chunks)], axis=0)
+        for at in (1, 2)
+    ]
+    upper = iota(slot_zone.shape, 1) >= HALF
+    slot_zone = jnp.where(upper, slot_zone, 0.0)
+    of_slot = jnp.take_along_axis(
+        jnp.broadcast_to(extra[0:1], slot_zone.shape), slot_zone.astype(jnp.int32) + HALF, axis=1
+    )
+    key = (jnp.where(upper, slot_weight, 0.0) / of_slot).astype(jnp.bfloat16).astype(jnp.float32)
+    key, slot_zone = [
+        jnp.concatenate([x[z:z + 1, HALF:] for z in range(chunks)], axis=1)
+        for x in (key, slot_zone)
+    ]
+    zone_id = iota((HALF, chunks * SLOTS), 0).astype(jnp.float32)
+    key = jnp.where(slot_zone == zone_id, key, 0.0).astype(jnp.bfloat16)
+
+    def across(first, count, lanes):
+        lanes = slice(lanes * SLOTS, (lanes + 1) * SLOTS)
+        return jnp.concatenate(
+            [parts_ref[z, first:first + count, lanes] for z in range(chunks)], axis=1
+        )
+
+    rows = SLOTS // 2
+    left = [across(at * SUB, SUB, side) for at in (0, 1) for side in (0, 1)]
+    left += [across(2 * SUB, rows, side) for side in (0, 1)]
+    zonal = dot_nt(jnp.concatenate(left, axis=0).astype(jnp.bfloat16), key)
+    zonal, switched = zonal[0:4 * SUB], zonal[4 * SUB:]
+    zonal = [
+        jnp.concatenate([zonal[at:at + SUB], zonal[at + SUB:at + 2 * SUB]], axis=1)
+        for at in (0, 2 * SUB)
+    ]
+    block_ref[0:rows, :] = jnp.concatenate([switched[:rows], switched[rows:]], axis=1)
+    block_ref[rows:, :] = extra
+    send_ref[0:BLOCK_ROWS, :] = block_ref[...]
+
     picks = meta_ref.shape[1] // 2
-    half = parts_ref.shape[1] - SUB
+    half = parts_ref.shape[1] - SUMMED
     y_here, y_size = lax.axis_index("yh"), lax.axis_size("yh")
     held = meta_ref[0:1, :].astype(jnp.int32)
     place = meta_ref[1:2, :].astype(jnp.int32)
@@ -271,7 +308,7 @@
     spread = slot_matrix([slot[:, at * picks:(at + 1) * picks] for at in (0, 1)], chunks * SLOTS)
     columns = [
         jnp.concatenate(
-            [parts_ref[z, 0:half, at * SLOTS:(at + 1) * SLOTS] for z in range(chunks)], axis=1
+            [parts_ref[z, SUMMED:, at * SLOTS:(at + 1) * SLOTS] for z in range(chunks)], axis=1
         )
         for at in (0, 1)
     ]
@@ -286,9 +323,9 @@
         jnp.concatenate([diff[g, :, at * half:(at + 1) * half] for g in range(4)], axis=1)
         for at in (0, 1)
     ]
-    for ref, first in ((mine_ref, lower), (theirs_ref, ~lower)):
-        ref[0:SUB, :] = jnp.where(first, local_ref[0:SUB, :], local_ref[SUB:2 * SUB, :])
-        ref[SUB:, :] = jnp.where(first, packed[0], packed[1])
+    for ref, at, first in ((mine_ref, 0, lower), (send_ref, BLOCK_ROWS, ~lower)):
+        ref[at:at + SUB, :] = jnp.where(first, zonal[0], zonal[1])
+        ref[at + SUB:, :] = jnp.where(first, packed[0], packed[1])
 
 
 def copy_kernel(*refs):
@@ -445,8 +482,6 @@
     weight, zone = [x.reshape(cols // LANES, LANES) for x in (shift_weight, bus_zone)]
     weight, zone = in_hbm(weight), in_hbm(zone)
     bus_scratch = [pltpu.VMEM((cols // LANES, LANES), kind) for kind in (f32, i32)]
-    swap = [(0, 1), (1, 0)]
-    turn = [(0, 3), (3, 0), (1, 2), (2, 1)]
     totals = pl.pallas_call(
         total_kernel,
         out_shape=jax.ShapeDtypeStruct((SUB, LANES), f32),
@@ -456,61 +491,50 @@
         compiler_params=params(),
         name="totals",
     )(weight, zone)
+    swap = [(0, 1), (1, 0)]
+    turn = [(0, 3), (3, 0), (1, 2), (2, 1)]
     totals = totals + lax.ppermute(totals, ("yl", "yh"), turn)
-    held, meta, extra, sens = pl.pallas_call(
+    pay, meta, extra = pl.pallas_call(
         column_kernel,
         out_shape=(
-            jax.ShapeDtypeStruct((n_z, share, LANES), f32),
+            jax.ShapeDtypeStruct((n_z, SUMMED + share, LANES), f32),
             jax.ShapeDtypeStruct((SUB, 2 * picks), f32),
-            jax.ShapeDtypeStruct((SLOTS + SUB, LANES), f32),
-            pltpu.VMEM((rows, cols), jnp.bfloat16),
+            jax.ShapeDtypeStruct((SUB, LANES), f32),
         ),
-        in_specs=[hbm] * 3,
-        out_specs=(vmem,) * 4,
+        in_specs=[hbm] * 5,
+        out_specs=(vmem,) * 3,
         scratch_shapes=[
             pltpu.VMEM((rank, actions), i32),
             pltpu.VMEM(branch_buses.shape, i32),
-            pltpu.VMEM((rows, SLOTS), f32),
+            *bus_scratch,
+            pltpu.VMEM((rows, cols), jnp.bfloat16),
+            pltpu.VMEM((cols // LANES, LANES), f32),
+            pltpu.VMEM((SLOTS, cols), jnp.bfloat16),
+            pltpu.VMEM((rows, 2 * SLOTS), f32),
             pltpu.VMEM((SLOTS, picks), f32),
-            pltpu.SemaphoreType.DMA((cols // BLOCK + 2,)),
+            pltpu.SemaphoreType.DMA((cols // BLOCK + 4,)),
         ],
         compiler_params=params(),
         name="columns",
-    )(*[in_hbm(x) for x in (switched_rows.T, branch_buses, nodal_sensitivity)])
-    coupled = jnp.broadcast_to((extra[SLOTS:] + totals)[None], (n_z, SUB, LANES))
-    parts = jnp.concatenate([held, coupled], axis=1)
-    parts = lax.all_to_all(parts, "z", 0, 0, tiled=True)
-    pay, coupled = pl.pallas_call(
-        zonal_kernel,
-        out_shape=(
-            jax.ShapeDtypeStruct((n_z, 2 * SUB + SLOTS // 2, LANES), f32),
-            jax.ShapeDtypeStruct((SUB, LANES), f32),
-        ),
-        in_specs=[vmem, hbm, hbm, vmem, vmem],
-        out_specs=(vmem, vmem),
-        scratch_shapes=[
-            *bus_scratch,
-            pltpu.VMEM((zones, cols), jnp.bfloat16),
-            pltpu.VMEM((cols // LANES, LANES), f32),
-            pltpu.VMEM((rows, zones), f32),
-            pltpu.SemaphoreType.DMA((2,)),
+    )(
+        in_hbm(switched_rows.T), in_hbm(branch_buses), weight, zone, in_hbm(nodal_sensitivity)
+    )
+    extra = jnp.broadcast_to((extra + totals)[None], (n_z, SUB, LANES))
+    pay = lax.dynamic_update_slice(pay, extra, (0, SUMMED - SUB, 0))
+    parts = lax.all_to_all(pay, "z", 0, 0, tiled=True)
+    mine, send, block = pl.pallas_call(
+        place_kernel,
+        out_shape=[
+            jax.ShapeDtypeStruct((count, LANES), f32)
+            for count in (SUB + 2 * share, BLOCK_ROWS + SUB + 2 * share, BLOCK_ROWS)
         ],
-        compiler_params=params(),
-        name="zonal",
-    )(parts, weight, zone, pltpu.with_memory_space_constraint(sens, pltpu.VMEM), extra)
-    local = jnp.sum(lax.all_to_all(pay, "z", 0, 0, tiled=True), axis=0)
-    part = jax.ShapeDtypeStruct((SUB + 2 * share, LANES), f32)
-    mine, theirs = pl.pallas_call(
-        place_kernel,
-        out_shape=(part, part),
-        in_specs=[vmem] * 3,
-        out_specs=(vmem, vmem),
+        in_specs=[vmem] * 2,
+        out_specs=[vmem] * 3,
         compiler_params=params(),
         name="place",
-    )(parts, local, meta)
-
-    block = jnp.concatenate([local[2 * SUB:], coupled], axis=0)
-    theirs = lax.ppermute(jnp.concatenate([block, theirs], axis=0), "yh", swap)
+    )(parts, meta)
+
+    theirs = lax.ppermute(send, "yh", swap)
     beside = lax.ppermute(block, "yl", swap)
     across = lax.ppermute(block, ("yl", "yh"), turn)
     here = jnp.concatenate([block + theirs[:BLOCK_ROWS], beside + across], axis=0)
@@ -545,7 +569,7 @@
         inputs = nodal_sensitivity, shift_weight, bus_zone, branch_buses, switched_rows
         return tuple(copied(plain(*copied(inputs), net_position, flow_limit)))
 
-    return lax.cond(meta[2, 0] > 0.5, general, compact)
+    return lax.cond(here[SLOTS // 2 + 3, HALF] > 0.5, general, compact)
 
 
 def sum_over(x, axes):

time: 73.5 us -> 51.2 us (0.70)
  blocking collectives: 30.9 us -> 22 us
  waiting for transfers between devices: 12.9 us -> 6.01 us
  Pallas kernels: 15.9 us -> 10.4 us
  other arithmetic: 3.01 us -> 0.02 us
  starting transfers between devices: 7.99 us -> 10.3 us
    all_to_all x2 -> x1, blocking collectives: 30.9 us -> 22 us  [body(): parts = lax.all_to_all(pay, 'z', 0, 0, tiled=True)]
    pallas_call x3 -> x2, Pallas kernels: 12.1 us -> 6.6 us  [the longest x1 6.09 us: body(): pl.pallas_call(column_kernel, out_shape=(jax.ShapeDtypeStruct((n_z, SUMME...]
    ppermute x1, waiting for transfers between devices: 5.05 us -> 0.01 us  [body(): theirs = lax.ppermute(send, 'yh', swap)]
    ppermute x1, waiting for transfers between devices: 2.5 us -> 0.32 us  [body(): beside = lax.ppermute(block, 'yl', swap)]
    ppermute x1, starting transfers between devices: 1.14 us -> 2.94 us  [body(): across = lax.ppermute(block, ('yl', 'yh'), turn)]
    concatenate x2 -> x0, other arithmetic: 1.61 us -> none  [the longest x1 0.92 us: body(): parts = jnp.concatenate([held, coupled], axis=1)]
  transfers between devices with their start and end apart: 8 -> 8, of which waited for: 5 -> 4; matrix products, arithmetic and copies ran while one was open for 1% -> 1% of each run, Pallas kernels for 8% -> 12%
where the time goes in v12:
time: 51.2 us; the launch traced here: 50.7 us
  blocking collectives  22 us (43%)
  Pallas kernels  10.4 us (20%)
  starting transfers between devices  10.3 us (20%)
  waiting for transfers between devices  6.01 us (12%)
  between operations  1.38 us (3%)
  local copies, waits for them, and re-layouts  0.6 us (1%)
    all_to_all x1, blocking collectives, body(): parts = lax.all_to_all(pay, 'z', 0, 0, tiled=True)  22 us
    pallas_call x1, Pallas kernels, body(): pl.pallas_call(column_kernel, out_shape=(jax.ShapeDtypeStruct((n_z, SUMME...  6.09 us
    ppermute x3, waiting for transfers between devices, body(): lax.ppermute(here, 'x', [(at, (at + by) % n_x) for at in range(n_x)])  3.95 us
    ppermute x1, starting transfers between devices, body(): totals = totals + lax.ppermute(totals, ('yl', 'yh'), turn)  3.1 us
    ppermute x3, starting transfers between devices, body(): lax.ppermute(here, 'x', [(at, (at + by) % n_x) for at in range(n_x)])  2.98 us
    ppermute x1, starting transfers between devices, body(): across = lax.ppermute(block, ('yl', 'yh'), turn)  2.94 us
    pallas_call x1, Pallas kernels, compact(): pl.pallas_call(final_kernel, out_shape=(jax.ShapeDtypeStruct((actions, sh...  2.69 us
    ppermute x1, waiting for transfers between devices, body(): across = lax.ppermute(block, ('yl', 'yh'), turn)  1.73 us
  transfers between devices with their start and end apart: 8, of which 4 were waited for; matrix products, arithmetic and copies ran while one was open for 1% of the time, Pallas kernels for 12%

profile of v12, /device:TPU:6, one launch (start us, length us, event | category | flops | bytes accessed | tf_op | source)
XLA Modules:
  0.0 50.7 jit_solution(18418092007737803788)
XLA Ops:
  0.6 1.1 %totals.1 = f32[8,128]{1,0:T(8,128)S(1)} custom-call(f32[64,128]{1,0:T(8,128)} %bitcast.190, s32[64,128]{1,0:T(8,128)} %bitcast.192), custom_call_target="tpu_custom_call" | custom-call | tf_op jit(solution)/shard_map/totals/pallas_call | solution.py:485
  1.8 3.1 %collective-permute-start = (f32[8,128]{1,0:T(8,128)S(1)}, f32[8,128]{1,0:T(8,128)S(1)}, u32[]{:S(2)}, u32[]{:S(2)}) collective-permute-start(f32[8,128]{1,0:T(8,128)S(1)} %totals.1), channel_id=1, source_target_pairs={{0,130},{130,0},{2,128},{128,2},{1,131},{131,1},{3,129},{129,3},{4... | collective-permute-start | bytes 12296 | tf_op jit(solution)/shard_map/ppermute | solution.py:496
  4.9 0.0 copy-start.4
  4.9 0.0 copy-start.5
  4.9 0.0 copy-start.6
  4.9 6.1 %columns.1 = (f32[8,88,128]{2,1,0:T(8,128)S(1)}, f32[8,512]{1,0:T(8,128)S(1)}, f32[8,128]{1,0:T(8,128)S(1)}) custom-call(s32[8,32]{1,0:T(8,128)} %bitcast.213, s32[2,4096]{1,0:T(2,128)} %branch_hbm.1, f32[64,128]{1,0:T(8,128)} %bitcast.191, s32[64,128]{1,0:T(8,128)} %bitcast.193, bf16[512,8192]{1,0:T(8,128)(2,1)} %sens_hbm.1), custom_call_target="tpu_custom_call" | custom-call | tf_op jit(solution)/shard_map/columns/pallas_call | solution.py:497
  11.0 0.0 collective-permute-done
  11.0 22.0 %all_to_all.26.parts_ref = f32[8,88,128]{2,1,0:T(8,128)S(1)} all-to-all(f32[8,88,128]{2,1,0:T(8,128)S(1)} %broadcast_dynamic-update-slice_fusion), channel_id=1, replica_groups=mesh['yl'=2,'x'=4,'z'=8,'yh'=2,'act'=2] {'z'}, dimensions={0} | all-to-all | bytes 720896 | tf_op jit(solution)/shard_map/all_to_all | solution.py:524
  33.0 0.5 %place.1 = (f32[72,128]{1,0:T(8,128)S(1)}, f32[112,128]{1,0:T(8,128)S(1)}, f32[40,128]{1,0:T(8,128)S(1)}) custom-call(f32[8,88,128]{2,1,0:T(8,128)S(1)} %all_to_all.26.parts_ref, f32[8,512]{1,0:T(8,128)S(1)} %get-tuple-element.68.meta_ref), custom_call_target="tpu_custom_call" | custom-call | tf_op jit(solution)/shard_map/place/pallas_call | solution.py:525
  33.5 0.7 %collective-permute-start.1 = (f32[112,128]{1,0:T(8,128)S(1)}, f32[112,128]{1,0:T(8,128)S(1)}, u32[]{:S(2)}, u32[]{:S(2)}) collective-permute-start(f32[112,128]{1,0:T(8,128)S(1)} %get-tuple-element.70), channel_id=1, source_target_pairs={{0,2},{2,0},{1,3},{3,1},{4,6},{6,4},{5,7},{7,5},{8,10},{10,8},{9,1... | collective-permute-start | bytes 172040 | tf_op jit(solution)/shard_map/ppermute | solution.py:537
  34.2 0.5 %collective-permute-start.3 = (f32[40,128]{1,0:T(8,128)S(1)}, f32[40,128]{1,0:T(8,128)S(1)}, u32[]{:S(2)}, u32[]{:S(2)}) collective-permute-start(f32[40,128]{1,0:T(8,128)S(1)} %get-tuple-element.69), channel_id=1, source_target_pairs={{0,128},{128,0},{1,129},{129,1},{2,130},{130,2},{3,131},{131,3},{4... | collective-permute-start | bytes 61448 | tf_op jit(solution)/shard_map/ppermute | solution.py:538
  34.7 2.9 %collective-permute-start.4 = (f32[40,128]{1,0:T(8,128)S(1)}, f32[40,128]{1,0:T(8,128)S(1)}, u32[]{:S(2)}, u32[]{:S(2)}) collective-permute-start(f32[40,128]{1,0:T(8,128)S(1)} %get-tuple-element.69), channel_id=1, source_target_pairs={{0,130},{130,0},{2,128},{128,2},{1,131},{131,1},{3,129},{129,3},{4... | collective-permute-start | bytes 61448 | tf_op jit(solution)/shard_map/ppermute | solution.py:539
  37.7 0.3 collective-permute-done.3
  38.0 1.7 %collective-permute-done.4 = f32[40,128]{1,0:T(8,128)S(1)} collective-permute-done((f32[40,128]{1,0:T(8,128)S(1)}, f32[40,128]{1,0:T(8,128)S(1)}, u32[]{:S(2)}, u32[]{:S(2)}) %collective-permute-start.4) | collective-permute-done | bytes 20512 | tf_op jit(solution)/shard_map/ppermute | solution.py:539
  39.7 0.0 collective-permute-done.1
  39.8 0.6 %collective-permute-start.5 = (f32[80,128]{1,0:T(8,128)S(1)}, f32[80,128]{1,0:T(8,128)S(1)}, u32[]{:S(2)}, u32[]{:S(2)}) collective-permute-start(f32[80,128]{1,0:T(8,128)S(1)} %pad_maximum_fusion.1), channel_id=1, source_target_pairs={{0,32},{32,64},{64,96},{96,0},{1,33},{33,65},{65,97},{97,1},{2,34}... | collective-permute-start | bytes 122888 | tf_op jit(solution)/shard_map/ppermute | solution.py:543
  40.3 2.4 %collective-permute-start.6 = (f32[80,128]{1,0:T(8,128)S(1)}, f32[80,128]{1,0:T(8,128)S(1)}, u32[]{:S(2)}, u32[]{:S(2)}) collective-permute-start(f32[80,128]{1,0:T(8,128)S(1)} %pad_maximum_fusion.1), channel_id=1, source_target_pairs={{0,64},{32,96},{64,0},{96,32},{1,65},{33,97},{65,1},{97,33},{2,66}... | collective-permute-start | bytes 122888 | tf_op jit(solution)/shard_map/ppermute | solution.py:543
  42.7 0.0 collective-permute-start.7
  42.7 0.0 collective-permute-start.2
  42.7 0.6 %slice.176 = f32[1,1]{1,0:T(1,128)} slice(f32[40,128]{1,0:T(8,128)S(1)} %slice_add_fusion), slice={[35:36], [64:65]} | slice | bytes 8 | tf_op jit(solution)/shard_map/slice | solution.py:572
  44.0 0.0 collective-permute-done.2
  44.0 0.0 collective-permute-done.5
  44.0 1.8 %collective-permute-done.6 = f32[80,128]{1,0:T(8,128)S(1)} collective-permute-done((f32[80,128]{1,0:T(8,128)S(1)}, f32[80,128]{1,0:T(8,128)S(1)}, u32[]{:S(2)}, u32[]{:S(2)}) %collective-permute-start.6) | collective-permute-done | bytes 40992 | tf_op jit(solution)/shard_map/ppermute | solution.py:543
  45.8 2.1 %collective-permute-done.7 = f32[80,128]{1,0:T(8,128)S(1)} collective-permute-done((f32[80,128]{1,0:T(8,128)S(1)}, f32[80,128]{1,0:T(8,128)S(1)}, u32[]{:S(2)}, u32[]{:S(2)}) %collective-permute-start.7) | collective-permute-done | bytes 40992 | tf_op jit(solution)/shard_map/ppermute | solution.py:543
  48.0 0.0 copy-done.4
  48.0 0.0 copy-done.5
  48.0 0.0 copy-done.6
  48.0 2.7 %conditional.1 = ((f32[32,32,64]{2,1,0:T(8,128)}, f32[32,32]{1,0:T(8,128)}, f32[32,32]{1,0:T(8,128)})) conditional(s32[]{:T(128)} %bitcast.59, (f32[64]{0:T(128)S(1)}, f32[32]{0:T(128)S(1)}, f32[8,512]{1,0:T(8,128)S(1)}, f32[72,128]{1,0:T(8,128)S(1)}, f32[112,128]{1,0:T(8,128)S(1)}, /*index=5*/f32[8,128]{1,0:T(8,128)S(1)}, f32[80,128]{1,0:T(8,128)S(1)}, ...), branch_computations={%region_0.0_spmd, %region_1.10_spmd} | conditional | flops 551126016 | bytes 46937896 | solution.py:572
  48.0 2.7 %update.1 = (f32[32,32,64]{2,1,0:T(8,128)}, f32[32,32]{1,0:T(8,128)}, f32[32,32]{1,0:T(8,128)}) custom-call(f32[8,512]{1,0:T(8,128)S(1)} %get-tuple-element.26.meta_ref, f32[72,128]{1,0:T(8,128)S(1)} %get-tuple-element.36.mine_ref, f32[112,128]{1,0:T(8,128)S(1)} %get-tuple-element.37.theirs_ref, f32[8,128]{1,0:T(8,128)S(1)} %get-tuple-element.38.other_ref, ...), custom_call_target="tpu_custom_call" | custom-call | tf_op jit(solution)/shard_map/cond/branch_0_fun/update/pallas_call | solution.py:551
  (6 shorter events, 0.0 us)
Async XLA Ops:
  1.8 9.2 %collective-permute-start = (f32[8,128]{1,0:T(8,128)S(1)}, f32[8,128]{1,0:T(8,128)S(1)}, u32[]{:S(2)}, u32[]{:S(2)}) collective-permute-start(f32[8,128]{1,0:T(8,128)S(1)} %totals.1), channel_id=1, source_target_pairs={{0,130},{130,0},{2,128},{128,2},{1,131},{131,1},{3,129},{129,3},{4... | collective-permute-start | bytes 12296 | tf_op jit(solution)/shard_map/ppermute | solution.py:496
  4.9 43.1 %copy-start.4 = (s32[32,8]{0,1:T(8,128)S(1)}, s32[32,8]{0,1:T(8,128)}, u32[]{:S(2)}) copy-start(s32[32,8]{0,1:T(8,128)} %param.15) | copy-start | bytes 3076
  4.9 43.1 %copy-start.5 = (f32[64]{0:T(128)S(1)}, f32[64]{0:T(128)}, u32[]{:S(2)}) copy-start(f32[64]{0:T(128)} %param.16) | copy-start | bytes 772
  4.9 43.1 %copy-start.6 = (f32[32]{0:T(128)S(1)}, f32[32]{0:T(128)}, u32[]{:S(2)}) copy-start(f32[32]{0:T(128)} %param.17) | copy-start | bytes 388
  33.5 6.2 %collective-permute-start.1 = (f32[112,128]{1,0:T(8,128)S(1)}, f32[112,128]{1,0:T(8,128)S(1)}, u32[]{:S(2)}, u32[]{:S(2)}) collective-permute-start(f32[112,128]{1,0:T(8,128)S(1)} %get-tuple-element.70), channel_id=1, source_target_pairs={{0,2},{2,0},{1,3},{3,1},{4,6},{6,4},{5,7},{7,5},{8,10},{10,8},{9,1... | collective-permute-start | bytes 172040 | tf_op jit(solution)/shard_map/ppermute | solution.py:537
  34.2 3.8 %collective-permute-start.3 = (f32[40,128]{1,0:T(8,128)S(1)}, f32[40,128]{1,0:T(8,128)S(1)}, u32[]{:S(2)}, u32[]{:S(2)}) collective-permute-start(f32[40,128]{1,0:T(8,128)S(1)} %get-tuple-element.69), channel_id=1, source_target_pairs={{0,128},{128,0},{1,129},{129,1},{2,130},{130,2},{3,131},{131,3},{4... | collective-permute-start | bytes 61448 | tf_op jit(solution)/shard_map/ppermute | solution.py:538
  34.7 5.0 %collective-permute-start.4 = (f32[40,128]{1,0:T(8,128)S(1)}, f32[40,128]{1,0:T(8,128)S(1)}, u32[]{:S(2)}, u32[]{:S(2)}) collective-permute-start(f32[40,128]{1,0:T(8,128)S(1)} %get-tuple-element.69), channel_id=1, source_target_pairs={{0,130},{130,0},{2,128},{128,2},{1,131},{131,1},{3,129},{129,3},{4... | collective-permute-start | bytes 61448 | tf_op jit(solution)/shard_map/ppermute | solution.py:539
  39.8 4.2 %collective-permute-start.5 = (f32[80,128]{1,0:T(8,128)S(1)}, f32[80,128]{1,0:T(8,128)S(1)}, u32[]{:S(2)}, u32[]{:S(2)}) collective-permute-start(f32[80,128]{1,0:T(8,128)S(1)} %pad_maximum_fusion.1), channel_id=1, source_target_pairs={{0,32},{32,64},{64,96},{96,0},{1,33},{33,65},{65,97},{97,1},{2,34}... | collective-permute-start | bytes 122888 | tf_op jit(solution)/shard_map/ppermute | solution.py:543
  40.3 5.5 %collective-permute-start.6 = (f32[80,128]{1,0:T(8,128)S(1)}, f32[80,128]{1,0:T(8,128)S(1)}, u32[]{:S(2)}, u32[]{:S(2)}) collective-permute-start(f32[80,128]{1,0:T(8,128)S(1)} %pad_maximum_fusion.1), channel_id=1, source_target_pairs={{0,64},{32,96},{64,0},{96,32},{1,65},{33,97},{65,1},{97,33},{2,66}... | collective-permute-start | bytes 122888 | tf_op jit(solution)/shard_map/ppermute | solution.py:543
  42.7 5.2 %collective-permute-start.7 = (f32[80,128]{1,0:T(8,128)S(1)}, f32[80,128]{1,0:T(8,128)S(1)}, u32[]{:S(2)}, u32[]{:S(2)}) collective-permute-start(f32[80,128]{1,0:T(8,128)S(1)} %pad_maximum_fusion.1), channel_id=1, source_target_pairs={{0,96},{32,0},{64,32},{96,64},{1,97},{33,1},{65,33},{97,65},{2,98}... | collective-permute-start | bytes 122888 | tf_op jit(solution)/shard_map/ppermute | solution.py:543
  42.7 1.2 %collective-permute-start.2 = (f32[8,128]{1,0:T(8,128)S(1)}, f32[8,128]{1,0:T(8,128)S(1)}, u32[]{:S(2)}, u32[]{:S(2)}) collective-permute-start(f32[8,128]{1,0:T(8,128)S(1)} %slice_add_fusion.1), channel_id=1, source_target_pairs={{0,1},{1,0},{2,3},{3,2},{4,5},{5,4},{6,7},{7,6},{8,9},{9,8},{10,11... | collective-permute-start | bytes 12296 | tf_op jit(solution)/shard_map/ppermute | solution.py:546

commit v13 on v12

--- a/solution.py
+++ b/solution.py
@@ -99,7 +99,7 @@
 
 def column_kernel(
     swt_hbm, branch_hbm, weight_hbm, zone_hbm, sens_hbm, pay_ref, meta_ref, extra_ref,
-    swt_ref, branch_ref, weight_ref, zone_ref, sens_ref, rank_ref, chosen_ref, acc_ref,
+    swt_ref, branch_ref, weight_ref, zone_ref, sens_ref, rank_ref, acc_ref,
     coupled_ref, sems
 ):
     rows, cols = sens_ref.shape
@@ -181,13 +181,31 @@
     over = over + jnp.where(most >= SLOTS, 1.0, 0.0)
     ids = iota((SLOTS, LANES), 0)
     slot_id = ids.astype(jnp.float32)
-    slot_weight = jnp.zeros((SLOTS, LANES), jnp.float32)
-    slot_zone = jnp.zeros((SLOTS, LANES), jnp.float32)
-    for at in range(lines):
-        match = rank_ref[at:at + 1, :] == slot_id
-        slot_weight += jnp.where(match, weight_ref[at:at + 1, :], 0.0)
-        slot_zone += jnp.where(match, zone_ref[at:at + 1, :].astype(jnp.float32), 0.0)
-        chosen_ref[:, at * LANES:(at + 1) * LANES] = jnp.where(match, 1.0, 0.0).astype(bf16)
+    choose = iota((SLOTS, rows), 1) == slot_row.astype(jnp.int32)
+    choose = jnp.where(choose, 1.0, 0.0).astype(bf16)
+    lane = iota((SLOTS, BLOCK), 1)
+
+    def select(buses, step):
+        return jnp.where(lane == buses - step * BLOCK, 1.0, 0.0).astype(bf16)
+
+    def step_body(step, sums):
+        at = pl.ds(pl.multiple_of(step * BLOCK, BLOCK), BLOCK)
+        slot_weight, slot_zone = sums
+        chosen = []
+        for part in range(BLOCK // LANES):
+            line = pl.ds(step * (BLOCK // LANES) + part, 1)
+            match = rank_ref[line, :] == slot_id
+            slot_weight += jnp.where(match, weight_ref[line, :], 0.0)
+            slot_zone += jnp.where(match, zone_ref[line, :].astype(jnp.float32), 0.0)
+            chosen.append(jnp.where(match, 1.0, 0.0).astype(bf16))
+        chosen = jnp.concatenate(chosen, axis=1)
+        chosen = jnp.concatenate([select(first_buses, step), chosen], axis=0)
+        block_copy(step).wait()
+        acc_ref[...] += dot_nt(sens_ref[:, at], chosen)
+        return slot_weight, slot_zone
+
+    zeros = jnp.zeros((SLOTS, LANES), jnp.float32)
+    slot_weight, slot_zone = lax.fori_loop(0, steps, step_body, (zeros, zeros))
     eye = ids + HALF == iota((SLOTS, LANES), 1)
     slot_weight, slot_zone = [
         jnp.sum(
@@ -195,21 +213,6 @@
         )
         for x in (slot_weight, slot_zone)
     ]
-    choose = iota((SLOTS, rows), 1) == slot_row.astype(jnp.int32)
-    choose = jnp.where(choose, 1.0, 0.0).astype(bf16)
-    lane = iota((SLOTS, BLOCK), 1)
-
-    def select(buses, step):
-        return jnp.where(lane == buses - step * BLOCK, 1.0, 0.0).astype(bf16)
-
-    def step_body(step, carry):
-        at = pl.ds(pl.multiple_of(step * BLOCK, BLOCK), BLOCK)
-        chosen = jnp.concatenate([select(first_buses, step), chosen_ref[:, at]], axis=0)
-        block_copy(step).wait()
-        acc_ref[...] += dot_nt(sens_ref[:, at], chosen)
-        return carry
-
-    lax.fori_loop(0, steps, step_body, 0)
 
     def coupled_of(columns, group):
         slots = [slot[:, at * picks:(at + 1) * picks] - group * SLOTS for at in (0, 1)]
@@ -509,7 +512,6 @@
             *bus_scratch,
             pltpu.VMEM((rows, cols), jnp.bfloat16),
             pltpu.VMEM((cols // LANES, LANES), f32),
-            pltpu.VMEM((SLOTS, cols), jnp.bfloat16),
             pltpu.VMEM((rows, 2 * SLOTS), f32),
             pltpu.VMEM((SLOTS, picks), f32),
             pltpu.SemaphoreType.DMA((cols // BLOCK + 4,)),

time: 51.2 us -> 50.9 us (level)
  no operation moved by 1% of the time
where the time goes in v13:
time: 50.9 us; the launch traced here: 50.3 us
  blocking collectives  22 us (43%)
  Pallas kernels  10.2 us (20%)
  starting transfers between devices  10.2 us (20%)
  waiting for transfers between devices  6.01 us (12%)
  between operations  1.38 us (3%)
  local copies, waits for them, and re-layouts  0.6 us (1%)
    all_to_all x1, blocking collectives, body(): parts = lax.all_to_all(pay, 'z', 0, 0, tiled=True)  22 us
    pallas_call x1, Pallas kernels, body(): pl.pallas_call(column_kernel, out_shape=(jax.ShapeDtypeStruct((n_z, SUMME...  5.84 us
    ppermute x3, waiting for transfers between devices, body(): lax.ppermute(here, 'x', [(at, (at + by) % n_x) for at in range(n_x)])  3.95 us
    ppermute x1, starting transfers between devices, body(): totals = totals + lax.ppermute(totals, ('yl', 'yh'), turn)  3.1 us
    ppermute x1, starting transfers between devices, body(): across = lax.ppermute(block, ('yl', 'yh'), turn)  2.94 us
    ppermute x3, starting transfers between devices, body(): lax.ppermute(here, 'x', [(at, (at + by) % n_x) for at in range(n_x)])  2.9 us
    pallas_call x1, Pallas kernels, compact(): pl.pallas_call(final_kernel, out_shape=(jax.ShapeDtypeStruct((actions, sh...  2.7 us
    ppermute x1, waiting for transfers between devices, body(): across = lax.ppermute(block, ('yl', 'yh'), turn)  1.8 us
  transfers between devices with their start and end apart: 8, of which 4 were waited for; matrix products, arithmetic and copies ran while one was open for 1% of the time, Pallas kernels for 12%

profile of v13, /device:TPU:6, one launch (start us, length us, event | category | flops | bytes accessed | tf_op | source)
XLA Modules:
  0.0 50.3 jit_solution(12909335554401964391)
XLA Ops:
  0.6 1.1 %totals.1 = f32[8,128]{1,0:T(8,128)S(1)} custom-call(f32[64,128]{1,0:T(8,128)} %bitcast.190, s32[64,128]{1,0:T(8,128)} %bitcast.192), custom_call_target="tpu_custom_call" | custom-call | tf_op jit(solution)/shard_map/totals/pallas_call | solution.py:488
  1.8 3.1 %collective-permute-start = (f32[8,128]{1,0:T(8,128)S(1)}, f32[8,128]{1,0:T(8,128)S(1)}, u32[]{:S(2)}, u32[]{:S(2)}) collective-permute-start(f32[8,128]{1,0:T(8,128)S(1)} %totals.1), channel_id=1, source_target_pairs={{0,130},{130,0},{2,128},{128,2},{1,131},{131,1},{3,129},{129,3},{4... | collective-permute-start | bytes 12296 | tf_op jit(solution)/shard_map/ppermute | solution.py:499
  4.9 0.0 copy-start.4
  4.9 0.0 copy-start.5
  4.9 0.0 copy-start.6
  4.9 5.8 %columns.1 = (f32[8,88,128]{2,1,0:T(8,128)S(1)}, f32[8,512]{1,0:T(8,128)S(1)}, f32[8,128]{1,0:T(8,128)S(1)}) custom-call(s32[8,32]{1,0:T(8,128)} %bitcast.213, s32[2,4096]{1,0:T(2,128)} %branch_hbm.1, f32[64,128]{1,0:T(8,128)} %bitcast.191, s32[64,128]{1,0:T(8,128)} %bitcast.193, bf16[512,8192]{1,0:T(8,128)(2,1)} %sens_hbm.1), custom_call_target="tpu_custom_call" | custom-call | tf_op jit(solution)/shard_map/columns/pallas_call | solution.py:500
  10.7 0.0 collective-permute-done
  10.8 22.0 %all_to_all.26.parts_ref = f32[8,88,128]{2,1,0:T(8,128)S(1)} all-to-all(f32[8,88,128]{2,1,0:T(8,128)S(1)} %broadcast_dynamic-update-slice_fusion), channel_id=1, replica_groups=mesh['yl'=2,'x'=4,'z'=8,'yh'=2,'act'=2] {'z'}, dimensions={0} | all-to-all | bytes 720896 | tf_op jit(solution)/shard_map/all_to_all | solution.py:526
  32.7 0.5 %place.1 = (f32[72,128]{1,0:T(8,128)S(1)}, f32[112,128]{1,0:T(8,128)S(1)}, f32[40,128]{1,0:T(8,128)S(1)}) custom-call(f32[8,88,128]{2,1,0:T(8,128)S(1)} %all_to_all.26.parts_ref, f32[8,512]{1,0:T(8,128)S(1)} %get-tuple-element.68.meta_ref), custom_call_target="tpu_custom_call" | custom-call | tf_op jit(solution)/shard_map/place/pallas_call | solution.py:527
  33.2 0.6 %collective-permute-start.1 = (f32[112,128]{1,0:T(8,128)S(1)}, f32[112,128]{1,0:T(8,128)S(1)}, u32[]{:S(2)}, u32[]{:S(2)}) collective-permute-start(f32[112,128]{1,0:T(8,128)S(1)} %get-tuple-element.70), channel_id=1, source_target_pairs={{0,2},{2,0},{1,3},{3,1},{4,6},{6,4},{5,7},{7,5},{8,10},{10,8},{9,1... | collective-permute-start | bytes 172040 | tf_op jit(solution)/shard_map/ppermute | solution.py:539
  33.9 0.6 %collective-permute-start.3 = (f32[40,128]{1,0:T(8,128)S(1)}, f32[40,128]{1,0:T(8,128)S(1)}, u32[]{:S(2)}, u32[]{:S(2)}) collective-permute-start(f32[40,128]{1,0:T(8,128)S(1)} %get-tuple-element.69), channel_id=1, source_target_pairs={{0,128},{128,0},{1,129},{129,1},{2,130},{130,2},{3,131},{131,3},{4... | collective-permute-start | bytes 61448 | tf_op jit(solution)/shard_map/ppermute | solution.py:540
  34.5 2.9 %collective-permute-start.4 = (f32[40,128]{1,0:T(8,128)S(1)}, f32[40,128]{1,0:T(8,128)S(1)}, u32[]{:S(2)}, u32[]{:S(2)}) collective-permute-start(f32[40,128]{1,0:T(8,128)S(1)} %get-tuple-element.69), channel_id=1, source_target_pairs={{0,130},{130,0},{2,128},{128,2},{1,131},{131,1},{3,129},{129,3},{4... | collective-permute-start | bytes 61448 | tf_op jit(solution)/shard_map/ppermute | solution.py:541
  37.4 0.2 collective-permute-done.3
  37.7 1.8 %collective-permute-done.4 = f32[40,128]{1,0:T(8,128)S(1)} collective-permute-done((f32[40,128]{1,0:T(8,128)S(1)}, f32[40,128]{1,0:T(8,128)S(1)}, u32[]{:S(2)}, u32[]{:S(2)}) %collective-permute-start.4) | collective-permute-done | bytes 20512 | tf_op jit(solution)/shard_map/ppermute | solution.py:541
  39.5 0.0 collective-permute-done.1
  39.5 0.6 %collective-permute-start.5 = (f32[80,128]{1,0:T(8,128)S(1)}, f32[80,128]{1,0:T(8,128)S(1)}, u32[]{:S(2)}, u32[]{:S(2)}) collective-permute-start(f32[80,128]{1,0:T(8,128)S(1)} %pad_maximum_fusion.1), channel_id=1, source_target_pairs={{0,32},{32,64},{64,96},{96,0},{1,33},{33,65},{65,97},{97,1},{2,34}... | collective-permute-start | bytes 122888 | tf_op jit(solution)/shard_map/ppermute | solution.py:545
  40.1 2.3 %collective-permute-start.6 = (f32[80,128]{1,0:T(8,128)S(1)}, f32[80,128]{1,0:T(8,128)S(1)}, u32[]{:S(2)}, u32[]{:S(2)}) collective-permute-start(f32[80,128]{1,0:T(8,128)S(1)} %pad_maximum_fusion.1), channel_id=1, source_target_pairs={{0,64},{32,96},{64,0},{96,32},{1,65},{33,97},{65,1},{97,33},{2,66}... | collective-permute-start | bytes 122888 | tf_op jit(solution)/shard_map/ppermute | solution.py:545
  42.4 0.0 collective-permute-start.7
  42.4 0.0 collective-permute-start.2
  42.4 0.6 %slice.176 = f32[1,1]{1,0:T(1,128)} slice(f32[40,128]{1,0:T(8,128)S(1)} %slice_add_fusion), slice={[35:36], [64:65]} | slice | bytes 8 | tf_op jit(solution)/shard_map/slice | solution.py:574
  43.7 0.0 collective-permute-done.2
  43.7 0.0 collective-permute-done.5
  43.7 1.9 %collective-permute-done.6 = f32[80,128]{1,0:T(8,128)S(1)} collective-permute-done((f32[80,128]{1,0:T(8,128)S(1)}, f32[80,128]{1,0:T(8,128)S(1)}, u32[]{:S(2)}, u32[]{:S(2)}) %collective-permute-start.6) | collective-permute-done | bytes 40992 | tf_op jit(solution)/shard_map/ppermute | solution.py:545
  45.6 2.0 %collective-permute-done.7 = f32[80,128]{1,0:T(8,128)S(1)} collective-permute-done((f32[80,128]{1,0:T(8,128)S(1)}, f32[80,128]{1,0:T(8,128)S(1)}, u32[]{:S(2)}, u32[]{:S(2)}) %collective-permute-start.7) | collective-permute-done | bytes 40992 | tf_op jit(solution)/shard_map/ppermute | solution.py:545
  47.6 0.0 copy-done.4
  47.6 0.0 copy-done.5
  47.6 0.0 copy-done.6
  47.6 2.7 %conditional.1 = ((f32[32,32,64]{2,1,0:T(8,128)}, f32[32,32]{1,0:T(8,128)}, f32[32,32]{1,0:T(8,128)})) conditional(s32[]{:T(128)} %bitcast.59, (f32[64]{0:T(128)S(1)}, f32[32]{0:T(128)S(1)}, f32[8,512]{1,0:T(8,128)S(1)}, f32[72,128]{1,0:T(8,128)S(1)}, f32[112,128]{1,0:T(8,128)S(1)}, /*index=5*/f32[8,128]{1,0:T(8,128)S(1)}, f32[80,128]{1,0:T(8,128)S(1)}, ...), branch_computations={%region_0.0_spmd, %region_1.10_spmd} | conditional | flops 551126016 | bytes 46937896 | solution.py:574
  47.6 2.7 %update.1 = (f32[32,32,64]{2,1,0:T(8,128)}, f32[32,32]{1,0:T(8,128)}, f32[32,32]{1,0:T(8,128)}) custom-call(f32[8,512]{1,0:T(8,128)S(1)} %get-tuple-element.26.meta_ref, f32[72,128]{1,0:T(8,128)S(1)} %get-tuple-element.36.mine_ref, f32[112,128]{1,0:T(8,128)S(1)} %get-tuple-element.37.theirs_ref, f32[8,128]{1,0:T(8,128)S(1)} %get-tuple-element.38.other_ref, ...), custom_call_target="tpu_custom_call" | custom-call | tf_op jit(solution)/shard_map/cond/branch_0_fun/update/pallas_call | solution.py:553
  (6 shorter events, 0.0 us)
Async XLA Ops:
  1.8 9.0 %collective-permute-start = (f32[8,128]{1,0:T(8,128)S(1)}, f32[8,128]{1,0:T(8,128)S(1)}, u32[]{:S(2)}, u32[]{:S(2)}) collective-permute-start(f32[8,128]{1,0:T(8,128)S(1)} %totals.1), channel_id=1, source_target_pairs={{0,130},{130,0},{2,128},{128,2},{1,131},{131,1},{3,129},{129,3},{4... | collective-permute-start | bytes 12296 | tf_op jit(solution)/shard_map/ppermute | solution.py:499
  4.9 42.8 %copy-start.4 = (s32[32,8]{0,1:T(8,128)S(1)}, s32[32,8]{0,1:T(8,128)}, u32[]{:S(2)}) copy-start(s32[32,8]{0,1:T(8,128)} %param.15) | copy-start | bytes 3076
  4.9 42.8 %copy-start.5 = (f32[64]{0:T(128)S(1)}, f32[64]{0:T(128)}, u32[]{:S(2)}) copy-start(f32[64]{0:T(128)} %param.16) | copy-start | bytes 772
  4.9 42.8 %copy-start.6 = (f32[32]{0:T(128)S(1)}, f32[32]{0:T(128)}, u32[]{:S(2)}) copy-start(f32[32]{0:T(128)} %param.17) | copy-start | bytes 388
  33.2 6.2 %collective-permute-start.1 = (f32[112,128]{1,0:T(8,128)S(1)}, f32[112,128]{1,0:T(8,128)S(1)}, u32[]{:S(2)}, u32[]{:S(2)}) collective-permute-start(f32[112,128]{1,0:T(8,128)S(1)} %get-tuple-element.70), channel_id=1, source_target_pairs={{0,2},{2,0},{1,3},{3,1},{4,6},{6,4},{5,7},{7,5},{8,10},{10,8},{9,1... | collective-permute-start | bytes 172040 | tf_op jit(solution)/shard_map/ppermute | solution.py:539
  33.9 3.8 %collective-permute-start.3 = (f32[40,128]{1,0:T(8,128)S(1)}, f32[40,128]{1,0:T(8,128)S(1)}, u32[]{:S(2)}, u32[]{:S(2)}) collective-permute-start(f32[40,128]{1,0:T(8,128)S(1)} %get-tuple-element.69), channel_id=1, source_target_pairs={{0,128},{128,0},{1,129},{129,1},{2,130},{130,2},{3,131},{131,3},{4... | collective-permute-start | bytes 61448 | tf_op jit(solution)/shard_map/ppermute | solution.py:540
  34.5 5.0 %collective-permute-start.4 = (f32[40,128]{1,0:T(8,128)S(1)}, f32[40,128]{1,0:T(8,128)S(1)}, u32[]{:S(2)}, u32[]{:S(2)}) collective-permute-start(f32[40,128]{1,0:T(8,128)S(1)} %get-tuple-element.69), channel_id=1, source_target_pairs={{0,130},{130,0},{2,128},{128,2},{1,131},{131,1},{3,129},{129,3},{4... | collective-permute-start | bytes 61448 | tf_op jit(solution)/shard_map/ppermute | solution.py:541
  39.5 4.2 %collective-permute-start.5 = (f32[80,128]{1,0:T(8,128)S(1)}, f32[80,128]{1,0:T(8,128)S(1)}, u32[]{:S(2)}, u32[]{:S(2)}) collective-permute-start(f32[80,128]{1,0:T(8,128)S(1)} %pad_maximum_fusion.1), channel_id=1, source_target_pairs={{0,32},{32,64},{64,96},{96,0},{1,33},{33,65},{65,97},{97,1},{2,34}... | collective-permute-start | bytes 122888 | tf_op jit(solution)/shard_map/ppermute | solution.py:545
  40.1 5.5 %collective-permute-start.6 = (f32[80,128]{1,0:T(8,128)S(1)}, f32[80,128]{1,0:T(8,128)S(1)}, u32[]{:S(2)}, u32[]{:S(2)}) collective-permute-start(f32[80,128]{1,0:T(8,128)S(1)} %pad_maximum_fusion.1), channel_id=1, source_target_pairs={{0,64},{32,96},{64,0},{96,32},{1,65},{33,97},{65,1},{97,33},{2,66}... | collective-permute-start | bytes 122888 | tf_op jit(solution)/shard_map/ppermute | solution.py:545
  42.4 5.2 %collective-permute-start.7 = (f32[80,128]{1,0:T(8,128)S(1)}, f32[80,128]{1,0:T(8,128)S(1)}, u32[]{:S(2)}, u32[]{:S(2)}) collective-permute-start(f32[80,128]{1,0:T(8,128)S(1)} %pad_maximum_fusion.1), channel_id=1, source_target_pairs={{0,96},{32,0},{64,32},{96,64},{1,97},{33,1},{65,33},{97,65},{2,98}... | collective-permute-start | bytes 122888 | tf_op jit(solution)/shard_map/ppermute | solution.py:545
  42.4 1.2 %collective-permute-start.2 = (f32[8,128]{1,0:T(8,128)S(1)}, f32[8,128]{1,0:T(8,128)S(1)}, u32[]{:S(2)}, u32[]{:S(2)}) collective-permute-start(f32[8,128]{1,0:T(8,128)S(1)} %slice_add_fusion.1), channel_id=1, source_target_pairs={{0,1},{1,0},{2,3},{3,2},{4,5},{5,4},{6,7},{7,6},{8,9},{9,8},{10,11... | collective-permute-start | bytes 12296 | tf_op jit(solution)/shard_map/ppermute | solution.py:548

commit v14 on v13

--- a/solution.py
+++ b/solution.py
@@ -10,7 +10,7 @@
 LANES = 128
 HALF = 64
 SUB = 8
-BLOCK = 2048
+BLOCK = 1024
 SLOTS = 64
 BLOCK_ROWS = SLOTS // 2 + SUB
 SUMMED = 2 * SUB + BLOCK_ROWS

time: 50.9 us -> 51.6 us (1.014)
  Pallas kernels: 10.2 us -> 10.8 us
    pallas_call x1, Pallas kernels: 5.84 us -> 6.43 us  [body(): pl.pallas_call(column_kernel, out_shape=(jax.ShapeDtypeStruct((n_z, SUMME...]
  transfers between devices with their start and end apart: 8 -> 8, of which waited for: 4 -> 4; matrix products, arithmetic and copies ran while one was open for 1% -> 1% of each run, Pallas kernels for 12% -> 13%
where the time goes in v14:
time: 51.6 us; the launch traced here: 51 us
  blocking collectives  22 us (43%)
  Pallas kernels  10.8 us (21%)
  starting transfers between devices  10.3 us (20%)
  waiting for transfers between devices  6.01 us (12%)
  between operations  1.38 us (3%)
  local copies, waits for them, and re-layouts  0.6 us (1%)
    all_to_all x1, blocking collectives, body(): parts = lax.all_to_all(pay, 'z', 0, 0, tiled=True)  22 us
    pallas_call x1, Pallas kernels, body(): pl.pallas_call(column_kernel, out_shape=(jax.ShapeDtypeStruct((n_z, SUMME...  6.43 us
    ppermute x3, waiting for transfers between devices, body(): lax.ppermute(here, 'x', [(at, (at + by) % n_x) for at in range(n_x)])  3.95 us
    ppermute x1, starting transfers between devices, body(): totals = totals + lax.ppermute(totals, ('yl', 'yh'), turn)  3.1 us
    ppermute x3, starting transfers between devices, body(): lax.ppermute(here, 'x', [(at, (at + by) % n_x) for at in range(n_x)])  2.98 us
    ppermute x1, starting transfers between devices, body(): across = lax.ppermute(block, ('yl', 'yh'), turn)  2.94 us
    pallas_call x1, Pallas kernels, compact(): pl.pallas_call(final_kernel, out_shape=(jax.ShapeDtypeStruct((actions, sh...  2.69 us
    ppermute x1, waiting for transfers between devices, body(): across = lax.ppermute(block, ('yl', 'yh'), turn)  1.73 us
  transfers between devices with their start and end apart: 8, of which 4 were waited for; matrix products, arithmetic and copies ran while one was open for 1% of the time, Pallas kernels for 13%

profile of v14, /device:TPU:6, one launch (start us, length us, event | category | flops | bytes accessed | tf_op | source)
XLA Modules:
  0.0 51.0 jit_solution(2703121632869466360)
XLA Ops:
  0.6 1.1 %totals.1 = f32[8,128]{1,0:T(8,128)S(1)} custom-call(f32[64,128]{1,0:T(8,128)} %bitcast.190, s32[64,128]{1,0:T(8,128)} %bitcast.192), custom_call_target="tpu_custom_call" | custom-call | tf_op jit(solution)/shard_map/totals/pallas_call | solution.py:488
  1.8 3.1 %collective-permute-start = (f32[8,128]{1,0:T(8,128)S(1)}, f32[8,128]{1,0:T(8,128)S(1)}, u32[]{:S(2)}, u32[]{:S(2)}) collective-permute-start(f32[8,128]{1,0:T(8,128)S(1)} %totals.1), channel_id=1, source_target_pairs={{0,130},{130,0},{2,128},{128,2},{1,131},{131,1},{3,129},{129,3},{4... | collective-permute-start | bytes 12296 | tf_op jit(solution)/shard_map/ppermute | solution.py:499
  4.9 0.0 copy-start.4
  4.9 0.0 copy-start.5
  4.9 0.0 copy-start.6
  4.9 6.4 %columns.1 = (f32[8,88,128]{2,1,0:T(8,128)S(1)}, f32[8,512]{1,0:T(8,128)S(1)}, f32[8,128]{1,0:T(8,128)S(1)}) custom-call(s32[8,32]{1,0:T(8,128)} %bitcast.213, s32[2,4096]{1,0:T(2,128)} %branch_hbm.1, f32[64,128]{1,0:T(8,128)} %bitcast.191, s32[64,128]{1,0:T(8,128)} %bitcast.193, bf16[512,8192]{1,0:T(8,128)(2,1)} %sens_hbm.1), custom_call_target="tpu_custom_call" | custom-call | tf_op jit(solution)/shard_map/columns/pallas_call | solution.py:500
  11.3 0.0 collective-permute-done
  11.3 22.0 %all_to_all.26.parts_ref = f32[8,88,128]{2,1,0:T(8,128)S(1)} all-to-all(f32[8,88,128]{2,1,0:T(8,128)S(1)} %broadcast_dynamic-update-slice_fusion), channel_id=1, replica_groups=mesh['yl'=2,'x'=4,'z'=8,'yh'=2,'act'=2] {'z'}, dimensions={0} | all-to-all | bytes 720896 | tf_op jit(solution)/shard_map/all_to_all | solution.py:526
  33.3 0.5 %place.1 = (f32[72,128]{1,0:T(8,128)S(1)}, f32[112,128]{1,0:T(8,128)S(1)}, f32[40,128]{1,0:T(8,128)S(1)}) custom-call(f32[8,88,128]{2,1,0:T(8,128)S(1)} %all_to_all.26.parts_ref, f32[8,512]{1,0:T(8,128)S(1)} %get-tuple-element.68.meta_ref), custom_call_target="tpu_custom_call" | custom-call | tf_op jit(solution)/shard_map/place/pallas_call | solution.py:527
  33.8 0.7 %collective-permute-start.1 = (f32[112,128]{1,0:T(8,128)S(1)}, f32[112,128]{1,0:T(8,128)S(1)}, u32[]{:S(2)}, u32[]{:S(2)}) collective-permute-start(f32[112,128]{1,0:T(8,128)S(1)} %get-tuple-element.70), channel_id=1, source_target_pairs={{0,2},{2,0},{1,3},{3,1},{4,6},{6,4},{5,7},{7,5},{8,10},{10,8},{9,1... | collective-permute-start | bytes 172040 | tf_op jit(solution)/shard_map/ppermute | solution.py:539
  34.6 0.5 %collective-permute-start.3 = (f32[40,128]{1,0:T(8,128)S(1)}, f32[40,128]{1,0:T(8,128)S(1)}, u32[]{:S(2)}, u32[]{:S(2)}) collective-permute-start(f32[40,128]{1,0:T(8,128)S(1)} %get-tuple-element.69), channel_id=1, source_target_pairs={{0,128},{128,0},{1,129},{129,1},{2,130},{130,2},{3,131},{131,3},{4... | collective-permute-start | bytes 61448 | tf_op jit(solution)/shard_map/ppermute | solution.py:540
  35.1 2.9 %collective-permute-start.4 = (f32[40,128]{1,0:T(8,128)S(1)}, f32[40,128]{1,0:T(8,128)S(1)}, u32[]{:S(2)}, u32[]{:S(2)}) collective-permute-start(f32[40,128]{1,0:T(8,128)S(1)} %get-tuple-element.69), channel_id=1, source_target_pairs={{0,130},{130,0},{2,128},{128,2},{1,131},{131,1},{3,129},{129,3},{4... | collective-permute-start | bytes 61448 | tf_op jit(solution)/shard_map/ppermute | solution.py:541
  38.0 0.3 collective-permute-done.3
  38.3 1.7 %collective-permute-done.4 = f32[40,128]{1,0:T(8,128)S(1)} collective-permute-done((f32[40,128]{1,0:T(8,128)S(1)}, f32[40,128]{1,0:T(8,128)S(1)}, u32[]{:S(2)}, u32[]{:S(2)}) %collective-permute-start.4) | collective-permute-done | bytes 20512 | tf_op jit(solution)/shard_map/ppermute | solution.py:541
  40.1 0.0 collective-permute-done.1
  40.1 0.6 %collective-permute-start.5 = (f32[80,128]{1,0:T(8,128)S(1)}, f32[80,128]{1,0:T(8,128)S(1)}, u32[]{:S(2)}, u32[]{:S(2)}) collective-permute-start(f32[80,128]{1,0:T(8,128)S(1)} %pad_maximum_fusion.1), channel_id=1, source_target_pairs={{0,32},{32,64},{64,96},{96,0},{1,33},{33,65},{65,97},{97,1},{2,34}... | collective-permute-start | bytes 122888 | tf_op jit(solution)/shard_map/ppermute | solution.py:545
  40.7 2.4 %collective-permute-start.6 = (f32[80,128]{1,0:T(8,128)S(1)}, f32[80,128]{1,0:T(8,128)S(1)}, u32[]{:S(2)}, u32[]{:S(2)}) collective-permute-start(f32[80,128]{1,0:T(8,128)S(1)} %pad_maximum_fusion.1), channel_id=1, source_target_pairs={{0,64},{32,96},{64,0},{96,32},{1,65},{33,97},{65,1},{97,33},{2,66}... | collective-permute-start | bytes 122888 | tf_op jit(solution)/shard_map/ppermute | solution.py:545
  43.1 0.0 collective-permute-start.7
  43.1 0.0 collective-permute-start.2
  43.1 0.6 %slice.176 = f32[1,1]{1,0:T(1,128)} slice(f32[40,128]{1,0:T(8,128)S(1)} %slice_add_fusion), slice={[35:36], [64:65]} | slice | bytes 8 | tf_op jit(solution)/shard_map/slice | solution.py:574
  44.3 0.0 collective-permute-done.2
  44.3 0.0 collective-permute-done.5
  44.4 1.8 %collective-permute-done.6 = f32[80,128]{1,0:T(8,128)S(1)} collective-permute-done((f32[80,128]{1,0:T(8,128)S(1)}, f32[80,128]{1,0:T(8,128)S(1)}, u32[]{:S(2)}, u32[]{:S(2)}) %collective-permute-start.6) | collective-permute-done | bytes 40992 | tf_op jit(solution)/shard_map/ppermute | solution.py:545
  46.2 2.1 %collective-permute-done.7 = f32[80,128]{1,0:T(8,128)S(1)} collective-permute-done((f32[80,128]{1,0:T(8,128)S(1)}, f32[80,128]{1,0:T(8,128)S(1)}, u32[]{:S(2)}, u32[]{:S(2)}) %collective-permute-start.7) | collective-permute-done | bytes 40992 | tf_op jit(solution)/shard_map/ppermute | solution.py:545
  48.3 0.0 copy-done.4
  48.3 0.0 copy-done.5
  48.3 0.0 copy-done.6
  48.3 2.7 %conditional.1 = ((f32[32,32,64]{2,1,0:T(8,128)}, f32[32,32]{1,0:T(8,128)}, f32[32,32]{1,0:T(8,128)})) conditional(s32[]{:T(128)} %bitcast.59, (f32[64]{0:T(128)S(1)}, f32[32]{0:T(128)S(1)}, f32[8,512]{1,0:T(8,128)S(1)}, f32[72,128]{1,0:T(8,128)S(1)}, f32[112,128]{1,0:T(8,128)S(1)}, /*index=5*/f32[8,128]{1,0:T(8,128)S(1)}, f32[80,128]{1,0:T(8,128)S(1)}, ...), branch_computations={%region_0.0_spmd, %region_1.10_spmd} | conditional | flops 551126016 | bytes 46937896 | solution.py:574
  48.3 2.7 %update.1 = (f32[32,32,64]{2,1,0:T(8,128)}, f32[32,32]{1,0:T(8,128)}, f32[32,32]{1,0:T(8,128)}) custom-call(f32[8,512]{1,0:T(8,128)S(1)} %get-tuple-element.26.meta_ref, f32[72,128]{1,0:T(8,128)S(1)} %get-tuple-element.36.mine_ref, f32[112,128]{1,0:T(8,128)S(1)} %get-tuple-element.37.theirs_ref, f32[8,128]{1,0:T(8,128)S(1)} %get-tuple-element.38.other_ref, ...), custom_call_target="tpu_custom_call" | custom-call | tf_op jit(solution)/shard_map/cond/branch_0_fun/update/pallas_call | solution.py:553
  (6 shorter events, 0.0 us)
Async XLA Ops:
  1.8 9.6 %collective-permute-start = (f32[8,128]{1,0:T(8,128)S(1)}, f32[8,128]{1,0:T(8,128)S(1)}, u32[]{:S(2)}, u32[]{:S(2)}) collective-permute-start(f32[8,128]{1,0:T(8,128)S(1)} %totals.1), channel_id=1, source_target_pairs={{0,130},{130,0},{2,128},{128,2},{1,131},{131,1},{3,129},{129,3},{4... | collective-permute-start | bytes 12296 | tf_op jit(solution)/shard_map/ppermute | solution.py:499
  4.9 43.4 %copy-start.4 = (s32[32,8]{0,1:T(8,128)S(1)}, s32[32,8]{0,1:T(8,128)}, u32[]{:S(2)}) copy-start(s32[32,8]{0,1:T(8,128)} %param.15) | copy-start | bytes 3076
  4.9 43.4 %copy-start.5 = (f32[64]{0:T(128)S(1)}, f32[64]{0:T(128)}, u32[]{:S(2)}) copy-start(f32[64]{0:T(128)} %param.16) | copy-start | bytes 772
  4.9 43.4 %copy-start.6 = (f32[32]{0:T(128)S(1)}, f32[32]{0:T(128)}, u32[]{:S(2)}) copy-start(f32[32]{0:T(128)} %param.17) | copy-start | bytes 388
  33.8 6.2 %collective-permute-start.1 = (f32[112,128]{1,0:T(8,128)S(1)}, f32[112,128]{1,0:T(8,128)S(1)}, u32[]{:S(2)}, u32[]{:S(2)}) collective-permute-start(f32[112,128]{1,0:T(8,128)S(1)} %get-tuple-element.70), channel_id=1, source_target_pairs={{0,2},{2,0},{1,3},{3,1},{4,6},{6,4},{5,7},{7,5},{8,10},{10,8},{9,1... | collective-permute-start | bytes 172040 | tf_op jit(solution)/shard_map/ppermute | solution.py:539
  34.6 3.8 %collective-permute-start.3 = (f32[40,128]{1,0:T(8,128)S(1)}, f32[40,128]{1,0:T(8,128)S(1)}, u32[]{:S(2)}, u32[]{:S(2)}) collective-permute-start(f32[40,128]{1,0:T(8,128)S(1)} %get-tuple-element.69), channel_id=1, source_target_pairs={{0,128},{128,0},{1,129},{129,1},{2,130},{130,2},{3,131},{131,3},{4... | collective-permute-start | bytes 61448 | tf_op jit(solution)/shard_map/ppermute | solution.py:540
  35.1 5.0 %collective-permute-start.4 = (f32[40,128]{1,0:T(8,128)S(1)}, f32[40,128]{1,0:T(8,128)S(1)}, u32[]{:S(2)}, u32[]{:S(2)}) collective-permute-start(f32[40,128]{1,0:T(8,128)S(1)} %get-tuple-element.69), channel_id=1, source_target_pairs={{0,130},{130,0},{2,128},{128,2},{1,131},{131,1},{3,129},{129,3},{4... | collective-permute-start | bytes 61448 | tf_op jit(solution)/shard_map/ppermute | solution.py:541
  40.1 4.2 %collective-permute-start.5 = (f32[80,128]{1,0:T(8,128)S(1)}, f32[80,128]{1,0:T(8,128)S(1)}, u32[]{:S(2)}, u32[]{:S(2)}) collective-permute-start(f32[80,128]{1,0:T(8,128)S(1)} %pad_maximum_fusion.1), channel_id=1, source_target_pairs={{0,32},{32,64},{64,96},{96,0},{1,33},{33,65},{65,97},{97,1},{2,34}... | collective-permute-start | bytes 122888 | tf_op jit(solution)/shard_map/ppermute | solution.py:545
  40.7 5.5 %collective-permute-start.6 = (f32[80,128]{1,0:T(8,128)S(1)}, f32[80,128]{1,0:T(8,128)S(1)}, u32[]{:S(2)}, u32[]{:S(2)}) collective-permute-start(f32[80,128]{1,0:T(8,128)S(1)} %pad_maximum_fusion.1), channel_id=1, source_target_pairs={{0,64},{32,96},{64,0},{96,32},{1,65},{33,97},{65,1},{97,33},{2,66}... | collective-permute-start | bytes 122888 | tf_op jit(solution)/shard_map/ppermute | solution.py:545
  43.1 5.2 %collective-permute-start.7 = (f32[80,128]{1,0:T(8,128)S(1)}, f32[80,128]{1,0:T(8,128)S(1)}, u32[]{:S(2)}, u32[]{:S(2)}) collective-permute-start(f32[80,128]{1,0:T(8,128)S(1)} %pad_maximum_fusion.1), channel_id=1, source_target_pairs={{0,96},{32,0},{64,32},{96,64},{1,97},{33,1},{65,33},{97,65},{2,98}... | collective-permute-start | bytes 122888 | tf_op jit(solution)/shard_map/ppermute | solution.py:545
  43.1 1.2 %collective-permute-start.2 = (f32[8,128]{1,0:T(8,128)S(1)}, f32[8,128]{1,0:T(8,128)S(1)}, u32[]{:S(2)}, u32[]{:S(2)}) collective-permute-start(f32[8,128]{1,0:T(8,128)S(1)} %slice_add_fusion.1), channel_id=1, source_target_pairs={{0,1},{1,0},{2,3},{3,2},{4,5},{5,4},{6,7},{7,6},{8,9},{9,8},{10,11... | collective-permute-start | bytes 12296 | tf_op jit(solution)/shard_map/ppermute | solution.py:548
